TPU v7x, 32 devices: a whole 2x2x4 slice. The times are simulated.
32 devices in a mesh: ctx: 16 (over z, y, core), fsdp: 2 (over x).
Axes of the slice: x: 2, y: 2, z: 4, core: 2. Of those that a mesh axis runs over, the one named last changes fastest.
Arguments:
- tokens: bfloat16 [2048, 16384], P(('ctx', 'fsdp')), may hold values from -64 to 64
- queries: bfloat16 [2048, 2048], P(('ctx', 'fsdp')), may hold values from -192 to 192, as said below
- key_weight: bfloat16 [16384, 128], P('fsdp'), may hold values from -0.046875 to 0.046875
- value_weight: bfloat16 [16384, 128], P('fsdp'), may hold values from -0.046875 to 0.046875
Outputs:
- kv_cache: bfloat16 [2048, 256], P(('ctx', 'fsdp'))
- attended: bfloat16 [2048, 2048], P(('ctx', 'fsdp'))
Inputs may be any that keep to these rules, and one draw needn't show every extreme that they name: `queries`: query projections of the same tokens, 16 heads of 128 features each.
All inputs are finite; a program needn't handle non-finite values.
Results may differ from a plain program's by a relative error of at most 0.011.
Values may be sent and summed in bfloat16 or wider, within the bound.
No kernel may reach another device: no remote copies, remote signals or barrier semaphores. Data moves between devices by JAX's collectives and lax.ppermute only.
A program may use at most 64 MiB of HBM per device.

v0:
```python
from functools import partial
import math

import jax
import jax.numpy as jnp
from jax import lax
from jax.sharding import PartitionSpec as P

rope_base = 500000.0
key_block = 1024
floor_value = -1e30


def rotate(vectors, cosine, sine_table):
    middle = vectors.shape[-1] // 2
    leading = vectors[..., :middle]
    back_half = vectors[..., middle:]
    return jnp.concatenate(
        [leading * cosine - back_half * sine_table, back_half * cosine + leading * sine_table],
        axis=-1,
    )


def tables(positions, head_size):
    middle = head_size // 2
    frequency = rope_base ** (-jnp.arange(middle, dtype=jnp.float32) * 2.0 / head_size)
    angles = positions.astype(jnp.float32)[:, None] * frequency[None, :]
    return (jnp.cos(angles), jnp.sin(angles))


def keep_state(state):
    return state


def absorb(state, key_part, value_part, key_pos, query_flat, query_pos, score_scale):
    running_max, denominator, numerator = state
    scores = (
        lax.dot_general(
            query_flat, key_part, (((1,), (1,)), ((), ())), preferred_element_type=jnp.float32
        )
        * score_scale
    )
    allowed = key_pos[None, :] <= query_pos[:, None]
    masked = jnp.where(allowed, scores, floor_value)
    new_max = jnp.maximum(running_max, jnp.max(masked, axis=1))
    weights = jnp.where(allowed, jnp.exp(scores - new_max[:, None]), 0.0)
    factor = jnp.exp(running_max - new_max)
    denominator = denominator * factor + jnp.sum(weights, axis=1)
    numerator = numerator * factor[:, None] + jnp.dot(
        weights.astype(jnp.bfloat16), value_part, preferred_element_type=jnp.float32
    )
    return (new_max, denominator, numerator)


def make_fold(query_groups, head_size, score_scale):

    def fold(states, piece, piece_start):
        length = piece.shape[0]
        block_width = math.gcd(length, key_block)
        blocks = piece.reshape(length // block_width, block_width, piece.shape[1])

        def scan_step(carried, scan_item):
            block_number, key_rows = scan_item
            block_start = block_number * block_width
            key_pos = block_start + jnp.arange(block_width, dtype=jnp.int32)
            key_part = key_rows[:, :head_size]
            value_part = key_rows[:, head_size:]
            updated = []
            for query_group, state in zip(query_groups, carried):
                query_flat, query_pos, last_pos = query_group
                update = partial(
                    absorb,
                    key_part=key_part,
                    value_part=value_part,
                    key_pos=key_pos,
                    query_flat=query_flat,
                    query_pos=query_pos,
                    score_scale=score_scale,
                )
                updated.append(lax.cond(block_start <= last_pos, update, keep_state, state))
            return (tuple(updated), None)

        states, unused = lax.scan(
            scan_step, states, (jnp.arange(length // block_width, dtype=jnp.int32), blocks)
        )
        return states

    return fold


def local(tokens, queries, key_weight, value_weight):
    row_count = tokens.shape[0]
    head_size = key_weight.shape[1]
    head_count = queries.shape[1] // head_size
    score_scale = head_size ** (-0.5)
    key_raw = jnp.dot(
        tokens,
        lax.all_gather(key_weight, "fsdp", axis=0, tiled=True),
        preferred_element_type=jnp.float32,
    )
    value_raw = jnp.dot(
        tokens,
        lax.all_gather(value_weight, "fsdp", axis=0, tiled=True),
        preferred_element_type=jnp.float32,
    )
    device_number = lax.axis_index(("ctx", "fsdp"))
    positions = device_number * row_count + jnp.arange(row_count, dtype=jnp.int32)
    cosine, sine_table = tables(positions, head_size)
    keys_rot = rotate(key_raw, cosine, sine_table).astype(jnp.bfloat16)
    kv_cache = jnp.concatenate([keys_rot, value_raw.astype(jnp.bfloat16)], axis=1)
    rotated = rotate(
        queries.astype(jnp.float32).reshape(row_count, head_count, head_size),
        cosine[:, None, :],
        sine_table[:, None, :],
    ).astype(jnp.bfloat16)

    def fresh(query_group):
        flat_rows = query_group[0].shape[0]
        return (
            jnp.full((flat_rows,), floor_value, jnp.float32),
            jnp.zeros((flat_rows,), jnp.float32),
            jnp.zeros((flat_rows, head_size), jnp.float32),
        )

    query_flat = rotated.reshape(-1, head_size)
    query_pos = jnp.repeat(positions, head_count)
    query_groups = [(query_flat, query_pos, positions[-1])]
    fold = make_fold(query_groups, head_size, score_scale)
    starting = tuple((fresh(query_group) for query_group in query_groups))
    states = fold(
        starting, lax.all_gather(kv_cache, ("ctx", "fsdp"), axis=0, tiled=True), jnp.int32(0)
    )
    running_max, denominator, numerator = states[0]
    attended = (
        (numerator / denominator[:, None])
        .reshape(row_count, head_count * head_size)
        .astype(jnp.bfloat16)
    )
    return (kv_cache, attended)


def solution(mesh):
    placed = (P(("ctx", "fsdp"), None), P(("ctx", "fsdp"), None), P("fsdp", None), P("fsdp", None))
    return jax.shard_map(
        local,
        mesh=mesh,
        in_specs=placed,
        out_specs=(P(("ctx", "fsdp"), None), P(("ctx", "fsdp"), None)),
        check_vma=False,
    )
```

profile of v0, /device:TPU:0, one launch (start us, length us, event | category | flops | bytes accessed | tf_op | source)
XLA Modules:
  0.0 200.7 jit_solution(4397087375606666276)
XLA Ops:
  7.2 0.0 copy-start
  7.2 0.0 all-gather.4.cloned.1.call-start
  7.2 0.7 all-gather.4.cloned.1.call-update
  7.9 0.0 all-gather.6.cloned.1.call-start
  8.0 0.7 all-gather.6.cloned.1.call-update
  8.7 0.0 all-gather.8.cloned.1.call-start
  8.7 60.3 %all-gather.4.cloned.1.call-done = bf16[16384,128]{1,0:T(8,128)(2,1)} async-done(((bf16[8192,128]{1,0:T(8,128)(2,1)}), bf16[16384,128]{1,0:T(8,128)(2,1)}) %all-gather.4.cloned.1.call-update) | async-done | bytes 4194320 | tf_op jit(solution)/shard_map/all_gather | solution.py:98
  69.0 0.0 copy-done
  69.0 3.1 %fusion.18 = f32[64,128]{1,0:T(8,128)S(1)} fusion(bf16[64,16384]{1,0:T(8,128)(2,1)S(1)} %copy-done, bf16[16384,128]{1,0:T(8,128)(2,1)} %all-gather.4.cloned.1.call-done), kind=kOutput, calls=%fused_computation.34 | convolution fusion | flops 268435456 | bytes 6324224 | tf_op jit(solution)/shard_map/dot_general | solution.py:96
  72.1 0.0 copy-start.1
  72.1 0.2 multiply_cosine_fusion
  72.3 55.1 %all-gather.6.cloned.1.call-done = bf16[16384,128]{1,0:T(8,128)(2,1)} async-done(((bf16[8192,128]{1,0:T(8,128)(2,1)}), bf16[16384,128]{1,0:T(8,128)(2,1)}) %all-gather.6.cloned.1.call-update) | async-done | bytes 4194320 | tf_op jit(solution)/shard_map/all_gather | solution.py:103
  127.4 3.0 %convolution_convert_fusion = bf16[64,128]{1,0:T(8,128)(2,1)S(1)} fusion(bf16[64,16384]{1,0:T(8,128)(2,1)S(1)} %copy-done, bf16[16384,128]{1,0:T(8,128)(2,1)} %all-gather.6.cloned.1.call-done), kind=kOutput, calls=%fused_computation.20 | convolution fusion | flops 268443648 | bytes 6307840 | tf_op jit(solution)/shard_map/dot_general | solution.py:101
  130.4 0.7 pad_maximum_fusion.1
  131.1 0.0 all-gather.8.cloned.1.call-update
  131.1 0.0 copy-done.1
  131.2 0.1 copy.6
  131.3 0.6 slice.27
  131.9 0.2 subtract_convert_fusion
  132.1 0.1 pad_maximum_fusion
  132.2 52.8 %all-gather.8.cloned.1.call-done = bf16[2048,256]{1,0:T(8,128)(2,1)} async-done(((bf16[64,256]{1,0:T(8,128)(2,1)}), bf16[2048,256]{1,0:T(8,128)(2,1)}) %all-gather.8.cloned.1.call-update) | async-done | bytes 1048592 | tf_op jit(solution)/shard_map/all_gather | solution.py:131
  185.1 8.1 %while.15 = (s32[]{:T(128)}, f32[1024]{0:T(1024)S(1)}, f32[1024]{0:T(1024)S(1)}, f32[1024,128]{1,0:T(8,128)S(1)}, s32[2]{0:T(128)S(1)}, /*index=5*/s32[]{:T(128)...) while((s32[]{:T(128)}, f32[1024]{0:T(1024)S(1)}, ...), condition=%wide.region_5.6_spmd.clone, body=%wide.region_0.5_spmd.clone.sunk | while | flops 551816192 | bytes 15581723 | solution.py:83
  185.1 0.6 dynamic_slice.13
  186.9 4.4 %conditional.3 = ((f32[1024]{0:T(1024)S(1)}, f32[1024]{0:T(1024)S(1)}, f32[1024,128]{1,0:T(8,128)S(1)})) conditional(s32[]{:T(128)} %convert_element_type.40, (f32[1024]{0:T(1024)S(1)}, f32[1024]{0:T(1024)S(1)}, f32[1024,128]{1,0:T(8,128)S(1)}) %tuple.47, (s32[]{:T(128)}, s32[1024]{0:T(1024)S(1)}, s32[64]{0:T(128)S(1)}, ...), branch_computations={%region_1.1_spmd, %region_2.4_spmd} | conditional | flops 551816192 | bytes 15577384 | solution.py:80
  186.9 0.1 broadcast_in_dim.37
  187.0 0.1 le.18
  187.1 1.1 dynamic-slice_bitcast_fusion
  188.2 0.8 fusion.2
  188.9 1.0 fusion.5
  189.9 1.3 fusion.9
  191.3 0.6 dynamic_slice.13
  193.2 0.2 divide_convert_fusion
  193.4 0.8 convert_element_type.30
  (15 shorter events, 0.1 us)
Async XLA Ops:
  7.2 61.9 %copy-start = (bf16[64,16384]{1,0:T(8,128)(2,1)S(1)}, bf16[64,16384]{1,0:T(8,128)(2,1)}, u32[]{:S(2)}) copy-start(bf16[64,16384]{1,0:T(8,128)(2,1)} %param.8) | copy-start | bytes 6291460
  7.2 61.9 %all-gather.4.cloned.1.call-start = ((), (), s32[]{:S(2)}) async-start(), calls=%async_computation | async-start | bytes 6291456 | tf_op jit(solution)/shard_map/all_gather | solution.py:98
  7.9 119.4 %all-gather.6.cloned.1.call-start = ((), (), s32[]{:S(2)}) async-start(), calls=%async_computation.1 | async-start | bytes 6291456 | tf_op jit(solution)/shard_map/all_gather | solution.py:103
  8.7 176.3 %all-gather.8.cloned.1.call-start = ((), (), s32[]{:S(2)}) async-start(), calls=%async_computation.2 | async-start | bytes 1081344 | tf_op jit(solution)/shard_map/all_gather | solution.py:131
  72.1 59.0 %copy-start.1 = (bf16[64,2048]{1,0:T(8,128)(2,1)S(1)}, bf16[64,2048]{1,0:T(8,128)(2,1)}, u32[]{:S(2)}) copy-start(bf16[64,2048]{1,0:T(8,128)(2,1)} %param.9) | copy-start | bytes 786436
Sparse Core Ops, SparseCore 0:
  9.6 59.4 all-gather.3
  70.6 56.7 all-gather.5
  131.2 53.7 all-gather.7
where the time goes:
time: 203 us; the launch traced here: 201 us
  waiting for transfers between devices  169 us (83%)
  between operations  13.9 us (7%)
  matrix products  8.17 us (4%)
  local copies, waits for them, and re-layouts  4.02 us (2%)
  loops' own time  2.54 us (1%)
  other arithmetic  2.52 us (1%)
    all_gather x1, waiting for transfers between devices, local(): lax.all_gather(key_weight, 'fsdp', axis=0, tiled=True)  60.3 us
    all_gather x1, waiting for transfers between devices, local(): lax.all_gather(value_weight, 'fsdp', axis=0, tiled=True)  55.1 us
    all_gather x1, waiting for transfers between devices, local(): lax.all_gather(kv_cache, ('ctx', 'fsdp'), axis=0, tiled=True)  52.8 us
  transfers between devices with their start and end apart: 3, of which 3 were waited for; matrix products, arithmetic and copies ran while one was open for 2% of the time, Pallas kernels for 0%

commit v1 on v0

v1 whole, which is shorter than its diff:
```python
from functools import partial
import math

import jax
import jax.numpy as jnp
from jax import lax
from jax.experimental import pallas as pl
from jax.experimental.pallas import tpu as pltpu
from jax.sharding import PartitionSpec as P

rope_base = 500000.0
floor_value = -1e30


def rotate(vectors, cosine, sine_table):
    middle = vectors.shape[-1] // 2
    leading = vectors[..., :middle]
    back_half = vectors[..., middle:]
    return jnp.concatenate(
        [leading * cosine - back_half * sine_table, back_half * cosine + leading * sine_table],
        axis=-1,
    )


def tables(positions, head_size):
    middle = head_size // 2
    frequency = rope_base ** (-jnp.arange(middle, dtype=jnp.float32) * 2.0 / head_size)
    angles = positions.astype(jnp.float32)[:, None] * frequency[None, :]
    return (jnp.cos(angles), jnp.sin(angles))


def attention_kernel(
    place_ref, query_ref, *refs, masks, rows, group_rows, head_size, heads, heads_at_once
):
    pieces, out_ref = refs[:-1], refs[-1]
    place = place_ref[0]
    shift = place_ref[1]
    factor = head_size ** (-0.5) * math.log2(math.e)
    chunk = rows * heads_at_once
    contract_last = (((1,), (1,)), ((), ()))
    query_pos = shift + lax.rem(
        lax.broadcasted_iota(jnp.int32, (chunk, group_rows), 0), jnp.int32(rows)
    )
    key_pos = lax.broadcasted_iota(jnp.int32, (chunk, group_rows), 1)
    diagonal = key_pos <= query_pos

    for part in range(heads // heads_at_once):
        query = query_ref[part * chunk : (part + 1) * chunk, :]
        scores = []
        values = []
        for piece, piece_masks in zip(pieces, masks):
            raw = (
                lax.dot_general(
                    query,
                    piece[:, :head_size],
                    contract_last,
                    preferred_element_type=jnp.float32,
                )
                * factor
            )
            for slot, mask in enumerate(piece_masks):
                block = raw[:, slot * group_rows : (slot + 1) * group_rows]
                if mask == 0:
                    block = jnp.where(diagonal, block, floor_value)
                else:
                    bias = jnp.where((place ^ mask) < place, 0.0, floor_value).astype(jnp.float32)
                    block = block + bias
                scores.append(block)
                values.append(piece[slot * group_rows : (slot + 1) * group_rows, head_size:])
        peak = scores[0]
        for block in scores[1:]:
            peak = jnp.maximum(peak, block)
        peak = jnp.max(peak, axis=1, keepdims=True)
        weights = [jnp.exp2(block - peak) for block in scores]
        total = weights[0]
        for block in weights[1:]:
            total = total + block
        denominator = jnp.sum(total, axis=1, keepdims=True)
        numerator = jnp.dot(
            jnp.concatenate([block.astype(jnp.bfloat16) for block in weights], axis=1),
            jnp.concatenate(values, axis=0),
            preferred_element_type=jnp.float32,
        )
        result = (numerator / denominator).astype(out_ref.dtype)
        for head in range(heads_at_once):
            column = (part * heads_at_once + head) * head_size
            out_ref[:, column : column + head_size] = result[head * rows : (head + 1) * rows, :]


def attend(place, query_flat, pieces, masks, rows, group_rows, head_size):
    heads = query_flat.shape[0] // rows
    heads_at_once = math.gcd(heads, 4)
    keys = sum(piece.shape[0] for piece in pieces)
    whole = pl.BlockSpec(memory_space=pltpu.VMEM)
    return pl.pallas_call(
        partial(
            attention_kernel,
            masks=masks,
            rows=rows,
            group_rows=group_rows,
            head_size=head_size,
            heads=heads,
            heads_at_once=heads_at_once,
        ),
        out_shape=jax.ShapeDtypeStruct((rows, heads * head_size), jnp.bfloat16),
        in_specs=[pl.BlockSpec(memory_space=pltpu.SMEM), whole] + [whole] * len(pieces),
        out_specs=whole,
        compiler_params=pltpu.CompilerParams(vmem_limit_bytes=48 * 1024 * 1024),
        cost_estimate=pl.CostEstimate(
            flops=4 * heads * rows * keys * head_size,
            bytes_accessed=4 * heads * rows * head_size + 4 * keys * head_size,
            transcendentals=heads * rows * keys,
        ),
        name="attend",
    )(place, query_flat, *pieces)


def make_local(contexts, shards):
    def local(tokens, queries, key_weight, value_weight):
        rows = tokens.shape[0]
        depth, head_size = key_weight.shape
        heads = queries.shape[1] // head_size
        group_rows = shards * rows
        context = lax.axis_index("ctx")
        shard = lax.axis_index("fsdp")

        received = [None] * shards
        for step in range(1, shards):
            target = lax.rem(shard + step, shards)
            columns = lax.dynamic_slice_in_dim(tokens, target * depth, depth, 1)
            received[step] = lax.ppermute(
                columns, "fsdp", [(i, (i + step) % shards) for i in range(shards)]
            )
        received[0] = lax.dynamic_slice_in_dim(tokens, shard * depth, depth, 1)

        positions = context * group_rows + jnp.arange(group_rows, dtype=jnp.int32)
        cosine, sine_table = tables(positions, head_size)
        own_cosine = lax.dynamic_slice_in_dim(cosine, shard * rows, rows, 0)
        own_sine = lax.dynamic_slice_in_dim(sine_table, shard * rows, rows, 0)
        by_head = queries.astype(jnp.float32).reshape(rows, heads, head_size).transpose(1, 0, 2)
        query_flat = (
            rotate(by_head, own_cosine[None], own_sine[None])
            .astype(jnp.bfloat16)
            .reshape(heads * rows, head_size)
        )

        products = []
        for columns in received:
            products.append(
                jnp.concatenate(
                    [
                        jnp.dot(columns, key_weight, preferred_element_type=jnp.float32),
                        jnp.dot(columns, value_weight, preferred_element_type=jnp.float32),
                    ],
                    axis=1,
                )
            )
        if shards == 2:
            ordered = [
                jnp.where(shard == 0, products[0], products[1]),
                jnp.where(shard == 0, products[1], products[0]),
            ]
            partial_sums = jnp.concatenate(ordered, axis=0)
        else:
            partial_sums = jnp.zeros((group_rows, 2 * head_size), jnp.float32)
            for step in range(shards):
                source = lax.rem(shard + shards - step, shards)
                partial_sums = lax.dynamic_update_slice_in_dim(
                    partial_sums, products[step], source * rows, 0
                )
        reach = 1
        while reach < shards:
            partial_sums = partial_sums + lax.ppermute(
                partial_sums, "fsdp", [(i, i ^ reach) for i in range(shards)]
            )
            reach *= 2

        keys_rot = rotate(partial_sums[:, :head_size], cosine, sine_table).astype(jnp.bfloat16)
        group = jnp.concatenate([keys_rot, partial_sums[:, head_size:].astype(jnp.bfloat16)], axis=1)
        kv_cache = lax.dynamic_slice_in_dim(group, shard * rows, rows, 0)

        pieces, masks = [group], [[0]]
        reach = contexts // 2
        order = []
        while reach > 1:
            order.append(reach)
            reach //= 2
        if contexts > 1:
            order.append(1)
        for bit in order:
            known = jnp.concatenate(pieces, axis=0) if len(pieces) > 1 else pieces[0]
            known_masks = [mask for piece_masks in masks for mask in piece_masks]
            pieces.append(lax.ppermute(known, "ctx", [(i, i ^ bit) for i in range(contexts)]))
            masks.append([mask ^ bit for mask in known_masks])

        place = jnp.stack([context, shard * rows]).astype(jnp.int32)
        attended = attend(place, query_flat, pieces, masks, rows, group_rows, head_size)
        return (kv_cache, attended)

    return local


def solution(mesh):
    placed = (P(("ctx", "fsdp"), None), P(("ctx", "fsdp"), None), P("fsdp", None), P("fsdp", None))
    return jax.shard_map(
        make_local(mesh.shape["ctx"], mesh.shape["fsdp"]),
        mesh=mesh,
        in_specs=placed,
        out_specs=(P(("ctx", "fsdp"), None), P(("ctx", "fsdp"), None)),
        check_vma=False,
    )
```

time: 203 us -> 60.1 us (0.30); the launches traced: 201 us -> 59.9 us
  waiting for transfers between devices: 169 us -> 34.7 us
  between operations: 13.9 us -> 0.79 us
  starting transfers between devices: 0.11 us -> 11.4 us
  Pallas kernels: 0 us -> 4.75 us
  matrix products: 8.17 us -> 3.71 us
  loops' own time: 2.54 us -> 0 us
    all_gather x3 -> x0, waiting for transfers between devices: 168 us -> none  [the longest x1 60.3 us: local(): lax.all_gather(key_weight, 'fsdp', axis=0, tiled=True)]
    ppermute x0 -> x6, waiting for transfers between devices: none -> 34.7 us  [the longest x1 20.6 us: local(): lax.ppermute(columns, 'fsdp', [(i, (i + step) % shards) for i in range(sh...]
    ppermute x0 -> x6, starting transfers between devices: none -> 11.4 us  [the longest x4 6.65 us: local(): lax.ppermute(known, 'ctx', [(i, i ^ bit) for i in range(contexts)])]
    pallas_call x0 -> x1, Pallas kernels: none -> 4.75 us  [attend(): pl.pallas_call(partial(attention_kernel, masks=masks, rows=rows, group_ro...]
    dot_general x4, matrix products: 8.17 us -> 3.71 us  [the longest x2 2.73 us: local(): jnp.dot(columns, value_weight, preferred_element_type=jnp.float32)]
    another operation x3 -> x0, loops' own time: 2.54 us -> none  [the longest x1 2.47 us: fold(): lax.scan(scan_step, states, (jnp.arange(length // block_width, dtype=jnp....]
  transfers between devices with their start and end apart: 3 -> 6, of which waited for: 3 -> 6; matrix products, arithmetic and copies ran while one was open for 2% -> 7% of each run, Pallas kernels for 0% -> 0%
where the time goes in v1:
time: 60.1 us; the launch traced here: 59.9 us
  waiting for transfers between devices  34.7 us (58%)
  starting transfers between devices  11.4 us (19%)
  Pallas kernels  4.75 us (8%)
  matrix products  3.71 us (6%)
  local copies, waits for them, and re-layouts  3.27 us (5%)
  other arithmetic  1.27 us (2%)
  between operations  0.79 us (1%)
    ppermute x1, waiting for transfers between devices, local(): lax.ppermute(columns, 'fsdp', [(i, (i + step) % shards) for i in range(sh...  20.6 us
    ppermute x4, waiting for transfers between devices, local(): lax.ppermute(known, 'ctx', [(i, i ^ bit) for i in range(contexts)])  10.9 us
    ppermute x4, starting transfers between devices, local(): lax.ppermute(known, 'ctx', [(i, i ^ bit) for i in range(contexts)])  6.65 us
    pallas_call x1, Pallas kernels, attend(): pl.pallas_call(partial(attention_kernel, masks=masks, rows=rows, group_ro...  4.75 us
    ppermute x1, waiting for transfers between devices, local(): lax.ppermute(partial_sums, 'fsdp', [(i, i ^ reach) for i in range(shards)])  3.21 us
    ppermute x1, starting transfers between devices, local(): lax.ppermute(columns, 'fsdp', [(i, (i + step) % shards) for i in range(sh...  2.94 us
    dot_general x2, matrix products, local(): jnp.dot(columns, value_weight, preferred_element_type=jnp.float32)  2.73 us
    ppermute x1, starting transfers between devices, local(): lax.ppermute(partial_sums, 'fsdp', [(i, i ^ reach) for i in range(shards)])  1.81 us
  transfers between devices with their start and end apart: 6, of which 6 were waited for; matrix products, arithmetic and copies ran while one was open for 7% of the time, Pallas kernels for 0%

profile of v1, /device:TPU:0, one launch (start us, length us, event | category | flops | bytes accessed | tf_op | source)
XLA Modules:
  0.0 59.9 jit_solution(17257469399301474596)
XLA Ops:
  0.6 0.0 copy-start
  0.7 1.6 %copy-done = bf16[64,16384]{1,0:T(8,128)(2,1)S(1)} copy-done((bf16[64,16384]{1,0:T(8,128)(2,1)S(1)}, bf16[64,16384]{1,0:T(8,128)(2,1)}, u32[]{:S(2)}) %copy-start) | copy-done | bytes 2097176
  2.2 1.0 %constant_dynamic-slice_fusion.3 = bf16[64,8192]{1,0:T(8,128)(2,1)} fusion(bf16[64,16384]{1,0:T(8,128)(2,1)S(1)} %copy-done, s32[]{:T(128)S(6)} %select_n.25), kind=kLoop, calls=%fused_computation.27 | loop fusion | bytes 2097156 | tf_op jit(solution)/shard_map/dynamic_slice | solution.py:130
  3.3 2.9 %collective-permute-start = (bf16[64,8192]{1,0:T(8,128)(2,1)}, bf16[64,8192]{1,0:T(8,128)(2,1)S(1)}, u32[]{:S(2)}, u32[]{:S(2)}) collective-permute-start(bf16[64,8192]{1,0:T(8,128)(2,1)} %constant_dynamic-slice_fusion.3), channel_id=1, source_target_pairs={{0,1},{1,0},{2,3},{3,2},{4,5},{5,4},{6,7},{7,6},{8,9},{9,8},{10,11... | collective-permute-start | bytes 3145736 | tf_op jit(solution)/shard_map/ppermute | solution.py:131
  6.2 0.0 copy-start.2
  6.2 2.2 %fusion = f32[64,128]{1,0:T(8,128)S(1)} fusion(bf16[8192,128]{1,0:T(8,128)(2,1)} %param.7, bf16[64,16384]{1,0:T(8,128)(2,1)S(1)} %copy-done, s32[]{:T(128)S(6)} %select_n.24), kind=kOutput, calls=%fused_computation | convolution fusion | flops 134217728 | bytes 3178500 | tf_op jit(solution)/shard_map/dot_general | solution.py:153
  8.4 0.0 copy-done.2
  8.5 0.0 copy-start.1
  8.5 0.5 fusion.2
  9.0 20.6 %collective-permute-done = bf16[64,8192]{1,0:T(8,128)(2,1)S(1)} collective-permute-done((bf16[64,8192]{1,0:T(8,128)(2,1)}, bf16[64,8192]{1,0:T(8,128)(2,1)S(1)}, u32[]{:S(2)}, u32[]{:S(2)}) %collective-permute-start) | collective-permute-done | bytes 1048608 | tf_op jit(solution)/shard_map/ppermute | solution.py:131
  29.6 0.0 copy-done.1
  29.6 0.5 fusion.10
  30.1 0.0 copy-start.3
  30.1 0.5 fusion.9
  30.6 1.8 %collective-permute-start.1 = (f32[128,256]{1,0:T(8,128)S(1)}, f32[128,256]{1,0:T(8,128)S(1)}, u32[]{:S(2)}, u32[]{:S(2)}) collective-permute-start(f32[128,256]{1,0:T(8,128)S(1)} %pad_maximum_fusion.3), channel_id=1, source_target_pairs={{0,1},{1,0},{2,3},{3,2},{4,5},{5,4},{6,7},{7,6},{8,9},{9,8},{10,11... | collective-permute-start | bytes 393224 | tf_op jit(solution)/shard_map/ppermute | solution.py:173
  32.4 3.2 %collective-permute-done.1 = f32[128,256]{1,0:T(8,128)S(1)} collective-permute-done((f32[128,256]{1,0:T(8,128)S(1)}, f32[128,256]{1,0:T(8,128)S(1)}, u32[]{:S(2)}, u32[]{:S(2)}) %collective-permute-start.1) | collective-permute-done | bytes 131104 | tf_op jit(solution)/shard_map/ppermute | solution.py:173
  35.7 0.3 multiply_cosine_fusion
  36.0 0.1 pad_maximum_fusion.7.refs_0_
  36.1 2.9 %collective-permute-start.2 = (bf16[128,256]{1,0:T(8,128)(2,1)S(1)}, bf16[128,256]{1,0:T(8,128)(2,1)S(1)}, u32[]{:S(2)}, u32[]{:S(2)}) collective-permute-start(bf16[128,256]{1,0:T(8,128)(2,1)S(1)} %pad_maximum_fusion.7.refs_0_), channel_id=1, source_target_pairs={{0,16},{2,18},{4,20},{6,22},{8,24},{10,26},{12,28},{14,30},{16,0},... | collective-permute-start | bytes 196616 | tf_op jit(solution)/shard_map/ppermute | solution.py:193
  39.0 2.4 %collective-permute-done.2.refs_1_ = bf16[128,256]{1,0:T(8,128)(2,1)S(1)} collective-permute-done((bf16[128,256]{1,0:T(8,128)(2,1)S(1)}, bf16[128,256]{1,0:T(8,128)(2,1)S(1)}, u32[]{:S(2)}, u32[]{:S(2)}) %collective-permute-start.2) | collective-permute-done | bytes 65568 | tf_op jit(solution)/shard_map/ppermute | solution.py:193
  41.4 0.1 pad_maximum_fusion.4
  41.5 1.8 %collective-permute-start.3 = (bf16[256,256]{1,0:T(8,128)(2,1)S(1)}, bf16[256,256]{1,0:T(8,128)(2,1)S(1)}, u32[]{:S(2)}, u32[]{:S(2)}) collective-permute-start(bf16[256,256]{1,0:T(8,128)(2,1)S(1)} %pad_maximum_fusion.4), channel_id=1, source_target_pairs={{0,8},{2,10},{4,12},{6,14},{8,0},{10,2},{12,4},{14,6},{16,24},{18,... | collective-permute-start | bytes 393224 | tf_op jit(solution)/shard_map/ppermute | solution.py:193
  43.3 3.2 %collective-permute-done.3.refs_2_ = bf16[256,256]{1,0:T(8,128)(2,1)S(1)} collective-permute-done((bf16[256,256]{1,0:T(8,128)(2,1)S(1)}, bf16[256,256]{1,0:T(8,128)(2,1)S(1)}, u32[]{:S(2)}, u32[]{:S(2)}) %collective-permute-start.3) | collective-permute-done | bytes 131104 | tf_op jit(solution)/shard_map/ppermute | solution.py:193
  46.5 0.1 pad_maximum_fusion.2
  46.6 1.8 %collective-permute-start.4 = (bf16[512,256]{1,0:T(8,128)(2,1)S(1)}, bf16[512,256]{1,0:T(8,128)(2,1)S(1)}, u32[]{:S(2)}, u32[]{:S(2)}) collective-permute-start(bf16[512,256]{1,0:T(8,128)(2,1)S(1)} %pad_maximum_fusion.2), channel_id=1, source_target_pairs={{0,4},{2,6},{4,0},{6,2},{8,12},{10,14},{12,8},{14,10},{16,20},{18,... | collective-permute-start | bytes 786440 | tf_op jit(solution)/shard_map/ppermute | solution.py:193
  48.5 0.1 pad_add_fusion.place_ref
  48.5 0.0 copy-done.3
  48.6 4.5 %collective-permute-done.4.refs_3_ = bf16[512,256]{1,0:T(8,128)(2,1)S(1)} collective-permute-done((bf16[512,256]{1,0:T(8,128)(2,1)S(1)}, bf16[512,256]{1,0:T(8,128)(2,1)S(1)}, u32[]{:S(2)}, u32[]{:S(2)}) %collective-permute-start.4) | collective-permute-done | bytes 262176 | tf_op jit(solution)/shard_map/ppermute | solution.py:193
  53.1 0.1 pad_maximum_fusion
  53.2 0.1 collective-permute-start.5
  53.2 0.6 %constant_dynamic-slice_fusion.2 = bf16[64,256]{1,0:T(8,128)(2,1)} fusion(bf16[128,256]{1,0:T(8,128)(2,1)S(1)} %pad_maximum_fusion.7.refs_0_, s32[]{:T(128)S(6)} %select_n.28), kind=kLoop, calls=%fused_computation.26 | loop fusion | bytes 65540 | tf_op jit(solution)/shard_map/dynamic_slice | solution.py:180
  53.9 0.3 subtract_convert_fusion
  54.1 0.1 pad_maximum_fusion.1.query_ref
  54.3 0.8 %collective-permute-done.5.refs_4_ = bf16[1024,256]{1,0:T(8,128)(2,1)S(1)} collective-permute-done((bf16[1024,256]{1,0:T(8,128)(2,1)S(1)}, bf16[1024,256]{1,0:T(8,128)(2,1)S(1)}, u32[]{:S(2)}, u32[]{:S(2)}) %collective-permute-start.5) | collective-permute-done | bytes 524320 | tf_op jit(solution)/shard_map/ppermute | solution.py:193
  55.1 4.8 %attend.1 = bf16[64,2048]{1,0:T(8,128)(2,1)} custom-call(s32[2]{0:T(128)S(1)} %pad_add_fusion.place_ref, bf16[1024,128]{1,0:T(8,128)(2,1)S(1)} %pad_maximum_fusion.1.query_ref, bf16[128,256]{1,0:T(8,128)(2,1)S(1)} %pad_maximum_fusion.7.refs_0_, bf16[128,256]{1,0:T(8,128)(2,1)S(1)} %collective-permute-done.2.refs_1_, ...), custom_call_target="tpu_custom_call" | custom-call | flops 1073741824 | bytes 1572864 | tf_op jit(solution)/shard_map/attend/pallas_call | solution.py:95
  (8 shorter events, 0.1 us)
Async XLA Ops:
  0.6 1.6 %copy-start = (bf16[64,16384]{1,0:T(8,128)(2,1)S(1)}, bf16[64,16384]{1,0:T(8,128)(2,1)}, u32[]{:S(2)}) copy-start(bf16[64,16384]{1,0:T(8,128)(2,1)} %param.4) | copy-start | bytes 6291460
  3.3 26.3 %collective-permute-start = (bf16[64,8192]{1,0:T(8,128)(2,1)}, bf16[64,8192]{1,0:T(8,128)(2,1)S(1)}, u32[]{:S(2)}, u32[]{:S(2)}) collective-permute-start(bf16[64,8192]{1,0:T(8,128)(2,1)} %constant_dynamic-slice_fusion.3), channel_id=1, source_target_pairs={{0,1},{1,0},{2,3},{3,2},{4,5},{5,4},{6,7},{7,6},{8,9},{9,8},{10,11... | collective-permute-start | bytes 3145736 | tf_op jit(solution)/shard_map/ppermute | solution.py:131
  6.2 2.2 %copy-start.2 = (bf16[8192,128]{1,0:T(8,128)(2,1)S(1)}, bf16[8192,128]{1,0:T(8,128)(2,1)}, u32[]{:S(2)}) copy-start(bf16[8192,128]{1,0:T(8,128)(2,1)} %param.6) | copy-start | bytes 6291460
  8.5 21.1 %copy-start.1 = (bf16[8192,128]{1,0:T(8,128)(2,1)S(1)}, bf16[8192,128]{1,0:T(8,128)(2,1)}, u32[]{:S(2)}) copy-start(bf16[8192,128]{1,0:T(8,128)(2,1)} %param.7) | copy-start | bytes 6291460
  30.1 18.5 %copy-start.3 = (bf16[64,2048]{1,0:T(8,128)(2,1)S(1)}, bf16[64,2048]{1,0:T(8,128)(2,1)}, u32[]{:S(2)}) copy-start(bf16[64,2048]{1,0:T(8,128)(2,1)} %param.5) | copy-start | bytes 786436
  30.6 5.0 %collective-permute-start.1 = (f32[128,256]{1,0:T(8,128)S(1)}, f32[128,256]{1,0:T(8,128)S(1)}, u32[]{:S(2)}, u32[]{:S(2)}) collective-permute-start(f32[128,256]{1,0:T(8,128)S(1)} %pad_maximum_fusion.3), channel_id=1, source_target_pairs={{0,1},{1,0},{2,3},{3,2},{4,5},{5,4},{6,7},{7,6},{8,9},{9,8},{10,11... | collective-permute-start | bytes 393224 | tf_op jit(solution)/shard_map/ppermute | solution.py:173
  36.1 5.3 %collective-permute-start.2 = (bf16[128,256]{1,0:T(8,128)(2,1)S(1)}, bf16[128,256]{1,0:T(8,128)(2,1)S(1)}, u32[]{:S(2)}, u32[]{:S(2)}) collective-permute-start(bf16[128,256]{1,0:T(8,128)(2,1)S(1)} %pad_maximum_fusion.7.refs_0_), channel_id=1, source_target_pairs={{0,16},{2,18},{4,20},{6,22},{8,24},{10,26},{12,28},{14,30},{16,0},... | collective-permute-start | bytes 196616 | tf_op jit(solution)/shard_map/ppermute | solution.py:193
  41.5 5.0 %collective-permute-start.3 = (bf16[256,256]{1,0:T(8,128)(2,1)S(1)}, bf16[256,256]{1,0:T(8,128)(2,1)S(1)}, u32[]{:S(2)}, u32[]{:S(2)}) collective-permute-start(bf16[256,256]{1,0:T(8,128)(2,1)S(1)} %pad_maximum_fusion.4), channel_id=1, source_target_pairs={{0,8},{2,10},{4,12},{6,14},{8,0},{10,2},{12,4},{14,6},{16,24},{18,... | collective-permute-start | bytes 393224 | tf_op jit(solution)/shard_map/ppermute | solution.py:193
  46.6 6.4 %collective-permute-start.4 = (bf16[512,256]{1,0:T(8,128)(2,1)S(1)}, bf16[512,256]{1,0:T(8,128)(2,1)S(1)}, u32[]{:S(2)}, u32[]{:S(2)}) collective-permute-start(bf16[512,256]{1,0:T(8,128)(2,1)S(1)} %pad_maximum_fusion.2), channel_id=1, source_target_pairs={{0,4},{2,6},{4,0},{6,2},{8,12},{10,14},{12,8},{14,10},{16,20},{18,... | collective-permute-start | bytes 786440 | tf_op jit(solution)/shard_map/ppermute | solution.py:193
  53.2 2.0 %collective-permute-start.5 = (bf16[1024,256]{1,0:T(8,128)(2,1)S(1)}, bf16[1024,256]{1,0:T(8,128)(2,1)S(1)}, u32[]{:S(2)}, u32[]{:S(2)}) collective-permute-start(bf16[1024,256]{1,0:T(8,128)(2,1)S(1)} %pad_maximum_fusion), channel_id=1, source_target_pairs={{0,2},{2,0},{4,6},{6,4},{8,10},{10,8},{12,14},{14,12},{16,18},{18,... | collective-permute-start | bytes 1572872 | tf_op jit(solution)/shard_map/ppermute | solution.py:193

commit v2 on v1

v2 whole, which is shorter than its diff:
```python
from functools import partial
import math

import jax
import jax.numpy as jnp
from jax import lax
from jax.experimental import pallas as pl
from jax.experimental.pallas import tpu as pltpu
from jax.sharding import PartitionSpec as P

rope_base = 500000.0
floor_value = -1e30


def rotate(vectors, cosine, sine_table):
    middle = vectors.shape[-1] // 2
    leading = vectors[..., :middle]
    back_half = vectors[..., middle:]
    return jnp.concatenate(
        [leading * cosine - back_half * sine_table, back_half * cosine + leading * sine_table],
        axis=-1,
    )


def tables(positions, head_size):
    middle = head_size // 2
    frequency = rope_base ** (-jnp.arange(middle, dtype=jnp.float32) * 2.0 / head_size)
    angles = positions.astype(jnp.float32)[:, None] * frequency[None, :]
    return (jnp.cos(angles), jnp.sin(angles))


def attention_kernel(
    span_ref, place_ref, query_ref, *refs, count, carry, final, rows, own, head_size, stride
):
    pieces, refs = refs[:count], refs[count:]
    if carry:
        old_peak, old_total, old_sum = refs[:3]
        refs = refs[3:]
    start = span_ref[0]
    first = span_ref[1]
    factor = head_size ** (-0.5) * math.log2(math.e)
    flat = query_ref.shape[0]
    keys = jnp.concatenate([piece[:, :head_size] for piece in pieces], axis=0)
    values = jnp.concatenate([piece[:, head_size:] for piece in pieces], axis=0)
    width = keys.shape[0]
    edge = min(width, -(-own // 128) * 128)
    query_pos = first + lax.rem(
        lax.broadcasted_iota(jnp.int32, (stride, edge), 0), jnp.int32(rows)
    )
    diagonal = place_ref[:, :edge] <= query_pos
    bias = jnp.where(place_ref[...] < start, 0.0, floor_value).astype(jnp.float32)

    def one(part):
        place = pl.ds(pl.multiple_of(part * stride, stride), stride)
        scores = (
            lax.dot_general(
                query_ref[place, :],
                keys,
                (((1,), (1,)), ((), ())),
                preferred_element_type=jnp.float32,
            )
            * factor
        )
        masked = jnp.where(diagonal, scores[:, :edge], floor_value)
        if edge < width:
            masked = jnp.concatenate([masked, scores[:, edge:] + bias[:, edge:]], axis=1)
        peak = jnp.max(masked, axis=1, keepdims=True)
        if carry:
            peak = jnp.maximum(peak, old_peak[place, :])
        weights = jnp.exp2(masked - peak)
        total = jnp.sum(weights, axis=1, keepdims=True)
        numerator = jnp.dot(
            weights.astype(jnp.bfloat16), values, preferred_element_type=jnp.float32
        )
        if carry:
            shrink = jnp.exp2(old_peak[place, :] - peak)
            total = total + shrink * old_total[place, :]
            numerator = numerator + shrink * old_sum[place, :]
        if final:
            out_ref, scratch = refs
            scratch[place, :] = (numerator / total).astype(jnp.bfloat16)
        else:
            peak_ref, total_ref, sum_ref = refs
            peak_ref[place, :] = peak
            total_ref[place, :] = total
            sum_ref[place, :] = numerator

    if width <= 2048:
        for part in range(flat // stride):
            one(part)
    else:

        @pl.loop(0, flat // stride)
        def each(part):
            one(part)

    if final:
        out_ref, scratch = refs
        for head in range(flat // rows):
            out_ref[:, head * head_size : (head + 1) * head_size] = scratch[
                head * rows : (head + 1) * rows, :
            ]


def attend(span, place, query_flat, pieces, state, final, rows):
    flat, head_size = query_flat.shape
    width = sum(piece.shape[0] for piece in pieces)
    stride = math.gcd(flat, 256 if width <= 2048 else rows)
    whole = pl.BlockSpec(memory_space=pltpu.VMEM)
    if final:
        shapes = jax.ShapeDtypeStruct((rows, flat // rows * head_size), jnp.bfloat16)
        out_specs, scratch = whole, [pltpu.VMEM((flat, head_size), jnp.bfloat16)]
    else:
        shapes = [
            jax.ShapeDtypeStruct((flat, 1), jnp.float32),
            jax.ShapeDtypeStruct((flat, 1), jnp.float32),
            jax.ShapeDtypeStruct((flat, head_size), jnp.float32),
        ]
        out_specs, scratch = [whole] * 3, []
    return pl.pallas_call(
        partial(
            attention_kernel,
            count=len(pieces),
            carry=state is not None,
            final=final,
            rows=rows,
            own=pieces[0].shape[0],
            head_size=head_size,
            stride=stride,
        ),
        out_shape=shapes,
        in_specs=[pl.BlockSpec(memory_space=pltpu.SMEM)]
        + [whole] * (2 + len(pieces) + (0 if state is None else 3)),
        out_specs=out_specs,
        scratch_shapes=scratch,
        compiler_params=pltpu.CompilerParams(vmem_limit_bytes=40 * 1024 * 1024),
        cost_estimate=pl.CostEstimate(
            flops=4 * flat * width * head_size,
            bytes_accessed=4 * flat * head_size + 4 * width * head_size,
            transcendentals=flat * width,
        ),
        name="attend_last" if final else "attend_part",
    )(span, place, query_flat, *pieces, *(() if state is None else state))


def stages_of(contexts):
    bits = []
    bit = contexts // 2
    while bit >= 1:
        bits.append(bit)
        bit //= 2
    core = bits[-1:]
    rest = bits[:-1]
    stages = [rest[i : i + 2] for i in range(0, len(rest), 2)] + ([core] if core else [])
    return stages


def spread(block, contexts):
    pieces, masks = [block], [[0]]
    for stage in stages_of(contexts):
        known = jnp.concatenate(pieces, axis=0) if len(pieces) > 1 else pieces[0]
        known_masks = [mask for piece_masks in masks for mask in piece_masks]
        moves = [0]
        for bit in stage:
            moves = moves + [move ^ bit for move in moves]
        for move in moves[1:]:
            pieces.append(lax.ppermute(known, "ctx", [(i, i ^ move) for i in range(contexts)]))
            masks.append([mask ^ move for mask in known_masks])
    return pieces, masks


def make_local(contexts, shards, parts):
    def local(tokens, queries, key_weight, value_weight):
        rows = tokens.shape[0]
        depth, head_size = key_weight.shape
        heads = queries.shape[1] // head_size
        group_rows = shards * rows
        part_rows = rows // parts
        context = lax.axis_index("ctx")
        shard = lax.axis_index("fsdp")

        received = []
        for part in range(parts):
            top = part * part_rows
            arrived = []
            for step in range(1, shards):
                target = lax.rem(shard + step, shards)
                columns = lax.dynamic_slice(
                    tokens, (jnp.int32(top), target * depth), (part_rows, depth)
                )
                arrived.append(
                    lax.ppermute(
                        columns, "fsdp", [(i, (i + step) % shards) for i in range(shards)]
                    )
                )
            received.append(arrived)
        own_columns = lax.dynamic_slice_in_dim(tokens, shard * depth, depth, 1)

        def project(columns):
            return jnp.concatenate(
                [
                    jnp.dot(columns, key_weight, preferred_element_type=jnp.float32),
                    jnp.dot(columns, value_weight, preferred_element_type=jnp.float32),
                ],
                axis=1,
            )

        own_product = project(own_columns)

        start = context * group_rows
        positions = start + jnp.arange(group_rows, dtype=jnp.int32)
        cosine, sine_table = tables(positions, head_size)
        own_cosine = lax.dynamic_slice_in_dim(cosine, shard * rows, rows, 0)
        own_sine = lax.dynamic_slice_in_dim(sine_table, shard * rows, rows, 0)
        by_head = queries.astype(jnp.float32).reshape(rows, heads, head_size).transpose(1, 0, 2)
        query_flat = (
            rotate(by_head, own_cosine[None], own_sine[None])
            .astype(jnp.bfloat16)
            .reshape(heads * rows, head_size)
        )
        span = jnp.stack([start, start + shard * rows]).astype(jnp.int32)

        def rows_of(table, top):
            return table.reshape(shards, rows, -1)[:, top : top + part_rows].reshape(
                shards * part_rows, -1
            )

        state = None
        cache_parts = []
        for part in range(parts):
            top = part * part_rows
            products = [own_product[top : top + part_rows]] + [
                project(columns) for columns in received[part]
            ]
            if shards == 2:
                partial_sums = jnp.concatenate(
                    [
                        jnp.where(shard == 0, products[0], products[1]),
                        jnp.where(shard == 0, products[1], products[0]),
                    ],
                    axis=0,
                )
            else:
                partial_sums = jnp.zeros((shards * part_rows, 2 * head_size), jnp.float32)
                for step in range(shards):
                    source = lax.rem(shard + shards - step, shards)
                    partial_sums = lax.dynamic_update_slice_in_dim(
                        partial_sums, products[step], source * part_rows, 0
                    )
            reach = 1
            while reach < shards:
                partial_sums = partial_sums + lax.ppermute(
                    partial_sums, "fsdp", [(i, i ^ reach) for i in range(shards)]
                )
                reach *= 2
            keys_rot = rotate(
                partial_sums[:, :head_size], rows_of(cosine, top), rows_of(sine_table, top)
            ).astype(jnp.bfloat16)
            block = jnp.concatenate(
                [keys_rot, partial_sums[:, head_size:].astype(jnp.bfloat16)], axis=1
            )
            cache_parts.append(lax.dynamic_slice_in_dim(block, shard * part_rows, part_rows, 0))
            pieces, masks = spread(block, contexts)
            local_pos = rows_of(jnp.arange(group_rows, dtype=jnp.int32)[:, None], top)[:, 0]
            order = jnp.array([mask for piece_masks in masks for mask in piece_masks], jnp.int32)
            place = ((context ^ order)[:, None] * group_rows + local_pos[None, :]).reshape(1, -1)
            last = part == parts - 1
            state = attend(span, place, query_flat, pieces, state, last, rows)
        kv_cache = jnp.concatenate(cache_parts, axis=0)
        return (kv_cache, state)

    return local


def solution(mesh):
    placed = (P(("ctx", "fsdp"), None), P(("ctx", "fsdp"), None), P("fsdp", None), P("fsdp", None))
    return jax.shard_map(
        make_local(mesh.shape["ctx"], mesh.shape["fsdp"], 2),
        mesh=mesh,
        in_specs=placed,
        out_specs=(P(("ctx", "fsdp"), None), P(("ctx", "fsdp"), None)),
        check_vma=False,
    )
```

time: 60.1 us -> 62.6 us (1.042)
  waiting for transfers between devices: 34.7 us -> 22.9 us
  starting transfers between devices: 11.4 us -> 17.3 us
  matrix products: 3.71 us -> 8.61 us
  Pallas kernels: 4.75 us -> 6.64 us
  other arithmetic: 1.27 us -> 2.82 us
    ppermute x1 -> x2, waiting for transfers between devices: 20.6 us -> 13.3 us  [local(): lax.ppermute(columns, 'fsdp', [(i, (i + step) % shards) for i in range(sh...]
    ppermute x4 -> x10, starting transfers between devices: 6.65 us -> 12.2 us  [spread(): lax.ppermute(known, 'ctx', [(i, i ^ move) for i in range(contexts)])]
    dot_general x4 -> x6, matrix products: 3.71 us -> 8.61 us  [the longest x3 4.96 us: project(): jnp.dot(columns, value_weight, preferred_element_type=jnp.float32)]
    ppermute x4 -> x10, waiting for transfers between devices: 10.9 us -> 7.21 us  [spread(): lax.ppermute(known, 'ctx', [(i, i ^ move) for i in range(contexts)])]
    pallas_call x1 -> x2, Pallas kernels: 4.75 us -> 6.64 us  [attend(): pl.pallas_call(partial(attention_kernel, count=len(pieces), carry=state i...]
    unnamed x8 -> x18, local copies, waits for them, and re-layouts: 1.59 us -> 0.06 us
    ppermute x1 -> x2, waiting for transfers between devices: 3.21 us -> 2.4 us  [local(): lax.ppermute(partial_sums, 'fsdp', [(i, i ^ reach) for i in range(shards)])]
    dynamic_slice x3, local copies, waits for them, and re-layouts: 1.67 us -> 2.45 us  [the longest x1 2.44 us: local(): lax.dynamic_slice(tokens, (jnp.int32(top), target * depth), (part_rows, d...]
  transfers between devices with their start and end apart: 6 -> 14, of which waited for: 6 -> 6; matrix products, arithmetic and copies ran while one was open for 7% -> 18% of each run, Pallas kernels for 0% -> 4%
where the time goes in v2:
time: 62.6 us; the launch traced here: 62.3 us
  waiting for transfers between devices  22.9 us (37%)
  starting transfers between devices  17.3 us (28%)
  matrix products  8.61 us (14%)
  Pallas kernels  6.64 us (11%)
  local copies, waits for them, and re-layouts  3.08 us (5%)
  other arithmetic  2.82 us (5%)
  between operations  0.98 us (2%)
    ppermute x2, waiting for transfers between devices, local(): lax.ppermute(columns, 'fsdp', [(i, (i + step) % shards) for i in range(sh...  13.3 us
    ppermute x10, starting transfers between devices, spread(): lax.ppermute(known, 'ctx', [(i, i ^ move) for i in range(contexts)])  12.2 us
    ppermute x10, waiting for transfers between devices, spread(): lax.ppermute(known, 'ctx', [(i, i ^ move) for i in range(contexts)])  7.21 us
    pallas_call x2, Pallas kernels, attend(): pl.pallas_call(partial(attention_kernel, count=len(pieces), carry=state i...  6.64 us
    dot_general x3, matrix products, project(): jnp.dot(columns, value_weight, preferred_element_type=jnp.float32)  4.96 us
    dot_general x3, matrix products, project(): jnp.dot(columns, key_weight, preferred_element_type=jnp.float32)  3.65 us
    ppermute x2, starting transfers between devices, local(): lax.ppermute(columns, 'fsdp', [(i, (i + step) % shards) for i in range(sh...  2.97 us
    dynamic_slice x1, local copies, waits for them, and re-layouts, local(): lax.dynamic_slice(tokens, (jnp.int32(top), target * depth), (part_rows, d...  2.44 us
  transfers between devices with their start and end apart: 14, of which 6 were waited for; matrix products, arithmetic and copies ran while one was open for 18% of the time, Pallas kernels for 4%

profile of v2, /device:TPU:0, one launch (start us, length us, event | category | flops | bytes accessed | tf_op | source)
XLA Modules:
  0.0 62.3 jit_solution(259090182599135485)
XLA Ops:
  0.7 2.4 %constant_dynamic-slice_fusion.2 = (bf16[32,8192]{1,0:T(8,128)(2,1)}, bf16[32,8192]{1,0:T(8,128)(2,1)}) fusion(bf16[64,16384]{1,0:T(8,128)(2,1)} %param.6, s32[]{:T(128)S(6)} %select_n.37), kind=kLoop, calls=%fused_computation.64 | loop fusion | bytes 2097156 | tf_op jit(solution)/shard_map/dynamic_slice | solution.py:188
  3.1 2.9 %collective-permute-start = (bf16[32,8192]{1,0:T(8,128)(2,1)}, bf16[32,8192]{1,0:T(8,128)(2,1)}, u32[]{:S(2)}, u32[]{:S(2)}) collective-permute-start(bf16[32,8192]{1,0:T(8,128)(2,1)} %get-tuple-element.12), channel_id=1, source_target_pairs={{0,1},{1,0},{2,3},{3,2},{4,5},{5,4},{6,7},{7,6},{8,9},{9,8},{10,11... | collective-permute-start | bytes 1572872 | tf_op jit(solution)/shard_map/ppermute | solution.py:192
  6.1 0.0 collective-permute-start.2
  6.1 0.3 multiply_cosine_fusion
  6.4 0.7 %broadcast_multiply_fusion = f32[128,64]{1,0:T(8,128)} fusion(f32[64]{0:T(128)S(1)} %multiply_power_fusion, f32[128]{0:T(128)S(1)} %add_convert_fusion.2), kind=kLoop, calls=%fused_computation.42 | loop fusion | flops 8192 | bytes 33536 | tf_op jit(solution)/shard_map/mul | solution.py:28
  7.3 0.1 fusion.23
  7.3 0.1 add.124
  7.4 0.1 add.133
  7.5 3.0 %fusion = f32[64,128]{1,0:T(8,128)} fusion(bf16[8192,128]{1,0:T(8,128)(2,1)} %param.9, bf16[64,16384]{1,0:T(8,128)(2,1)} %param.6, s32[]{:T(128)S(6)} %select_n.36), kind=kOutput, calls=%fused_computation | convolution fusion | flops 134217728 | bytes 3178500 | tf_op jit(solution)/shard_map/dot_general | solution.py:203
  10.5 0.1 dynamic-slice_cosine_fusion
  10.7 0.3 subtract_convert_fusion
  10.9 0.1 pad_maximum_fusion.query_ref
  11.1 0.1 broadcast_add_fusion
  11.2 0.1 pad_add_fusion.span_ref
  11.2 0.1 add.136.place_ref
  11.3 0.1 add.127.place_ref
  11.4 1.7 %fusion.2 = f32[64,128]{1,0:T(8,128)S(1)} fusion(bf16[8192,128]{1,0:T(8,128)(2,1)S(1)} %copy-done, bf16[64,16384]{1,0:T(8,128)(2,1)} %param.6, s32[]{:T(128)S(6)} %select_n.36), kind=kOutput, calls=%fused_computation.2 | convolution fusion | flops 134217728 | bytes 3178500 | tf_op jit(solution)/shard_map/dot_general | solution.py:202
  13.2 6.0 %collective-permute-done = bf16[32,8192]{1,0:T(8,128)(2,1)} collective-permute-done((bf16[32,8192]{1,0:T(8,128)(2,1)}, bf16[32,8192]{1,0:T(8,128)(2,1)}, u32[]{:S(2)}, u32[]{:S(2)}) %collective-permute-start) | collective-permute-done | bytes 524320 | tf_op jit(solution)/shard_map/ppermute | solution.py:192
  19.1 1.5 %fusion.24 = f32[32,128]{1,0:T(8,128)S(1)} fusion(bf16[32,8192]{1,0:T(8,128)(2,1)} %collective-permute-done, bf16[8192,128]{1,0:T(8,128)(2,1)S(1)} %copy-done), kind=kOutput, calls=%fused_computation.78 | convolution fusion | flops 67108864 | bytes 2637824 | tf_op jit(solution)/shard_map/dot_general | solution.py:202
  20.6 1.5 %fusion.25 = f32[32,128]{1,0:T(8,128)S(1)} fusion(bf16[32,8192]{1,0:T(8,128)(2,1)} %collective-permute-done, bf16[8192,128]{1,0:T(8,128)(2,1)S(1)} %copy-done.1), kind=kOutput, calls=%fused_computation.79 | convolution fusion | flops 67108864 | bytes 2637824 | tf_op jit(solution)/shard_map/dot_general | solution.py:203
  22.1 7.3 %collective-permute-done.2 = bf16[32,8192]{1,0:T(8,128)(2,1)S(1)} collective-permute-done((bf16[32,8192]{1,0:T(8,128)(2,1)}, bf16[32,8192]{1,0:T(8,128)(2,1)S(1)}, u32[]{:S(2)}, u32[]{:S(2)}) %collective-permute-start.2) | collective-permute-done | bytes 524320 | tf_op jit(solution)/shard_map/ppermute | solution.py:192
  29.4 0.4 fusion.26
  29.9 0.4 fusion.27
  30.4 1.8 %collective-permute-start.1 = (f32[64,256]{1,0:T(8,128)S(1)}, f32[64,256]{1,0:T(8,128)S(1)}, u32[]{:S(2)}, u32[]{:S(2)}) collective-permute-start(f32[64,256]{1,0:T(8,128)S(1)} %pad_maximum_fusion.3), channel_id=1, source_target_pairs={{0,1},{1,0},{2,3},{3,2},{4,5},{5,4},{6,7},{7,6},{8,9},{9,8},{10,11... | collective-permute-start | bytes 196616 | tf_op jit(solution)/shard_map/ppermute | solution.py:252
  32.2 0.3 collective-permute-start.3
  32.5 2.4 %collective-permute-done.1 = f32[64,256]{1,0:T(8,128)S(1)} collective-permute-done((f32[64,256]{1,0:T(8,128)S(1)}, f32[64,256]{1,0:T(8,128)S(1)}, u32[]{:S(2)}, u32[]{:S(2)}) %collective-permute-start.1) | collective-permute-done | bytes 65568 | tf_op jit(solution)/shard_map/ppermute | solution.py:252
  34.9 0.1 fusion.10
  35.0 0.1 constant_dynamic-update-slice_fusion.9
  35.1 2.7 %collective-permute-start.9 = (bf16[64,256]{1,0:T(8,128)(2,1)S(1)}, bf16[64,256]{1,0:T(8,128)(2,1)S(1)}, u32[]{:S(2)}, u32[]{:S(2)}) collective-permute-start(bf16[64,256]{1,0:T(8,128)(2,1)S(1)} %get-tuple-element.9.refs_0_), channel_id=1, source_target_pairs={{0,16},{2,18},{4,20},{6,22},{8,24},{10,26},{12,28},{14,30},{16,0},... | collective-permute-start | bytes 98312 | tf_op jit(solution)/shard_map/ppermute | solution.py:167
  37.8 1.6 %collective-permute-start.10 = (bf16[64,256]{1,0:T(8,128)(2,1)S(1)}, bf16[64,256]{1,0:T(8,128)(2,1)S(1)}, u32[]{:S(2)}, u32[]{:S(2)}) collective-permute-start(bf16[64,256]{1,0:T(8,128)(2,1)S(1)} %get-tuple-element.9.refs_0_), channel_id=1, source_target_pairs={{0,8},{2,10},{4,12},{6,14},{8,0},{10,2},{12,4},{14,6},{16,24},{18,... | collective-permute-start | bytes 98312 | tf_op jit(solution)/shard_map/ppermute | solution.py:167
  39.4 0.1 collective-permute-start.11
  39.6 0.1 fusion.6
  39.7 0.1 constant_dynamic-update-slice_fusion.4
  39.7 1.8 %collective-permute-start.4 = (bf16[64,256]{1,0:T(8,128)(2,1)S(1)}, bf16[64,256]{1,0:T(8,128)(2,1)S(1)}, u32[]{:S(2)}, u32[]{:S(2)}) collective-permute-start(bf16[64,256]{1,0:T(8,128)(2,1)S(1)} %get-tuple-element.11.refs_0_), channel_id=1, source_target_pairs={{0,16},{2,18},{4,20},{6,22},{8,24},{10,26},{12,28},{14,30},{16,0},... | collective-permute-start | bytes 98312 | tf_op jit(solution)/shard_map/ppermute | solution.py:167
  41.6 2.5 %collective-permute-start.5 = (bf16[64,256]{1,0:T(8,128)(2,1)S(1)}, bf16[64,256]{1,0:T(8,128)(2,1)S(1)}, u32[]{:S(2)}, u32[]{:S(2)}) collective-permute-start(bf16[64,256]{1,0:T(8,128)(2,1)S(1)} %get-tuple-element.11.refs_0_), channel_id=1, source_target_pairs={{0,8},{2,10},{4,12},{6,14},{8,0},{10,2},{12,4},{14,6},{16,24},{18,... | collective-permute-start | bytes 98312 | tf_op jit(solution)/shard_map/ppermute | solution.py:167
  44.1 0.1 collective-permute-start.6
  44.2 1.1 %collective-permute-done.11.refs_3_ = bf16[64,256]{1,0:T(8,128)(2,1)S(1)} collective-permute-done((bf16[64,256]{1,0:T(8,128)(2,1)S(1)}, bf16[64,256]{1,0:T(8,128)(2,1)S(1)}, u32[]{:S(2)}, u32[]{:S(2)}) %collective-permute-start.11) | collective-permute-done | bytes 32800 | tf_op jit(solution)/shard_map/ppermute | solution.py:167
  45.3 0.1 pad_maximum_fusion.2
  45.4 1.6 %collective-permute-start.12 = (bf16[256,256]{1,0:T(8,128)(2,1)S(1)}, bf16[256,256]{1,0:T(8,128)(2,1)S(1)}, u32[]{:S(2)}, u32[]{:S(2)}) collective-permute-start(bf16[256,256]{1,0:T(8,128)(2,1)S(1)} %pad_maximum_fusion.2), channel_id=1, source_target_pairs={{0,4},{2,6},{4,0},{6,2},{8,12},{10,14},{12,8},{14,10},{16,20},{18,... | collective-permute-start | bytes 393224 | tf_op jit(solution)/shard_map/ppermute | solution.py:167
  47.0 2.8 %collective-permute-done.6.refs_3_ = bf16[64,256]{1,0:T(8,128)(2,1)S(1)} collective-permute-done((bf16[64,256]{1,0:T(8,128)(2,1)S(1)}, bf16[64,256]{1,0:T(8,128)(2,1)S(1)}, u32[]{:S(2)}, u32[]{:S(2)}) %collective-permute-start.6) | collective-permute-done | bytes 32800 | tf_op jit(solution)/shard_map/ppermute | solution.py:167
  49.8 0.1 pad_maximum_fusion.1
  49.9 1.6 %collective-permute-start.7 = (bf16[256,256]{1,0:T(8,128)(2,1)S(1)}, bf16[256,256]{1,0:T(8,128)(2,1)S(1)}, u32[]{:S(2)}, u32[]{:S(2)}) collective-permute-start(bf16[256,256]{1,0:T(8,128)(2,1)S(1)} %pad_maximum_fusion.1), channel_id=1, source_target_pairs={{0,4},{2,6},{4,0},{6,2},{8,12},{10,14},{12,8},{14,10},{16,20},{18,... | collective-permute-start | bytes 393224 | tf_op jit(solution)/shard_map/ppermute | solution.py:167
  51.5 0.1 collective-permute-start.13
  51.6 3.3 %collective-permute-done.7.refs_4_ = bf16[256,256]{1,0:T(8,128)(2,1)S(1)} collective-permute-done((bf16[256,256]{1,0:T(8,128)(2,1)S(1)}, bf16[256,256]{1,0:T(8,128)(2,1)S(1)}, u32[]{:S(2)}, u32[]{:S(2)}) %collective-permute-start.7) | collective-permute-done | bytes 131104 | tf_op jit(solution)/shard_map/ppermute | solution.py:167
  54.9 0.1 collective-permute-start.8
  55.0 0.6 pad_maximum_fusion.10
  55.6 2.7 %attend_part.1 = (f32[1024,1]{1,0:T(8,128)S(1)}, f32[1024,1]{1,0:T(8,128)S(1)}, f32[1024,128]{1,0:T(8,128)S(1)}) custom-call(s32[2]{0:T(128)S(1)} %pad_add_fusion.span_ref, s32[1,1024]{1,0:T(1,128)S(1)} %add.136.place_ref, bf16[1024,128]{1,0:T(8,128)(2,1)S(1)} %pad_maximum_fusion.query_ref, bf16[64,256]{1,0:T(8,128)(2,1)S(1)} %get-tuple-element.9.refs_0_, ...), custom_call_target="tpu_custom_call" | custom-call | flops 536870912 | bytes 1048576 | tf_op jit(solution)/shard_map/attend_part/pallas_call | solution.py:120
  58.3 4.0 %attend_last.1 = bf16[64,2048]{1,0:T(8,128)(2,1)} custom-call(s32[2]{0:T(128)S(1)} %pad_add_fusion.span_ref, s32[1,1024]{1,0:T(1,128)S(1)} %add.127.place_ref, bf16[1024,128]{1,0:T(8,128)(2,1)S(1)} %pad_maximum_fusion.query_ref, bf16[64,256]{1,0:T(8,128)(2,1)S(1)} %get-tuple-element.11.refs_0_, bf16[64,256]{1,0:T(8,128)(2,1)S(1)} %collective-permute-done.4.refs_1_, ...), custom_call_target="tpu_custom_call" | custom-call | flops 536870912 | bytes 1048576 | tf_op jit(solution)/shard_map/attend_last/pallas_call | solution.py:120
  (44 shorter events, 0.3 us)
Async XLA Ops:
  0.6 10.8 %copy-start = (bf16[8192,128]{1,0:T(8,128)(2,1)S(1)}, bf16[8192,128]{1,0:T(8,128)(2,1)}, u32[]{:S(2)}) copy-start(bf16[8192,128]{1,0:T(8,128)(2,1)} %param.8) | copy-start | bytes 6291460
  0.6 6.6 %copy-start.5 = (s32[16]{0:T(128)S(1)}, s32[16]{0:T(128)}, u32[]{:S(2)}) copy-start(s32[16]{0:T(128)} %constant.37.clone) | copy-start | bytes 196
  0.7 6.5 %copy-start.2 = (bf16[64,2048]{1,0:T(8,128)(2,1)S(1)}, bf16[64,2048]{1,0:T(8,128)(2,1)}, u32[]{:S(2)}) copy-start(bf16[64,2048]{1,0:T(8,128)(2,1)} %param.7) | copy-start | bytes 786436
  3.1 16.0 %collective-permute-start = (bf16[32,8192]{1,0:T(8,128)(2,1)}, bf16[32,8192]{1,0:T(8,128)(2,1)}, u32[]{:S(2)}, u32[]{:S(2)}) collective-permute-start(bf16[32,8192]{1,0:T(8,128)(2,1)} %get-tuple-element.12), channel_id=1, source_target_pairs={{0,1},{1,0},{2,3},{3,2},{4,5},{5,4},{6,7},{7,6},{8,9},{9,8},{10,11... | collective-permute-start | bytes 1572872 | tf_op jit(solution)/shard_map/ppermute | solution.py:192
  6.1 23.4 %collective-permute-start.2 = (bf16[32,8192]{1,0:T(8,128)(2,1)}, bf16[32,8192]{1,0:T(8,128)(2,1)S(1)}, u32[]{:S(2)}, u32[]{:S(2)}) collective-permute-start(bf16[32,8192]{1,0:T(8,128)(2,1)} %get-tuple-element.13), channel_id=1, source_target_pairs={{0,1},{1,0},{2,3},{3,2},{4,5},{5,4},{6,7},{7,6},{8,9},{9,8},{10,11... | collective-permute-start | bytes 1572872 | tf_op jit(solution)/shard_map/ppermute | solution.py:192
  7.2 3.3 %copy-start.3 = (f32[128,64]{1,0:T(8,128)S(1)}, f32[128,64]{1,0:T(8,128)}, u32[]{:S(2)}) copy-start(f32[128,64]{1,0:T(8,128)} %broadcast_multiply_fusion) | copy-start | bytes 98308
  13.1 7.5 %copy-start.1 = (bf16[8192,128]{1,0:T(8,128)(2,1)S(1)}, bf16[8192,128]{1,0:T(8,128)(2,1)}, u32[]{:S(2)}) copy-start(bf16[8192,128]{1,0:T(8,128)(2,1)} %param.9) | copy-start | bytes 6291460
  22.1 8.2 %copy-start.4 = (f32[64,128]{1,0:T(8,128)S(1)}, f32[64,128]{1,0:T(8,128)}, u32[]{:S(2)}) copy-start(f32[64,128]{1,0:T(8,128)} %fusion) | copy-start | bytes 98308
  30.4 4.5 %collective-permute-start.1 = (f32[64,256]{1,0:T(8,128)S(1)}, f32[64,256]{1,0:T(8,128)S(1)}, u32[]{:S(2)}, u32[]{:S(2)}) collective-permute-start(f32[64,256]{1,0:T(8,128)S(1)} %pad_maximum_fusion.3), channel_id=1, source_target_pairs={{0,1},{1,0},{2,3},{3,2},{4,5},{5,4},{6,7},{7,6},{8,9},{9,8},{10,11... | collective-permute-start | bytes 196616 | tf_op jit(solution)/shard_map/ppermute | solution.py:252
  32.2 7.3 %collective-permute-start.3 = (f32[64,256]{1,0:T(8,128)S(1)}, f32[64,256]{1,0:T(8,128)S(1)}, u32[]{:S(2)}, u32[]{:S(2)}) collective-permute-start(f32[64,256]{1,0:T(8,128)S(1)} %pad_maximum_fusion.4), channel_id=1, source_target_pairs={{0,1},{1,0},{2,3},{3,2},{4,5},{5,4},{6,7},{7,6},{8,9},{9,8},{10,11... | collective-permute-start | bytes 196616 | tf_op jit(solution)/shard_map/ppermute | solution.py:252
  35.1 9.0 %collective-permute-start.9 = (bf16[64,256]{1,0:T(8,128)(2,1)S(1)}, bf16[64,256]{1,0:T(8,128)(2,1)S(1)}, u32[]{:S(2)}, u32[]{:S(2)}) collective-permute-start(bf16[64,256]{1,0:T(8,128)(2,1)S(1)} %get-tuple-element.9.refs_0_), channel_id=1, source_target_pairs={{0,16},{2,18},{4,20},{6,22},{8,24},{10,26},{12,28},{14,30},{16,0},... | collective-permute-start | bytes 98312 | tf_op jit(solution)/shard_map/ppermute | solution.py:167
  37.8 6.4 %collective-permute-start.10 = (bf16[64,256]{1,0:T(8,128)(2,1)S(1)}, bf16[64,256]{1,0:T(8,128)(2,1)S(1)}, u32[]{:S(2)}, u32[]{:S(2)}) collective-permute-start(bf16[64,256]{1,0:T(8,128)(2,1)S(1)} %get-tuple-element.9.refs_0_), channel_id=1, source_target_pairs={{0,8},{2,10},{4,12},{6,14},{8,0},{10,2},{12,4},{14,6},{16,24},{18,... | collective-permute-start | bytes 98312 | tf_op jit(solution)/shard_map/ppermute | solution.py:167
  39.4 5.9 %collective-permute-start.11 = (bf16[64,256]{1,0:T(8,128)(2,1)S(1)}, bf16[64,256]{1,0:T(8,128)(2,1)S(1)}, u32[]{:S(2)}, u32[]{:S(2)}) collective-permute-start(bf16[64,256]{1,0:T(8,128)(2,1)S(1)} %get-tuple-element.9.refs_0_), channel_id=1, source_target_pairs={{0,24},{2,26},{4,28},{6,30},{8,16},{10,18},{12,20},{14,22},{16,8},... | collective-permute-start | bytes 98312 | tf_op jit(solution)/shard_map/ppermute | solution.py:167
  39.7 7.3 %collective-permute-start.4 = (bf16[64,256]{1,0:T(8,128)(2,1)S(1)}, bf16[64,256]{1,0:T(8,128)(2,1)S(1)}, u32[]{:S(2)}, u32[]{:S(2)}) collective-permute-start(bf16[64,256]{1,0:T(8,128)(2,1)S(1)} %get-tuple-element.11.refs_0_), channel_id=1, source_target_pairs={{0,16},{2,18},{4,20},{6,22},{8,24},{10,26},{12,28},{14,30},{16,0},... | collective-permute-start | bytes 98312 | tf_op jit(solution)/shard_map/ppermute | solution.py:167
  41.6 5.4 %collective-permute-start.5 = (bf16[64,256]{1,0:T(8,128)(2,1)S(1)}, bf16[64,256]{1,0:T(8,128)(2,1)S(1)}, u32[]{:S(2)}, u32[]{:S(2)}) collective-permute-start(bf16[64,256]{1,0:T(8,128)(2,1)S(1)} %get-tuple-element.11.refs_0_), channel_id=1, source_target_pairs={{0,8},{2,10},{4,12},{6,14},{8,0},{10,2},{12,4},{14,6},{16,24},{18,... | collective-permute-start | bytes 98312 | tf_op jit(solution)/shard_map/ppermute | solution.py:167
  44.1 5.7 %collective-permute-start.6 = (bf16[64,256]{1,0:T(8,128)(2,1)S(1)}, bf16[64,256]{1,0:T(8,128)(2,1)S(1)}, u32[]{:S(2)}, u32[]{:S(2)}) collective-permute-start(bf16[64,256]{1,0:T(8,128)(2,1)S(1)} %get-tuple-element.11.refs_0_), channel_id=1, source_target_pairs={{0,24},{2,26},{4,28},{6,30},{8,16},{10,18},{12,20},{14,22},{16,8},... | collective-permute-start | bytes 98312 | tf_op jit(solution)/shard_map/ppermute | solution.py:167
  45.4 6.1 %collective-permute-start.12 = (bf16[256,256]{1,0:T(8,128)(2,1)S(1)}, bf16[256,256]{1,0:T(8,128)(2,1)S(1)}, u32[]{:S(2)}, u32[]{:S(2)}) collective-permute-start(bf16[256,256]{1,0:T(8,128)(2,1)S(1)} %pad_maximum_fusion.2), channel_id=1, source_target_pairs={{0,4},{2,6},{4,0},{6,2},{8,12},{10,14},{12,8},{14,10},{16,20},{18,... | collective-permute-start | bytes 393224 | tf_op jit(solution)/shard_map/ppermute | solution.py:167
  49.9 5.0 %collective-permute-start.7 = (bf16[256,256]{1,0:T(8,128)(2,1)S(1)}, bf16[256,256]{1,0:T(8,128)(2,1)S(1)}, u32[]{:S(2)}, u32[]{:S(2)}) collective-permute-start(bf16[256,256]{1,0:T(8,128)(2,1)S(1)} %pad_maximum_fusion.1), channel_id=1, source_target_pairs={{0,4},{2,6},{4,0},{6,2},{8,12},{10,14},{12,8},{14,10},{16,20},{18,... | collective-permute-start | bytes 393224 | tf_op jit(solution)/shard_map/ppermute | solution.py:167
  51.5 4.1 %collective-permute-start.13 = (bf16[512,256]{1,0:T(8,128)(2,1)S(1)}, bf16[512,256]{1,0:T(8,128)(2,1)S(1)}, u32[]{:S(2)}, u32[]{:S(2)}) collective-permute-start(bf16[512,256]{1,0:T(8,128)(2,1)S(1)} %constant_dynamic-update-slice_fusion.5), channel_id=1, source_target_pairs={{0,2},{2,0},{4,6},{6,4},{8,10},{10,8},{12,14},{14,12},{16,18},{18,... | collective-permute-start | bytes 786440 | tf_op jit(solution)/shard_map/ppermute | solution.py:167
  54.9 3.4 %collective-permute-start.8 = (bf16[512,256]{1,0:T(8,128)(2,1)S(1)}, bf16[512,256]{1,0:T(8,128)(2,1)S(1)}, u32[]{:S(2)}, u32[]{:S(2)}) collective-permute-start(bf16[512,256]{1,0:T(8,128)(2,1)S(1)} %constant_dynamic-update-slice_fusion), channel_id=1, source_target_pairs={{0,2},{2,0},{4,6},{6,4},{8,10},{10,8},{12,14},{14,12},{16,18},{18,... | collective-permute-start | bytes 786440 | tf_op jit(solution)/shard_map/ppermute | solution.py:167

commit v3 on v2

--- a/solution.py
+++ b/solution.py
@@ -155,57 +155,70 @@
     return stages
 
 
-def spread(block, contexts):
-    pieces, masks = [block], [[0]]
-    for stage in stages_of(contexts):
-        known = jnp.concatenate(pieces, axis=0) if len(pieces) > 1 else pieces[0]
-        known_masks = [mask for piece_masks in masks for mask in piece_masks]
-        moves = [0]
-        for bit in stage:
-            moves = moves + [move ^ bit for move in moves]
-        for move in moves[1:]:
-            pieces.append(lax.ppermute(known, "ctx", [(i, i ^ move) for i in range(contexts)]))
-            masks.append([mask ^ move for mask in known_masks])
-    return pieces, masks
-
-
-def make_local(contexts, shards, parts):
+def after(value, *earlier):
+    return lax.optimization_barrier((value, *earlier))[0]
+
+
+def make_local(contexts, shards, plan):
     def local(tokens, queries, key_weight, value_weight):
         rows = tokens.shape[0]
         depth, head_size = key_weight.shape
         heads = queries.shape[1] // head_size
         group_rows = shards * rows
-        part_rows = rows // parts
         context = lax.axis_index("ctx")
         shard = lax.axis_index("fsdp")
-
-        received = []
-        for part in range(parts):
-            top = part * part_rows
-            arrived = []
+        unit = rows // sum(sum(part) for part in plan)
+
+        def send_rows(top, count, *earlier):
+            source = after(tokens, *earlier) if earlier else tokens
+            arrived, sent = [], []
             for step in range(1, shards):
                 target = lax.rem(shard + step, shards)
                 columns = lax.dynamic_slice(
-                    tokens, (jnp.int32(top), target * depth), (part_rows, depth)
-                )
+                    source, (jnp.int32(top), target * depth), (count, depth)
+                )
+                sent.append(columns)
                 arrived.append(
                     lax.ppermute(
                         columns, "fsdp", [(i, (i + step) % shards) for i in range(shards)]
                     )
                 )
-            received.append(arrived)
+            return arrived, sent
+
+        def rows_of(table, top, count):
+            return table.reshape(shards, rows, -1)[:, top : top + count].reshape(
+                shards * count, -1
+            )
+
+        class Part:
+            pass
+
+        parts = []
+        chunks = []
+        top = 0
+        for sizes in plan:
+            part = Part()
+            part.top = top
+            part.rows = sum(sizes) * unit
+            part.first = len(chunks)
+            for size in sizes:
+                chunks.append((top, size * unit))
+                top += size * unit
+            part.end = len(chunks)
+            part.stage = None
+            parts.append(part)
+        stages = stages_of(contexts)
+        ahead = parts[0].end + 1
+
+        flying = []
+        sent = ()
+        for chunk in chunks[:ahead]:
+            arrived, sent = send_rows(*chunk, *sent)
+            flying.append(arrived)
+
+        weight = after(jnp.concatenate([key_weight, value_weight], axis=1), *sent)
         own_columns = lax.dynamic_slice_in_dim(tokens, shard * depth, depth, 1)
-
-        def project(columns):
-            return jnp.concatenate(
-                [
-                    jnp.dot(columns, key_weight, preferred_element_type=jnp.float32),
-                    jnp.dot(columns, value_weight, preferred_element_type=jnp.float32),
-                ],
-                axis=1,
-            )
-
-        own_product = project(own_columns)
+        own_product = jnp.dot(own_columns, weight, preferred_element_type=jnp.float32)
 
         start = context * group_rows
         positions = start + jnp.arange(group_rows, dtype=jnp.int32)
@@ -219,21 +232,20 @@
             .reshape(heads * rows, head_size)
         )
         span = jnp.stack([start, start + shard * rows]).astype(jnp.int32)
-
-        def rows_of(table, top):
-            return table.reshape(shards, rows, -1)[:, top : top + part_rows].reshape(
-                shards * part_rows, -1
-            )
-
-        state = None
-        cache_parts = []
-        for part in range(parts):
-            top = part * part_rows
-            products = [own_product[top : top + part_rows]] + [
-                project(columns) for columns in received[part]
+        own_product, cosine, sine_table, query_flat, span = lax.optimization_barrier(
+            (own_product, cosine, sine_table, query_flat, span)
+        )
+
+        def exchange(part, arrived):
+            columns = [
+                jnp.concatenate([chunk[s] for chunk in arrived], axis=0)
+                for s in range(shards - 1)
+            ]
+            products = [own_product[part.top : part.top + part.rows]] + [
+                jnp.dot(c, weight, preferred_element_type=jnp.float32) for c in columns
             ]
             if shards == 2:
-                partial_sums = jnp.concatenate(
+                sums = jnp.concatenate(
                     [
                         jnp.where(shard == 0, products[0], products[1]),
                         jnp.where(shard == 0, products[1], products[0]),
@@ -241,32 +253,89 @@
                     axis=0,
                 )
             else:
-                partial_sums = jnp.zeros((shards * part_rows, 2 * head_size), jnp.float32)
+                sums = jnp.zeros((shards * part.rows, 2 * head_size), jnp.float32)
                 for step in range(shards):
                     source = lax.rem(shard + shards - step, shards)
-                    partial_sums = lax.dynamic_update_slice_in_dim(
-                        partial_sums, products[step], source * part_rows, 0
+                    sums = lax.dynamic_update_slice_in_dim(
+                        sums, products[step], source * part.rows, 0
                     )
+            part.sums = after(sums)
+            part.other = jnp.zeros_like(sums)
             reach = 1
             while reach < shards:
-                partial_sums = partial_sums + lax.ppermute(
-                    partial_sums, "fsdp", [(i, i ^ reach) for i in range(shards)]
+                if reach > 1:
+                    part.sums = part.sums + part.other
+                part.other = lax.ppermute(
+                    part.sums, "fsdp", [(i, i ^ reach) for i in range(shards)]
                 )
                 reach *= 2
-            keys_rot = rotate(
-                partial_sums[:, :head_size], rows_of(cosine, top), rows_of(sine_table, top)
-            ).astype(jnp.bfloat16)
-            block = jnp.concatenate(
-                [keys_rot, partial_sums[:, head_size:].astype(jnp.bfloat16)], axis=1
-            )
-            cache_parts.append(lax.dynamic_slice_in_dim(block, shard * part_rows, part_rows, 0))
-            pieces, masks = spread(block, contexts)
-            local_pos = rows_of(jnp.arange(group_rows, dtype=jnp.int32)[:, None], top)[:, 0]
-            order = jnp.array([mask for piece_masks in masks for mask in piece_masks], jnp.int32)
+            part.stage = 0
+
+        def held(part):
+            return (part.sums, part.other) if part.stage == 0 else tuple(part.pieces)
+
+        def advance(part, values):
+            if part.stage == 0:
+                sums = values[0] + values[1]
+                keys_rot = rotate(
+                    sums[:, :head_size],
+                    rows_of(cosine, part.top, part.rows),
+                    rows_of(sine_table, part.top, part.rows),
+                ).astype(jnp.bfloat16)
+                block = after(
+                    jnp.concatenate([keys_rot, sums[:, head_size:].astype(jnp.bfloat16)], axis=1)
+                )
+                part.cache = lax.dynamic_slice_in_dim(block, shard * part.rows, part.rows, 0)
+                part.pieces, part.masks = [block], [[0]]
+            else:
+                part.pieces = list(values)
+            known = jnp.concatenate(part.pieces, axis=0)
+            if part.stage < len(stages):
+                known_masks = [mask for piece_masks in part.masks for mask in piece_masks]
+                moves = [0]
+                for bit in stages[part.stage]:
+                    moves = moves + [move ^ bit for move in moves]
+                for move in moves[1:]:
+                    part.pieces.append(
+                        lax.ppermute(known, "ctx", [(i, i ^ move) for i in range(contexts)])
+                    )
+                    part.masks.append([mask ^ move for mask in known_masks])
+            part.stage += 1
+
+        def step_all(going, extra=()):
+            gated = lax.optimization_barrier((tuple(held(part) for part in going), extra))
+            for part, values in zip(going, gated[0]):
+                advance(part, values)
+            return gated[1]
+
+        def finish(part, state, last):
+            local_pos = rows_of(
+                jnp.arange(group_rows, dtype=jnp.int32)[:, None], part.top, part.rows
+            )[:, 0]
+            order = jnp.array([mask for masks in part.masks for mask in masks], jnp.int32)
             place = ((context ^ order)[:, None] * group_rows + local_pos[None, :]).reshape(1, -1)
-            last = part == parts - 1
-            state = attend(span, place, query_flat, pieces, state, last, rows)
-        kv_cache = jnp.concatenate(cache_parts, axis=0)
+            return attend(span, place, query_flat, part.pieces, state, last, rows)
+
+        for index, part in enumerate(parts):
+            going = [p for p in parts[:index] if p.stage <= len(stages)]
+            arrived = flying[part.first : part.end]
+            arrived = list(lax.optimization_barrier((arrived, own_product))[0])
+            exchange(part, arrived)
+            for chunk in chunks[len(flying) : part.end + 2]:
+                flying.append(send_rows(*chunk, part.sums)[0])
+            if index + 1 < len(parts):
+                nearest = flying[parts[index + 1].first]
+                nearest = step_all(going + [part], tuple(nearest))
+                flying[parts[index + 1].first] = list(nearest)
+        state = None
+        going = list(parts)
+        while going:
+            step_all(going)
+            ready = [part for part in going if part.stage > len(stages)]
+            going = [part for part in going if part.stage <= len(stages)]
+            for part in ready:
+                state = finish(part, state, part is parts[-1])
+        kv_cache = jnp.concatenate([part.cache for part in parts], axis=0)
         return (kv_cache, state)
 
     return local
@@ -275,7 +344,7 @@
 def solution(mesh):
     placed = (P(("ctx", "fsdp"), None), P(("ctx", "fsdp"), None), P("fsdp", None), P("fsdp", None))
     return jax.shard_map(
-        make_local(mesh.shape["ctx"], mesh.shape["fsdp"], 2),
+        make_local(mesh.shape["ctx"], mesh.shape["fsdp"], ((1, 5), (1, 1))),
         mesh=mesh,
         in_specs=placed,
         out_specs=(P(("ctx", "fsdp"), None), P(("ctx", "fsdp"), None)),

time: 62.6 us -> 67.5 us (1.078)
  waiting for transfers between devices: 22.9 us -> 17.3 us
  other arithmetic: 2.82 us -> 7.58 us
  starting transfers between devices: 17.3 us -> 21.6 us
  local copies, waits for them, and re-layouts: 3.08 us -> 6.6 us
  matrix products: 8.61 us -> 6.9 us
    ppermute x14 -> x16, waiting for transfers between devices: 22.9 us -> 17.3 us  [the longest x10 7.64 us: advance(): lax.ppermute(known, 'ctx', [(i, i ^ move) for i in range(contexts)])]
    concatenate x5 -> x8, other arithmetic: 0.8 us -> 5.44 us  [the longest x1 4.61 us: local(): weight = after(jnp.concatenate([key_weight, value_weight], axis=1), *sent)]
    ppermute x14 -> x16, starting transfers between devices: 17.3 us -> 21.6 us  [the longest x10 12.7 us: advance(): lax.ppermute(known, 'ctx', [(i, i ^ move) for i in range(contexts)])]
    unnamed x18 -> x14, local copies, waits for them, and re-layouts: 0.06 us -> 4.07 us
    dot_general x6 -> x3, matrix products: 8.61 us -> 6.9 us  [the longest x2 3.49 us: exchange(): jnp.dot(c, weight, preferred_element_type=jnp.float32)]
    dynamic_slice x3 -> x7, local copies, waits for them, and re-layouts: 2.45 us -> 1.42 us  [the longest x4 1.4 us: send_rows(): lax.dynamic_slice(source, (jnp.int32(top), target * depth), (count, depth))]
    transpose x1, other arithmetic: 0.05 us -> 1 us  [local(): queries.astype(jnp.float32).reshape(rows, heads, head_size)]
    mul x2 -> x1, other arithmetic: 0.72 us -> 0.01 us  [finish(): (context ^ order)[:, None] * group_rows + local_pos[None, :]]
  transfers between devices with their start and end apart: 14 -> 16, of which waited for: 6 -> 8; matrix products, arithmetic and copies ran while one was open for 18% -> 23% of each run, Pallas kernels for 4% -> 5%
where the time goes in v3:
time: 67.5 us; the launch traced here: 67.2 us
  starting transfers between devices  21.6 us (32%)
  waiting for transfers between devices  17.3 us (26%)
  other arithmetic  7.58 us (11%)
  matrix products  6.9 us (10%)
  local copies, waits for them, and re-layouts  6.6 us (10%)
  Pallas kernels  6.39 us (9%)
  between operations  0.88 us (1%)
    ppermute x10, starting transfers between devices, advance(): lax.ppermute(known, 'ctx', [(i, i ^ move) for i in range(contexts)])  12.7 us
    ppermute x10, waiting for transfers between devices, advance(): lax.ppermute(known, 'ctx', [(i, i ^ move) for i in range(contexts)])  7.64 us
    pallas_call x2, Pallas kernels, attend(): pl.pallas_call(partial(attention_kernel, count=len(pieces), carry=state i...  6.39 us
    ppermute x4, waiting for transfers between devices, send_rows(): lax.ppermute(columns, 'fsdp', [(i, (i + step) % shards) for i in range(sh...  5.93 us
    ppermute x4, starting transfers between devices, send_rows(): lax.ppermute(columns, 'fsdp', [(i, (i + step) % shards) for i in range(sh...  5.11 us
    concatenate x1, other arithmetic, local(): weight = after(jnp.concatenate([key_weight, value_weight], axis=1), *sent)  4.61 us
    unnamed x14, local copies, waits for them, and re-layouts  4.07 us
    ppermute x2, starting transfers between devices, exchange(): lax.ppermute(part.sums, 'fsdp', [(i, i ^ reach) for i in range(shards)])  3.8 us
  transfers between devices with their start and end apart: 16, of which 8 were waited for; matrix products, arithmetic and copies ran while one was open for 23% of the time, Pallas kernels for 5%

profile of v3, /device:TPU:0, one launch (start us, length us, event | category | flops | bytes accessed | tf_op | source)
XLA Modules:
  0.0 67.2 jit_solution(12931999622296302362)
XLA Ops:
  0.7 1.6 %copy-done = bf16[64,16384]{1,0:T(8,128)(2,1)S(1)} copy-done((bf16[64,16384]{1,0:T(8,128)(2,1)S(1)}, bf16[64,16384]{1,0:T(8,128)(2,1)}, u32[]{:S(2)}) %copy-start) | copy-done | bytes 2097176
  2.2 0.7 %constant_dynamic-slice_fusion.4 = bf16[8,8192]{1,0:T(8,128)(2,1)} fusion(bf16[64,16384]{1,0:T(8,128)(2,1)S(1)} %copy-done, s32[]{:T(128)S(6)} %select_n.45), kind=kLoop, calls=%fused_computation.63 | loop fusion | bytes 262148 | tf_op jit(solution)/shard_map/dynamic_slice | solution.py:177
  2.9 2.9 %collective-permute-start = (bf16[8,8192]{1,0:T(8,128)(2,1)}, bf16[8,8192]{1,0:T(8,128)(2,1)}, u32[]{:S(2)}, u32[]{:S(2)}) collective-permute-start(bf16[8,8192]{1,0:T(8,128)(2,1)} %constant_dynamic-slice_fusion.4), channel_id=1, source_target_pairs={{0,1},{1,0},{2,3},{3,2},{4,5},{5,4},{6,7},{7,6},{8,9},{9,8},{10,11... | collective-permute-start | bytes 393224 | tf_op jit(solution)/shard_map/ppermute | solution.py:182
  5.9 0.1 collective-permute-start.1
  6.0 0.7 %constant_dynamic-slice_fusion.7 = bf16[8,8192]{1,0:T(8,128)(2,1)} fusion(bf16[64,16384]{1,0:T(8,128)(2,1)S(1)} %copy-done, s32[]{:T(128)S(6)} %select_n.45), kind=kLoop, calls=%fused_computation.72 | loop fusion | bytes 262148 | tf_op jit(solution)/shard_map/dynamic_slice | solution.py:177
  6.6 2.0 %collective-permute-start.3 = (bf16[8,8192]{1,0:T(8,128)(2,1)}, bf16[8,8192]{1,0:T(8,128)(2,1)}, u32[]{:S(2)}, u32[]{:S(2)}) collective-permute-start(bf16[8,8192]{1,0:T(8,128)(2,1)} %constant_dynamic-slice_fusion.7), channel_id=1, source_target_pairs={{0,1},{1,0},{2,3},{3,2},{4,5},{5,4},{6,7},{7,6},{8,9},{9,8},{10,11... | collective-permute-start | bytes 393224 | tf_op jit(solution)/shard_map/ppermute | solution.py:182
  8.7 1.0 %bitcast_bitcast_fusion = f32[16,64,128]{2,1,0:T(8,128)S(1)} fusion(bf16[64,2048]{1,0:T(8,128)(2,1)} %param.7), kind=kLoop, calls=%fused_computation.7 | loop fusion | flops 131072 | bytes 786432 | tf_op jit(solution)/shard_map/transpose | solution.py:228
  9.7 4.6 %pad_maximum_fusion = bf16[8192,256]{1,0:T(8,128)(2,1)} fusion(bf16[8192,128]{1,0:T(8,128)(2,1)} %param.9, bf16[8192,128]{1,0:T(8,128)(2,1)} %param.8), kind=kLoop, calls=%fused_computation | loop fusion | flops 8388608 | bytes 8388608 | tf_op jit(solution)/shard_map/concatenate | solution.py:219
  14.3 0.3 multiply_sine_fusion
  14.6 0.3 subtract_convert_fusion
  14.9 0.1 pad_maximum_fusion.1.query_ref
  15.1 0.1 pad_add_fusion.span_ref
  15.1 3.4 %fusion = f32[64,256]{1,0:T(8,128)S(1)} fusion(bf16[8192,256]{1,0:T(8,128)(2,1)} %pad_maximum_fusion, bf16[64,16384]{1,0:T(8,128)(2,1)S(1)} %copy-done, s32[]{:T(128)S(6)} %select_n.44), kind=kOutput, calls=%fused_computation.1 | convolution fusion | flops 268435456 | bytes 5308420 | tf_op jit(solution)/shard_map/dot_general | solution.py:221
  18.6 5.9 %collective-permute-done.1 = bf16[40,8192]{1,0:T(8,128)(2,1)} collective-permute-done((bf16[40,8192]{1,0:T(8,128)(2,1)S(1)}, bf16[40,8192]{1,0:T(8,128)(2,1)}, u32[]{:S(2)}, u32[]{:S(2)}) %collective-permute-start.1) | collective-permute-done | bytes 655392 | tf_op jit(solution)/shard_map/ppermute | solution.py:182
  24.5 1.9 %slice_select_fusion.1 = (f32[48,256]{1,0:T(8,128)S(1)}, f32[48,256]{1,0:T(8,128)S(1)}) fusion(f32[64,256]{1,0:T(8,128)S(1)} %fusion, pred[]{:T(512)S(6)} %eq.2, bf16[8192,256]{1,0:T(8,128)(2,1)S(1)} %copy-done.1, bf16[40,8192]{1,0:T(8,128)(2,1)} %collective-permute-done.1, bf16[8,8192]{1,0:T(8,128)(2,1)} %collective-permute-done), kind=kOutput, calls=%fused_computation.32 | convolution fusion | flops 202924032 | bytes 5128193 | tf_op jit(solution)/shard_map/dot_general | solution.py:245
  26.5 2.1 %collective-permute-start.2 = (f32[96,256]{1,0:T(8,128)S(1)}, f32[96,256]{1,0:T(8,128)S(1)}, u32[]{:S(2)}, u32[]{:S(2)}) collective-permute-start(f32[96,256]{1,0:T(8,128)S(1)} %pad_maximum_fusion.3), channel_id=1, source_target_pairs={{0,1},{1,0},{2,3},{3,2},{4,5},{5,4},{6,7},{7,6},{8,9},{9,8},{10,11... | collective-permute-start | bytes 294920 | tf_op jit(solution)/shard_map/ppermute | solution.py:268
  28.6 0.1 collective-permute-start.7
  28.7 2.6 %collective-permute-done.2 = f32[96,256]{1,0:T(8,128)S(1)} collective-permute-done((f32[96,256]{1,0:T(8,128)S(1)}, f32[96,256]{1,0:T(8,128)S(1)}, u32[]{:S(2)}, u32[]{:S(2)}) %collective-permute-start.2) | collective-permute-done | bytes 98336 | tf_op jit(solution)/shard_map/ppermute | solution.py:268
  31.3 0.1 fusion.11
  31.4 0.1 pad_maximum_fusion.5.refs_0_
  31.5 4.1 %collective-permute-start.6 = (bf16[96,256]{1,0:T(8,128)(2,1)S(1)}, bf16[96,256]{1,0:T(8,128)(2,1)S(1)}, u32[]{:S(2)}, u32[]{:S(2)}) collective-permute-start(bf16[96,256]{1,0:T(8,128)(2,1)S(1)} %pad_maximum_fusion.5.refs_0_), channel_id=1, source_target_pairs={{0,24},{2,26},{4,28},{6,30},{8,16},{10,18},{12,20},{14,22},{16,8},... | collective-permute-start | bytes 147464 | tf_op jit(solution)/shard_map/ppermute | solution.py:300
  35.6 0.6 collective-permute-start.4
  36.3 1.6 %slice_select_fusion.3 = (f32[16,256]{1,0:T(8,128)S(1)}, f32[16,256]{1,0:T(8,128)S(1)}) fusion(f32[64,256]{1,0:T(8,128)S(1)} %fusion, pred[]{:T(512)S(6)} %eq.2, bf16[8192,256]{1,0:T(8,128)(2,1)S(1)} %copy-done.1, bf16[8,8192]{1,0:T(8,128)(2,1)S(1)} %collective-permute-done.7, bf16[8,8192]{1,0:T(8,128)(2,1)} %collective-permute-done.3), kind=kOutput, calls=%fused_computation.56 | convolution fusion | flops 67641344 | bytes 4505601 | tf_op jit(solution)/shard_map/dot_general | solution.py:245
  37.8 1.7 %collective-permute-start.8 = (f32[32,256]{1,0:T(8,128)S(1)}, f32[32,256]{1,0:T(8,128)S(1)}, u32[]{:S(2)}, u32[]{:S(2)}) collective-permute-start(f32[32,256]{1,0:T(8,128)S(1)} %pad_maximum_fusion.6), channel_id=1, source_target_pairs={{0,1},{1,0},{2,3},{3,2},{4,5},{5,4},{6,7},{7,6},{8,9},{9,8},{10,11... | collective-permute-start | bytes 98312 | tf_op jit(solution)/shard_map/ppermute | solution.py:268
  39.6 0.1 add.127
  39.7 0.9 %collective-permute-done.4.refs_1_ = bf16[96,256]{1,0:T(8,128)(2,1)S(1)} collective-permute-done((bf16[96,256]{1,0:T(8,128)(2,1)S(1)}, bf16[96,256]{1,0:T(8,128)(2,1)S(1)}, u32[]{:S(2)}, u32[]{:S(2)}) %collective-permute-start.4) | collective-permute-done | bytes 49184 | tf_op jit(solution)/shard_map/ppermute | solution.py:300
  40.6 1.2 %collective-permute-done.8 = f32[32,256]{1,0:T(8,128)S(1)} collective-permute-done((f32[32,256]{1,0:T(8,128)S(1)}, f32[32,256]{1,0:T(8,128)S(1)}, u32[]{:S(2)}, u32[]{:S(2)}) %collective-permute-start.8) | collective-permute-done | bytes 32800 | tf_op jit(solution)/shard_map/ppermute | solution.py:268
  41.8 0.1 fusion.15
  41.9 0.1 pad_maximum_fusion.8.refs_0_
  42.0 3.7 %collective-permute-start.12 = (bf16[32,256]{1,0:T(8,128)(2,1)S(1)}, bf16[32,256]{1,0:T(8,128)(2,1)S(1)}, u32[]{:S(2)}, u32[]{:S(2)}) collective-permute-start(bf16[32,256]{1,0:T(8,128)(2,1)S(1)} %pad_maximum_fusion.8.refs_0_), channel_id=1, source_target_pairs={{0,24},{2,26},{4,28},{6,30},{8,16},{10,18},{12,20},{14,22},{16,8},... | collective-permute-start | bytes 49160 | tf_op jit(solution)/shard_map/ppermute | solution.py:300
  45.7 0.6 collective-permute-start.10
  46.4 1.7 %collective-permute-start.9 = (bf16[384,256]{1,0:T(8,128)(2,1)S(1)}, bf16[384,256]{1,0:T(8,128)(2,1)S(1)}, u32[]{:S(2)}, u32[]{:S(2)}) collective-permute-start(bf16[384,256]{1,0:T(8,128)(2,1)S(1)} %pad_maximum_fusion.2), channel_id=1, source_target_pairs={{0,4},{2,6},{4,0},{6,2},{8,12},{10,14},{12,8},{14,10},{16,20},{18,... | collective-permute-start | bytes 589832 | tf_op jit(solution)/shard_map/ppermute | solution.py:300
  48.2 0.1 add.132
  48.3 1.2 %collective-permute-done.11.refs_2_ = bf16[32,256]{1,0:T(8,128)(2,1)S(1)} collective-permute-done((bf16[32,256]{1,0:T(8,128)(2,1)S(1)}, bf16[32,256]{1,0:T(8,128)(2,1)S(1)}, u32[]{:S(2)}, u32[]{:S(2)}) %collective-permute-start.11) | collective-permute-done | bytes 16416 | tf_op jit(solution)/shard_map/ppermute | solution.py:300
  49.5 0.9 %collective-permute-done.10.refs_1_ = bf16[32,256]{1,0:T(8,128)(2,1)S(1)} collective-permute-done((bf16[32,256]{1,0:T(8,128)(2,1)S(1)}, bf16[32,256]{1,0:T(8,128)(2,1)S(1)}, u32[]{:S(2)}, u32[]{:S(2)}) %collective-permute-start.10) | collective-permute-done | bytes 16416 | tf_op jit(solution)/shard_map/ppermute | solution.py:300
  50.4 1.8 %collective-permute-done.9.refs_4_ = bf16[384,256]{1,0:T(8,128)(2,1)S(1)} collective-permute-done((bf16[384,256]{1,0:T(8,128)(2,1)S(1)}, bf16[384,256]{1,0:T(8,128)(2,1)S(1)}, u32[]{:S(2)}, u32[]{:S(2)}) %collective-permute-start.9) | collective-permute-done | bytes 196640 | tf_op jit(solution)/shard_map/ppermute | solution.py:300
  52.1 0.6 constant_dynamic-update-slice_fusion.4
  52.7 0.6 constant_dynamic-update-slice_fusion.3
  53.3 0.6 constant_dynamic-update-slice_fusion.2
  54.0 0.6 constant_dynamic-update-slice_fusion.1
  54.6 0.7 %constant_dynamic-update-slice_fusion = bf16[768,256]{1,0:T(8,128)(2,1)} fusion(bf16[768,256]{1,0:T(8,128)(2,1)} %constant_dynamic-update-slice_fusion.1, bf16[384,256]{1,0:T(8,128)(2,1)S(1)} %collective-permute-done.9.refs_4_), kind=kLoop, calls=%fused_computation.35 | loop fusion | bytes 393216 | tf_op jit(solution)/shard_map/concatenate | solution.py:292
  55.3 0.1 add.130.place_ref
  55.4 0.1 add.135.place_ref
  55.5 1.7 %collective-permute-start.14 = (bf16[128,256]{1,0:T(8,128)(2,1)S(1)}, bf16[128,256]{1,0:T(8,128)(2,1)S(1)}, u32[]{:S(2)}, u32[]{:S(2)}) collective-permute-start(bf16[128,256]{1,0:T(8,128)(2,1)S(1)} %pad_maximum_fusion.4), channel_id=1, source_target_pairs={{0,4},{2,6},{4,0},{6,2},{8,12},{10,14},{12,8},{14,10},{16,20},{18,... | collective-permute-start | bytes 196616 | tf_op jit(solution)/shard_map/ppermute | solution.py:300
  57.3 2.8 %collective-permute-done.14.refs_4_ = bf16[128,256]{1,0:T(8,128)(2,1)S(1)} collective-permute-done((bf16[128,256]{1,0:T(8,128)(2,1)S(1)}, bf16[128,256]{1,0:T(8,128)(2,1)S(1)}, u32[]{:S(2)}, u32[]{:S(2)}) %collective-permute-start.14) | collective-permute-done | bytes 65568 | tf_op jit(solution)/shard_map/ppermute | solution.py:300
  60.2 0.6 pad_maximum_fusion.7
  60.8 3.4 %attend_part.1 = (f32[1024,1]{1,0:T(8,128)S(1)}, f32[1024,1]{1,0:T(8,128)S(1)}, f32[1024,128]{1,0:T(8,128)S(1)}) custom-call(s32[2]{0:T(128)S(1)} %pad_add_fusion.span_ref, s32[1,1536]{1,0:T(1,128)S(1)} %add.135.place_ref, bf16[1024,128]{1,0:T(8,128)(2,1)S(1)} %pad_maximum_fusion.1.query_ref, bf16[96,256]{1,0:T(8,128)(2,1)S(1)} %pad_maximum_fusion.5.refs_0_, ...), custom_call_target="tpu_custom_call" | custom-call | flops 805306368 | bytes 1310720 | tf_op jit(solution)/shard_map/attend_part/pallas_call | solution.py:120
  64.2 3.0 %attend_last.1 = bf16[64,2048]{1,0:T(8,128)(2,1)} custom-call(s32[2]{0:T(128)S(1)} %pad_add_fusion.span_ref, s32[1,512]{1,0:T(1,128)S(1)} %add.130.place_ref, bf16[1024,128]{1,0:T(8,128)(2,1)S(1)} %pad_maximum_fusion.1.query_ref, bf16[32,256]{1,0:T(8,128)(2,1)S(1)} %pad_maximum_fusion.8.refs_0_, bf16[32,256]{1,0:T(8,128)(2,1)S(1)} %collective-permute-done.10.refs_1_, ...), custom_call_target="tpu_custom_call" | custom-call | flops 268435456 | bytes 786432 | tf_op jit(solution)/shard_map/attend_last/pallas_call | solution.py:120
  (46 shorter events, 0.6 us)
Async XLA Ops:
  0.6 1.6 %copy-start = (bf16[64,16384]{1,0:T(8,128)(2,1)S(1)}, bf16[64,16384]{1,0:T(8,128)(2,1)}, u32[]{:S(2)}) copy-start(bf16[64,16384]{1,0:T(8,128)(2,1)} %param.6) | copy-start | bytes 6291460
  2.9 15.7 %collective-permute-start = (bf16[8,8192]{1,0:T(8,128)(2,1)}, bf16[8,8192]{1,0:T(8,128)(2,1)}, u32[]{:S(2)}, u32[]{:S(2)}) collective-permute-start(bf16[8,8192]{1,0:T(8,128)(2,1)} %constant_dynamic-slice_fusion.4), channel_id=1, source_target_pairs={{0,1},{1,0},{2,3},{3,2},{4,5},{5,4},{6,7},{7,6},{8,9},{9,8},{10,11... | collective-permute-start | bytes 393224 | tf_op jit(solution)/shard_map/ppermute | solution.py:182
  5.9 18.6 %collective-permute-start.1 = (bf16[40,8192]{1,0:T(8,128)(2,1)S(1)}, bf16[40,8192]{1,0:T(8,128)(2,1)}, u32[]{:S(2)}, u32[]{:S(2)}) collective-permute-start(bf16[40,8192]{1,0:T(8,128)(2,1)S(1)} %constant_dynamic-slice_fusion.6), channel_id=1, source_target_pairs={{0,1},{1,0},{2,3},{3,2},{4,5},{5,4},{6,7},{7,6},{8,9},{9,8},{10,11... | collective-permute-start | bytes 1966088 | tf_op jit(solution)/shard_map/ppermute | solution.py:182
  6.6 22.1 %collective-permute-start.3 = (bf16[8,8192]{1,0:T(8,128)(2,1)}, bf16[8,8192]{1,0:T(8,128)(2,1)}, u32[]{:S(2)}, u32[]{:S(2)}) collective-permute-start(bf16[8,8192]{1,0:T(8,128)(2,1)} %constant_dynamic-slice_fusion.7), channel_id=1, source_target_pairs={{0,1},{1,0},{2,3},{3,2},{4,5},{5,4},{6,7},{7,6},{8,9},{9,8},{10,11... | collective-permute-start | bytes 393224 | tf_op jit(solution)/shard_map/ppermute | solution.py:182
  14.3 4.3 %copy-start.2 = (s32[16]{0:T(128)S(1)}, s32[16]{0:T(128)}, u32[]{:S(2)}) copy-start(s32[16]{0:T(128)} %constant.46.clone) | copy-start | bytes 196
  14.3 10.2 %copy-start.1 = (bf16[8192,256]{1,0:T(8,128)(2,1)S(1)}, bf16[8192,256]{1,0:T(8,128)(2,1)}, u32[]{:S(2)}) copy-start(bf16[8192,256]{1,0:T(8,128)(2,1)} %pad_maximum_fusion) | copy-start | bytes 12582916
  26.5 4.8 %collective-permute-start.2 = (f32[96,256]{1,0:T(8,128)S(1)}, f32[96,256]{1,0:T(8,128)S(1)}, u32[]{:S(2)}, u32[]{:S(2)}) collective-permute-start(f32[96,256]{1,0:T(8,128)S(1)} %pad_maximum_fusion.3), channel_id=1, source_target_pairs={{0,1},{1,0},{2,3},{3,2},{4,5},{5,4},{6,7},{7,6},{8,9},{9,8},{10,11... | collective-permute-start | bytes 294920 | tf_op jit(solution)/shard_map/ppermute | solution.py:268
  28.6 7.6 %collective-permute-start.7 = (bf16[8,8192]{1,0:T(8,128)(2,1)S(1)}, bf16[8,8192]{1,0:T(8,128)(2,1)S(1)}, u32[]{:S(2)}, u32[]{:S(2)}) collective-permute-start(bf16[8,8192]{1,0:T(8,128)(2,1)S(1)} %constant_dynamic-slice_fusion.5), channel_id=1, source_target_pairs={{0,1},{1,0},{2,3},{3,2},{4,5},{5,4},{6,7},{7,6},{8,9},{9,8},{10,11... | collective-permute-start | bytes 393224 | tf_op jit(solution)/shard_map/ppermute | solution.py:182
  31.5 8.2 %collective-permute-start.6 = (bf16[96,256]{1,0:T(8,128)(2,1)S(1)}, bf16[96,256]{1,0:T(8,128)(2,1)S(1)}, u32[]{:S(2)}, u32[]{:S(2)}) collective-permute-start(bf16[96,256]{1,0:T(8,128)(2,1)S(1)} %pad_maximum_fusion.5.refs_0_), channel_id=1, source_target_pairs={{0,24},{2,26},{4,28},{6,30},{8,16},{10,18},{12,20},{14,22},{16,8},... | collective-permute-start | bytes 147464 | tf_op jit(solution)/shard_map/ppermute | solution.py:300
  35.6 4.1 %collective-permute-start.5 = (bf16[96,256]{1,0:T(8,128)(2,1)S(1)}, bf16[96,256]{1,0:T(8,128)(2,1)S(1)}, u32[]{:S(2)}, u32[]{:S(2)}) collective-permute-start(bf16[96,256]{1,0:T(8,128)(2,1)S(1)} %pad_maximum_fusion.5.refs_0_), channel_id=1, source_target_pairs={{0,8},{2,10},{4,12},{6,14},{8,0},{10,2},{12,4},{14,6},{16,24},{18,... | collective-permute-start | bytes 147464 | tf_op jit(solution)/shard_map/ppermute | solution.py:300
  35.6 5.0 %collective-permute-start.4 = (bf16[96,256]{1,0:T(8,128)(2,1)S(1)}, bf16[96,256]{1,0:T(8,128)(2,1)S(1)}, u32[]{:S(2)}, u32[]{:S(2)}) collective-permute-start(bf16[96,256]{1,0:T(8,128)(2,1)S(1)} %pad_maximum_fusion.5.refs_0_), channel_id=1, source_target_pairs={{0,16},{2,18},{4,20},{6,22},{8,24},{10,26},{12,28},{14,30},{16,0},... | collective-permute-start | bytes 147464 | tf_op jit(solution)/shard_map/ppermute | solution.py:300
  37.8 4.0 %collective-permute-start.8 = (f32[32,256]{1,0:T(8,128)S(1)}, f32[32,256]{1,0:T(8,128)S(1)}, u32[]{:S(2)}, u32[]{:S(2)}) collective-permute-start(f32[32,256]{1,0:T(8,128)S(1)} %pad_maximum_fusion.6), channel_id=1, source_target_pairs={{0,1},{1,0},{2,3},{3,2},{4,5},{5,4},{6,7},{7,6},{8,9},{9,8},{10,11... | collective-permute-start | bytes 98312 | tf_op jit(solution)/shard_map/ppermute | solution.py:268
  42.0 6.3 %collective-permute-start.12 = (bf16[32,256]{1,0:T(8,128)(2,1)S(1)}, bf16[32,256]{1,0:T(8,128)(2,1)S(1)}, u32[]{:S(2)}, u32[]{:S(2)}) collective-permute-start(bf16[32,256]{1,0:T(8,128)(2,1)S(1)} %pad_maximum_fusion.8.refs_0_), channel_id=1, source_target_pairs={{0,24},{2,26},{4,28},{6,30},{8,16},{10,18},{12,20},{14,22},{16,8},... | collective-permute-start | bytes 49160 | tf_op jit(solution)/shard_map/ppermute | solution.py:300
  45.7 3.7 %collective-permute-start.11 = (bf16[32,256]{1,0:T(8,128)(2,1)S(1)}, bf16[32,256]{1,0:T(8,128)(2,1)S(1)}, u32[]{:S(2)}, u32[]{:S(2)}) collective-permute-start(bf16[32,256]{1,0:T(8,128)(2,1)S(1)} %pad_maximum_fusion.8.refs_0_), channel_id=1, source_target_pairs={{0,8},{2,10},{4,12},{6,14},{8,0},{10,2},{12,4},{14,6},{16,24},{18,... | collective-permute-start | bytes 49160 | tf_op jit(solution)/shard_map/ppermute | solution.py:300
  45.7 4.6 %collective-permute-start.10 = (bf16[32,256]{1,0:T(8,128)(2,1)S(1)}, bf16[32,256]{1,0:T(8,128)(2,1)S(1)}, u32[]{:S(2)}, u32[]{:S(2)}) collective-permute-start(bf16[32,256]{1,0:T(8,128)(2,1)S(1)} %pad_maximum_fusion.8.refs_0_), channel_id=1, source_target_pairs={{0,16},{2,18},{4,20},{6,22},{8,24},{10,26},{12,28},{14,30},{16,0},... | collective-permute-start | bytes 49160 | tf_op jit(solution)/shard_map/ppermute | solution.py:300
  46.4 5.7 %collective-permute-start.9 = (bf16[384,256]{1,0:T(8,128)(2,1)S(1)}, bf16[384,256]{1,0:T(8,128)(2,1)S(1)}, u32[]{:S(2)}, u32[]{:S(2)}) collective-permute-start(bf16[384,256]{1,0:T(8,128)(2,1)S(1)} %pad_maximum_fusion.2), channel_id=1, source_target_pairs={{0,4},{2,6},{4,0},{6,2},{8,12},{10,14},{12,8},{14,10},{16,20},{18,... | collective-permute-start | bytes 589832 | tf_op jit(solution)/shard_map/ppermute | solution.py:300
  55.3 4.8 %collective-permute-start.13 = (bf16[768,256]{1,0:T(8,128)(2,1)}, bf16[768,256]{1,0:T(8,128)(2,1)S(1)}, u32[]{:S(2)}, u32[]{:S(2)}) collective-permute-start(bf16[768,256]{1,0:T(8,128)(2,1)} %constant_dynamic-update-slice_fusion), channel_id=1, source_target_pairs={{0,2},{2,0},{4,6},{6,4},{8,10},{10,8},{12,14},{14,12},{16,18},{18,... | collective-permute-start | bytes 1179656 | tf_op jit(solution)/shard_map/ppermute | solution.py:300
  55.5 4.6 %collective-permute-start.14 = (bf16[128,256]{1,0:T(8,128)(2,1)S(1)}, bf16[128,256]{1,0:T(8,128)(2,1)S(1)}, u32[]{:S(2)}, u32[]{:S(2)}) collective-permute-start(bf16[128,256]{1,0:T(8,128)(2,1)S(1)} %pad_maximum_fusion.4), channel_id=1, source_target_pairs={{0,4},{2,6},{4,0},{6,2},{8,12},{10,14},{12,8},{14,10},{16,20},{18,... | collective-permute-start | bytes 196616 | tf_op jit(solution)/shard_map/ppermute | solution.py:300
  60.1 4.1 %collective-permute-start.15 = (bf16[256,256]{1,0:T(8,128)(2,1)S(1)}, bf16[256,256]{1,0:T(8,128)(2,1)S(1)}, u32[]{:S(2)}, u32[]{:S(2)}) collective-permute-start(bf16[256,256]{1,0:T(8,128)(2,1)S(1)} %constant_dynamic-update-slice_fusion.5), channel_id=1, source_target_pairs={{0,2},{2,0},{4,6},{6,4},{8,10},{10,8},{12,14},{14,12},{16,18},{18,... | collective-permute-start | bytes 393224 | tf_op jit(solution)/shard_map/ppermute | solution.py:300

commit v4 on v3

--- a/solution.py
+++ b/solution.py
@@ -30,7 +30,7 @@
 
 
 def attention_kernel(
-    span_ref, place_ref, query_ref, *refs, count, carry, final, rows, own, head_size, stride
+    span_ref, place_ref, query_ref, *refs, count, carry, final, rows, edge, head_size, stride
 ):
     pieces, refs = refs[:count], refs[count:]
     if carry:
@@ -43,11 +43,11 @@
     keys = jnp.concatenate([piece[:, :head_size] for piece in pieces], axis=0)
     values = jnp.concatenate([piece[:, head_size:] for piece in pieces], axis=0)
     width = keys.shape[0]
-    edge = min(width, -(-own // 128) * 128)
-    query_pos = first + lax.rem(
-        lax.broadcasted_iota(jnp.int32, (stride, edge), 0), jnp.int32(rows)
-    )
-    diagonal = place_ref[:, :edge] <= query_pos
+    if edge:
+        query_pos = first + lax.rem(
+            lax.broadcasted_iota(jnp.int32, (stride, edge), 0), jnp.int32(rows)
+        )
+        diagonal = place_ref[:, :edge] <= query_pos
     bias = jnp.where(place_ref[...] < start, 0.0, floor_value).astype(jnp.float32)
 
     def one(part):
@@ -61,9 +61,12 @@
             )
             * factor
         )
-        masked = jnp.where(diagonal, scores[:, :edge], floor_value)
+        masked = []
+        if edge:
+            masked.append(jnp.where(diagonal, scores[:, :edge], floor_value))
         if edge < width:
-            masked = jnp.concatenate([masked, scores[:, edge:] + bias[:, edge:]], axis=1)
+            masked.append(scores[:, edge:] + bias[:, edge:])
+        masked = jnp.concatenate(masked, axis=1) if len(masked) > 1 else masked[0]
         peak = jnp.max(masked, axis=1, keepdims=True)
         if carry:
             peak = jnp.maximum(peak, old_peak[place, :])
@@ -102,7 +105,7 @@
             ]
 
 
-def attend(span, place, query_flat, pieces, state, final, rows):
+def attend(span, place, query_flat, pieces, edge, state, final, rows):
     flat, head_size = query_flat.shape
     width = sum(piece.shape[0] for piece in pieces)
     stride = math.gcd(flat, 256 if width <= 2048 else rows)
@@ -124,7 +127,7 @@
             carry=state is not None,
             final=final,
             rows=rows,
-            own=pieces[0].shape[0],
+            edge=edge,
             head_size=head_size,
             stride=stride,
         ),
@@ -133,7 +136,7 @@
         + [whole] * (2 + len(pieces) + (0 if state is None else 3)),
         out_specs=out_specs,
         scratch_shapes=scratch,
-        compiler_params=pltpu.CompilerParams(vmem_limit_bytes=40 * 1024 * 1024),
+        compiler_params=pltpu.CompilerParams(vmem_limit_bytes=24 * 1024 * 1024),
         cost_estimate=pl.CostEstimate(
             flops=4 * flat * width * head_size,
             bytes_accessed=4 * flat * head_size + 4 * width * head_size,
@@ -286,20 +289,33 @@
                     jnp.concatenate([keys_rot, sums[:, head_size:].astype(jnp.bfloat16)], axis=1)
                 )
                 part.cache = lax.dynamic_slice_in_dim(block, shard * part.rows, part.rows, 0)
-                part.pieces, part.masks = [block], [[0]]
+                part.pieces, part.places = [block], [context[None]]
+                part.edge = block.shape[0]
             else:
                 part.pieces = list(values)
-            known = jnp.concatenate(part.pieces, axis=0)
             if part.stage < len(stages):
-                known_masks = [mask for piece_masks in part.masks for mask in piece_masks]
-                moves = [0]
-                for bit in stages[part.stage]:
-                    moves = moves + [move ^ bit for move in moves]
-                for move in moves[1:]:
-                    part.pieces.append(
-                        lax.ppermute(known, "ctx", [(i, i ^ move) for i in range(contexts)])
-                    )
-                    part.masks.append([mask ^ move for mask in known_masks])
+                known = jnp.concatenate(part.pieces, axis=0)
+                places = jnp.concatenate(part.places)
+                bits = stages[part.stage]
+                if len(bits) == 1:
+                    pairs = [(i, i ^ bits[0]) for i in range(contexts)]
+                    part.pieces.append(lax.ppermute(known, "ctx", pairs))
+                    part.places.append(places ^ bits[0])
+                else:
+                    low = min(bits)
+                    count = (sum(bits) // low) + 1
+                    groups = [
+                        [base + low * turn for turn in range(count)]
+                        for base in range(contexts)
+                        if base & sum(bits) == 0
+                    ]
+                    copies = jnp.broadcast_to(known[None], (count,) + known.shape)
+                    gathered = lax.all_to_all(copies, "ctx", 0, 0, axis_index_groups=groups)
+                    part.pieces = [gathered.reshape(-1, known.shape[1])]
+                    turns = low * jnp.arange(count, dtype=jnp.int32)
+                    kept = places & ~jnp.int32(sum(bits))
+                    part.places = [(turns[:, None] | kept[None, :]).reshape(-1)]
+                    part.edge = part.pieces[0].shape[0]
             part.stage += 1
 
         def step_all(going, extra=()):
@@ -312,12 +328,20 @@
             local_pos = rows_of(
                 jnp.arange(group_rows, dtype=jnp.int32)[:, None], part.top, part.rows
             )[:, 0]
-            order = jnp.array([mask for masks in part.masks for mask in masks], jnp.int32)
-            place = ((context ^ order)[:, None] * group_rows + local_pos[None, :]).reshape(1, -1)
-            return attend(span, place, query_flat, part.pieces, state, last, rows)
+
+            def one(pieces, places, edge, state, last):
+                place = (
+                    jnp.concatenate(places)[:, None] * group_rows + local_pos[None, :]
+                ).reshape(1, -1)
+                return attend(span, place, query_flat, pieces, edge, state, last, rows)
+
+            if last:
+                state = one(part.pieces[:-1], part.places[:-1], part.edge, state, False)
+                return one(part.pieces[-1:], part.places[-1:], 0, state, True)
+            return one(part.pieces, part.places, part.edge, state, False)
 
         for index, part in enumerate(parts):
-            going = [p for p in parts[:index] if p.stage <= len(stages)]
+            going = [p for p in parts[:index] if p.stage < len(stages)]
             arrived = flying[part.first : part.end]
             arrived = list(lax.optimization_barrier((arrived, own_product))[0])
             exchange(part, arrived)
@@ -331,8 +355,8 @@
         going = list(parts)
         while going:
             step_all(going)
-            ready = [part for part in going if part.stage > len(stages)]
-            going = [part for part in going if part.stage <= len(stages)]
+            ready = [part for part in going if part.stage >= len(stages)]
+            going = [part for part in going if part.stage < len(stages)]
             for part in ready:
                 state = finish(part, state, part is parts[-1])
         kv_cache = jnp.concatenate([part.cache for part in parts], axis=0)
@@ -344,7 +368,7 @@
 def solution(mesh):
     placed = (P(("ctx", "fsdp"), None), P(("ctx", "fsdp"), None), P("fsdp", None), P("fsdp", None))
     return jax.shard_map(
-        make_local(mesh.shape["ctx"], mesh.shape["fsdp"], ((1, 5), (1, 1))),
+        make_local(mesh.shape["ctx"], mesh.shape["fsdp"], ((1, 7),)),
         mesh=mesh,
         in_specs=placed,
         out_specs=(P(("ctx", "fsdp"), None), P(("ctx", "fsdp"), None)),

time: 67.5 us -> 63.2 us (0.936)
  starting transfers between devices: 21.6 us -> 6.42 us
  blocking collectives: 0 us -> 12 us
  waiting for transfers between devices: 17.3 us -> 20.8 us
  local copies, waits for them, and re-layouts: 6.6 us -> 3.24 us
  other arithmetic: 7.58 us -> 6.89 us
    all_to_all x0 -> x1, blocking collectives: none -> 12 us  [advance(): gathered = lax.all_to_all(copies, 'ctx', 0, 0, axis_index_groups=groups)]
    ppermute x10 -> x2, starting transfers between devices: 12.7 us -> 1.59 us  [advance(): part.pieces.append(lax.ppermute(known, 'ctx', pairs))]
    ppermute x4 -> x2, waiting for transfers between devices: 5.93 us -> 12.8 us  [send_rows(): lax.ppermute(columns, 'fsdp', [(i, (i + step) % shards) for i in range(sh...]
    ppermute x10 -> x2, waiting for transfers between devices: 7.64 us -> 4.77 us  [advance(): part.pieces.append(lax.ppermute(known, 'ctx', pairs))]
    unnamed x14 -> x2, local copies, waits for them, and re-layouts: 4.07 us -> 1.58 us
    ppermute x4 -> x2, starting transfers between devices: 5.11 us -> 3.03 us  [send_rows(): lax.ppermute(columns, 'fsdp', [(i, (i + step) % shards) for i in range(sh...]
    ppermute x2 -> x1, starting transfers between devices: 3.8 us -> 1.81 us  [exchange(): lax.ppermute(part.sums, 'fsdp', [(i, i ^ reach) for i in range(shards)])]
    concatenate x2 -> x0, local copies, waits for them, and re-layouts: 0.69 us -> none  [advance(): known = jnp.concatenate(part.pieces, axis=0)]
  transfers between devices with their start and end apart: 16 -> 5, of which waited for: 8 -> 3; matrix products, arithmetic and copies ran while one was open for 23% -> 18% of each run, Pallas kernels for 5% -> 4%
where the time goes in v4:
time: 63.2 us; the launch traced here: 62.9 us
  waiting for transfers between devices  20.8 us (33%)
  blocking collectives  12 us (19%)
  other arithmetic  6.89 us (11%)
  Pallas kernels  6.51 us (10%)
  starting transfers between devices  6.42 us (10%)
  matrix products  6.26 us (10%)
  local copies, waits for them, and re-layouts  3.24 us (5%)
  between operations  0.79 us (1%)
    ppermute x2, waiting for transfers between devices, send_rows(): lax.ppermute(columns, 'fsdp', [(i, (i + step) % shards) for i in range(sh...  12.8 us
    all_to_all x1, blocking collectives, advance(): gathered = lax.all_to_all(copies, 'ctx', 0, 0, axis_index_groups=groups)  12 us
    pallas_call x2, Pallas kernels, attend(): pl.pallas_call(partial(attention_kernel, count=len(pieces), carry=state i...  6.51 us
    ppermute x2, waiting for transfers between devices, advance(): part.pieces.append(lax.ppermute(known, 'ctx', pairs))  4.77 us
    concatenate x1, other arithmetic, local(): weight = after(jnp.concatenate([key_weight, value_weight], axis=1), *sent)  4.62 us
    dot_general x1, matrix products, exchange(): jnp.dot(c, weight, preferred_element_type=jnp.float32)  3.27 us
    ppermute x1, waiting for transfers between devices, exchange(): lax.ppermute(part.sums, 'fsdp', [(i, i ^ reach) for i in range(shards)])  3.23 us
    ppermute x2, starting transfers between devices, send_rows(): lax.ppermute(columns, 'fsdp', [(i, (i + step) % shards) for i in range(sh...  3.03 us
  transfers between devices with their start and end apart: 5, of which 3 were waited for; matrix products, arithmetic and copies ran while one was open for 18% of the time, Pallas kernels for 4%

profile of v4, /device:TPU:0, one launch (start us, length us, event | category | flops | bytes accessed | tf_op | source)
XLA Modules:
  0.0 62.9 jit_solution(17888893480518213357)
XLA Ops:
  0.6 0.0 copy-start
  0.7 1.6 %copy-done = bf16[64,16384]{1,0:T(8,128)(2,1)S(1)} copy-done((bf16[64,16384]{1,0:T(8,128)(2,1)S(1)}, bf16[64,16384]{1,0:T(8,128)(2,1)}, u32[]{:S(2)}) %copy-start) | copy-done | bytes 2097176
  2.2 3.0 %collective-permute-start = (bf16[8,8192]{1,0:T(8,128)(2,1)S(1)}, bf16[8,8192]{1,0:T(8,128)(2,1)S(1)}, u32[]{:S(2)}, u32[]{:S(2)}) collective-permute-start(bf16[8,8192]{1,0:T(8,128)(2,1)S(1)} %constant_dynamic-slice_fusion.3), channel_id=1, source_target_pairs={{0,1},{1,0},{2,3},{3,2},{4,5},{5,4},{6,7},{7,6},{8,9},{9,8},{10,11... | collective-permute-start | bytes 393224 | tf_op jit(solution)/shard_map/ppermute | solution.py:185
  5.2 1.0 %constant_dynamic-slice_fusion.4 = bf16[56,8192]{1,0:T(8,128)(2,1)} fusion(bf16[64,16384]{1,0:T(8,128)(2,1)S(1)} %copy-done, s32[]{:T(128)S(6)} %select_n.26), kind=kLoop, calls=%fused_computation.35 | loop fusion | bytes 1835012 | tf_op jit(solution)/shard_map/dynamic_slice | solution.py:180
  6.2 0.0 collective-permute-start.1
  6.3 1.0 %bitcast_bitcast_fusion = f32[16,64,128]{2,1,0:T(8,128)S(1)} fusion(bf16[64,2048]{1,0:T(8,128)(2,1)} %param.5), kind=kLoop, calls=%fused_computation.7 | loop fusion | flops 131072 | bytes 786432 | tf_op jit(solution)/shard_map/transpose | solution.py:231
  7.3 4.6 %pad_maximum_fusion = bf16[8192,256]{1,0:T(8,128)(2,1)} fusion(bf16[8192,128]{1,0:T(8,128)(2,1)} %param.7, bf16[8192,128]{1,0:T(8,128)(2,1)} %param.6), kind=kLoop, calls=%fused_computation | loop fusion | flops 8388608 | bytes 8388608 | tf_op jit(solution)/shard_map/concatenate | solution.py:222
  11.9 0.3 multiply_sine_fusion
  12.2 0.3 subtract_convert_fusion
  12.5 3.0 %fusion.4 = f32[64,256]{1,0:T(8,128)S(1)} fusion(bf16[8192,256]{1,0:T(8,128)(2,1)} %pad_maximum_fusion, bf16[64,16384]{1,0:T(8,128)(2,1)S(1)} %copy-done, s32[]{:T(128)S(6)} %select_n.25), kind=kOutput, calls=%fused_computation.5 | convolution fusion | flops 268435456 | bytes 5308420 | tf_op jit(solution)/shard_map/dot_general | solution.py:224
  15.5 0.1 pad_add_fusion.span_ref
  15.6 0.1 pad_maximum_fusion.2.query_ref
  15.7 0.0 collective-permute-done
  15.7 12.8 %collective-permute-done.1 = bf16[56,8192]{1,0:T(8,128)(2,1)} collective-permute-done((bf16[56,8192]{1,0:T(8,128)(2,1)}, bf16[56,8192]{1,0:T(8,128)(2,1)}, u32[]{:S(2)}, u32[]{:S(2)}) %collective-permute-start.1) | collective-permute-done | bytes 917536 | tf_op jit(solution)/shard_map/ppermute | solution.py:185
  28.5 3.3 %broadcast_select_fusion.1 = (f32[64,256]{1,0:T(8,128)S(1)}, f32[64,256]{1,0:T(8,128)S(1)}) fusion(f32[64,256]{1,0:T(8,128)S(1)} %fusion.4, pred[]{:T(512)S(6)} %eq.4, bf16[8192,256]{1,0:T(8,128)(2,1)} %pad_maximum_fusion, bf16[56,8192]{1,0:T(8,128)(2,1)} %collective-permute-done.1, bf16[8,8192]{1,0:T(8,128)(2,1)S(1)} %collective-permute-done), kind=kOutput, calls=%fused_computation.21 | convolution fusion | flops 270565376 | bytes 5439489 | tf_op jit(solution)/shard_map/dot_general | solution.py:248
  31.8 1.8 %collective-permute-start.2 = (f32[128,256]{1,0:T(8,128)S(1)}, f32[128,256]{1,0:T(8,128)S(1)}, u32[]{:S(2)}, u32[]{:S(2)}) collective-permute-start(f32[128,256]{1,0:T(8,128)S(1)} %pad_maximum_fusion.3), channel_id=1, source_target_pairs={{0,1},{1,0},{2,3},{3,2},{4,5},{5,4},{6,7},{7,6},{8,9},{9,8},{10,11... | collective-permute-start | bytes 393224 | tf_op jit(solution)/shard_map/ppermute | solution.py:271
  33.6 3.2 %collective-permute-done.2 = f32[128,256]{1,0:T(8,128)S(1)} collective-permute-done((f32[128,256]{1,0:T(8,128)S(1)}, f32[128,256]{1,0:T(8,128)S(1)}, u32[]{:S(2)}, u32[]{:S(2)}) %collective-permute-start.2) | collective-permute-done | bytes 131104 | tf_op jit(solution)/shard_map/ppermute | solution.py:271
  36.9 0.1 subtract_convert_fusion.1
  37.0 0.1 pad_maximum_fusion.4
  37.1 12.0 %all_to_all.5 = bf16[4,128,256]{2,1,0:T(8,128)(2,1)S(1)} all-to-all(bf16[4,128,256]{2,1,0:T(8,128)(2,1)S(1)} %broadcast_in_dim.2), channel_id=1, replica_groups={{0,8,16,24},{2,10,18,26},{4,12,20,28},{6,14,22,30},{1,9,17,25},{3,11,19..., dimensions={0} | all-to-all | bytes 524288 | tf_op jit(solution)/shard_map/all_to_all | solution.py:313
  49.1 1.5 %collective-permute-start.3 = (bf16[512,256]{1,0:T(8,128)(2,1)S(1)}, bf16[512,256]{1,0:T(8,128)(2,1)S(1)}, u32[]{:S(2)}, u32[]{:S(2)}) collective-permute-start(bf16[512,256]{1,0:T(8,128)(2,1)S(1)} %bitcast.16), channel_id=1, source_target_pairs={{0,4},{2,6},{4,0},{6,2},{8,12},{10,14},{12,8},{14,10},{16,20},{18,... | collective-permute-start | bytes 786440 | tf_op jit(solution)/shard_map/ppermute | solution.py:302
  50.7 0.1 broadcast_multiply_fusion
  50.7 4.8 %collective-permute-done.3.refs_1_ = bf16[512,256]{1,0:T(8,128)(2,1)S(1)} collective-permute-done((bf16[512,256]{1,0:T(8,128)(2,1)S(1)}, bf16[512,256]{1,0:T(8,128)(2,1)S(1)}, u32[]{:S(2)}, u32[]{:S(2)}) %collective-permute-start.3) | collective-permute-done | bytes 262176 | tf_op jit(solution)/shard_map/ppermute | solution.py:302
  55.6 0.1 collective-permute-start.4
  55.6 0.1 iota_add_fusion
  55.7 0.1 iota_add_fusion.1
  55.8 0.6 constant_dynamic-slice_fusion
  56.4 2.6 %attend_part.1 = (f32[1024,1]{1,0:T(8,128)S(1)}, f32[1024,1]{1,0:T(8,128)S(1)}, f32[1024,128]{1,0:T(8,128)S(1)}) custom-call(s32[2]{0:T(128)S(1)} %pad_add_fusion.span_ref, s32[1,1024]{1,0:T(1,128)S(1)} %bitcast.20, bf16[1024,128]{1,0:T(8,128)(2,1)S(1)} %pad_maximum_fusion.2.query_ref, bf16[512,256]{1,0:T(8,128)(2,1)S(1)} %bitcast.18, ...), custom_call_target="tpu_custom_call" | custom-call | flops 536870912 | bytes 1048576 | tf_op jit(solution)/shard_map/attend_part/pallas_call | solution.py:123
  59.0 0.0 collective-permute-done.4.refs_0_
  59.0 3.9 %attend_last.1 = bf16[64,2048]{1,0:T(8,128)(2,1)} custom-call(s32[2]{0:T(128)S(1)} %pad_add_fusion.span_ref, s32[1,1024]{1,0:T(1,128)S(1)} %bitcast.19, bf16[1024,128]{1,0:T(8,128)(2,1)S(1)} %pad_maximum_fusion.2.query_ref, bf16[1024,256]{1,0:T(8,128)(2,1)S(1)} %collective-permute-done.4.refs_0_, f32[1024,1]{1,0:T(8,128)S(1)} %get-tuple-element.31.refs_1_, ...), custom_call_target="tpu_custom_call" | custom-call | flops 536870912 | bytes 1048576 | tf_op jit(solution)/shard_map/attend_last/pallas_call | solution.py:123
  (10 shorter events, 0.1 us)
Async XLA Ops:
  0.6 1.6 %copy-start = (bf16[64,16384]{1,0:T(8,128)(2,1)S(1)}, bf16[64,16384]{1,0:T(8,128)(2,1)}, u32[]{:S(2)}) copy-start(bf16[64,16384]{1,0:T(8,128)(2,1)} %param.4) | copy-start | bytes 6291460
  2.2 13.5 %collective-permute-start = (bf16[8,8192]{1,0:T(8,128)(2,1)S(1)}, bf16[8,8192]{1,0:T(8,128)(2,1)S(1)}, u32[]{:S(2)}, u32[]{:S(2)}) collective-permute-start(bf16[8,8192]{1,0:T(8,128)(2,1)S(1)} %constant_dynamic-slice_fusion.3), channel_id=1, source_target_pairs={{0,1},{1,0},{2,3},{3,2},{4,5},{5,4},{6,7},{7,6},{8,9},{9,8},{10,11... | collective-permute-start | bytes 393224 | tf_op jit(solution)/shard_map/ppermute | solution.py:185
  6.2 22.3 %collective-permute-start.1 = (bf16[56,8192]{1,0:T(8,128)(2,1)}, bf16[56,8192]{1,0:T(8,128)(2,1)}, u32[]{:S(2)}, u32[]{:S(2)}) collective-permute-start(bf16[56,8192]{1,0:T(8,128)(2,1)} %constant_dynamic-slice_fusion.4), channel_id=1, source_target_pairs={{0,1},{1,0},{2,3},{3,2},{4,5},{5,4},{6,7},{7,6},{8,9},{9,8},{10,11... | collective-permute-start | bytes 2752520 | tf_op jit(solution)/shard_map/ppermute | solution.py:185
  31.8 5.0 %collective-permute-start.2 = (f32[128,256]{1,0:T(8,128)S(1)}, f32[128,256]{1,0:T(8,128)S(1)}, u32[]{:S(2)}, u32[]{:S(2)}) collective-permute-start(f32[128,256]{1,0:T(8,128)S(1)} %pad_maximum_fusion.3), channel_id=1, source_target_pairs={{0,1},{1,0},{2,3},{3,2},{4,5},{5,4},{6,7},{7,6},{8,9},{9,8},{10,11... | collective-permute-start | bytes 393224 | tf_op jit(solution)/shard_map/ppermute | solution.py:271
  49.1 6.4 %collective-permute-start.3 = (bf16[512,256]{1,0:T(8,128)(2,1)S(1)}, bf16[512,256]{1,0:T(8,128)(2,1)S(1)}, u32[]{:S(2)}, u32[]{:S(2)}) collective-permute-start(bf16[512,256]{1,0:T(8,128)(2,1)S(1)} %bitcast.16), channel_id=1, source_target_pairs={{0,4},{2,6},{4,0},{6,2},{8,12},{10,14},{12,8},{14,10},{16,20},{18,... | collective-permute-start | bytes 786440 | tf_op jit(solution)/shard_map/ppermute | solution.py:302
  55.6 3.4 %collective-permute-start.4 = (bf16[1024,256]{1,0:T(8,128)(2,1)S(1)}, bf16[1024,256]{1,0:T(8,128)(2,1)S(1)}, u32[]{:S(2)}, u32[]{:S(2)}) collective-permute-start(bf16[1024,256]{1,0:T(8,128)(2,1)S(1)} %pad_maximum_fusion.1), channel_id=1, source_target_pairs={{0,2},{2,0},{4,6},{6,4},{8,10},{10,8},{12,14},{14,12},{16,18},{18,... | collective-permute-start | bytes 1572872 | tf_op jit(solution)/shard_map/ppermute | solution.py:302

commit v5 on v3

--- a/solution.py
+++ b/solution.py
@@ -102,7 +102,7 @@
             ]
 
 
-def attend(span, place, query_flat, pieces, state, final, rows):
+def attend(span, place, query_flat, pieces, own, state, final, rows):
     flat, head_size = query_flat.shape
     width = sum(piece.shape[0] for piece in pieces)
     stride = math.gcd(flat, 256 if width <= 2048 else rows)
@@ -124,7 +124,7 @@
             carry=state is not None,
             final=final,
             rows=rows,
-            own=pieces[0].shape[0],
+            own=own,
             head_size=head_size,
             stride=stride,
         ),
@@ -133,7 +133,7 @@
         + [whole] * (2 + len(pieces) + (0 if state is None else 3)),
         out_specs=out_specs,
         scratch_shapes=scratch,
-        compiler_params=pltpu.CompilerParams(vmem_limit_bytes=40 * 1024 * 1024),
+        compiler_params=pltpu.CompilerParams(vmem_limit_bytes=24 * 1024 * 1024),
         cost_estimate=pl.CostEstimate(
             flops=4 * flat * width * head_size,
             bytes_accessed=4 * flat * head_size + 4 * width * head_size,
@@ -216,9 +216,14 @@
             arrived, sent = send_rows(*chunk, *sent)
             flying.append(arrived)
 
-        weight = after(jnp.concatenate([key_weight, value_weight], axis=1), *sent)
-        own_columns = lax.dynamic_slice_in_dim(tokens, shard * depth, depth, 1)
-        own_product = jnp.dot(own_columns, weight, preferred_element_type=jnp.float32)
+        def project(columns):
+            return [
+                jnp.dot(columns, weight, preferred_element_type=jnp.float32)
+                for weight in (key_weight, value_weight)
+            ]
+
+        own_columns = lax.dynamic_slice_in_dim(after(tokens, *sent), shard * depth, depth, 1)
+        own_product = jnp.concatenate(project(own_columns), axis=1)
 
         start = context * group_rows
         positions = start + jnp.arange(group_rows, dtype=jnp.int32)
@@ -237,12 +242,9 @@
         )
 
         def exchange(part, arrived):
-            columns = [
-                jnp.concatenate([chunk[s] for chunk in arrived], axis=0)
-                for s in range(shards - 1)
-            ]
             products = [own_product[part.top : part.top + part.rows]] + [
-                jnp.dot(c, weight, preferred_element_type=jnp.float32) for c in columns
+                jnp.concatenate([chunk[step] for chunk in arrived], axis=0)
+                for step in range(shards - 1)
             ]
             if shards == 2:
                 sums = jnp.concatenate(
@@ -289,9 +291,10 @@
                 part.pieces, part.masks = [block], [[0]]
             else:
                 part.pieces = list(values)
-            known = jnp.concatenate(part.pieces, axis=0)
             if part.stage < len(stages):
+                known = jnp.concatenate(part.pieces, axis=0)
                 known_masks = [mask for piece_masks in part.masks for mask in piece_masks]
+                part.pieces, part.masks = [known], [known_masks]
                 moves = [0]
                 for bit in stages[part.stage]:
                     moves = moves + [move ^ bit for move in moves]
@@ -314,12 +317,16 @@
             )[:, 0]
             order = jnp.array([mask for masks in part.masks for mask in masks], jnp.int32)
             place = ((context ^ order)[:, None] * group_rows + local_pos[None, :]).reshape(1, -1)
-            return attend(span, place, query_flat, part.pieces, state, last, rows)
+            return attend(span, place, query_flat, part.pieces, shards * part.rows, state, last, rows)
 
         for index, part in enumerate(parts):
             going = [p for p in parts[:index] if p.stage <= len(stages)]
-            arrived = flying[part.first : part.end]
-            arrived = list(lax.optimization_barrier((arrived, own_product))[0])
+            gate = own_product
+            arrived = []
+            for number in range(part.first, part.end):
+                chunk, gate = lax.optimization_barrier((flying[number], gate))
+                gate = [jnp.concatenate(project(columns), axis=1) for columns in chunk]
+                arrived.append(gate)
             exchange(part, arrived)
             for chunk in chunks[len(flying) : part.end + 2]:
                 flying.append(send_rows(*chunk, part.sums)[0])
@@ -344,7 +351,7 @@
 def solution(mesh):
     placed = (P(("ctx", "fsdp"), None), P(("ctx", "fsdp"), None), P("fsdp", None), P("fsdp", None))
     return jax.shard_map(
-        make_local(mesh.shape["ctx"], mesh.shape["fsdp"], ((1, 5), (1, 1))),
+        make_local(mesh.shape["ctx"], mesh.shape["fsdp"], ((1, 3), (2, 2))),
         mesh=mesh,
         in_specs=placed,
         out_specs=(P(("ctx", "fsdp"), None), P(("ctx", "fsdp"), None)),

time: 67.5 us -> 59.7 us (0.88)
  other arithmetic: 7.58 us -> 2.58 us
  waiting for transfers between devices: 17.3 us -> 13.6 us
  local copies, waits for them, and re-layouts: 6.6 us -> 4.78 us
  matrix products: 6.9 us -> 8.71 us
    concatenate x3 -> x1, other arithmetic: 4.64 us -> 0.64 us  [local(): own_product = jnp.concatenate(project(own_columns), axis=1)]
    ppermute x4, waiting for transfers between devices: 5.93 us -> 3.58 us  [send_rows(): lax.ppermute(columns, 'fsdp', [(i, (i + step) % shards) for i in range(sh...]
    ppermute x2, waiting for transfers between devices: 3.73 us -> 1.68 us  [exchange(): lax.ppermute(part.sums, 'fsdp', [(i, i ^ reach) for i in range(shards)])]
    unnamed x14 -> x22, local copies, waits for them, and re-layouts: 4.07 us -> 2.13 us
    dot_general x3 -> x10, matrix products: 6.9 us -> 8.71 us  [project(): jnp.dot(columns, weight, preferred_element_type=jnp.float32)]
    transpose x1, other arithmetic: 1 us -> 0.04 us  [local(): queries.astype(jnp.float32).reshape(rows, heads, head_size)]
    dynamic_slice x4, local copies, waits for them, and re-layouts: 1.4 us -> 2.17 us  [send_rows(): lax.dynamic_slice(source, (jnp.int32(top), target * depth), (count, depth))]
    ppermute x10, waiting for transfers between devices: 7.64 us -> 8.38 us  [advance(): lax.ppermute(known, 'ctx', [(i, i ^ move) for i in range(contexts)])]
  transfers between devices with their start and end apart: 16 -> 16, of which waited for: 8 -> 8; matrix products, arithmetic and copies ran while one was open for 23% -> 22% of each run, Pallas kernels for 5% -> 4%
where the time goes in v5:
time: 59.7 us; the launch traced here: 59.4 us
  starting transfers between devices  22.1 us (37%)
  waiting for transfers between devices  13.6 us (23%)
  matrix products  8.71 us (15%)
  Pallas kernels  6.6 us (11%)
  local copies, waits for them, and re-layouts  4.78 us (8%)
  other arithmetic  2.58 us (4%)
  between operations  1.02 us (2%)
    ppermute x10, starting transfers between devices, advance(): lax.ppermute(known, 'ctx', [(i, i ^ move) for i in range(contexts)])  12.9 us
    dot_general x10, matrix products, project(): jnp.dot(columns, weight, preferred_element_type=jnp.float32)  8.71 us
    ppermute x10, waiting for transfers between devices, advance(): lax.ppermute(known, 'ctx', [(i, i ^ move) for i in range(contexts)])  8.38 us
    pallas_call x2, Pallas kernels, attend(): pl.pallas_call(partial(attention_kernel, count=len(pieces), carry=state i...  6.6 us
    ppermute x4, starting transfers between devices, send_rows(): lax.ppermute(columns, 'fsdp', [(i, (i + step) % shards) for i in range(sh...  5.06 us
    ppermute x2, starting transfers between devices, exchange(): lax.ppermute(part.sums, 'fsdp', [(i, i ^ reach) for i in range(shards)])  4.13 us
    ppermute x4, waiting for transfers between devices, send_rows(): lax.ppermute(columns, 'fsdp', [(i, (i + step) % shards) for i in range(sh...  3.58 us
    dynamic_slice x4, local copies, waits for them, and re-layouts, send_rows(): lax.dynamic_slice(source, (jnp.int32(top), target * depth), (count, depth))  2.17 us
  transfers between devices with their start and end apart: 16, of which 8 were waited for; matrix products, arithmetic and copies ran while one was open for 22% of the time, Pallas kernels for 4%

profile of v5, /device:TPU:0, one launch (start us, length us, event | category | flops | bytes accessed | tf_op | source)
XLA Modules:
  0.0 59.4 jit_solution(10758587576313046155)
XLA Ops:
  0.7 1.6 %copy-done = bf16[64,16384]{1,0:T(8,128)(2,1)S(1)} copy-done((bf16[64,16384]{1,0:T(8,128)(2,1)S(1)}, bf16[64,16384]{1,0:T(8,128)(2,1)}, u32[]{:S(2)}) %copy-start) | copy-done | bytes 2097176
  2.2 0.7 %constant_dynamic-slice_fusion.4 = bf16[8,8192]{1,0:T(8,128)(2,1)} fusion(bf16[64,16384]{1,0:T(8,128)(2,1)S(1)} %copy-done, s32[]{:T(128)S(6)} %select_n.38), kind=kLoop, calls=%fused_computation.61 | loop fusion | bytes 262148 | tf_op jit(solution)/shard_map/dynamic_slice | solution.py:177
  2.9 2.9 %collective-permute-start = (bf16[8,8192]{1,0:T(8,128)(2,1)}, bf16[8,8192]{1,0:T(8,128)(2,1)}, u32[]{:S(2)}, u32[]{:S(2)}) collective-permute-start(bf16[8,8192]{1,0:T(8,128)(2,1)} %constant_dynamic-slice_fusion.4), channel_id=1, source_target_pairs={{0,1},{1,0},{2,3},{3,2},{4,5},{5,4},{6,7},{7,6},{8,9},{9,8},{10,11... | collective-permute-start | bytes 393224 | tf_op jit(solution)/shard_map/ppermute | solution.py:182
  5.8 0.8 %constant_dynamic-slice_fusion.6 = bf16[24,8192]{1,0:T(8,128)(2,1)} fusion(bf16[64,16384]{1,0:T(8,128)(2,1)S(1)} %copy-done, s32[]{:T(128)S(6)} %select_n.38), kind=kLoop, calls=%fused_computation.68 | loop fusion | bytes 786436 | tf_op jit(solution)/shard_map/dynamic_slice | solution.py:177
  6.6 0.7 %constant_dynamic-slice_fusion.7 = bf16[16,8192]{1,0:T(8,128)(2,1)} fusion(bf16[64,16384]{1,0:T(8,128)(2,1)S(1)} %copy-done, s32[]{:T(128)S(6)} %select_n.38), kind=kLoop, calls=%fused_computation.69 | loop fusion | bytes 524292 | tf_op jit(solution)/shard_map/dynamic_slice | solution.py:177
  7.3 2.0 %collective-permute-start.3 = (bf16[16,8192]{1,0:T(8,128)(2,1)}, bf16[16,8192]{1,0:T(8,128)(2,1)S(1)}, u32[]{:S(2)}, u32[]{:S(2)}) collective-permute-start(bf16[16,8192]{1,0:T(8,128)(2,1)} %constant_dynamic-slice_fusion.7), channel_id=1, source_target_pairs={{0,1},{1,0},{2,3},{3,2},{4,5},{5,4},{6,7},{7,6},{8,9},{9,8},{10,11... | collective-permute-start | bytes 786440 | tf_op jit(solution)/shard_map/ppermute | solution.py:182
  9.4 2.2 %fusion.2 = f32[64,128]{1,0:T(8,128)S(1)} fusion(bf16[8192,128]{1,0:T(8,128)(2,1)} %param.8, bf16[64,16384]{1,0:T(8,128)(2,1)S(1)} %copy-done, s32[]{:T(128)S(6)} %select_n.39), kind=kOutput, calls=%fused_computation.2 | convolution fusion | flops 134217728 | bytes 3178500 | tf_op jit(solution)/shard_map/dot_general | solution.py:221
  11.6 0.5 fusion
  12.2 0.4 copy-done.4
  12.6 0.6 %pad_maximum_fusion.1 = f32[64,256]{1,0:T(8,128)} fusion(f32[64,128]{1,0:T(8,128)S(1)} %fusion, f32[64,128]{1,0:T(8,128)S(1)} %fusion.2), kind=kLoop, calls=%fused_computation.11 | loop fusion | flops 16384 | bytes 131072 | tf_op jit(solution)/shard_map/concatenate | solution.py:226
  13.3 0.3 multiply_sine_fusion
  13.6 0.3 subtract_convert_fusion
  13.9 0.1 pad_maximum_fusion.query_ref
  14.2 2.2 %fusion.17 = f32[8,128]{1,0:T(8,128)S(1)} fusion(bf16[8,8192]{1,0:T(8,128)(2,1)} %collective-permute-done, bf16[8192,128]{1,0:T(8,128)(2,1)} %param.8), kind=kOutput, calls=%fused_computation.73 | convolution fusion | flops 16777216 | bytes 2232320 | tf_op jit(solution)/shard_map/dot_general | solution.py:221
  16.4 1.3 %fusion.18 = f32[8,128]{1,0:T(8,128)S(1)} fusion(bf16[8,8192]{1,0:T(8,128)(2,1)} %collective-permute-done, bf16[8192,128]{1,0:T(8,128)(2,1)S(1)} %copy-done.3), kind=kOutput, calls=%fused_computation.74 | convolution fusion | flops 16777216 | bytes 2232320 | tf_op jit(solution)/shard_map/dot_general | solution.py:221
  17.7 1.1 %collective-permute-done.1 = bf16[24,8192]{1,0:T(8,128)(2,1)S(1)} collective-permute-done((bf16[24,8192]{1,0:T(8,128)(2,1)}, bf16[24,8192]{1,0:T(8,128)(2,1)S(1)}, u32[]{:S(2)}, u32[]{:S(2)}) %collective-permute-start.1) | collective-permute-done | bytes 393248 | tf_op jit(solution)/shard_map/ppermute | solution.py:182
  18.9 0.5 fusion.19
  19.3 0.5 fusion.20
  19.9 2.1 %collective-permute-start.2 = (f32[64,256]{1,0:T(8,128)S(1)}, f32[64,256]{1,0:T(8,128)S(1)}, u32[]{:S(2)}, u32[]{:S(2)}) collective-permute-start(f32[64,256]{1,0:T(8,128)S(1)} %pad_maximum_fusion.2), channel_id=1, source_target_pairs={{0,1},{1,0},{2,3},{3,2},{4,5},{5,4},{6,7},{7,6},{8,9},{9,8},{10,11... | collective-permute-start | bytes 196616 | tf_op jit(solution)/shard_map/ppermute | solution.py:270
  21.9 0.1 collective-permute-start.7
  22.0 2.4 %collective-permute-done.3 = bf16[16,8192]{1,0:T(8,128)(2,1)S(1)} collective-permute-done((bf16[16,8192]{1,0:T(8,128)(2,1)}, bf16[16,8192]{1,0:T(8,128)(2,1)S(1)}, u32[]{:S(2)}, u32[]{:S(2)}) %collective-permute-start.3) | collective-permute-done | bytes 262176 | tf_op jit(solution)/shard_map/ppermute | solution.py:182
  24.5 1.4 %collective-permute-done.2 = f32[64,256]{1,0:T(8,128)S(1)} collective-permute-done((f32[64,256]{1,0:T(8,128)S(1)}, f32[64,256]{1,0:T(8,128)S(1)}, u32[]{:S(2)}, u32[]{:S(2)}) %collective-permute-start.2) | collective-permute-done | bytes 65568 | tf_op jit(solution)/shard_map/ppermute | solution.py:270
  25.9 0.1 fusion.9
  26.0 0.1 pad_maximum_fusion.4
  26.1 2.9 %collective-permute-start.4 = (bf16[64,256]{1,0:T(8,128)(2,1)S(1)}, bf16[64,256]{1,0:T(8,128)(2,1)S(1)}, u32[]{:S(2)}, u32[]{:S(2)}) collective-permute-start(bf16[64,256]{1,0:T(8,128)(2,1)S(1)} %pad_maximum_fusion.4), channel_id=1, source_target_pairs={{0,16},{2,18},{4,20},{6,22},{8,24},{10,26},{12,28},{14,30},{16,0},... | collective-permute-start | bytes 98312 | tf_op jit(solution)/shard_map/ppermute | solution.py:303
  28.9 1.6 %collective-permute-start.5 = (bf16[64,256]{1,0:T(8,128)(2,1)S(1)}, bf16[64,256]{1,0:T(8,128)(2,1)S(1)}, u32[]{:S(2)}, u32[]{:S(2)}) collective-permute-start(bf16[64,256]{1,0:T(8,128)(2,1)S(1)} %pad_maximum_fusion.4), channel_id=1, source_target_pairs={{0,8},{2,10},{4,12},{6,14},{8,0},{10,2},{12,4},{14,6},{16,24},{18,... | collective-permute-start | bytes 98312 | tf_op jit(solution)/shard_map/ppermute | solution.py:303
  30.5 0.4 fusion.21
  30.9 0.4 fusion.22
  31.4 0.4 fusion.23
  31.8 0.4 fusion.24
  32.2 2.1 %collective-permute-start.8 = (f32[64,256]{1,0:T(8,128)S(1)}, f32[64,256]{1,0:T(8,128)S(1)}, u32[]{:S(2)}, u32[]{:S(2)}) collective-permute-start(f32[64,256]{1,0:T(8,128)S(1)} %pad_maximum_fusion.3), channel_id=1, source_target_pairs={{0,1},{1,0},{2,3},{3,2},{4,5},{5,4},{6,7},{7,6},{8,9},{9,8},{10,11... | collective-permute-start | bytes 196616 | tf_op jit(solution)/shard_map/ppermute | solution.py:270
  34.3 1.9 %collective-permute-done.6 = bf16[64,256]{1,0:T(8,128)(2,1)S(1)} collective-permute-done((bf16[64,256]{1,0:T(8,128)(2,1)S(1)}, bf16[64,256]{1,0:T(8,128)(2,1)S(1)}, u32[]{:S(2)}, u32[]{:S(2)}) %collective-permute-start.6) | collective-permute-done | bytes 32800 | tf_op jit(solution)/shard_map/ppermute | solution.py:303
  36.2 0.3 collective-permute-done.8
  36.5 0.1 fusion.5
  36.6 0.1 pad_maximum_fusion.5
  36.7 2.2 %collective-permute-start.10 = (bf16[64,256]{1,0:T(8,128)(2,1)S(1)}, bf16[64,256]{1,0:T(8,128)(2,1)S(1)}, u32[]{:S(2)}, u32[]{:S(2)}) collective-permute-start(bf16[64,256]{1,0:T(8,128)(2,1)S(1)} %pad_maximum_fusion.5), channel_id=1, source_target_pairs={{0,16},{2,18},{4,20},{6,22},{8,24},{10,26},{12,28},{14,30},{16,0},... | collective-permute-start | bytes 98312 | tf_op jit(solution)/shard_map/ppermute | solution.py:303
  38.9 2.3 %collective-permute-start.11 = (bf16[64,256]{1,0:T(8,128)(2,1)S(1)}, bf16[64,256]{1,0:T(8,128)(2,1)S(1)}, u32[]{:S(2)}, u32[]{:S(2)}) collective-permute-start(bf16[64,256]{1,0:T(8,128)(2,1)S(1)} %pad_maximum_fusion.5), channel_id=1, source_target_pairs={{0,8},{2,10},{4,12},{6,14},{8,0},{10,2},{12,4},{14,6},{16,24},{18,... | collective-permute-start | bytes 98312 | tf_op jit(solution)/shard_map/ppermute | solution.py:303
  41.2 1.8 %collective-permute-start.9 = (bf16[256,256]{1,0:T(8,128)(2,1)S(1)}, bf16[256,256]{1,0:T(8,128)(2,1)S(1)}, u32[]{:S(2)}, u32[]{:S(2)}) collective-permute-start(bf16[256,256]{1,0:T(8,128)(2,1)S(1)} %constant_dynamic-update-slice_fusion), channel_id=1, source_target_pairs={{0,4},{2,6},{4,0},{6,2},{8,12},{10,14},{12,8},{14,10},{16,20},{18,... | collective-permute-start | bytes 393224 | tf_op jit(solution)/shard_map/ppermute | solution.py:303
  43.0 0.1 add.124
  43.1 0.1 add.129
  43.2 3.7 %collective-permute-done.12 = bf16[64,256]{1,0:T(8,128)(2,1)S(1)} collective-permute-done((bf16[64,256]{1,0:T(8,128)(2,1)S(1)}, bf16[64,256]{1,0:T(8,128)(2,1)S(1)}, u32[]{:S(2)}, u32[]{:S(2)}) %collective-permute-start.12) | collective-permute-done | bytes 32800 | tf_op jit(solution)/shard_map/ppermute | solution.py:303
  46.9 0.1 collective-permute-done.9
  47.0 2.1 %collective-permute-start.14 = (bf16[256,256]{1,0:T(8,128)(2,1)S(1)}, bf16[256,256]{1,0:T(8,128)(2,1)S(1)}, u32[]{:S(2)}, u32[]{:S(2)}) collective-permute-start(bf16[256,256]{1,0:T(8,128)(2,1)S(1)} %constant_dynamic-update-slice_fusion.6), channel_id=1, source_target_pairs={{0,4},{2,6},{4,0},{6,2},{8,12},{10,14},{12,8},{14,10},{16,20},{18,... | collective-permute-start | bytes 393224 | tf_op jit(solution)/shard_map/ppermute | solution.py:303
  49.3 0.1 add.132.place_ref
  49.5 2.6 %collective-permute-done.14 = bf16[256,256]{1,0:T(8,128)(2,1)S(1)} collective-permute-done((bf16[256,256]{1,0:T(8,128)(2,1)S(1)}, bf16[256,256]{1,0:T(8,128)(2,1)S(1)}, u32[]{:S(2)}, u32[]{:S(2)}) %collective-permute-start.14) | collective-permute-done | bytes 131104 | tf_op jit(solution)/shard_map/ppermute | solution.py:303
  52.2 0.6 %pad_maximum_fusion.6 = bf16[64,256]{1,0:T(8,128)(2,1)} fusion(bf16[32,256]{1,0:T(8,128)(2,1)S(1)} %constant_dynamic-slice_fusion, bf16[32,256]{1,0:T(8,128)(2,1)S(1)} %constant_dynamic-slice_fusion.1), kind=kLoop, calls=%fused_computation.20 | loop fusion | flops 65536 | bytes 65536 | tf_op jit(solution)/shard_map/concatenate | solution.py:345
  52.8 2.6 %attend_part.1 = (f32[1024,1]{1,0:T(8,128)S(1)}, f32[1024,1]{1,0:T(8,128)S(1)}, f32[1024,128]{1,0:T(8,128)S(1)}) custom-call(s32[2]{0:T(128)S(1)} %pad_add_fusion.span_ref, s32[1,1024]{1,0:T(1,128)S(1)} %add.132.place_ref, bf16[1024,128]{1,0:T(8,128)(2,1)S(1)} %pad_maximum_fusion.query_ref, bf16[512,256]{1,0:T(8,128)(2,1)S(1)} %constant_dynamic-update-slice_fusion.4.refs_0_, ...), custom_call_target="tpu_custom_call" | custom-call | flops 536870912 | bytes 1048576 | tf_op jit(solution)/shard_map/attend_part/pallas_call | solution.py:120
  55.5 4.0 %attend_last.1 = bf16[64,2048]{1,0:T(8,128)(2,1)} custom-call(s32[2]{0:T(128)S(1)} %pad_add_fusion.span_ref, s32[1,1024]{1,0:T(1,128)S(1)} %add.127.place_ref, bf16[1024,128]{1,0:T(8,128)(2,1)S(1)} %pad_maximum_fusion.query_ref, bf16[512,256]{1,0:T(8,128)(2,1)S(1)} %constant_dynamic-update-slice_fusion.10.refs_0_, ...), custom_call_target="tpu_custom_call" | custom-call | flops 536870912 | bytes 1048576 | tf_op jit(solution)/shard_map/attend_last/pallas_call | solution.py:120
  (60 shorter events, 0.9 us)
Async XLA Ops:
  0.6 1.6 %copy-start = (bf16[64,16384]{1,0:T(8,128)(2,1)S(1)}, bf16[64,16384]{1,0:T(8,128)(2,1)}, u32[]{:S(2)}) copy-start(bf16[64,16384]{1,0:T(8,128)(2,1)} %param.6) | copy-start | bytes 6291460
  2.9 11.3 %collective-permute-start = (bf16[8,8192]{1,0:T(8,128)(2,1)}, bf16[8,8192]{1,0:T(8,128)(2,1)}, u32[]{:S(2)}, u32[]{:S(2)}) collective-permute-start(bf16[8,8192]{1,0:T(8,128)(2,1)} %constant_dynamic-slice_fusion.4), channel_id=1, source_target_pairs={{0,1},{1,0},{2,3},{3,2},{4,5},{5,4},{6,7},{7,6},{8,9},{9,8},{10,11... | collective-permute-start | bytes 393224 | tf_op jit(solution)/shard_map/ppermute | solution.py:182
  6.6 12.3 %collective-permute-start.1 = (bf16[24,8192]{1,0:T(8,128)(2,1)}, bf16[24,8192]{1,0:T(8,128)(2,1)S(1)}, u32[]{:S(2)}, u32[]{:S(2)}) collective-permute-start(bf16[24,8192]{1,0:T(8,128)(2,1)} %constant_dynamic-slice_fusion.6), channel_id=1, source_target_pairs={{0,1},{1,0},{2,3},{3,2},{4,5},{5,4},{6,7},{7,6},{8,9},{9,8},{10,11... | collective-permute-start | bytes 1179656 | tf_op jit(solution)/shard_map/ppermute | solution.py:182
  7.3 17.1 %collective-permute-start.3 = (bf16[16,8192]{1,0:T(8,128)(2,1)}, bf16[16,8192]{1,0:T(8,128)(2,1)S(1)}, u32[]{:S(2)}, u32[]{:S(2)}) collective-permute-start(bf16[16,8192]{1,0:T(8,128)(2,1)} %constant_dynamic-slice_fusion.7), channel_id=1, source_target_pairs={{0,1},{1,0},{2,3},{3,2},{4,5},{5,4},{6,7},{7,6},{8,9},{9,8},{10,11... | collective-permute-start | bytes 786440 | tf_op jit(solution)/shard_map/ppermute | solution.py:182
  9.4 2.3 %copy-start.2 = (bf16[8192,128]{1,0:T(8,128)(2,1)S(1)}, bf16[8192,128]{1,0:T(8,128)(2,1)}, u32[]{:S(2)}) copy-start(bf16[8192,128]{1,0:T(8,128)(2,1)} %param.9) | copy-start | bytes 6291460
  11.6 1.0 %copy-start.4 = (bf16[64,2048]{1,0:T(8,128)(2,1)S(1)}, bf16[64,2048]{1,0:T(8,128)(2,1)}, u32[]{:S(2)}) copy-start(bf16[64,2048]{1,0:T(8,128)(2,1)} %param.7) | copy-start | bytes 786436
  14.1 2.3 %copy-start.3 = (bf16[8192,128]{1,0:T(8,128)(2,1)S(1)}, bf16[8192,128]{1,0:T(8,128)(2,1)}, u32[]{:S(2)}) copy-start(bf16[8192,128]{1,0:T(8,128)(2,1)} %param.9) | copy-start | bytes 6291460
  14.2 4.7 %copy-start.1 = (bf16[8192,128]{1,0:T(8,128)(2,1)S(1)}, bf16[8192,128]{1,0:T(8,128)(2,1)}, u32[]{:S(2)}) copy-start(bf16[8192,128]{1,0:T(8,128)(2,1)} %param.8) | copy-start | bytes 6291460
  17.7 2.1 %copy-start.5 = (f32[64,256]{1,0:T(8,128)S(1)}, f32[64,256]{1,0:T(8,128)}, u32[]{:S(2)}) copy-start(f32[64,256]{1,0:T(8,128)} %pad_maximum_fusion.1) | copy-start | bytes 196612
  19.9 6.0 %collective-permute-start.2 = (f32[64,256]{1,0:T(8,128)S(1)}, f32[64,256]{1,0:T(8,128)S(1)}, u32[]{:S(2)}, u32[]{:S(2)}) collective-permute-start(f32[64,256]{1,0:T(8,128)S(1)} %pad_maximum_fusion.2), channel_id=1, source_target_pairs={{0,1},{1,0},{2,3},{3,2},{4,5},{5,4},{6,7},{7,6},{8,9},{9,8},{10,11... | collective-permute-start | bytes 196616 | tf_op jit(solution)/shard_map/ppermute | solution.py:270
  21.9 9.4 %collective-permute-start.7 = (bf16[16,8192]{1,0:T(8,128)(2,1)S(1)}, bf16[16,8192]{1,0:T(8,128)(2,1)S(1)}, u32[]{:S(2)}, u32[]{:S(2)}) collective-permute-start(bf16[16,8192]{1,0:T(8,128)(2,1)S(1)} %constant_dynamic-slice_fusion.5), channel_id=1, source_target_pairs={{0,1},{1,0},{2,3},{3,2},{4,5},{5,4},{6,7},{7,6},{8,9},{9,8},{10,11... | collective-permute-start | bytes 786440 | tf_op jit(solution)/shard_map/ppermute | solution.py:182
  26.1 8.2 %collective-permute-start.4 = (bf16[64,256]{1,0:T(8,128)(2,1)S(1)}, bf16[64,256]{1,0:T(8,128)(2,1)S(1)}, u32[]{:S(2)}, u32[]{:S(2)}) collective-permute-start(bf16[64,256]{1,0:T(8,128)(2,1)S(1)} %pad_maximum_fusion.4), channel_id=1, source_target_pairs={{0,16},{2,18},{4,20},{6,22},{8,24},{10,26},{12,28},{14,30},{16,0},... | collective-permute-start | bytes 98312 | tf_op jit(solution)/shard_map/ppermute | solution.py:303
  28.9 5.4 %collective-permute-start.5 = (bf16[64,256]{1,0:T(8,128)(2,1)S(1)}, bf16[64,256]{1,0:T(8,128)(2,1)S(1)}, u32[]{:S(2)}, u32[]{:S(2)}) collective-permute-start(bf16[64,256]{1,0:T(8,128)(2,1)S(1)} %pad_maximum_fusion.4), channel_id=1, source_target_pairs={{0,8},{2,10},{4,12},{6,14},{8,0},{10,2},{12,4},{14,6},{16,24},{18,... | collective-permute-start | bytes 98312 | tf_op jit(solution)/shard_map/ppermute | solution.py:303
  30.5 5.7 %collective-permute-start.6 = (bf16[64,256]{1,0:T(8,128)(2,1)S(1)}, bf16[64,256]{1,0:T(8,128)(2,1)S(1)}, u32[]{:S(2)}, u32[]{:S(2)}) collective-permute-start(bf16[64,256]{1,0:T(8,128)(2,1)S(1)} %pad_maximum_fusion.4), channel_id=1, source_target_pairs={{0,24},{2,26},{4,28},{6,30},{8,16},{10,18},{12,20},{14,22},{16,8},... | collective-permute-start | bytes 98312 | tf_op jit(solution)/shard_map/ppermute | solution.py:303
  31.7 11.2 %copy-start.6 = (s32[16]{0:T(128)S(1)}, s32[16]{0:T(128)}, u32[]{:S(2)}) copy-start(s32[16]{0:T(128)} %constant.40.clone) | copy-start | bytes 196
  32.2 4.3 %collective-permute-start.8 = (f32[64,256]{1,0:T(8,128)S(1)}, f32[64,256]{1,0:T(8,128)S(1)}, u32[]{:S(2)}, u32[]{:S(2)}) collective-permute-start(f32[64,256]{1,0:T(8,128)S(1)} %pad_maximum_fusion.3), channel_id=1, source_target_pairs={{0,1},{1,0},{2,3},{3,2},{4,5},{5,4},{6,7},{7,6},{8,9},{9,8},{10,11... | collective-permute-start | bytes 196616 | tf_op jit(solution)/shard_map/ppermute | solution.py:270
  36.7 6.4 %collective-permute-start.10 = (bf16[64,256]{1,0:T(8,128)(2,1)S(1)}, bf16[64,256]{1,0:T(8,128)(2,1)S(1)}, u32[]{:S(2)}, u32[]{:S(2)}) collective-permute-start(bf16[64,256]{1,0:T(8,128)(2,1)S(1)} %pad_maximum_fusion.5), channel_id=1, source_target_pairs={{0,16},{2,18},{4,20},{6,22},{8,24},{10,26},{12,28},{14,30},{16,0},... | collective-permute-start | bytes 98312 | tf_op jit(solution)/shard_map/ppermute | solution.py:303
  38.9 4.3 %collective-permute-start.11 = (bf16[64,256]{1,0:T(8,128)(2,1)S(1)}, bf16[64,256]{1,0:T(8,128)(2,1)S(1)}, u32[]{:S(2)}, u32[]{:S(2)}) collective-permute-start(bf16[64,256]{1,0:T(8,128)(2,1)S(1)} %pad_maximum_fusion.5), channel_id=1, source_target_pairs={{0,8},{2,10},{4,12},{6,14},{8,0},{10,2},{12,4},{14,6},{16,24},{18,... | collective-permute-start | bytes 98312 | tf_op jit(solution)/shard_map/ppermute | solution.py:303
  41.2 5.7 %collective-permute-start.12 = (bf16[64,256]{1,0:T(8,128)(2,1)S(1)}, bf16[64,256]{1,0:T(8,128)(2,1)S(1)}, u32[]{:S(2)}, u32[]{:S(2)}) collective-permute-start(bf16[64,256]{1,0:T(8,128)(2,1)S(1)} %pad_maximum_fusion.5), channel_id=1, source_target_pairs={{0,24},{2,26},{4,28},{6,30},{8,16},{10,18},{12,20},{14,22},{16,8},... | collective-permute-start | bytes 98312 | tf_op jit(solution)/shard_map/ppermute | solution.py:303
  41.2 5.8 %collective-permute-start.9 = (bf16[256,256]{1,0:T(8,128)(2,1)S(1)}, bf16[256,256]{1,0:T(8,128)(2,1)S(1)}, u32[]{:S(2)}, u32[]{:S(2)}) collective-permute-start(bf16[256,256]{1,0:T(8,128)(2,1)S(1)} %constant_dynamic-update-slice_fusion), channel_id=1, source_target_pairs={{0,4},{2,6},{4,0},{6,2},{8,12},{10,14},{12,8},{14,10},{16,20},{18,... | collective-permute-start | bytes 393224 | tf_op jit(solution)/shard_map/ppermute | solution.py:303
  47.0 5.0 %collective-permute-start.14 = (bf16[256,256]{1,0:T(8,128)(2,1)S(1)}, bf16[256,256]{1,0:T(8,128)(2,1)S(1)}, u32[]{:S(2)}, u32[]{:S(2)}) collective-permute-start(bf16[256,256]{1,0:T(8,128)(2,1)S(1)} %constant_dynamic-update-slice_fusion.6), channel_id=1, source_target_pairs={{0,4},{2,6},{4,0},{6,2},{8,12},{10,14},{12,8},{14,10},{16,20},{18,... | collective-permute-start | bytes 393224 | tf_op jit(solution)/shard_map/ppermute | solution.py:303
  49.1 2.9 %collective-permute-start.13 = (bf16[512,256]{1,0:T(8,128)(2,1)S(1)}, bf16[512,256]{1,0:T(8,128)(2,1)S(1)}, u32[]{:S(2)}, u32[]{:S(2)}) collective-permute-start(bf16[512,256]{1,0:T(8,128)(2,1)S(1)} %constant_dynamic-update-slice_fusion.4.refs_0_), channel_id=1, source_target_pairs={{0,2},{2,0},{4,6},{6,4},{8,10},{10,8},{12,14},{14,12},{16,18},{18,... | collective-permute-start | bytes 786440 | tf_op jit(solution)/shard_map/ppermute | solution.py:303
  52.1 3.4 %collective-permute-start.15 = (bf16[512,256]{1,0:T(8,128)(2,1)S(1)}, bf16[512,256]{1,0:T(8,128)(2,1)S(1)}, u32[]{:S(2)}, u32[]{:S(2)}) collective-permute-start(bf16[512,256]{1,0:T(8,128)(2,1)S(1)} %constant_dynamic-update-slice_fusion.10.refs_0_), channel_id=1, source_target_pairs={{0,2},{2,0},{4,6},{6,4},{8,10},{10,8},{12,14},{14,12},{16,18},{18,... | collective-permute-start | bytes 786440 | tf_op jit(solution)/shard_map/ppermute | solution.py:303

commit v6 on v5

--- a/solution.py
+++ b/solution.py
@@ -44,10 +44,11 @@
     values = jnp.concatenate([piece[:, head_size:] for piece in pieces], axis=0)
     width = keys.shape[0]
     edge = min(width, -(-own // 128) * 128)
-    query_pos = first + lax.rem(
-        lax.broadcasted_iota(jnp.int32, (stride, edge), 0), jnp.int32(rows)
-    )
-    diagonal = place_ref[:, :edge] <= query_pos
+    if edge:
+        query_pos = first + lax.rem(
+            lax.broadcasted_iota(jnp.int32, (stride, edge), 0), jnp.int32(rows)
+        )
+        diagonal = place_ref[:, :edge] <= query_pos
     bias = jnp.where(place_ref[...] < start, 0.0, floor_value).astype(jnp.float32)
 
     def one(part):
@@ -61,9 +62,12 @@
             )
             * factor
         )
-        masked = jnp.where(diagonal, scores[:, :edge], floor_value)
+        masked = []
+        if edge:
+            masked.append(jnp.where(diagonal, scores[:, :edge], floor_value))
         if edge < width:
-            masked = jnp.concatenate([masked, scores[:, edge:] + bias[:, edge:]], axis=1)
+            masked.append(scores[:, edge:] + bias[:, edge:])
+        masked = jnp.concatenate(masked, axis=1) if len(masked) > 1 else masked[0]
         peak = jnp.max(masked, axis=1, keepdims=True)
         if carry:
             peak = jnp.maximum(peak, old_peak[place, :])
@@ -143,6 +147,47 @@
     )(span, place, query_flat, *pieces, *(() if state is None else state))
 
 
+def pick_kernel(tokens_ref, *refs, top, count, depth, shards, own):
+    shard = lax.axis_index("fsdp")
+    outs, sems = refs[:-1], refs[-1]
+    copies = []
+    for step in range(1, shards):
+        start = pl.multiple_of(lax.rem(shard + step, shards) * depth, depth)
+        copies.append(
+            pltpu.make_async_copy(
+                tokens_ref.at[pl.ds(top, count), pl.ds(start, depth)],
+                outs[step - 1],
+                sems.at[step - 1],
+            )
+        )
+    if own:
+        start = pl.multiple_of(shard * depth, depth)
+        copies.append(
+            pltpu.make_async_copy(
+                tokens_ref.at[:, pl.ds(start, depth)], outs[shards - 1], sems.at[shards - 1]
+            )
+        )
+    for copy in copies:
+        copy.start()
+    for copy in copies:
+        copy.wait()
+
+
+def pick(tokens, top, count, depth, shards, own):
+    shapes = [jax.ShapeDtypeStruct((count, depth), tokens.dtype)] * (shards - 1)
+    if own:
+        shapes.append(jax.ShapeDtypeStruct((tokens.shape[0], depth), tokens.dtype))
+    return pl.pallas_call(
+        partial(pick_kernel, top=top, count=count, depth=depth, shards=shards, own=own),
+        out_shape=shapes,
+        in_specs=[pl.BlockSpec(memory_space=pl.ANY)],
+        out_specs=[pl.BlockSpec(memory_space=pltpu.VMEM)] * len(shapes),
+        scratch_shapes=[pltpu.SemaphoreType.DMA((shards,))],
+        compiler_params=pltpu.CompilerParams(vmem_limit_bytes=60 * 1024 * 1024),
+        name="pick_rest" if own else "pick_first",
+    )(tokens)
+
+
 def stages_of(contexts):
     bits = []
     bit = contexts // 2
@@ -168,22 +213,15 @@
         context = lax.axis_index("ctx")
         shard = lax.axis_index("fsdp")
         unit = rows // sum(sum(part) for part in plan)
-
-        def send_rows(top, count, *earlier):
-            source = after(tokens, *earlier) if earlier else tokens
-            arrived, sent = [], []
-            for step in range(1, shards):
-                target = lax.rem(shard + step, shards)
-                columns = lax.dynamic_slice(
-                    source, (jnp.int32(top), target * depth), (count, depth)
+        stages = stages_of(contexts)
+
+        def send(columns):
+            return [
+                lax.ppermute(
+                    columns[step - 1], "fsdp", [(i, (i + step) % shards) for i in range(shards)]
                 )
-                sent.append(columns)
-                arrived.append(
-                    lax.ppermute(
-                        columns, "fsdp", [(i, (i + step) % shards) for i in range(shards)]
-                    )
-                )
-            return arrived, sent
+                for step in range(1, shards)
+            ]
 
         def rows_of(table, top, count):
             return table.reshape(shards, rows, -1)[:, top : top + count].reshape(
@@ -205,25 +243,40 @@
                 chunks.append((top, size * unit))
                 top += size * unit
             part.end = len(chunks)
-            part.stage = None
+            part.stage = 0
             parts.append(part)
-        stages = stages_of(contexts)
-        ahead = parts[0].end + 1
-
-        flying = []
-        sent = ()
-        for chunk in chunks[:ahead]:
-            arrived, sent = send_rows(*chunk, *sent)
-            flying.append(arrived)
+        early, late = parts
+
+        first_rows = chunks[0][1]
+        first_columns = pick(tokens, 0, first_rows, depth, shards, False)
+        rest = pick(
+            after(tokens, *first_columns), first_rows, rows - first_rows, depth, shards, True
+        )
+        own_columns = rest[-1]
+        flying = [send(first_columns)]
+
+        def send_rows(chunk, *earlier):
+            top, count = chunk
+            source = [after(columns, *earlier) if earlier else columns for columns in rest[:-1]]
+            columns = [
+                lax.slice_in_dim(block, top - first_rows, top - first_rows + count, axis=0)
+                for block in source
+            ]
+            return send(columns)
+
+        for chunk in chunks[1 : early.end + 1]:
+            flying.append(send_rows(chunk))
 
         def project(columns):
-            return [
-                jnp.dot(columns, weight, preferred_element_type=jnp.float32)
-                for weight in (key_weight, value_weight)
-            ]
-
-        own_columns = lax.dynamic_slice_in_dim(after(tokens, *sent), shard * depth, depth, 1)
-        own_product = jnp.concatenate(project(own_columns), axis=1)
+            return jnp.concatenate(
+                [
+                    jnp.dot(columns, weight, preferred_element_type=jnp.float32)
+                    for weight in (key_weight, value_weight)
+                ],
+                axis=1,
+            )
+
+        own_product = project(own_columns)
 
         start = context * group_rows
         positions = start + jnp.arange(group_rows, dtype=jnp.int32)
@@ -241,7 +294,13 @@
             (own_product, cosine, sine_table, query_flat, span)
         )
 
-        def exchange(part, arrived):
+        def exchange(part):
+            gate = own_product
+            arrived = []
+            for number in range(part.first, part.end):
+                chunk, gate = lax.optimization_barrier((flying[number], gate))
+                gate = [project(columns) for columns in chunk]
+                arrived.append(gate)
             products = [own_product[part.top : part.top + part.rows]] + [
                 jnp.concatenate([chunk[step] for chunk in arrived], axis=0)
                 for step in range(shards - 1)
@@ -271,79 +330,77 @@
                     part.sums, "fsdp", [(i, i ^ reach) for i in range(shards)]
                 )
                 reach *= 2
-            part.stage = 0
-
-        def held(part):
-            return (part.sums, part.other) if part.stage == 0 else tuple(part.pieces)
-
-        def advance(part, values):
-            if part.stage == 0:
-                sums = values[0] + values[1]
-                keys_rot = rotate(
-                    sums[:, :head_size],
-                    rows_of(cosine, part.top, part.rows),
-                    rows_of(sine_table, part.top, part.rows),
-                ).astype(jnp.bfloat16)
-                block = after(
-                    jnp.concatenate([keys_rot, sums[:, head_size:].astype(jnp.bfloat16)], axis=1)
-                )
-                part.cache = lax.dynamic_slice_in_dim(block, shard * part.rows, part.rows, 0)
-                part.pieces, part.masks = [block], [[0]]
-            else:
-                part.pieces = list(values)
+
+        def combine(part, *gate):
+            own, other = lax.optimization_barrier((part.sums, part.other, *gate))[:2]
+            sums = own + other
+            keys_rot = rotate(
+                sums[:, :head_size],
+                rows_of(cosine, part.top, part.rows),
+                rows_of(sine_table, part.top, part.rows),
+            ).astype(jnp.bfloat16)
+            block = after(
+                jnp.concatenate([keys_rot, sums[:, head_size:].astype(jnp.bfloat16)], axis=1)
+            )
+            part.cache = lax.dynamic_slice_in_dim(block, shard * part.rows, part.rows, 0)
+            part.known, part.fresh, part.masks = block, [], [0]
+
+        def advance(part, *gate):
+            fresh = lax.optimization_barrier((part.known, part.fresh, *gate))
+            part.known = after(jnp.concatenate([fresh[0]] + list(fresh[1]), axis=0))
+            part.fresh = []
             if part.stage < len(stages):
-                known = jnp.concatenate(part.pieces, axis=0)
-                known_masks = [mask for piece_masks in part.masks for mask in piece_masks]
-                part.pieces, part.masks = [known], [known_masks]
                 moves = [0]
                 for bit in stages[part.stage]:
                     moves = moves + [move ^ bit for move in moves]
-                for move in moves[1:]:
-                    part.pieces.append(
-                        lax.ppermute(known, "ctx", [(i, i ^ move) for i in range(contexts)])
-                    )
-                    part.masks.append([mask ^ move for mask in known_masks])
+                part.fresh = [
+                    lax.ppermute(part.known, "ctx", [(i, i ^ move) for i in range(contexts)])
+                    for move in moves[1:]
+                ]
+                part.known_masks = part.masks
+                part.masks = [mask ^ move for move in moves for mask in part.masks]
             part.stage += 1
 
-        def step_all(going, extra=()):
-            gated = lax.optimization_barrier((tuple(held(part) for part in going), extra))
-            for part, values in zip(going, gated[0]):
-                advance(part, values)
-            return gated[1]
-
-        def finish(part, state, last):
+        def absorb(part, pieces, masks, own, state, last, *gate):
             local_pos = rows_of(
                 jnp.arange(group_rows, dtype=jnp.int32)[:, None], part.top, part.rows
             )[:, 0]
-            order = jnp.array([mask for masks in part.masks for mask in masks], jnp.int32)
+            order = jnp.array(masks, jnp.int32)
             place = ((context ^ order)[:, None] * group_rows + local_pos[None, :]).reshape(1, -1)
-            return attend(span, place, query_flat, part.pieces, shards * part.rows, state, last, rows)
-
-        for index, part in enumerate(parts):
-            going = [p for p in parts[:index] if p.stage <= len(stages)]
-            gate = own_product
-            arrived = []
-            for number in range(part.first, part.end):
-                chunk, gate = lax.optimization_barrier((flying[number], gate))
-                gate = [jnp.concatenate(project(columns), axis=1) for columns in chunk]
-                arrived.append(gate)
-            exchange(part, arrived)
-            for chunk in chunks[len(flying) : part.end + 2]:
-                flying.append(send_rows(*chunk, part.sums)[0])
-            if index + 1 < len(parts):
-                nearest = flying[parts[index + 1].first]
-                nearest = step_all(going + [part], tuple(nearest))
-                flying[parts[index + 1].first] = list(nearest)
-        state = None
-        going = list(parts)
-        while going:
-            step_all(going)
-            ready = [part for part in going if part.stage > len(stages)]
-            going = [part for part in going if part.stage <= len(stages)]
-            for part in ready:
-                state = finish(part, state, part is parts[-1])
+            query = after(query_flat, *gate)
+            return attend(span, place, query, pieces, own, state, last, rows)
+
+        exchange(early)
+        for chunk in chunks[early.end + 1 :]:
+            flying.append(send_rows(chunk, early.sums))
+        combine(early, *flying[early.end])
+        advance(early)
+        exchange(late)
+        for stage in range(len(stages)):
+            if early.stage < len(stages):
+                advance(early, late.sums if stage == 0 else late.known)
+            if stage == 0:
+                combine(late, early.known)
+                advance(late)
+            elif stage < len(stages) - 1:
+                advance(late, early.known)
+        state = absorb(
+            early,
+            [early.known] + list(early.fresh),
+            early.masks,
+            shards * early.rows,
+            None,
+            False,
+            late.known,
+        )
+        advance(late, *state)
+        state = absorb(
+            late, [late.known], late.known_masks, shards * late.rows, state, False
+        )
+        fresh_masks = late.masks[len(late.known_masks) :]
+        attended = absorb(late, list(late.fresh), fresh_masks, 0, state, True)
         kv_cache = jnp.concatenate([part.cache for part in parts], axis=0)
-        return (kv_cache, state)
+        return (kv_cache, attended)
 
     return local
 
@@ -351,7 +408,7 @@
 def solution(mesh):
     placed = (P(("ctx", "fsdp"), None), P(("ctx", "fsdp"), None), P("fsdp", None), P("fsdp", None))
     return jax.shard_map(
-        make_local(mesh.shape["ctx"], mesh.shape["fsdp"], ((1, 3), (2, 2))),
+        make_local(mesh.shape["ctx"], mesh.shape["fsdp"], ((2, 3), (2, 1))),
         mesh=mesh,
         in_specs=placed,
         out_specs=(P(("ctx", "fsdp"), None), P(("ctx", "fsdp"), None)),

time: 59.7 us -> 63.6 us (1.065)
  Pallas kernels: 6.6 us -> 12.9 us
  waiting for transfers between devices: 13.6 us -> 7.78 us
  local copies, waits for them, and re-layouts: 4.78 us -> 8.44 us
  starting transfers between devices: 22.1 us -> 19.5 us
  matrix products: 8.71 us -> 10 us
  other arithmetic: 2.58 us -> 3.24 us
    ppermute x14, waiting for transfers between devices: 12 us -> 5.95 us  [the longest x10 5.94 us: advance(): lax.ppermute(part.known, 'ctx', [(i, i ^ move) for i in range(contexts)])]
    pallas_call x0 -> x2, Pallas kernels: none -> 4.56 us  [pick(): pl.pallas_call(partial(pick_kernel, top=top, count=count, depth=depth, sh...]
    slice x2 -> x5, local copies, waits for them, and re-layouts: 0.01 us -> 4.38 us  [the longest x3 4.37 us: send_rows(): lax.slice_in_dim(block, top - first_rows, top - first_rows + count, axis=0)]
    ppermute x2, starting transfers between devices: 4.13 us -> 0.28 us  [exchange(): lax.ppermute(part.sums, 'fsdp', [(i, i ^ reach) for i in range(shards)])]
    slice x3 -> x5, local copies, waits for them, and re-layouts: 0.08 us -> 3.11 us  [rows_of(): table.reshape(shards, rows, -1)[:, top:top + count]]
    dynamic_slice x6 -> x2, local copies, waits for them, and re-layouts: 2.19 us -> 0.01 us  [combine(): lax.dynamic_slice_in_dim(block, shard * part.rows, part.rows, 0)]
    pallas_call x2 -> x3, Pallas kernels: 6.6 us -> 8.37 us  [attend(): pl.pallas_call(partial(attention_kernel, count=len(pieces), carry=state i...]
    unnamed x22 -> x26, local copies, waits for them, and re-layouts: 2.13 us -> 0.51 us
  transfers between devices with their start and end apart: 16 -> 16, of which waited for: 8 -> 7; matrix products, arithmetic and copies ran while one was open for 22% -> 32% of each run, Pallas kernels for 4% -> 13%
where the time goes in v6:
time: 63.6 us; the launch traced here: 63 us
  starting transfers between devices  19.5 us (31%)
  Pallas kernels  12.9 us (20%)
  matrix products  10 us (16%)
  local copies, waits for them, and re-layouts  8.44 us (13%)
  waiting for transfers between devices  7.78 us (12%)
  other arithmetic  3.24 us (5%)
  between operations  1.03 us (2%)
    ppermute x10, starting transfers between devices, advance(): lax.ppermute(part.known, 'ctx', [(i, i ^ move) for i in range(contexts)])  12.3 us
    dot_general x10, matrix products, project(): jnp.dot(columns, weight, preferred_element_type=jnp.float32)  10 us
    pallas_call x3, Pallas kernels, attend(): pl.pallas_call(partial(attention_kernel, count=len(pieces), carry=state i...  8.37 us
    ppermute x4, starting transfers between devices, send(): lax.ppermute(columns[step - 1], 'fsdp', [(i, (i + step) % shards) for i i...  6.98 us
    ppermute x10, waiting for transfers between devices, advance(): lax.ppermute(part.known, 'ctx', [(i, i ^ move) for i in range(contexts)])  5.94 us
    pallas_call x2, Pallas kernels, pick(): pl.pallas_call(partial(pick_kernel, top=top, count=count, depth=depth, sh...  4.56 us
    slice x3, local copies, waits for them, and re-layouts, send_rows(): lax.slice_in_dim(block, top - first_rows, top - first_rows + count, axis=0)  4.37 us
    slice x5, local copies, waits for them, and re-layouts, rows_of(): table.reshape(shards, rows, -1)[:, top:top + count]  3.11 us
  transfers between devices with their start and end apart: 16, of which 7 were waited for; matrix products, arithmetic and copies ran while one was open for 32% of the time, Pallas kernels for 13%

profile of v6, /device:TPU:0, one launch (start us, length us, event | category | flops | bytes accessed | tf_op | source)
XLA Modules:
  0.0 63.0 jit_solution(9948020835719823128)
XLA Ops:
  0.6 1.9 %pick_first.1 = bf16[16,8192]{1,0:T(8,128)(2,1)} custom-call(bf16[64,16384]{1,0:T(8,128)(2,1)} %tokens_ref.2), custom_call_target="tpu_custom_call" | custom-call | tf_op jit(solution)/shard_map/pick_first/pallas_call | solution.py:180
  2.5 3.0 %collective-permute-start = (bf16[16,8192]{1,0:T(8,128)(2,1)}, bf16[16,8192]{1,0:T(8,128)(2,1)}, u32[]{:S(2)}, u32[]{:S(2)}) collective-permute-start(bf16[16,8192]{1,0:T(8,128)(2,1)} %pick_first.1), channel_id=1, source_target_pairs={{0,1},{1,0},{2,3},{3,2},{4,5},{5,4},{6,7},{7,6},{8,9},{9,8},{10,11... | collective-permute-start | bytes 786440 | tf_op jit(solution)/shard_map/ppermute | solution.py:220
  5.5 2.7 %pick_rest.1 = (bf16[48,8192]{1,0:T(8,128)(2,1)}, bf16[64,8192]{1,0:T(8,128)(2,1)}) custom-call(bf16[64,16384]{1,0:T(8,128)(2,1)} %tokens_ref.2), custom_call_target="tpu_custom_call" | custom-call | tf_op jit(solution)/shard_map/pick_rest/pallas_call | solution.py:180
  8.2 1.7 %slice.72 = bf16[16,8192]{1,0:T(8,128)(2,1)} slice(bf16[48,8192]{1,0:T(8,128)(2,1)} %get-tuple-element.49), slice={[24:40], [0:8192]} | slice | bytes 524288 | tf_op jit(solution)/shard_map/slice | solution.py:262
  9.9 1.8 %slice.71 = bf16[24,8192]{1,0:T(8,128)(2,1)} slice(bf16[48,8192]{1,0:T(8,128)(2,1)} %get-tuple-element.49), slice={[0:24], [0:8192]} | slice | bytes 786432 | tf_op jit(solution)/shard_map/slice | solution.py:262
  11.7 2.0 %collective-permute-start.1 = (bf16[24,8192]{1,0:T(8,128)(2,1)}, bf16[24,8192]{1,0:T(8,128)(2,1)S(1)}, u32[]{:S(2)}, u32[]{:S(2)}) collective-permute-start(bf16[24,8192]{1,0:T(8,128)(2,1)} %slice.71), channel_id=1, source_target_pairs={{0,1},{1,0},{2,3},{3,2},{4,5},{5,4},{6,7},{7,6},{8,9},{9,8},{10,11... | collective-permute-start | bytes 1179656 | tf_op jit(solution)/shard_map/ppermute | solution.py:220
  13.7 0.6 multiply_power_fusion
  14.3 0.6 xor_multiply_fusion.1
  15.0 2.3 %fusion.9 = f32[64,128]{1,0:T(8,128)} fusion(bf16[64,8192]{1,0:T(8,128)(2,1)} %get-tuple-element.39, bf16[8192,128]{1,0:T(8,128)(2,1)S(1)} %copy-done), kind=kOutput, calls=%fused_computation.56 | convolution fusion | flops 134217728 | bytes 3178496 | tf_op jit(solution)/shard_map/dot_general | solution.py:273
  17.3 2.4 %fusion.8 = f32[64,128]{1,0:T(8,128)} fusion(bf16[64,8192]{1,0:T(8,128)(2,1)} %get-tuple-element.39, bf16[8192,128]{1,0:T(8,128)(2,1)S(1)} %copy-done.1), kind=kOutput, calls=%fused_computation.55 | convolution fusion | flops 134217728 | bytes 3178496 | tf_op jit(solution)/shard_map/dot_general | solution.py:273
  19.7 0.3 multiply_sine_fusion
  20.1 0.3 subtract_convert_fusion
  20.4 0.3 copy-done.3
  20.7 0.1 pad_maximum_fusion.1.query_ref
  21.0 0.7 %slice.97 = f32[2,24,64]{2,1,0:T(8,128)S(1)} slice(f32[2,64,64]{2,1,0:T(8,128)} %bitcast.78), slice={[0:2], [40:64], [0:64]} | slice | bytes 24576 | tf_op jit(solution)/shard_map/slice | solution.py:227
  21.7 0.8 %slice.92 = f32[2,40,64]{2,1,0:T(8,128)S(1)} slice(f32[2,64,64]{2,1,0:T(8,128)} %bitcast.79), slice={[0:2], [0:40], [0:64]} | slice | bytes 40960 | tf_op jit(solution)/shard_map/slice | solution.py:227
  22.5 0.7 %slice.95 = f32[2,24,64]{2,1,0:T(8,128)S(1)} slice(f32[2,64,64]{2,1,0:T(8,128)} %bitcast.76), slice={[0:2], [40:64], [0:64]} | slice | bytes 24576 | tf_op jit(solution)/shard_map/slice | solution.py:227
  23.2 0.8 %slice.90 = f32[2,40,64]{2,1,0:T(8,128)S(1)} slice(f32[2,64,64]{2,1,0:T(8,128)} %bitcast.77), slice={[0:2], [0:40], [0:64]} | slice | bytes 40960 | tf_op jit(solution)/shard_map/slice | solution.py:227
  24.3 1.5 %fusion.11 = f32[16,128]{1,0:T(8,128)S(1)} fusion(bf16[16,8192]{1,0:T(8,128)(2,1)} %collective-permute-done, bf16[8192,128]{1,0:T(8,128)(2,1)S(1)} %copy-done), kind=kOutput, calls=%fused_computation.58 | convolution fusion | flops 33554432 | bytes 2367488 | tf_op jit(solution)/shard_map/dot_general | solution.py:273
  25.8 0.1 copy-done.2
  25.9 1.3 %fusion.10 = f32[16,128]{1,0:T(8,128)S(1)} fusion(bf16[16,8192]{1,0:T(8,128)(2,1)} %collective-permute-done, bf16[8192,128]{1,0:T(8,128)(2,1)S(1)} %copy-done.2), kind=kOutput, calls=%fused_computation.57 | convolution fusion | flops 33554432 | bytes 2367488 | tf_op jit(solution)/shard_map/dot_general | solution.py:273
  27.3 0.4 fusion.15
  27.7 0.5 fusion.13
  28.2 0.5 fusion.12
  28.7 0.2 collective-permute-start.2
  28.9 0.4 fusion.14
  29.3 0.9 %slice.79 = bf16[8,8192]{1,0:T(8,128)(2,1)S(1)} slice(bf16[48,8192]{1,0:T(8,128)(2,1)} %get-tuple-element.49), slice={[40:48], [0:8192]} | slice | bytes 262144 | tf_op jit(solution)/shard_map/slice | solution.py:262
  30.2 1.9 %collective-permute-start.4 = (bf16[8,8192]{1,0:T(8,128)(2,1)S(1)}, bf16[8,8192]{1,0:T(8,128)(2,1)S(1)}, u32[]{:S(2)}, u32[]{:S(2)}) collective-permute-start(bf16[8,8192]{1,0:T(8,128)(2,1)S(1)} %slice.79), channel_id=1, source_target_pairs={{0,1},{1,0},{2,3},{3,2},{4,5},{5,4},{6,7},{7,6},{8,9},{9,8},{10,11... | collective-permute-start | bytes 393224 | tf_op jit(solution)/shard_map/ppermute | solution.py:220
  32.2 1.8 %collective-permute-done.2 = f32[80,256]{1,0:T(8,128)S(1)} collective-permute-done((f32[80,256]{1,0:T(8,128)S(1)}, f32[80,256]{1,0:T(8,128)S(1)}, u32[]{:S(2)}, u32[]{:S(2)}) %collective-permute-start.2) | collective-permute-done | bytes 81952 | tf_op jit(solution)/shard_map/ppermute | solution.py:329
  34.1 0.1 pad_maximum_fusion.8
  34.2 3.7 %collective-permute-start.8 = (bf16[80,256]{1,0:T(8,128)(2,1)S(1)}, bf16[80,256]{1,0:T(8,128)(2,1)S(1)}, u32[]{:S(2)}, u32[]{:S(2)}) collective-permute-start(bf16[80,256]{1,0:T(8,128)(2,1)S(1)} %pad_maximum_fusion.8), channel_id=1, source_target_pairs={{0,24},{2,26},{4,28},{6,30},{8,16},{10,18},{12,20},{14,22},{16,8},... | collective-permute-start | bytes 122888 | tf_op jit(solution)/shard_map/ppermute | solution.py:357
  37.9 0.7 %collective-permute-start.6 = (bf16[80,256]{1,0:T(8,128)(2,1)S(1)}, bf16[80,256]{1,0:T(8,128)(2,1)S(1)}, u32[]{:S(2)}, u32[]{:S(2)}) collective-permute-start(bf16[80,256]{1,0:T(8,128)(2,1)S(1)} %pad_maximum_fusion.8), channel_id=1, source_target_pairs={{0,16},{2,18},{4,20},{6,22},{8,24},{10,26},{12,28},{14,30},{16,0},... | collective-permute-start | bytes 122888 | tf_op jit(solution)/shard_map/ppermute | solution.py:357
  38.7 0.4 fusion.17
  39.0 0.4 fusion.16
  39.5 0.7 %collective-permute-done.8 = bf16[80,256]{1,0:T(8,128)(2,1)S(1)} collective-permute-done((bf16[80,256]{1,0:T(8,128)(2,1)S(1)}, bf16[80,256]{1,0:T(8,128)(2,1)S(1)}, u32[]{:S(2)}, u32[]{:S(2)}) %collective-permute-start.8) | collective-permute-done | bytes 40992 | tf_op jit(solution)/shard_map/ppermute | solution.py:357
  40.2 1.7 %collective-permute-done.7 = bf16[80,256]{1,0:T(8,128)(2,1)S(1)} collective-permute-done((bf16[80,256]{1,0:T(8,128)(2,1)S(1)}, bf16[80,256]{1,0:T(8,128)(2,1)S(1)}, u32[]{:S(2)}, u32[]{:S(2)}) %collective-permute-start.7) | collective-permute-done | bytes 40992 | tf_op jit(solution)/shard_map/ppermute | solution.py:357
  41.9 0.9 %collective-permute-done.6 = bf16[80,256]{1,0:T(8,128)(2,1)S(1)} collective-permute-done((bf16[80,256]{1,0:T(8,128)(2,1)S(1)}, bf16[80,256]{1,0:T(8,128)(2,1)S(1)}, u32[]{:S(2)}, u32[]{:S(2)}) %collective-permute-start.6) | collective-permute-done | bytes 40992 | tf_op jit(solution)/shard_map/ppermute | solution.py:357
  42.8 1.7 %collective-permute-start.12 = (bf16[320,256]{1,0:T(8,128)(2,1)S(1)}, bf16[320,256]{1,0:T(8,128)(2,1)S(1)}, u32[]{:S(2)}, u32[]{:S(2)}) collective-permute-start(bf16[320,256]{1,0:T(8,128)(2,1)S(1)} %pad_maximum_fusion.3), channel_id=1, source_target_pairs={{0,4},{2,6},{4,0},{6,2},{8,12},{10,14},{12,8},{14,10},{16,20},{18,... | collective-permute-start | bytes 491528 | tf_op jit(solution)/shard_map/ppermute | solution.py:357
  44.7 2.8 %collective-permute-start.11 = (bf16[48,256]{1,0:T(8,128)(2,1)S(1)}, bf16[48,256]{1,0:T(8,128)(2,1)S(1)}, u32[]{:S(2)}, u32[]{:S(2)}) collective-permute-start(bf16[48,256]{1,0:T(8,128)(2,1)S(1)} %pad_maximum_fusion.10), channel_id=1, source_target_pairs={{0,24},{2,26},{4,28},{6,30},{8,16},{10,18},{12,20},{14,22},{16,8},... | collective-permute-start | bytes 73736 | tf_op jit(solution)/shard_map/ppermute | solution.py:357
  47.5 1.6 %collective-permute-start.9 = (bf16[48,256]{1,0:T(8,128)(2,1)S(1)}, bf16[48,256]{1,0:T(8,128)(2,1)S(1)}, u32[]{:S(2)}, u32[]{:S(2)}) collective-permute-start(bf16[48,256]{1,0:T(8,128)(2,1)S(1)} %pad_maximum_fusion.10), channel_id=1, source_target_pairs={{0,16},{2,18},{4,20},{6,22},{8,24},{10,26},{12,28},{14,30},{16,0},... | collective-permute-start | bytes 73736 | tf_op jit(solution)/shard_map/ppermute | solution.py:357
  49.6 0.9 %collective-permute-done.11 = bf16[48,256]{1,0:T(8,128)(2,1)S(1)} collective-permute-done((bf16[48,256]{1,0:T(8,128)(2,1)S(1)}, bf16[48,256]{1,0:T(8,128)(2,1)S(1)}, u32[]{:S(2)}, u32[]{:S(2)}) %collective-permute-start.11) | collective-permute-done | bytes 24608 | tf_op jit(solution)/shard_map/ppermute | solution.py:357
  50.5 0.9 %collective-permute-done.10 = bf16[48,256]{1,0:T(8,128)(2,1)S(1)} collective-permute-done((bf16[48,256]{1,0:T(8,128)(2,1)S(1)}, bf16[48,256]{1,0:T(8,128)(2,1)S(1)}, u32[]{:S(2)}, u32[]{:S(2)}) %collective-permute-start.10) | collective-permute-done | bytes 24608 | tf_op jit(solution)/shard_map/ppermute | solution.py:357
  51.3 0.9 %collective-permute-done.9 = bf16[48,256]{1,0:T(8,128)(2,1)S(1)} collective-permute-done((bf16[48,256]{1,0:T(8,128)(2,1)S(1)}, bf16[48,256]{1,0:T(8,128)(2,1)S(1)}, u32[]{:S(2)}, u32[]{:S(2)}) %collective-permute-start.9) | collective-permute-done | bytes 24608 | tf_op jit(solution)/shard_map/ppermute | solution.py:357
  52.2 1.6 %collective-permute-start.13 = (bf16[192,256]{1,0:T(8,128)(2,1)S(1)}, bf16[192,256]{1,0:T(8,128)(2,1)S(1)}, u32[]{:S(2)}, u32[]{:S(2)}) collective-permute-start(bf16[192,256]{1,0:T(8,128)(2,1)S(1)} %pad_maximum_fusion.4), channel_id=1, source_target_pairs={{0,4},{2,6},{4,0},{6,2},{8,12},{10,14},{12,8},{14,10},{16,20},{18,... | collective-permute-start | bytes 294920 | tf_op jit(solution)/shard_map/ppermute | solution.py:357
  53.8 3.1 %attend_part.2 = (f32[1024,1]{1,0:T(8,128)S(1)}, f32[1024,1]{1,0:T(8,128)S(1)}, f32[1024,128]{1,0:T(8,128)S(1)}) custom-call(s32[2]{0:T(128)S(1)} %pad_add_fusion.span_ref, s32[1,1280]{1,0:T(1,128)S(1)} %add.142.place_ref, bf16[1024,128]{1,0:T(8,128)(2,1)S(1)} %pad_maximum_fusion.1.query_ref, bf16[640,256]{1,0:T(8,128)(2,1)S(1)} %pad_maximum_fusion.refs_0_, ...), custom_call_target="tpu_custom_call" | custom-call | flops 671088640 | bytes 1179648 | tf_op jit(solution)/shard_map/attend_part/pallas_call | solution.py:124
  57.0 0.6 pad_maximum_fusion.9
  57.7 2.3 %attend_part.3 = (f32[1024,1]{1,0:T(8,128)S(1)}, f32[1024,1]{1,0:T(8,128)S(1)}, f32[1024,128]{1,0:T(8,128)S(1)}) custom-call(s32[2]{0:T(128)S(1)} %pad_add_fusion.span_ref, s32[1,384]{1,0:T(1,128)S(1)} %add.145.place_ref, bf16[1024,128]{1,0:T(8,128)(2,1)S(1)} %pad_maximum_fusion.1.query_ref, bf16[384,256]{1,0:T(8,128)(2,1)S(1)} %pad_maximum_fusion.2.refs_0_, ...), custom_call_target="tpu_custom_call" | custom-call | flops 201326592 | bytes 720896 | tf_op jit(solution)/shard_map/attend_part/pallas_call | solution.py:124
  60.0 3.0 %attend_last.1 = bf16[64,2048]{1,0:T(8,128)(2,1)} custom-call(s32[2]{0:T(128)S(1)} %pad_add_fusion.span_ref, s32[1,384]{1,0:T(1,128)S(1)} %add.137.place_ref, bf16[1024,128]{1,0:T(8,128)(2,1)S(1)} %pad_maximum_fusion.1.query_ref, bf16[384,256]{1,0:T(8,128)(2,1)S(1)} %collective-permute-done.15.refs_0_, f32[1024,1]{1,0:T(8,128)S(1)} %get-tuple-element.71.refs_1_, ...), custom_call_target="tpu_custom_call" | custom-call | flops 201326592 | bytes 720896 | tf_op jit(solution)/shard_map/attend_last/pallas_call | solution.py:124
  (71 shorter events, 1.5 us)
Async XLA Ops:
  0.6 14.3 %copy-start = (bf16[8192,128]{1,0:T(8,128)(2,1)S(1)}, bf16[8192,128]{1,0:T(8,128)(2,1)}, u32[]{:S(2)}) copy-start(bf16[8192,128]{1,0:T(8,128)(2,1)} %param.10) | copy-start | bytes 6291460
  2.5 11.8 %copy-start.12 = (s32[16]{0:T(128)S(1)}, s32[16]{0:T(128)}, u32[]{:S(2)}) copy-start(s32[16]{0:T(128)} %constant.38.clone) | copy-start | bytes 196
  2.5 12.4 %copy-start.5 = (bf16[64,2048]{1,0:T(8,128)(2,1)S(1)}, bf16[64,2048]{1,0:T(8,128)(2,1)}, u32[]{:S(2)}) copy-start(bf16[64,2048]{1,0:T(8,128)(2,1)} %param.8) | copy-start | bytes 786436
  2.5 21.8 %collective-permute-start = (bf16[16,8192]{1,0:T(8,128)(2,1)}, bf16[16,8192]{1,0:T(8,128)(2,1)}, u32[]{:S(2)}, u32[]{:S(2)}) collective-permute-start(bf16[16,8192]{1,0:T(8,128)(2,1)} %pick_first.1), channel_id=1, source_target_pairs={{0,1},{1,0},{2,3},{3,2},{4,5},{5,4},{6,7},{7,6},{8,9},{9,8},{10,11... | collective-permute-start | bytes 786440 | tf_op jit(solution)/shard_map/ppermute | solution.py:220
  9.9 17.4 %collective-permute-start.3 = (bf16[16,8192]{1,0:T(8,128)(2,1)}, bf16[16,8192]{1,0:T(8,128)(2,1)S(1)}, u32[]{:S(2)}, u32[]{:S(2)}) collective-permute-start(bf16[16,8192]{1,0:T(8,128)(2,1)} %slice.72), channel_id=1, source_target_pairs={{0,1},{1,0},{2,3},{3,2},{4,5},{5,4},{6,7},{7,6},{8,9},{9,8},{10,11... | collective-permute-start | bytes 786440 | tf_op jit(solution)/shard_map/ppermute | solution.py:220
  11.7 16.0 %collective-permute-start.1 = (bf16[24,8192]{1,0:T(8,128)(2,1)}, bf16[24,8192]{1,0:T(8,128)(2,1)S(1)}, u32[]{:S(2)}, u32[]{:S(2)}) collective-permute-start(bf16[24,8192]{1,0:T(8,128)(2,1)} %slice.71), channel_id=1, source_target_pairs={{0,1},{1,0},{2,3},{3,2},{4,5},{5,4},{6,7},{7,6},{8,9},{9,8},{10,11... | collective-permute-start | bytes 1179656 | tf_op jit(solution)/shard_map/ppermute | solution.py:220
  14.3 3.0 %copy-start.1 = (bf16[8192,128]{1,0:T(8,128)(2,1)S(1)}, bf16[8192,128]{1,0:T(8,128)(2,1)}, u32[]{:S(2)}) copy-start(bf16[8192,128]{1,0:T(8,128)(2,1)} %param.9) | copy-start | bytes 6291460
  17.3 2.4 %copy-start.10 = (s32[8]{0:T(128)S(1)}, s32[8]{0:T(128)}, u32[]{:S(2)}) copy-start(s32[8]{0:T(128)} %constant.40.clone) | copy-start | bytes 100
  17.3 2.4 %copy-start.11 = (s32[8]{0:T(128)S(1)}, s32[8]{0:T(128)}, u32[]{:S(2)}) copy-start(s32[8]{0:T(128)} %constant.39.clone) | copy-start | bytes 100
  17.3 2.4 %copy-start.8 = (f32[64]{0:T(128)S(1)}, f32[64]{0:T(128)}, u32[]{:S(2)}) copy-start(f32[64]{0:T(128)} %multiply_power_fusion) | copy-start | bytes 772
  19.7 1.2 %copy-start.6 = (f32[64,128]{1,0:T(8,128)S(1)}, f32[64,128]{1,0:T(8,128)}, u32[]{:S(2)}) copy-start(f32[64,128]{1,0:T(8,128)} %fusion.9) | copy-start | bytes 98308
  19.7 1.2 %copy-start.7 = (f32[64,128]{1,0:T(8,128)S(1)}, f32[64,128]{1,0:T(8,128)}, u32[]{:S(2)}) copy-start(f32[64,128]{1,0:T(8,128)} %fusion.8) | copy-start | bytes 98308
  20.0 0.6 copy-start.3
  20.1 0.6 %copy-start.4 = (f32[128,64]{1,0:T(8,128)}, f32[128,64]{1,0:T(8,128)S(1)}, u32[]{:S(2)}) copy-start(f32[128,64]{1,0:T(8,128)S(1)} %get-tuple-element.47) | copy-start | bytes 98308
  24.2 1.7 %copy-start.2 = (bf16[8192,128]{1,0:T(8,128)(2,1)S(1)}, bf16[8192,128]{1,0:T(8,128)(2,1)}, u32[]{:S(2)}) copy-start(bf16[8192,128]{1,0:T(8,128)(2,1)} %param.9) | copy-start | bytes 6291460
  28.7 5.3 %collective-permute-start.2 = (f32[80,256]{1,0:T(8,128)S(1)}, f32[80,256]{1,0:T(8,128)S(1)}, u32[]{:S(2)}, u32[]{:S(2)}) collective-permute-start(f32[80,256]{1,0:T(8,128)S(1)} %pad_maximum_fusion.5), channel_id=1, source_target_pairs={{0,1},{1,0},{2,3},{3,2},{4,5},{5,4},{6,7},{7,6},{8,9},{9,8},{10,11... | collective-permute-start | bytes 245768 | tf_op jit(solution)/shard_map/ppermute | solution.py:329
  30.2 8.4 %collective-permute-start.4 = (bf16[8,8192]{1,0:T(8,128)(2,1)S(1)}, bf16[8,8192]{1,0:T(8,128)(2,1)S(1)}, u32[]{:S(2)}, u32[]{:S(2)}) collective-permute-start(bf16[8,8192]{1,0:T(8,128)(2,1)S(1)} %slice.79), channel_id=1, source_target_pairs={{0,1},{1,0},{2,3},{3,2},{4,5},{5,4},{6,7},{7,6},{8,9},{9,8},{10,11... | collective-permute-start | bytes 393224 | tf_op jit(solution)/shard_map/ppermute | solution.py:220
  34.2 6.0 %collective-permute-start.8 = (bf16[80,256]{1,0:T(8,128)(2,1)S(1)}, bf16[80,256]{1,0:T(8,128)(2,1)S(1)}, u32[]{:S(2)}, u32[]{:S(2)}) collective-permute-start(bf16[80,256]{1,0:T(8,128)(2,1)S(1)} %pad_maximum_fusion.8), channel_id=1, source_target_pairs={{0,24},{2,26},{4,28},{6,30},{8,16},{10,18},{12,20},{14,22},{16,8},... | collective-permute-start | bytes 122888 | tf_op jit(solution)/shard_map/ppermute | solution.py:357
  37.9 4.0 %collective-permute-start.7 = (bf16[80,256]{1,0:T(8,128)(2,1)S(1)}, bf16[80,256]{1,0:T(8,128)(2,1)S(1)}, u32[]{:S(2)}, u32[]{:S(2)}) collective-permute-start(bf16[80,256]{1,0:T(8,128)(2,1)S(1)} %pad_maximum_fusion.8), channel_id=1, source_target_pairs={{0,8},{2,10},{4,12},{6,14},{8,0},{10,2},{12,4},{14,6},{16,24},{18,... | collective-permute-start | bytes 122888 | tf_op jit(solution)/shard_map/ppermute | solution.py:357
  37.9 4.9 %collective-permute-start.6 = (bf16[80,256]{1,0:T(8,128)(2,1)S(1)}, bf16[80,256]{1,0:T(8,128)(2,1)S(1)}, u32[]{:S(2)}, u32[]{:S(2)}) collective-permute-start(bf16[80,256]{1,0:T(8,128)(2,1)S(1)} %pad_maximum_fusion.8), channel_id=1, source_target_pairs={{0,16},{2,18},{4,20},{6,22},{8,24},{10,26},{12,28},{14,30},{16,0},... | collective-permute-start | bytes 122888 | tf_op jit(solution)/shard_map/ppermute | solution.py:357
  39.0 10.2 %copy-start.9 = (s32[16]{0:T(128)S(1)}, s32[16]{0:T(128)}, u32[]{:S(2)}) copy-start(s32[16]{0:T(128)} %xor_multiply_fusion.1) | copy-start | bytes 196
  39.5 5.1 %collective-permute-start.5 = (f32[48,256]{1,0:T(8,128)S(1)}, f32[48,256]{1,0:T(8,128)S(1)}, u32[]{:S(2)}, u32[]{:S(2)}) collective-permute-start(f32[48,256]{1,0:T(8,128)S(1)} %pad_maximum_fusion.7), channel_id=1, source_target_pairs={{0,1},{1,0},{2,3},{3,2},{4,5},{5,4},{6,7},{7,6},{8,9},{9,8},{10,11... | collective-permute-start | bytes 147464 | tf_op jit(solution)/shard_map/ppermute | solution.py:329
  42.8 6.3 %collective-permute-start.12 = (bf16[320,256]{1,0:T(8,128)(2,1)S(1)}, bf16[320,256]{1,0:T(8,128)(2,1)S(1)}, u32[]{:S(2)}, u32[]{:S(2)}) collective-permute-start(bf16[320,256]{1,0:T(8,128)(2,1)S(1)} %pad_maximum_fusion.3), channel_id=1, source_target_pairs={{0,4},{2,6},{4,0},{6,2},{8,12},{10,14},{12,8},{14,10},{16,20},{18,... | collective-permute-start | bytes 491528 | tf_op jit(solution)/shard_map/ppermute | solution.py:357
  44.7 5.7 %collective-permute-start.11 = (bf16[48,256]{1,0:T(8,128)(2,1)S(1)}, bf16[48,256]{1,0:T(8,128)(2,1)S(1)}, u32[]{:S(2)}, u32[]{:S(2)}) collective-permute-start(bf16[48,256]{1,0:T(8,128)(2,1)S(1)} %pad_maximum_fusion.10), channel_id=1, source_target_pairs={{0,24},{2,26},{4,28},{6,30},{8,16},{10,18},{12,20},{14,22},{16,8},... | collective-permute-start | bytes 73736 | tf_op jit(solution)/shard_map/ppermute | solution.py:357
  47.5 3.8 %collective-permute-start.10 = (bf16[48,256]{1,0:T(8,128)(2,1)S(1)}, bf16[48,256]{1,0:T(8,128)(2,1)S(1)}, u32[]{:S(2)}, u32[]{:S(2)}) collective-permute-start(bf16[48,256]{1,0:T(8,128)(2,1)S(1)} %pad_maximum_fusion.10), channel_id=1, source_target_pairs={{0,8},{2,10},{4,12},{6,14},{8,0},{10,2},{12,4},{14,6},{16,24},{18,... | collective-permute-start | bytes 73736 | tf_op jit(solution)/shard_map/ppermute | solution.py:357
  47.5 4.7 %collective-permute-start.9 = (bf16[48,256]{1,0:T(8,128)(2,1)S(1)}, bf16[48,256]{1,0:T(8,128)(2,1)S(1)}, u32[]{:S(2)}, u32[]{:S(2)}) collective-permute-start(bf16[48,256]{1,0:T(8,128)(2,1)S(1)} %pad_maximum_fusion.10), channel_id=1, source_target_pairs={{0,16},{2,18},{4,20},{6,22},{8,24},{10,26},{12,28},{14,30},{16,0},... | collective-permute-start | bytes 73736 | tf_op jit(solution)/shard_map/ppermute | solution.py:357
  49.2 4.7 %collective-permute-start.14 = (bf16[640,256]{1,0:T(8,128)(2,1)S(1)}, bf16[640,256]{1,0:T(8,128)(2,1)S(1)}, u32[]{:S(2)}, u32[]{:S(2)}) collective-permute-start(bf16[640,256]{1,0:T(8,128)(2,1)S(1)} %pad_maximum_fusion.refs_0_), channel_id=1, source_target_pairs={{0,2},{2,0},{4,6},{6,4},{8,10},{10,8},{12,14},{14,12},{16,18},{18,... | collective-permute-start | bytes 983048 | tf_op jit(solution)/shard_map/ppermute | solution.py:357
  52.2 4.7 %collective-permute-start.13 = (bf16[192,256]{1,0:T(8,128)(2,1)S(1)}, bf16[192,256]{1,0:T(8,128)(2,1)S(1)}, u32[]{:S(2)}, u32[]{:S(2)}) collective-permute-start(bf16[192,256]{1,0:T(8,128)(2,1)S(1)} %pad_maximum_fusion.4), channel_id=1, source_target_pairs={{0,4},{2,6},{4,0},{6,2},{8,12},{10,14},{12,8},{14,10},{16,20},{18,... | collective-permute-start | bytes 294920 | tf_op jit(solution)/shard_map/ppermute | solution.py:357
  56.9 3.0 %collective-permute-start.15 = (bf16[384,256]{1,0:T(8,128)(2,1)S(1)}, bf16[384,256]{1,0:T(8,128)(2,1)S(1)}, u32[]{:S(2)}, u32[]{:S(2)}) collective-permute-start(bf16[384,256]{1,0:T(8,128)(2,1)S(1)} %pad_maximum_fusion.2.refs_0_), channel_id=1, source_target_pairs={{0,2},{2,0},{4,6},{6,4},{8,10},{10,8},{12,14},{14,12},{16,18},{18,... | collective-permute-start | bytes 589832 | tf_op jit(solution)/shard_map/ppermute | solution.py:357

commit v7 on v6

--- a/solution.py
+++ b/solution.py
@@ -147,47 +147,6 @@
     )(span, place, query_flat, *pieces, *(() if state is None else state))
 
 
-def pick_kernel(tokens_ref, *refs, top, count, depth, shards, own):
-    shard = lax.axis_index("fsdp")
-    outs, sems = refs[:-1], refs[-1]
-    copies = []
-    for step in range(1, shards):
-        start = pl.multiple_of(lax.rem(shard + step, shards) * depth, depth)
-        copies.append(
-            pltpu.make_async_copy(
-                tokens_ref.at[pl.ds(top, count), pl.ds(start, depth)],
-                outs[step - 1],
-                sems.at[step - 1],
-            )
-        )
-    if own:
-        start = pl.multiple_of(shard * depth, depth)
-        copies.append(
-            pltpu.make_async_copy(
-                tokens_ref.at[:, pl.ds(start, depth)], outs[shards - 1], sems.at[shards - 1]
-            )
-        )
-    for copy in copies:
-        copy.start()
-    for copy in copies:
-        copy.wait()
-
-
-def pick(tokens, top, count, depth, shards, own):
-    shapes = [jax.ShapeDtypeStruct((count, depth), tokens.dtype)] * (shards - 1)
-    if own:
-        shapes.append(jax.ShapeDtypeStruct((tokens.shape[0], depth), tokens.dtype))
-    return pl.pallas_call(
-        partial(pick_kernel, top=top, count=count, depth=depth, shards=shards, own=own),
-        out_shape=shapes,
-        in_specs=[pl.BlockSpec(memory_space=pl.ANY)],
-        out_specs=[pl.BlockSpec(memory_space=pltpu.VMEM)] * len(shapes),
-        scratch_shapes=[pltpu.SemaphoreType.DMA((shards,))],
-        compiler_params=pltpu.CompilerParams(vmem_limit_bytes=60 * 1024 * 1024),
-        name="pick_rest" if own else "pick_first",
-    )(tokens)
-
-
 def stages_of(contexts):
     bits = []
     bit = contexts // 2
@@ -215,18 +174,26 @@
         unit = rows // sum(sum(part) for part in plan)
         stages = stages_of(contexts)
 
-        def send(columns):
-            return [
-                lax.ppermute(
-                    columns[step - 1], "fsdp", [(i, (i + step) % shards) for i in range(shards)]
+        def send_rows(chunk, *earlier):
+            top, count = chunk
+            source = after(tokens, *earlier) if earlier else tokens
+            arrived, sent = [], []
+            for step in range(1, shards):
+                target = lax.rem(shard + step, shards)
+                columns = lax.dynamic_slice(
+                    source, (jnp.int32(top), target * depth), (count, depth)
                 )
-                for step in range(1, shards)
-            ]
-
-        def rows_of(table, top, count):
-            return table.reshape(shards, rows, -1)[:, top : top + count].reshape(
-                shards * count, -1
-            )
+                sent.append(columns)
+                arrived.append(
+                    lax.ppermute(
+                        columns, "fsdp", [(i, (i + step) % shards) for i in range(shards)]
+                    )
+                )
+            return arrived, sent
+
+        def places_of(top, count):
+            turns = jnp.arange(shards, dtype=jnp.int32) * rows + top
+            return (turns[:, None] + jnp.arange(count, dtype=jnp.int32)[None, :]).reshape(-1)
 
         class Part:
             pass
@@ -247,25 +214,11 @@
             parts.append(part)
         early, late = parts
 
-        first_rows = chunks[0][1]
-        first_columns = pick(tokens, 0, first_rows, depth, shards, False)
-        rest = pick(
-            after(tokens, *first_columns), first_rows, rows - first_rows, depth, shards, True
-        )
-        own_columns = rest[-1]
-        flying = [send(first_columns)]
-
-        def send_rows(chunk, *earlier):
-            top, count = chunk
-            source = [after(columns, *earlier) if earlier else columns for columns in rest[:-1]]
-            columns = [
-                lax.slice_in_dim(block, top - first_rows, top - first_rows + count, axis=0)
-                for block in source
-            ]
-            return send(columns)
-
-        for chunk in chunks[1 : early.end + 1]:
-            flying.append(send_rows(chunk))
+        flying = []
+        sent = ()
+        for chunk in chunks[: early.end + 1]:
+            arrived, sent = send_rows(chunk, *sent)
+            flying.append(arrived)
 
         def project(columns):
             return jnp.concatenate(
@@ -276,26 +229,26 @@
                 axis=1,
             )
 
+        own_columns = lax.dynamic_slice_in_dim(after(tokens, *sent), shard * depth, depth, 1)
         own_product = project(own_columns)
 
         start = context * group_rows
-        positions = start + jnp.arange(group_rows, dtype=jnp.int32)
-        cosine, sine_table = tables(positions, head_size)
-        own_cosine = lax.dynamic_slice_in_dim(cosine, shard * rows, rows, 0)
-        own_sine = lax.dynamic_slice_in_dim(sine_table, shard * rows, rows, 0)
+        first = start + shard * rows
+        own_cosine, own_sine = tables(first + jnp.arange(rows, dtype=jnp.int32), head_size)
         by_head = queries.astype(jnp.float32).reshape(rows, heads, head_size).transpose(1, 0, 2)
         query_flat = (
             rotate(by_head, own_cosine[None], own_sine[None])
             .astype(jnp.bfloat16)
             .reshape(heads * rows, head_size)
         )
-        span = jnp.stack([start, start + shard * rows]).astype(jnp.int32)
-        own_product, cosine, sine_table, query_flat, span = lax.optimization_barrier(
-            (own_product, cosine, sine_table, query_flat, span)
-        )
-
-        def exchange(part):
-            gate = own_product
+        span = jnp.stack([start, first]).astype(jnp.int32)
+        for part in parts:
+            part.tables = tables(start + places_of(part.top, part.rows), head_size)
+        own_product, early.tables, late.tables, query_flat, span = lax.optimization_barrier(
+            (own_product, early.tables, late.tables, query_flat, span)
+        )
+
+        def exchange(part, gate):
             arrived = []
             for number in range(part.first, part.end):
                 chunk, gate = lax.optimization_barrier((flying[number], gate))
@@ -334,11 +287,7 @@
         def combine(part, *gate):
             own, other = lax.optimization_barrier((part.sums, part.other, *gate))[:2]
             sums = own + other
-            keys_rot = rotate(
-                sums[:, :head_size],
-                rows_of(cosine, part.top, part.rows),
-                rows_of(sine_table, part.top, part.rows),
-            ).astype(jnp.bfloat16)
+            keys_rot = rotate(sums[:, :head_size], *part.tables).astype(jnp.bfloat16)
             block = after(
                 jnp.concatenate([keys_rot, sums[:, head_size:].astype(jnp.bfloat16)], axis=1)
             )
@@ -362,20 +311,18 @@
             part.stage += 1
 
         def absorb(part, pieces, masks, own, state, last, *gate):
-            local_pos = rows_of(
-                jnp.arange(group_rows, dtype=jnp.int32)[:, None], part.top, part.rows
-            )[:, 0]
+            local_pos = places_of(part.top, part.rows)
             order = jnp.array(masks, jnp.int32)
             place = ((context ^ order)[:, None] * group_rows + local_pos[None, :]).reshape(1, -1)
             query = after(query_flat, *gate)
             return attend(span, place, query, pieces, own, state, last, rows)
 
-        exchange(early)
+        exchange(early, own_product)
         for chunk in chunks[early.end + 1 :]:
-            flying.append(send_rows(chunk, early.sums))
+            flying.append(send_rows(chunk, early.sums)[0])
         combine(early, *flying[early.end])
         advance(early)
-        exchange(late)
+        exchange(late, early.known)
         for stage in range(len(stages)):
             if early.stage < len(stages):
                 advance(early, late.sums if stage == 0 else late.known)
@@ -408,7 +355,7 @@
 def solution(mesh):
     placed = (P(("ctx", "fsdp"), None), P(("ctx", "fsdp"), None), P("fsdp", None), P("fsdp", None))
     return jax.shard_map(
-        make_local(mesh.shape["ctx"], mesh.shape["fsdp"], ((2, 3), (2, 1))),
+        make_local(mesh.shape["ctx"], mesh.shape["fsdp"], ((1, 4), (2, 1))),
         mesh=mesh,
         in_specs=placed,
         out_specs=(P(("ctx", "fsdp"), None), P(("ctx", "fsdp"), None)),

time: 63.6 us -> 59.2 us (0.931)
  waiting for transfers between devices: 7.78 us -> 12.9 us
  Pallas kernels: 12.9 us -> 8.38 us
  matrix products: 10 us -> 5.91 us
  local copies, waits for them, and re-layouts: 8.44 us -> 4.93 us
  starting transfers between devices: 19.5 us -> 21.4 us
  other arithmetic: 3.24 us -> 4.43 us
    slice x8 -> x0, local copies, waits for them, and re-layouts: 7.48 us -> none  [the longest x3 4.37 us: send_rows(): lax.slice_in_dim(block, top - first_rows, top - first_rows + count, axis=0)]
    ppermute x4, waiting for transfers between devices: 0.01 us -> 6.97 us  [send_rows(): lax.ppermute(columns, 'fsdp', [(i, (i + step) % shards) for i in range(sh...]
    pallas_call x2 -> x0, Pallas kernels: 4.56 us -> none  [pick(): pl.pallas_call(partial(pick_kernel, top=top, count=count, depth=depth, sh...]
    dot_general x10, matrix products: 10 us -> 5.91 us  [project(): jnp.dot(columns, weight, preferred_element_type=jnp.float32)]
    ppermute x2, starting transfers between devices: 0.28 us -> 4.03 us  [exchange(): lax.ppermute(part.sums, 'fsdp', [(i, i ^ reach) for i in range(shards)])]
    unnamed x26 -> x30, local copies, waits for them, and re-layouts: 0.51 us -> 2.99 us
    ppermute x4, starting transfers between devices: 6.98 us -> 5.17 us  [send_rows(): lax.ppermute(columns, 'fsdp', [(i, (i + step) % shards) for i in range(sh...]
    ppermute x10, waiting for transfers between devices: 5.94 us -> 4.16 us  [advance(): lax.ppermute(part.known, 'ctx', [(i, i ^ move) for i in range(contexts)])]
  transfers between devices with their start and end apart: 16 -> 16, of which waited for: 7 -> 8; matrix products, arithmetic and copies ran while one was open for 32% -> 20% of each run, Pallas kernels for 13% -> 9%
where the time goes in v7:
time: 59.2 us; the launch traced here: 59 us
  starting transfers between devices  21.4 us (36%)
  waiting for transfers between devices  12.9 us (22%)
  Pallas kernels  8.38 us (14%)
  matrix products  5.91 us (10%)
  local copies, waits for them, and re-layouts  4.93 us (8%)
  other arithmetic  4.43 us (7%)
  between operations  1.04 us (2%)
    ppermute x10, starting transfers between devices, advance(): lax.ppermute(part.known, 'ctx', [(i, i ^ move) for i in range(contexts)])  12.2 us
    pallas_call x3, Pallas kernels, attend(): pl.pallas_call(partial(attention_kernel, count=len(pieces), carry=state i...  8.38 us
    ppermute x4, waiting for transfers between devices, send_rows(): lax.ppermute(columns, 'fsdp', [(i, (i + step) % shards) for i in range(sh...  6.97 us
    dot_general x10, matrix products, project(): jnp.dot(columns, weight, preferred_element_type=jnp.float32)  5.91 us
    ppermute x4, starting transfers between devices, send_rows(): lax.ppermute(columns, 'fsdp', [(i, (i + step) % shards) for i in range(sh...  5.17 us
    ppermute x10, waiting for transfers between devices, advance(): lax.ppermute(part.known, 'ctx', [(i, i ^ move) for i in range(contexts)])  4.16 us
    ppermute x2, starting transfers between devices, exchange(): lax.ppermute(part.sums, 'fsdp', [(i, i ^ reach) for i in range(shards)])  4.03 us
    unnamed x30, local copies, waits for them, and re-layouts  2.99 us
  transfers between devices with their start and end apart: 16, of which 8 were waited for; matrix products, arithmetic and copies ran while one was open for 20% of the time, Pallas kernels for 9%

profile of v7, /device:TPU:0, one launch (start us, length us, event | category | flops | bytes accessed | tf_op | source)
XLA Modules:
  0.0 59.0 jit_solution(10485950368639742689)
XLA Ops:
  0.7 1.6 %copy-done = bf16[64,16384]{1,0:T(8,128)(2,1)S(1)} copy-done((bf16[64,16384]{1,0:T(8,128)(2,1)S(1)}, bf16[64,16384]{1,0:T(8,128)(2,1)}, u32[]{:S(2)}) %copy-start) | copy-done | bytes 2097176
  2.2 0.7 %constant_dynamic-slice_fusion.2 = bf16[8,8192]{1,0:T(8,128)(2,1)} fusion(bf16[64,16384]{1,0:T(8,128)(2,1)S(1)} %copy-done, s32[]{:T(128)S(6)} %select_n.40), kind=kLoop, calls=%fused_computation.46 | loop fusion | bytes 262148 | tf_op jit(solution)/shard_map/dynamic_slice | solution.py:183
  2.9 2.9 %collective-permute-start = (bf16[8,8192]{1,0:T(8,128)(2,1)}, bf16[8,8192]{1,0:T(8,128)(2,1)S(1)}, u32[]{:S(2)}, u32[]{:S(2)}) collective-permute-start(bf16[8,8192]{1,0:T(8,128)(2,1)} %constant_dynamic-slice_fusion.2), channel_id=1, source_target_pairs={{0,1},{1,0},{2,3},{3,2},{4,5},{5,4},{6,7},{7,6},{8,9},{9,8},{10,11... | collective-permute-start | bytes 393224 | tf_op jit(solution)/shard_map/ppermute | solution.py:188
  5.8 0.8 %constant_dynamic-slice_fusion.4 = bf16[32,8192]{1,0:T(8,128)(2,1)} fusion(bf16[64,16384]{1,0:T(8,128)(2,1)S(1)} %copy-done, s32[]{:T(128)S(6)} %select_n.40), kind=kLoop, calls=%fused_computation.57 | loop fusion | bytes 1048580 | tf_op jit(solution)/shard_map/dynamic_slice | solution.py:183
  6.7 2.1 %collective-permute-start.3 = (bf16[16,8192]{1,0:T(8,128)(2,1)S(1)}, bf16[16,8192]{1,0:T(8,128)(2,1)S(1)}, u32[]{:S(2)}, u32[]{:S(2)}) collective-permute-start(bf16[16,8192]{1,0:T(8,128)(2,1)S(1)} %constant_dynamic-slice_fusion.5), channel_id=1, source_target_pairs={{0,1},{1,0},{2,3},{3,2},{4,5},{5,4},{6,7},{7,6},{8,9},{9,8},{10,11... | collective-permute-start | bytes 786440 | tf_op jit(solution)/shard_map/ppermute | solution.py:188
  8.9 0.1 add.260
  9.0 0.1 add.253
  9.1 0.8 %multiply_sine_fusion.2 = (f32[48,64]{1,0:T(8,128)}, f32[48,64]{1,0:T(8,128)}) fusion(f32[64]{0:T(128)S(1)} %multiply_power_fusion, f32[48]{0:T(128)S(1)} %add_convert_fusion.4), kind=kLoop, calls=%fused_computation.27 | loop fusion | flops 3072 | bytes 25024 | tf_op jit(solution)/shard_map/sin | solution.py:29
  9.9 0.8 %multiply_cosine_fusion.1 = (f32[64,64]{1,0:T(8,128)}, f32[64,64]{1,0:T(8,128)}) fusion(f32[64]{0:T(128)S(1)} %multiply_power_fusion, f32[64]{0:T(128)S(1)} %add_convert_fusion.3), kind=kLoop, calls=%fused_computation.19 | loop fusion | flops 4096 | bytes 33280 | tf_op jit(solution)/shard_map/cos | solution.py:29
  10.7 0.9 %multiply_sine_fusion = (f32[80,64]{1,0:T(8,128)}, f32[80,64]{1,0:T(8,128)}) fusion(f32[64]{0:T(128)S(1)} %multiply_power_fusion, f32[80]{0:T(128)S(1)} %add_convert_fusion.5), kind=kLoop, calls=%fused_computation.15 | loop fusion | flops 5120 | bytes 41536 | tf_op jit(solution)/shard_map/sin | solution.py:29
  11.6 2.2 %fusion = f32[64,128]{1,0:T(8,128)S(1)} fusion(bf16[8192,128]{1,0:T(8,128)(2,1)} %param.10, bf16[64,16384]{1,0:T(8,128)(2,1)S(1)} %copy-done, s32[]{:T(128)S(6)} %select_n.41), kind=kOutput, calls=%fused_computation | convolution fusion | flops 134217728 | bytes 3178500 | tf_op jit(solution)/shard_map/dot_general | solution.py:226
  13.9 0.5 fusion.2
  14.4 0.4 copy-done.3
  15.0 0.3 subtract_convert_fusion
  15.3 0.1 pad_maximum_fusion.1.query_ref
  15.6 0.9 %copy-done.1 = bf16[8192,128]{1,0:T(8,128)(2,1)S(1)} copy-done((bf16[8192,128]{1,0:T(8,128)(2,1)S(1)}, bf16[8192,128]{1,0:T(8,128)(2,1)}, u32[]{:S(2)}) %copy-start.1) | copy-done | bytes 2097176
  16.5 0.4 fusion.7
  16.9 0.4 fusion.6
  17.2 4.5 %collective-permute-done.1 = bf16[32,8192]{1,0:T(8,128)(2,1)S(1)} collective-permute-done((bf16[32,8192]{1,0:T(8,128)(2,1)}, bf16[32,8192]{1,0:T(8,128)(2,1)S(1)}, u32[]{:S(2)}, u32[]{:S(2)}) %collective-permute-start.1) | collective-permute-done | bytes 524320 | tf_op jit(solution)/shard_map/ppermute | solution.py:188
  21.7 0.4 fusion.9
  22.2 0.4 fusion.8
  22.7 2.0 %collective-permute-start.2 = (f32[80,256]{1,0:T(8,128)S(1)}, f32[80,256]{1,0:T(8,128)S(1)}, u32[]{:S(2)}, u32[]{:S(2)}) collective-permute-start(f32[80,256]{1,0:T(8,128)S(1)} %pad_maximum_fusion.5), channel_id=1, source_target_pairs={{0,1},{1,0},{2,3},{3,2},{4,5},{5,4},{6,7},{7,6},{8,9},{9,8},{10,11... | collective-permute-start | bytes 245768 | tf_op jit(solution)/shard_map/ppermute | solution.py:282
  24.7 0.1 collective-permute-start.4
  24.8 2.5 %collective-permute-done.3 = bf16[16,8192]{1,0:T(8,128)(2,1)S(1)} collective-permute-done((bf16[16,8192]{1,0:T(8,128)(2,1)S(1)}, bf16[16,8192]{1,0:T(8,128)(2,1)S(1)}, u32[]{:S(2)}, u32[]{:S(2)}) %collective-permute-start.3) | collective-permute-done | bytes 262176 | tf_op jit(solution)/shard_map/ppermute | solution.py:188
  27.3 1.8 %collective-permute-done.2 = f32[80,256]{1,0:T(8,128)S(1)} collective-permute-done((f32[80,256]{1,0:T(8,128)S(1)}, f32[80,256]{1,0:T(8,128)S(1)}, u32[]{:S(2)}, u32[]{:S(2)}) %collective-permute-start.2) | collective-permute-done | bytes 81952 | tf_op jit(solution)/shard_map/ppermute | solution.py:282
  29.1 0.1 subtract_convert_fusion.1
  29.2 0.1 pad_maximum_fusion.8
  29.3 0.4 fusion.11
  29.7 0.4 fusion.10
  30.1 3.8 %collective-permute-start.8 = (bf16[80,256]{1,0:T(8,128)(2,1)S(1)}, bf16[80,256]{1,0:T(8,128)(2,1)S(1)}, u32[]{:S(2)}, u32[]{:S(2)}) collective-permute-start(bf16[80,256]{1,0:T(8,128)(2,1)S(1)} %pad_maximum_fusion.8), channel_id=1, source_target_pairs={{0,24},{2,26},{4,28},{6,30},{8,16},{10,18},{12,20},{14,22},{16,8},... | collective-permute-start | bytes 122888 | tf_op jit(solution)/shard_map/ppermute | solution.py:306
  33.9 0.7 %collective-permute-start.6 = (bf16[80,256]{1,0:T(8,128)(2,1)S(1)}, bf16[80,256]{1,0:T(8,128)(2,1)S(1)}, u32[]{:S(2)}, u32[]{:S(2)}) collective-permute-start(bf16[80,256]{1,0:T(8,128)(2,1)S(1)} %pad_maximum_fusion.8), channel_id=1, source_target_pairs={{0,16},{2,18},{4,20},{6,22},{8,24},{10,26},{12,28},{14,30},{16,0},... | collective-permute-start | bytes 122888 | tf_op jit(solution)/shard_map/ppermute | solution.py:306
  34.6 0.4 fusion.13
  35.0 0.4 fusion.12
  35.4 2.0 %collective-permute-start.5 = (f32[48,256]{1,0:T(8,128)S(1)}, f32[48,256]{1,0:T(8,128)S(1)}, u32[]{:S(2)}, u32[]{:S(2)}) collective-permute-start(f32[48,256]{1,0:T(8,128)S(1)} %pad_maximum_fusion.7), channel_id=1, source_target_pairs={{0,1},{1,0},{2,3},{3,2},{4,5},{5,4},{6,7},{7,6},{8,9},{9,8},{10,11... | collective-permute-start | bytes 147464 | tf_op jit(solution)/shard_map/ppermute | solution.py:282
  37.4 0.5 collective-permute-done.7
  37.9 0.9 %collective-permute-done.6 = bf16[80,256]{1,0:T(8,128)(2,1)S(1)} collective-permute-done((bf16[80,256]{1,0:T(8,128)(2,1)S(1)}, bf16[80,256]{1,0:T(8,128)(2,1)S(1)}, u32[]{:S(2)}, u32[]{:S(2)}) %collective-permute-start.6) | collective-permute-done | bytes 40992 | tf_op jit(solution)/shard_map/ppermute | solution.py:306
  38.8 1.6 %collective-permute-start.12 = (bf16[320,256]{1,0:T(8,128)(2,1)S(1)}, bf16[320,256]{1,0:T(8,128)(2,1)S(1)}, u32[]{:S(2)}, u32[]{:S(2)}) collective-permute-start(bf16[320,256]{1,0:T(8,128)(2,1)S(1)} %pad_maximum_fusion.3), channel_id=1, source_target_pairs={{0,4},{2,6},{4,0},{6,2},{8,12},{10,14},{12,8},{14,10},{16,20},{18,... | collective-permute-start | bytes 491528 | tf_op jit(solution)/shard_map/ppermute | solution.py:306
  40.6 2.9 %collective-permute-start.11 = (bf16[48,256]{1,0:T(8,128)(2,1)S(1)}, bf16[48,256]{1,0:T(8,128)(2,1)S(1)}, u32[]{:S(2)}, u32[]{:S(2)}) collective-permute-start(bf16[48,256]{1,0:T(8,128)(2,1)S(1)} %pad_maximum_fusion.10), channel_id=1, source_target_pairs={{0,24},{2,26},{4,28},{6,30},{8,16},{10,18},{12,20},{14,22},{16,8},... | collective-permute-start | bytes 73736 | tf_op jit(solution)/shard_map/ppermute | solution.py:306
  43.5 1.5 %collective-permute-start.9 = (bf16[48,256]{1,0:T(8,128)(2,1)S(1)}, bf16[48,256]{1,0:T(8,128)(2,1)S(1)}, u32[]{:S(2)}, u32[]{:S(2)}) collective-permute-start(bf16[48,256]{1,0:T(8,128)(2,1)S(1)} %pad_maximum_fusion.10), channel_id=1, source_target_pairs={{0,16},{2,18},{4,20},{6,22},{8,24},{10,26},{12,28},{14,30},{16,0},... | collective-permute-start | bytes 73736 | tf_op jit(solution)/shard_map/ppermute | solution.py:306
  45.4 0.1 add.279.place_ref
  45.4 0.8 %collective-permute-done.11 = bf16[48,256]{1,0:T(8,128)(2,1)S(1)} collective-permute-done((bf16[48,256]{1,0:T(8,128)(2,1)S(1)}, bf16[48,256]{1,0:T(8,128)(2,1)S(1)}, u32[]{:S(2)}, u32[]{:S(2)}) %collective-permute-start.11) | collective-permute-done | bytes 24608 | tf_op jit(solution)/shard_map/ppermute | solution.py:306
  46.3 1.0 %collective-permute-done.10 = bf16[48,256]{1,0:T(8,128)(2,1)S(1)} collective-permute-done((bf16[48,256]{1,0:T(8,128)(2,1)S(1)}, bf16[48,256]{1,0:T(8,128)(2,1)S(1)}, u32[]{:S(2)}, u32[]{:S(2)}) %collective-permute-start.10) | collective-permute-done | bytes 24608 | tf_op jit(solution)/shard_map/ppermute | solution.py:306
  47.3 0.9 %collective-permute-done.9 = bf16[48,256]{1,0:T(8,128)(2,1)S(1)} collective-permute-done((bf16[48,256]{1,0:T(8,128)(2,1)S(1)}, bf16[48,256]{1,0:T(8,128)(2,1)S(1)}, u32[]{:S(2)}, u32[]{:S(2)}) %collective-permute-start.9) | collective-permute-done | bytes 24608 | tf_op jit(solution)/shard_map/ppermute | solution.py:306
  48.2 1.6 %collective-permute-start.13 = (bf16[192,256]{1,0:T(8,128)(2,1)S(1)}, bf16[192,256]{1,0:T(8,128)(2,1)S(1)}, u32[]{:S(2)}, u32[]{:S(2)}) collective-permute-start(bf16[192,256]{1,0:T(8,128)(2,1)S(1)} %pad_maximum_fusion.4), channel_id=1, source_target_pairs={{0,4},{2,6},{4,0},{6,2},{8,12},{10,14},{12,8},{14,10},{16,20},{18,... | collective-permute-start | bytes 294920 | tf_op jit(solution)/shard_map/ppermute | solution.py:306
  49.8 3.1 %attend_part.2 = (f32[1024,1]{1,0:T(8,128)S(1)}, f32[1024,1]{1,0:T(8,128)S(1)}, f32[1024,128]{1,0:T(8,128)S(1)}) custom-call(s32[2]{0:T(128)S(1)} %pad_add_fusion.span_ref, s32[1,1280]{1,0:T(1,128)S(1)} %add.279.place_ref, bf16[1024,128]{1,0:T(8,128)(2,1)S(1)} %pad_maximum_fusion.1.query_ref, bf16[640,256]{1,0:T(8,128)(2,1)S(1)} %pad_maximum_fusion.refs_0_, ...), custom_call_target="tpu_custom_call" | custom-call | flops 671088640 | bytes 1179648 | tf_op jit(solution)/shard_map/attend_part/pallas_call | solution.py:124
  53.0 0.6 %pad_maximum_fusion.9 = bf16[64,256]{1,0:T(8,128)(2,1)} fusion(bf16[24,256]{1,0:T(8,128)(2,1)S(1)} %constant_dynamic-slice_fusion, bf16[40,256]{1,0:T(8,128)(2,1)S(1)} %constant_dynamic-slice_fusion.1), kind=kLoop, calls=%fused_computation.29 | loop fusion | flops 65536 | bytes 65536 | tf_op jit(solution)/shard_map/concatenate | solution.py:349
  53.7 2.3 %attend_part.3 = (f32[1024,1]{1,0:T(8,128)S(1)}, f32[1024,1]{1,0:T(8,128)S(1)}, f32[1024,128]{1,0:T(8,128)S(1)}) custom-call(s32[2]{0:T(128)S(1)} %pad_add_fusion.span_ref, s32[1,384]{1,0:T(1,128)S(1)} %add.282.place_ref, bf16[1024,128]{1,0:T(8,128)(2,1)S(1)} %pad_maximum_fusion.1.query_ref, bf16[384,256]{1,0:T(8,128)(2,1)S(1)} %pad_maximum_fusion.2.refs_0_, ...), custom_call_target="tpu_custom_call" | custom-call | flops 201326592 | bytes 720896 | tf_op jit(solution)/shard_map/attend_part/pallas_call | solution.py:124
  56.0 3.0 %attend_last.1 = bf16[64,2048]{1,0:T(8,128)(2,1)} custom-call(s32[2]{0:T(128)S(1)} %pad_add_fusion.span_ref, s32[1,384]{1,0:T(1,128)S(1)} %add.275.place_ref, bf16[1024,128]{1,0:T(8,128)(2,1)S(1)} %pad_maximum_fusion.1.query_ref, bf16[384,256]{1,0:T(8,128)(2,1)S(1)} %collective-permute-done.15.refs_0_, f32[1024,1]{1,0:T(8,128)S(1)} %get-tuple-element.75.refs_1_, ...), custom_call_target="tpu_custom_call" | custom-call | flops 201326592 | bytes 720896 | tf_op jit(solution)/shard_map/attend_last/pallas_call | solution.py:124
  (75 shorter events, 1.3 us)
Async XLA Ops:
  0.6 1.6 %copy-start = (bf16[64,16384]{1,0:T(8,128)(2,1)S(1)}, bf16[64,16384]{1,0:T(8,128)(2,1)}, u32[]{:S(2)}) copy-start(bf16[64,16384]{1,0:T(8,128)(2,1)} %param.7) | copy-start | bytes 6291460
  2.9 12.7 %collective-permute-start = (bf16[8,8192]{1,0:T(8,128)(2,1)}, bf16[8,8192]{1,0:T(8,128)(2,1)S(1)}, u32[]{:S(2)}, u32[]{:S(2)}) collective-permute-start(bf16[8,8192]{1,0:T(8,128)(2,1)} %constant_dynamic-slice_fusion.2), channel_id=1, source_target_pairs={{0,1},{1,0},{2,3},{3,2},{4,5},{5,4},{6,7},{7,6},{8,9},{9,8},{10,11... | collective-permute-start | bytes 393224 | tf_op jit(solution)/shard_map/ppermute | solution.py:188
  6.6 15.1 %collective-permute-start.1 = (bf16[32,8192]{1,0:T(8,128)(2,1)}, bf16[32,8192]{1,0:T(8,128)(2,1)S(1)}, u32[]{:S(2)}, u32[]{:S(2)}) collective-permute-start(bf16[32,8192]{1,0:T(8,128)(2,1)} %constant_dynamic-slice_fusion.4), channel_id=1, source_target_pairs={{0,1},{1,0},{2,3},{3,2},{4,5},{5,4},{6,7},{7,6},{8,9},{9,8},{10,11... | collective-permute-start | bytes 1572872 | tf_op jit(solution)/shard_map/ppermute | solution.py:188
  6.7 20.7 %collective-permute-start.3 = (bf16[16,8192]{1,0:T(8,128)(2,1)S(1)}, bf16[16,8192]{1,0:T(8,128)(2,1)S(1)}, u32[]{:S(2)}, u32[]{:S(2)}) collective-permute-start(bf16[16,8192]{1,0:T(8,128)(2,1)S(1)} %constant_dynamic-slice_fusion.5), channel_id=1, source_target_pairs={{0,1},{1,0},{2,3},{3,2},{4,5},{5,4},{6,7},{7,6},{8,9},{9,8},{10,11... | collective-permute-start | bytes 786440 | tf_op jit(solution)/shard_map/ppermute | solution.py:188
  9.0 2.7 %copy-start.12 = (s32[48]{0:T(128)}, s32[48]{0:T(128)S(1)}, u32[]{:S(2)}) copy-start(s32[48]{0:T(128)S(1)} %add.260) | copy-start | bytes 580
  11.6 2.2 %copy-start.2 = (bf16[8192,128]{1,0:T(8,128)(2,1)S(1)}, bf16[8192,128]{1,0:T(8,128)(2,1)}, u32[]{:S(2)}) copy-start(bf16[8192,128]{1,0:T(8,128)(2,1)} %param.9) | copy-start | bytes 6291460
  13.9 1.0 %copy-start.3 = (bf16[64,2048]{1,0:T(8,128)(2,1)S(1)}, bf16[64,2048]{1,0:T(8,128)(2,1)}, u32[]{:S(2)}) copy-start(bf16[64,2048]{1,0:T(8,128)(2,1)} %param.8) | copy-start | bytes 786436
  13.9 1.1 %copy-start.6 = (f32[64,64]{1,0:T(8,128)S(1)}, f32[64,64]{1,0:T(8,128)}, u32[]{:S(2)}) copy-start(f32[64,64]{1,0:T(8,128)} %get-tuple-element.88) | copy-start | bytes 49156
  13.9 1.1 %copy-start.7 = (f32[64,64]{1,0:T(8,128)S(1)}, f32[64,64]{1,0:T(8,128)}, u32[]{:S(2)}) copy-start(f32[64,64]{1,0:T(8,128)} %get-tuple-element.89) | copy-start | bytes 49156
  14.8 0.7 %copy-start.10 = (s32[8]{0:T(128)S(1)}, s32[8]{0:T(128)}, u32[]{:S(2)}) copy-start(s32[8]{0:T(128)} %constant.54.clone) | copy-start | bytes 100
  14.8 0.7 %copy-start.11 = (s32[8]{0:T(128)S(1)}, s32[8]{0:T(128)}, u32[]{:S(2)}) copy-start(s32[8]{0:T(128)} %constant.53.clone) | copy-start | bytes 100
  14.8 0.7 %copy-start.13 = (s32[48]{0:T(128)S(1)}, s32[48]{0:T(128)}, u32[]{:S(2)}) copy-start(s32[48]{0:T(128)} %copy-done.12) | copy-start | bytes 580
  14.8 0.8 %copy-start.14 = (s32[16]{0:T(128)S(1)}, s32[16]{0:T(128)}, u32[]{:S(2)}) copy-start(s32[16]{0:T(128)} %constant.52.clone) | copy-start | bytes 196
  14.8 1.6 %copy-start.1 = (bf16[8192,128]{1,0:T(8,128)(2,1)S(1)}, bf16[8192,128]{1,0:T(8,128)(2,1)}, u32[]{:S(2)}) copy-start(bf16[8192,128]{1,0:T(8,128)(2,1)} %param.10) | copy-start | bytes 6291460
  22.2 7.0 %copy-start.4 = (f32[80,64]{1,0:T(8,128)S(1)}, f32[80,64]{1,0:T(8,128)}, u32[]{:S(2)}) copy-start(f32[80,64]{1,0:T(8,128)} %get-tuple-element.49) | copy-start | bytes 61444
  22.2 7.0 %copy-start.5 = (f32[80,64]{1,0:T(8,128)S(1)}, f32[80,64]{1,0:T(8,128)}, u32[]{:S(2)}) copy-start(f32[80,64]{1,0:T(8,128)} %get-tuple-element.48) | copy-start | bytes 61444
  22.7 6.4 %collective-permute-start.2 = (f32[80,256]{1,0:T(8,128)S(1)}, f32[80,256]{1,0:T(8,128)S(1)}, u32[]{:S(2)}, u32[]{:S(2)}) collective-permute-start(f32[80,256]{1,0:T(8,128)S(1)} %pad_maximum_fusion.5), channel_id=1, source_target_pairs={{0,1},{1,0},{2,3},{3,2},{4,5},{5,4},{6,7},{7,6},{8,9},{9,8},{10,11... | collective-permute-start | bytes 245768 | tf_op jit(solution)/shard_map/ppermute | solution.py:282
  24.7 9.9 %collective-permute-start.4 = (bf16[8,8192]{1,0:T(8,128)(2,1)S(1)}, bf16[8,8192]{1,0:T(8,128)(2,1)S(1)}, u32[]{:S(2)}, u32[]{:S(2)}) collective-permute-start(bf16[8,8192]{1,0:T(8,128)(2,1)S(1)} %constant_dynamic-slice_fusion.3), channel_id=1, source_target_pairs={{0,1},{1,0},{2,3},{3,2},{4,5},{5,4},{6,7},{7,6},{8,9},{9,8},{10,11... | collective-permute-start | bytes 393224 | tf_op jit(solution)/shard_map/ppermute | solution.py:188
  30.1 10.3 %copy-start.8 = (f32[48,64]{1,0:T(8,128)S(1)}, f32[48,64]{1,0:T(8,128)}, u32[]{:S(2)}) copy-start(f32[48,64]{1,0:T(8,128)} %get-tuple-element.60) | copy-start | bytes 36868
  30.1 10.3 %copy-start.9 = (f32[48,64]{1,0:T(8,128)S(1)}, f32[48,64]{1,0:T(8,128)}, u32[]{:S(2)}) copy-start(f32[48,64]{1,0:T(8,128)} %get-tuple-element.59) | copy-start | bytes 36868
  30.1 7.3 %collective-permute-start.8 = (bf16[80,256]{1,0:T(8,128)(2,1)S(1)}, bf16[80,256]{1,0:T(8,128)(2,1)S(1)}, u32[]{:S(2)}, u32[]{:S(2)}) collective-permute-start(bf16[80,256]{1,0:T(8,128)(2,1)S(1)} %pad_maximum_fusion.8), channel_id=1, source_target_pairs={{0,24},{2,26},{4,28},{6,30},{8,16},{10,18},{12,20},{14,22},{16,8},... | collective-permute-start | bytes 122888 | tf_op jit(solution)/shard_map/ppermute | solution.py:306
  33.9 4.0 %collective-permute-start.7 = (bf16[80,256]{1,0:T(8,128)(2,1)S(1)}, bf16[80,256]{1,0:T(8,128)(2,1)S(1)}, u32[]{:S(2)}, u32[]{:S(2)}) collective-permute-start(bf16[80,256]{1,0:T(8,128)(2,1)S(1)} %pad_maximum_fusion.8), channel_id=1, source_target_pairs={{0,8},{2,10},{4,12},{6,14},{8,0},{10,2},{12,4},{14,6},{16,24},{18,... | collective-permute-start | bytes 122888 | tf_op jit(solution)/shard_map/ppermute | solution.py:306
  33.9 4.9 %collective-permute-start.6 = (bf16[80,256]{1,0:T(8,128)(2,1)S(1)}, bf16[80,256]{1,0:T(8,128)(2,1)S(1)}, u32[]{:S(2)}, u32[]{:S(2)}) collective-permute-start(bf16[80,256]{1,0:T(8,128)(2,1)S(1)} %pad_maximum_fusion.8), channel_id=1, source_target_pairs={{0,16},{2,18},{4,20},{6,22},{8,24},{10,26},{12,28},{14,30},{16,0},... | collective-permute-start | bytes 122888 | tf_op jit(solution)/shard_map/ppermute | solution.py:306
  35.4 5.0 %collective-permute-start.5 = (f32[48,256]{1,0:T(8,128)S(1)}, f32[48,256]{1,0:T(8,128)S(1)}, u32[]{:S(2)}, u32[]{:S(2)}) collective-permute-start(f32[48,256]{1,0:T(8,128)S(1)} %pad_maximum_fusion.7), channel_id=1, source_target_pairs={{0,1},{1,0},{2,3},{3,2},{4,5},{5,4},{6,7},{7,6},{8,9},{9,8},{10,11... | collective-permute-start | bytes 147464 | tf_op jit(solution)/shard_map/ppermute | solution.py:282
  38.8 6.2 %collective-permute-start.12 = (bf16[320,256]{1,0:T(8,128)(2,1)S(1)}, bf16[320,256]{1,0:T(8,128)(2,1)S(1)}, u32[]{:S(2)}, u32[]{:S(2)}) collective-permute-start(bf16[320,256]{1,0:T(8,128)(2,1)S(1)} %pad_maximum_fusion.3), channel_id=1, source_target_pairs={{0,4},{2,6},{4,0},{6,2},{8,12},{10,14},{12,8},{14,10},{16,20},{18,... | collective-permute-start | bytes 491528 | tf_op jit(solution)/shard_map/ppermute | solution.py:306
  40.6 5.6 %collective-permute-start.11 = (bf16[48,256]{1,0:T(8,128)(2,1)S(1)}, bf16[48,256]{1,0:T(8,128)(2,1)S(1)}, u32[]{:S(2)}, u32[]{:S(2)}) collective-permute-start(bf16[48,256]{1,0:T(8,128)(2,1)S(1)} %pad_maximum_fusion.10), channel_id=1, source_target_pairs={{0,24},{2,26},{4,28},{6,30},{8,16},{10,18},{12,20},{14,22},{16,8},... | collective-permute-start | bytes 73736 | tf_op jit(solution)/shard_map/ppermute | solution.py:306
  43.5 3.8 %collective-permute-start.10 = (bf16[48,256]{1,0:T(8,128)(2,1)S(1)}, bf16[48,256]{1,0:T(8,128)(2,1)S(1)}, u32[]{:S(2)}, u32[]{:S(2)}) collective-permute-start(bf16[48,256]{1,0:T(8,128)(2,1)S(1)} %pad_maximum_fusion.10), channel_id=1, source_target_pairs={{0,8},{2,10},{4,12},{6,14},{8,0},{10,2},{12,4},{14,6},{16,24},{18,... | collective-permute-start | bytes 73736 | tf_op jit(solution)/shard_map/ppermute | solution.py:306
  43.5 4.7 %collective-permute-start.9 = (bf16[48,256]{1,0:T(8,128)(2,1)S(1)}, bf16[48,256]{1,0:T(8,128)(2,1)S(1)}, u32[]{:S(2)}, u32[]{:S(2)}) collective-permute-start(bf16[48,256]{1,0:T(8,128)(2,1)S(1)} %pad_maximum_fusion.10), channel_id=1, source_target_pairs={{0,16},{2,18},{4,20},{6,22},{8,24},{10,26},{12,28},{14,30},{16,0},... | collective-permute-start | bytes 73736 | tf_op jit(solution)/shard_map/ppermute | solution.py:306
  45.0 4.8 %collective-permute-start.14 = (bf16[640,256]{1,0:T(8,128)(2,1)S(1)}, bf16[640,256]{1,0:T(8,128)(2,1)S(1)}, u32[]{:S(2)}, u32[]{:S(2)}) collective-permute-start(bf16[640,256]{1,0:T(8,128)(2,1)S(1)} %pad_maximum_fusion.refs_0_), channel_id=1, source_target_pairs={{0,2},{2,0},{4,6},{6,4},{8,10},{10,8},{12,14},{14,12},{16,18},{18,... | collective-permute-start | bytes 983048 | tf_op jit(solution)/shard_map/ppermute | solution.py:306
  48.2 4.7 %collective-permute-start.13 = (bf16[192,256]{1,0:T(8,128)(2,1)S(1)}, bf16[192,256]{1,0:T(8,128)(2,1)S(1)}, u32[]{:S(2)}, u32[]{:S(2)}) collective-permute-start(bf16[192,256]{1,0:T(8,128)(2,1)S(1)} %pad_maximum_fusion.4), channel_id=1, source_target_pairs={{0,4},{2,6},{4,0},{6,2},{8,12},{10,14},{12,8},{14,10},{16,20},{18,... | collective-permute-start | bytes 294920 | tf_op jit(solution)/shard_map/ppermute | solution.py:306
  52.9 3.1 %collective-permute-start.15 = (bf16[384,256]{1,0:T(8,128)(2,1)S(1)}, bf16[384,256]{1,0:T(8,128)(2,1)S(1)}, u32[]{:S(2)}, u32[]{:S(2)}) collective-permute-start(bf16[384,256]{1,0:T(8,128)(2,1)S(1)} %pad_maximum_fusion.2.refs_0_), channel_id=1, source_target_pairs={{0,2},{2,0},{4,6},{6,4},{8,10},{10,8},{12,14},{14,12},{16,18},{18,... | collective-permute-start | bytes 589832 | tf_op jit(solution)/shard_map/ppermute | solution.py:306

commit v8 on v7

--- a/solution.py
+++ b/solution.py
@@ -30,8 +30,9 @@
 
 
 def attention_kernel(
-    span_ref, place_ref, query_ref, *refs, count, carry, final, rows, own, head_size, stride
+    span_ref, place_ref, query_ref, *refs, groups, carry, final, rows, own, head_size, stride
 ):
+    count = len(groups)
     pieces, refs = refs[:count], refs[count:]
     if carry:
         old_peak, old_total, old_sum = refs[:3]
@@ -40,63 +41,81 @@
     first = span_ref[1]
     factor = head_size ** (-0.5) * math.log2(math.e)
     flat = query_ref.shape[0]
-    keys = jnp.concatenate([piece[:, :head_size] for piece in pieces], axis=0)
-    values = jnp.concatenate([piece[:, head_size:] for piece in pieces], axis=0)
-    width = keys.shape[0]
-    edge = min(width, -(-own // 128) * 128)
-    if edge:
-        query_pos = first + lax.rem(
-            lax.broadcasted_iota(jnp.int32, (stride, edge), 0), jnp.int32(rows)
-        )
-        diagonal = place_ref[:, :edge] <= query_pos
-    bias = jnp.where(place_ref[...] < start, 0.0, floor_value).astype(jnp.float32)
-
-    def one(part):
-        place = pl.ds(pl.multiple_of(part * stride, stride), stride)
-        scores = (
-            lax.dot_general(
-                query_ref[place, :],
-                keys,
-                (((1,), (1,)), ((), ())),
-                preferred_element_type=jnp.float32,
-            )
-            * factor
-        )
-        masked = []
+    ordered = []
+    for half in range(2):
+        for piece, group in zip(pieces, groups):
+            for top in range(0, piece.shape[0], group):
+                begin = top + half * (group // 2)
+                ordered.append(piece[begin : begin + group // 2, :])
+    everything = jnp.concatenate(ordered, axis=0)
+
+    def run(width):
+        keys = everything[:width, :head_size]
+        values = everything[:width, head_size:]
+        edge = min(width, -(-own // 128) * 128)
         if edge:
-            masked.append(jnp.where(diagonal, scores[:, :edge], floor_value))
-        if edge < width:
-            masked.append(scores[:, edge:] + bias[:, edge:])
-        masked = jnp.concatenate(masked, axis=1) if len(masked) > 1 else masked[0]
-        peak = jnp.max(masked, axis=1, keepdims=True)
-        if carry:
-            peak = jnp.maximum(peak, old_peak[place, :])
-        weights = jnp.exp2(masked - peak)
-        total = jnp.sum(weights, axis=1, keepdims=True)
-        numerator = jnp.dot(
-            weights.astype(jnp.bfloat16), values, preferred_element_type=jnp.float32
-        )
-        if carry:
-            shrink = jnp.exp2(old_peak[place, :] - peak)
-            total = total + shrink * old_total[place, :]
-            numerator = numerator + shrink * old_sum[place, :]
-        if final:
-            out_ref, scratch = refs
-            scratch[place, :] = (numerator / total).astype(jnp.bfloat16)
+            query_pos = first + lax.rem(
+                lax.broadcasted_iota(jnp.int32, (stride, edge), 0), jnp.int32(rows)
+            )
+            diagonal = place_ref[:, :edge] <= query_pos
+        bias = jnp.where(place_ref[:, :width] < start, 0.0, floor_value).astype(jnp.float32)
+
+        def one(part):
+            place = pl.ds(pl.multiple_of(part * stride, stride), stride)
+            scores = (
+                lax.dot_general(
+                    query_ref[place, :],
+                    keys,
+                    (((1,), (1,)), ((), ())),
+                    preferred_element_type=jnp.float32,
+                )
+                * factor
+            )
+            masked = []
+            if edge:
+                masked.append(jnp.where(diagonal, scores[:, :edge], floor_value))
+            if edge < width:
+                masked.append(scores[:, edge:] + bias[:, edge:])
+            masked = jnp.concatenate(masked, axis=1) if len(masked) > 1 else masked[0]
+            peak = jnp.max(masked, axis=1, keepdims=True)
+            if carry:
+                peak = jnp.maximum(peak, old_peak[place, :])
+            weights = jnp.exp2(masked - peak)
+            total = jnp.sum(weights, axis=1, keepdims=True)
+            numerator = jnp.dot(
+                weights.astype(jnp.bfloat16), values, preferred_element_type=jnp.float32
+            )
+            if carry:
+                shrink = jnp.exp2(old_peak[place, :] - peak)
+                total = total + shrink * old_total[place, :]
+                numerator = numerator + shrink * old_sum[place, :]
+            if final:
+                out_ref, scratch = refs
+                scratch[place, :] = (numerator / total).astype(jnp.bfloat16)
+            else:
+                peak_ref, total_ref, sum_ref = refs
+                peak_ref[place, :] = peak
+                total_ref[place, :] = total
+                sum_ref[place, :] = numerator
+
+        if flat // stride <= 4:
+            for part in range(flat // stride):
+                one(part)
         else:
-            peak_ref, total_ref, sum_ref = refs
-            peak_ref[place, :] = peak
-            total_ref[place, :] = total
-            sum_ref[place, :] = numerator
-
-    if width <= 2048:
-        for part in range(flat // stride):
-            one(part)
-    else:
-
-        @pl.loop(0, flat // stride)
-        def each(part):
-            one(part)
+
+            @pl.loop(0, flat // stride)
+            def each(part):
+                one(part)
+
+    upper = span_ref[2]
+
+    @pl.when(upper == 1)
+    def all_keys():
+        run(everything.shape[0])
+
+    @pl.when(upper == 0)
+    def lower_keys():
+        run(everything.shape[0] // 2)
 
     if final:
         out_ref, scratch = refs
@@ -106,10 +125,10 @@
             ]
 
 
-def attend(span, place, query_flat, pieces, own, state, final, rows):
+def attend(span, place, query_flat, pieces, groups, own, state, final, rows):
     flat, head_size = query_flat.shape
     width = sum(piece.shape[0] for piece in pieces)
-    stride = math.gcd(flat, 256 if width <= 2048 else rows)
+    stride = math.gcd(flat, 1024 if width <= 2048 else rows)
     whole = pl.BlockSpec(memory_space=pltpu.VMEM)
     if final:
         shapes = jax.ShapeDtypeStruct((rows, flat // rows * head_size), jnp.bfloat16)
@@ -124,7 +143,7 @@
     return pl.pallas_call(
         partial(
             attention_kernel,
-            count=len(pieces),
+            groups=groups,
             carry=state is not None,
             final=final,
             rows=rows,
@@ -137,7 +156,7 @@
         + [whole] * (2 + len(pieces) + (0 if state is None else 3)),
         out_specs=out_specs,
         scratch_shapes=scratch,
-        compiler_params=pltpu.CompilerParams(vmem_limit_bytes=24 * 1024 * 1024),
+        compiler_params=pltpu.CompilerParams(vmem_limit_bytes=32 * 1024 * 1024),
         cost_estimate=pl.CostEstimate(
             flops=4 * flat * width * head_size,
             bytes_accessed=4 * flat * head_size + 4 * width * head_size,
@@ -241,7 +260,11 @@
             .astype(jnp.bfloat16)
             .reshape(heads * rows, head_size)
         )
-        span = jnp.stack([start, first]).astype(jnp.int32)
+        top_unit = min(stages[0])
+        top_count = contexts // top_unit
+        level = context // top_unit
+        upper = (2 * level >= top_count).astype(jnp.int32)
+        span = jnp.stack([start, first, upper]).astype(jnp.int32)
         for part in parts:
             part.tables = tables(start + places_of(part.top, part.rows), head_size)
         own_product, early.tables, late.tables, query_flat, span = lax.optimization_barrier(
@@ -292,13 +315,25 @@
                 jnp.concatenate([keys_rot, sums[:, head_size:].astype(jnp.bfloat16)], axis=1)
             )
             part.cache = lax.dynamic_slice_in_dim(block, shard * part.rows, part.rows, 0)
-            part.known, part.fresh, part.masks = block, [], [0]
+            part.known, part.fresh, part.masks = block, [], [(0, 0)]
 
         def advance(part, *gate):
             fresh = lax.optimization_barrier((part.known, part.fresh, *gate))
             part.known = after(jnp.concatenate([fresh[0]] + list(fresh[1]), axis=0))
             part.fresh = []
-            if part.stage < len(stages):
+            if part.stage == 0:
+                climbs = range(1, top_count)
+                part.fresh = [
+                    lax.ppermute(
+                        part.known,
+                        "ctx",
+                        [(i, i + top_unit * up) for i in range(contexts - top_unit * up)],
+                    )
+                    for up in climbs
+                ]
+                part.masks = [(0, up) for up in range(top_count)]
+                part.group = top_count * part.known.shape[0]
+            elif part.stage < len(stages):
                 moves = [0]
                 for bit in stages[part.stage]:
                     moves = moves + [move ^ bit for move in moves]
@@ -307,15 +342,26 @@
                     for move in moves[1:]
                 ]
                 part.known_masks = part.masks
-                part.masks = [mask ^ move for move in moves for mask in part.masks]
+                part.masks = [(mask ^ move, up) for move in moves for mask, up in part.masks]
             part.stage += 1
 
         def absorb(part, pieces, masks, own, state, last, *gate):
             local_pos = places_of(part.top, part.rows)
-            order = jnp.array(masks, jnp.int32)
-            place = ((context ^ order)[:, None] * group_rows + local_pos[None, :]).reshape(1, -1)
+            turns, climbs = [], []
+            for half in range(2):
+                for index, (mask, up) in enumerate(masks):
+                    if (2 * up >= top_count) == (half == 1):
+                        turns.append(mask)
+                        climbs.append(up)
+            climbs = jnp.array(climbs, jnp.int32)
+            sources = (context ^ jnp.array(turns, jnp.int32)) - climbs * top_unit
+            place = sources[:, None] * group_rows + local_pos[None, :]
+            place = jnp.where((climbs <= level)[:, None], place, contexts * group_rows)
             query = after(query_flat, *gate)
-            return attend(span, place, query, pieces, own, state, last, rows)
+            groups = tuple(min(part.group, piece.shape[0]) for piece in pieces)
+            return attend(
+                span, place.reshape(1, -1), query, pieces, groups, own, state, last, rows
+            )
 
         exchange(early, own_product)
         for chunk in chunks[early.end + 1 :]:

time: 59.2 us -> 65.3 us (1.10)
  starting transfers between devices: 21.4 us -> 26.2 us
  waiting for transfers between devices: 12.9 us -> 11.3 us
  Pallas kernels: 8.38 us -> 9.83 us
    ppermute x0 -> x6, starting transfers between devices: none -> 14.9 us  [advance(): lax.ppermute(part.known, 'ctx', [(i, i + top_unit * up) for i in range(co...]
    ppermute x10 -> x4, starting transfers between devices: 12.2 us -> 2.23 us  [advance(): lax.ppermute(part.known, 'ctx', [(i, i ^ move) for i in range(contexts)])]
    ppermute x10 -> x4, waiting for transfers between devices: 4.16 us -> 1.91 us  [advance(): lax.ppermute(part.known, 'ctx', [(i, i ^ move) for i in range(contexts)])]
    pallas_call x3, Pallas kernels: 8.38 us -> 9.83 us  [attend(): pl.pallas_call(partial(attention_kernel, groups=groups, carry=state is no...]
    le x0 -> x2, other arithmetic: none -> 1.25 us  [absorb(): place = jnp.where((climbs <= level)[:, None], place, contexts * group_rows)]
    ppermute x0 -> x6, waiting for transfers between devices: none -> 1.05 us  [advance(): lax.ppermute(part.known, 'ctx', [(i, i + top_unit * up) for i in range(co...]
    ppermute x4, waiting for transfers between devices: 6.97 us -> 5.95 us  [send_rows(): lax.ppermute(columns, 'fsdp', [(i, (i + step) % shards) for i in range(sh...]
    unnamed x30 -> x34, local copies, waits for them, and re-layouts: 2.99 us -> 3.38 us
  transfers between devices with their start and end apart: 16 -> 16, of which waited for: 8 -> 6; matrix products, arithmetic and copies ran while one was open for 20% -> 19% of each run, Pallas kernels for 9% -> 9%
where the time goes in v8:
time: 65.3 us; the launch traced here: 64.8 us
  starting transfers between devices  26.2 us (40%)
  waiting for transfers between devices  11.3 us (17%)
  Pallas kernels  9.83 us (15%)
  matrix products  5.95 us (9%)
  local copies, waits for them, and re-layouts  5.34 us (8%)
  other arithmetic  5.02 us (8%)
  between operations  1.14 us (2%)
    ppermute x6, starting transfers between devices, advance(): lax.ppermute(part.known, 'ctx', [(i, i + top_unit * up) for i in range(co...  14.9 us
    pallas_call x3, Pallas kernels, attend(): pl.pallas_call(partial(attention_kernel, groups=groups, carry=state is no...  9.83 us
    dot_general x10, matrix products, project(): jnp.dot(columns, weight, preferred_element_type=jnp.float32)  5.95 us
    ppermute x4, waiting for transfers between devices, send_rows(): lax.ppermute(columns, 'fsdp', [(i, (i + step) % shards) for i in range(sh...  5.95 us
    ppermute x4, starting transfers between devices, send_rows(): lax.ppermute(columns, 'fsdp', [(i, (i + step) % shards) for i in range(sh...  5.19 us
    ppermute x2, starting transfers between devices, exchange(): lax.ppermute(part.sums, 'fsdp', [(i, i ^ reach) for i in range(shards)])  3.92 us
    unnamed x34, local copies, waits for them, and re-layouts  3.38 us
    ppermute x2, waiting for transfers between devices, exchange(): lax.ppermute(part.sums, 'fsdp', [(i, i ^ reach) for i in range(shards)])  2.37 us
  transfers between devices with their start and end apart: 16, of which 6 were waited for; matrix products, arithmetic and copies ran while one was open for 19% of the time, Pallas kernels for 9%

profile of v8, /device:TPU:0, one launch (start us, length us, event | category | flops | bytes accessed | tf_op | source)
XLA Modules:
  0.0 64.8 jit_solution(13502009485861480003)
XLA Ops:
  0.7 1.6 %copy-done = bf16[64,16384]{1,0:T(8,128)(2,1)S(1)} copy-done((bf16[64,16384]{1,0:T(8,128)(2,1)S(1)}, bf16[64,16384]{1,0:T(8,128)(2,1)}, u32[]{:S(2)}) %copy-start) | copy-done | bytes 2097176
  2.2 0.7 %constant_dynamic-slice_fusion.2 = bf16[8,8192]{1,0:T(8,128)(2,1)} fusion(bf16[64,16384]{1,0:T(8,128)(2,1)S(1)} %copy-done, s32[]{:T(128)S(6)} %select_n.86), kind=kLoop, calls=%fused_computation.46 | loop fusion | bytes 262148 | tf_op jit(solution)/shard_map/dynamic_slice | solution.py:202
  2.9 2.9 %collective-permute-start = (bf16[8,8192]{1,0:T(8,128)(2,1)}, bf16[8,8192]{1,0:T(8,128)(2,1)S(1)}, u32[]{:S(2)}, u32[]{:S(2)}) collective-permute-start(bf16[8,8192]{1,0:T(8,128)(2,1)} %constant_dynamic-slice_fusion.2), channel_id=1, source_target_pairs={{0,1},{1,0},{2,3},{3,2},{4,5},{5,4},{6,7},{7,6},{8,9},{9,8},{10,11... | collective-permute-start | bytes 393224 | tf_op jit(solution)/shard_map/ppermute | solution.py:207
  5.8 0.8 %constant_dynamic-slice_fusion.4 = bf16[32,8192]{1,0:T(8,128)(2,1)} fusion(bf16[64,16384]{1,0:T(8,128)(2,1)S(1)} %copy-done, s32[]{:T(128)S(6)} %select_n.86), kind=kLoop, calls=%fused_computation.57 | loop fusion | bytes 1048580 | tf_op jit(solution)/shard_map/dynamic_slice | solution.py:202
  6.7 2.1 %collective-permute-start.3 = (bf16[16,8192]{1,0:T(8,128)(2,1)S(1)}, bf16[16,8192]{1,0:T(8,128)(2,1)S(1)}, u32[]{:S(2)}, u32[]{:S(2)}) collective-permute-start(bf16[16,8192]{1,0:T(8,128)(2,1)S(1)} %constant_dynamic-slice_fusion.5), channel_id=1, source_target_pairs={{0,1},{1,0},{2,3},{3,2},{4,5},{5,4},{6,7},{7,6},{8,9},{9,8},{10,11... | collective-permute-start | bytes 786440 | tf_op jit(solution)/shard_map/ppermute | solution.py:207
  8.8 1.2 %broadcast_compare_fusion.1 = pred[8]{0:T(512)(128)(4,1)} fusion(s32[8]{0:T(128)} %constant.77.clone, s32[]{:T(128)S(6)} %select_n.88), kind=kLoop, calls=%fused_computation.59 | loop fusion | flops 8 | bytes 44 | tf_op jit(solution)/shard_map/le | solution.py:359
  10.1 0.1 add.255
  10.3 0.1 add.248
  10.4 0.4 copy-done.9
  10.8 0.8 %multiply_sine_fusion.2 = (f32[48,64]{1,0:T(8,128)}, f32[48,64]{1,0:T(8,128)}) fusion(f32[64]{0:T(128)S(1)} %multiply_power_fusion, f32[48]{0:T(128)S(1)} %add_convert_fusion.4), kind=kLoop, calls=%fused_computation.27 | loop fusion | flops 3072 | bytes 25024 | tf_op jit(solution)/shard_map/sin | solution.py:29
  11.5 0.2 multiply_cosine_fusion.1
  11.7 0.9 %multiply_sine_fusion = (f32[80,64]{1,0:T(8,128)}, f32[80,64]{1,0:T(8,128)}) fusion(f32[64]{0:T(128)S(1)} %multiply_power_fusion, f32[80]{0:T(128)S(1)} %add_convert_fusion.5), kind=kLoop, calls=%fused_computation.15 | loop fusion | flops 5120 | bytes 41536 | tf_op jit(solution)/shard_map/sin | solution.py:29
  12.6 2.2 %fusion = f32[64,128]{1,0:T(8,128)S(1)} fusion(bf16[8192,128]{1,0:T(8,128)(2,1)} %param.13, bf16[64,16384]{1,0:T(8,128)(2,1)S(1)} %copy-done, s32[]{:T(128)S(6)} %select_n.87), kind=kOutput, calls=%fused_computation | convolution fusion | flops 134217728 | bytes 3178500 | tf_op jit(solution)/shard_map/dot_general | solution.py:245
  14.9 0.5 fusion.2
  15.4 0.4 copy-done.3
  15.9 0.3 subtract_convert_fusion
  16.2 0.1 pad_maximum_fusion.1.query_ref
  16.6 0.8 %copy-done.1 = bf16[8192,128]{1,0:T(8,128)(2,1)S(1)} copy-done((bf16[8192,128]{1,0:T(8,128)(2,1)S(1)}, bf16[8192,128]{1,0:T(8,128)(2,1)}, u32[]{:S(2)}) %copy-start.1) | copy-done | bytes 2097176
  17.5 0.4 fusion.7
  17.9 0.4 fusion.6
  18.3 3.5 %collective-permute-done.1 = bf16[32,8192]{1,0:T(8,128)(2,1)S(1)} collective-permute-done((bf16[32,8192]{1,0:T(8,128)(2,1)}, bf16[32,8192]{1,0:T(8,128)(2,1)S(1)}, u32[]{:S(2)}, u32[]{:S(2)}) %collective-permute-start.1) | collective-permute-done | bytes 524320 | tf_op jit(solution)/shard_map/ppermute | solution.py:207
  21.7 0.4 fusion.9
  22.2 0.4 fusion.8
  22.7 2.0 %collective-permute-start.2 = (f32[80,256]{1,0:T(8,128)S(1)}, f32[80,256]{1,0:T(8,128)S(1)}, u32[]{:S(2)}, u32[]{:S(2)}) collective-permute-start(f32[80,256]{1,0:T(8,128)S(1)} %pad_maximum_fusion.5), channel_id=1, source_target_pairs={{0,1},{1,0},{2,3},{3,2},{4,5},{5,4},{6,7},{7,6},{8,9},{9,8},{10,11... | collective-permute-start | bytes 245768 | tf_op jit(solution)/shard_map/ppermute | solution.py:305
  24.7 0.2 collective-permute-start.4
  24.9 2.5 %collective-permute-done.3 = bf16[16,8192]{1,0:T(8,128)(2,1)S(1)} collective-permute-done((bf16[16,8192]{1,0:T(8,128)(2,1)S(1)}, bf16[16,8192]{1,0:T(8,128)(2,1)S(1)}, u32[]{:S(2)}, u32[]{:S(2)}) %collective-permute-start.3) | collective-permute-done | bytes 262176 | tf_op jit(solution)/shard_map/ppermute | solution.py:207
  27.3 1.8 %collective-permute-done.2 = f32[80,256]{1,0:T(8,128)S(1)} collective-permute-done((f32[80,256]{1,0:T(8,128)S(1)}, f32[80,256]{1,0:T(8,128)S(1)}, u32[]{:S(2)}, u32[]{:S(2)}) %collective-permute-start.2) | collective-permute-done | bytes 81952 | tf_op jit(solution)/shard_map/ppermute | solution.py:305
  29.2 0.1 pad_maximum_fusion.8
  29.3 0.4 fusion.11
  29.7 0.4 fusion.10
  30.2 5.7 %collective-permute-start.8 = (bf16[80,256]{1,0:T(8,128)(2,1)S(1)}, bf16[80,256]{1,0:T(8,128)(2,1)S(1)}, u32[]{:S(2)}, u32[]{:S(2)}) collective-permute-start(bf16[80,256]{1,0:T(8,128)(2,1)S(1)} %pad_maximum_fusion.8), channel_id=1, source_target_pairs={{0,24},{2,26},{4,28},{6,30},{1,25},{3,27},{5,29},{7,31}} | collective-permute-start | bytes 122888 | tf_op jit(solution)/shard_map/ppermute | solution.py:327
  35.9 1.3 %collective-permute-start.7 = (bf16[80,256]{1,0:T(8,128)(2,1)S(1)}, bf16[80,256]{1,0:T(8,128)(2,1)S(1)}, u32[]{:S(2)}, u32[]{:S(2)}) collective-permute-start(bf16[80,256]{1,0:T(8,128)(2,1)S(1)} %pad_maximum_fusion.8), channel_id=1, source_target_pairs={{0,16},{2,18},{4,20},{6,22},{8,24},{10,26},{12,28},{14,30},{1,17},... | collective-permute-start | bytes 122888 | tf_op jit(solution)/shard_map/ppermute | solution.py:327
  37.2 2.5 %collective-permute-start.6 = (bf16[80,256]{1,0:T(8,128)(2,1)S(1)}, bf16[80,256]{1,0:T(8,128)(2,1)S(1)}, u32[]{:S(2)}, u32[]{:S(2)}) collective-permute-start(bf16[80,256]{1,0:T(8,128)(2,1)S(1)} %pad_maximum_fusion.8), channel_id=1, source_target_pairs={{0,8},{2,10},{4,12},{6,14},{8,16},{10,18},{12,20},{14,22},{16,24},... | collective-permute-start | bytes 122888 | tf_op jit(solution)/shard_map/ppermute | solution.py:327
  39.7 0.4 fusion.13
  40.1 0.4 fusion.12
  40.5 1.9 %collective-permute-start.5 = (f32[48,256]{1,0:T(8,128)S(1)}, f32[48,256]{1,0:T(8,128)S(1)}, u32[]{:S(2)}, u32[]{:S(2)}) collective-permute-start(f32[48,256]{1,0:T(8,128)S(1)} %pad_maximum_fusion.7), channel_id=1, source_target_pairs={{0,1},{1,0},{2,3},{3,2},{4,5},{5,4},{6,7},{7,6},{8,9},{9,8},{10,11... | collective-permute-start | bytes 147464 | tf_op jit(solution)/shard_map/ppermute | solution.py:305
  42.4 1.6 %collective-permute-start.12 = (bf16[320,256]{1,0:T(8,128)(2,1)S(1)}, bf16[320,256]{1,0:T(8,128)(2,1)S(1)}, u32[]{:S(2)}, u32[]{:S(2)}) collective-permute-start(bf16[320,256]{1,0:T(8,128)(2,1)S(1)} %pad_maximum_fusion.3), channel_id=1, source_target_pairs={{0,4},{2,6},{4,0},{6,2},{8,12},{10,14},{12,8},{14,10},{16,20},{18,... | collective-permute-start | bytes 491528 | tf_op jit(solution)/shard_map/ppermute | solution.py:341
  44.0 0.6 collective-permute-done.5
  44.8 1.6 %collective-permute-start.11 = (bf16[48,256]{1,0:T(8,128)(2,1)S(1)}, bf16[48,256]{1,0:T(8,128)(2,1)S(1)}, u32[]{:S(2)}, u32[]{:S(2)}) collective-permute-start(bf16[48,256]{1,0:T(8,128)(2,1)S(1)} %pad_maximum_fusion.10), channel_id=1, source_target_pairs={{0,24},{2,26},{4,28},{6,30},{1,25},{3,27},{5,29},{7,31}} | collective-permute-start | bytes 73736 | tf_op jit(solution)/shard_map/ppermute | solution.py:327
  46.5 1.3 %collective-permute-start.10 = (bf16[48,256]{1,0:T(8,128)(2,1)S(1)}, bf16[48,256]{1,0:T(8,128)(2,1)S(1)}, u32[]{:S(2)}, u32[]{:S(2)}) collective-permute-start(bf16[48,256]{1,0:T(8,128)(2,1)S(1)} %pad_maximum_fusion.10), channel_id=1, source_target_pairs={{0,16},{2,18},{4,20},{6,22},{8,24},{10,26},{12,28},{14,30},{1,17},... | collective-permute-start | bytes 73736 | tf_op jit(solution)/shard_map/ppermute | solution.py:327
  47.8 2.5 %collective-permute-start.9 = (bf16[48,256]{1,0:T(8,128)(2,1)S(1)}, bf16[48,256]{1,0:T(8,128)(2,1)S(1)}, u32[]{:S(2)}, u32[]{:S(2)}) collective-permute-start(bf16[48,256]{1,0:T(8,128)(2,1)S(1)} %pad_maximum_fusion.10), channel_id=1, source_target_pairs={{0,8},{2,10},{4,12},{6,14},{8,16},{10,18},{12,20},{14,22},{16,24},... | collective-permute-start | bytes 73736 | tf_op jit(solution)/shard_map/ppermute | solution.py:327
  50.7 1.0 %collective-permute-done.9 = bf16[48,256]{1,0:T(8,128)(2,1)S(1)} collective-permute-done((bf16[48,256]{1,0:T(8,128)(2,1)S(1)}, bf16[48,256]{1,0:T(8,128)(2,1)S(1)}, u32[]{:S(2)}, u32[]{:S(2)}) %collective-permute-start.9) | collective-permute-done | bytes 24608 | tf_op jit(solution)/shard_map/ppermute | solution.py:327
  51.8 0.5 collective-permute-start.13
  52.3 2.2 %attend_part.2 = (f32[1024,1]{1,0:T(8,128)S(1)}, f32[1024,1]{1,0:T(8,128)S(1)}, f32[1024,128]{1,0:T(8,128)S(1)}) custom-call(s32[3]{0:T(128)S(1)} %pad_add_fusion.span_ref, s32[1,1280]{1,0:T(1,128)S(1)} %select_n.99.place_ref, bf16[1024,128]{1,0:T(8,128)(2,1)S(1)} %pad_maximum_fusion.1.query_ref, bf16[640,256]{1,0:T(8,128)(2,1)S(1)} %pad_maximum_fusion.refs_0_, ...), custom_call_target="tpu_custom_call" | custom-call | flops 671088640 | bytes 1179648 | tf_op jit(solution)/shard_map/attend_part/pallas_call | solution.py:143
  54.5 1.9 %collective-permute-done.13 = bf16[192,256]{1,0:T(8,128)(2,1)S(1)} collective-permute-done((bf16[192,256]{1,0:T(8,128)(2,1)S(1)}, bf16[192,256]{1,0:T(8,128)(2,1)S(1)}, u32[]{:S(2)}, u32[]{:S(2)}) %collective-permute-start.13) | collective-permute-done | bytes 98336 | tf_op jit(solution)/shard_map/ppermute | solution.py:341
  56.5 0.6 pad_maximum_fusion.9
  57.1 3.4 %attend_part.3 = (f32[1024,1]{1,0:T(8,128)S(1)}, f32[1024,1]{1,0:T(8,128)S(1)}, f32[1024,128]{1,0:T(8,128)S(1)}) custom-call(s32[3]{0:T(128)S(1)} %pad_add_fusion.span_ref, s32[1,384]{1,0:T(1,128)S(1)} %select_n.101.place_ref, bf16[1024,128]{1,0:T(8,128)(2,1)S(1)} %pad_maximum_fusion.1.query_ref, bf16[384,256]{1,0:T(8,128)(2,1)S(1)} %pad_maximum_fusion.2.refs_0_, ...), custom_call_target="tpu_custom_call" | custom-call | flops 201326592 | bytes 720896 | tf_op jit(solution)/shard_map/attend_part/pallas_call | solution.py:143
  60.5 4.2 %attend_last.1 = bf16[64,2048]{1,0:T(8,128)(2,1)} custom-call(s32[3]{0:T(128)S(1)} %pad_add_fusion.span_ref, s32[1,384]{1,0:T(1,128)S(1)} %select_n.97.place_ref, bf16[1024,128]{1,0:T(8,128)(2,1)S(1)} %pad_maximum_fusion.1.query_ref, bf16[384,256]{1,0:T(8,128)(2,1)S(1)} %collective-permute-done.15.refs_0_, f32[1024,1]{1,0:T(8,128)S(1)} %get-tuple-element.75.refs_1_, ...), custom_call_target="tpu_custom_call" | custom-call | flops 201326592 | bytes 720896 | tf_op jit(solution)/shard_map/attend_last/pallas_call | solution.py:143
  (81 shorter events, 1.5 us)
Async XLA Ops:
  0.6 1.6 %copy-start = (bf16[64,16384]{1,0:T(8,128)(2,1)S(1)}, bf16[64,16384]{1,0:T(8,128)(2,1)}, u32[]{:S(2)}) copy-start(bf16[64,16384]{1,0:T(8,128)(2,1)} %param.10) | copy-start | bytes 6291460
  2.9 13.7 %collective-permute-start = (bf16[8,8192]{1,0:T(8,128)(2,1)}, bf16[8,8192]{1,0:T(8,128)(2,1)S(1)}, u32[]{:S(2)}, u32[]{:S(2)}) collective-permute-start(bf16[8,8192]{1,0:T(8,128)(2,1)} %constant_dynamic-slice_fusion.2), channel_id=1, source_target_pairs={{0,1},{1,0},{2,3},{3,2},{4,5},{5,4},{6,7},{7,6},{8,9},{9,8},{10,11... | collective-permute-start | bytes 393224 | tf_op jit(solution)/shard_map/ppermute | solution.py:207
  6.7 15.1 %collective-permute-start.1 = (bf16[32,8192]{1,0:T(8,128)(2,1)}, bf16[32,8192]{1,0:T(8,128)(2,1)S(1)}, u32[]{:S(2)}, u32[]{:S(2)}) collective-permute-start(bf16[32,8192]{1,0:T(8,128)(2,1)} %constant_dynamic-slice_fusion.4), channel_id=1, source_target_pairs={{0,1},{1,0},{2,3},{3,2},{4,5},{5,4},{6,7},{7,6},{8,9},{9,8},{10,11... | collective-permute-start | bytes 1572872 | tf_op jit(solution)/shard_map/ppermute | solution.py:207
  6.7 20.7 %collective-permute-start.3 = (bf16[16,8192]{1,0:T(8,128)(2,1)S(1)}, bf16[16,8192]{1,0:T(8,128)(2,1)S(1)}, u32[]{:S(2)}, u32[]{:S(2)}) collective-permute-start(bf16[16,8192]{1,0:T(8,128)(2,1)S(1)} %constant_dynamic-slice_fusion.5), channel_id=1, source_target_pairs={{0,1},{1,0},{2,3},{3,2},{4,5},{5,4},{6,7},{7,6},{8,9},{9,8},{10,11... | collective-permute-start | bytes 786440 | tf_op jit(solution)/shard_map/ppermute | solution.py:207
  10.2 0.5 copy-start.9
  12.6 2.2 %copy-start.2 = (bf16[8192,128]{1,0:T(8,128)(2,1)S(1)}, bf16[8192,128]{1,0:T(8,128)(2,1)}, u32[]{:S(2)}) copy-start(bf16[8192,128]{1,0:T(8,128)(2,1)} %param.12) | copy-start | bytes 6291460
  14.8 1.0 %copy-start.3 = (bf16[64,2048]{1,0:T(8,128)(2,1)S(1)}, bf16[64,2048]{1,0:T(8,128)(2,1)}, u32[]{:S(2)}) copy-start(bf16[64,2048]{1,0:T(8,128)(2,1)} %param.11) | copy-start | bytes 786436
  15.8 0.7 %copy-start.14 = (s32[16]{0:T(128)S(1)}, s32[16]{0:T(128)}, u32[]{:S(2)}) copy-start(s32[16]{0:T(128)} %constant.83) | copy-start | bytes 196
  15.8 0.7 %copy-start.15 = (s32[16]{0:T(128)S(1)}, s32[16]{0:T(128)}, u32[]{:S(2)}) copy-start(s32[16]{0:T(128)} %constant.76.clone) | copy-start | bytes 196
  15.8 0.7 %copy-start.11 = (s32[8]{0:T(128)S(1)}, s32[8]{0:T(128)}, u32[]{:S(2)}) copy-start(s32[8]{0:T(128)} %constant.82) | copy-start | bytes 100
  15.8 0.7 %copy-start.12 = (s32[8]{0:T(128)S(1)}, s32[8]{0:T(128)}, u32[]{:S(2)}) copy-start(s32[8]{0:T(128)} %constant.79.clone) | copy-start | bytes 100
  15.8 0.7 %copy-start.13 = (s32[8]{0:T(128)S(1)}, s32[8]{0:T(128)}, u32[]{:S(2)}) copy-start(s32[8]{0:T(128)} %constant.78.clone) | copy-start | bytes 100
  15.8 0.7 %copy-start.8 = (pred[8]{0:T(512)(128)(4,1)S(1)}, pred[8]{0:T(512)(128)(4,1)}, u32[]{:S(2)}) copy-start(pred[8]{0:T(512)(128)(4,1)} %broadcast_compare_fusion.1) | copy-start | bytes 28
  15.8 0.7 %copy-start.10 = (s32[48]{0:T(128)S(1)}, s32[48]{0:T(128)}, u32[]{:S(2)}) copy-start(s32[48]{0:T(128)} %copy-done.9) | copy-start | bytes 580
  15.8 0.8 %copy-start.16 = (s32[16]{0:T(128)S(1)}, s32[16]{0:T(128)}, u32[]{:S(2)}) copy-start(s32[16]{0:T(128)} %constant.75.clone) | copy-start | bytes 196
  15.9 1.6 %copy-start.1 = (bf16[8192,128]{1,0:T(8,128)(2,1)S(1)}, bf16[8192,128]{1,0:T(8,128)(2,1)}, u32[]{:S(2)}) copy-start(bf16[8192,128]{1,0:T(8,128)(2,1)} %param.13) | copy-start | bytes 6291460
  22.2 7.0 %copy-start.4 = (f32[80,64]{1,0:T(8,128)S(1)}, f32[80,64]{1,0:T(8,128)}, u32[]{:S(2)}) copy-start(f32[80,64]{1,0:T(8,128)} %get-tuple-element.49) | copy-start | bytes 61444
  22.2 7.0 %copy-start.5 = (f32[80,64]{1,0:T(8,128)S(1)}, f32[80,64]{1,0:T(8,128)}, u32[]{:S(2)}) copy-start(f32[80,64]{1,0:T(8,128)} %get-tuple-element.48) | copy-start | bytes 61444
  22.7 6.4 %collective-permute-start.2 = (f32[80,256]{1,0:T(8,128)S(1)}, f32[80,256]{1,0:T(8,128)S(1)}, u32[]{:S(2)}, u32[]{:S(2)}) collective-permute-start(f32[80,256]{1,0:T(8,128)S(1)} %pad_maximum_fusion.5), channel_id=1, source_target_pairs={{0,1},{1,0},{2,3},{3,2},{4,5},{5,4},{6,7},{7,6},{8,9},{9,8},{10,11... | collective-permute-start | bytes 245768 | tf_op jit(solution)/shard_map/ppermute | solution.py:305
  24.7 15.0 %collective-permute-start.4 = (bf16[8,8192]{1,0:T(8,128)(2,1)S(1)}, bf16[8,8192]{1,0:T(8,128)(2,1)S(1)}, u32[]{:S(2)}, u32[]{:S(2)}) collective-permute-start(bf16[8,8192]{1,0:T(8,128)(2,1)S(1)} %constant_dynamic-slice_fusion.3), channel_id=1, source_target_pairs={{0,1},{1,0},{2,3},{3,2},{4,5},{5,4},{6,7},{7,6},{8,9},{9,8},{10,11... | collective-permute-start | bytes 393224 | tf_op jit(solution)/shard_map/ppermute | solution.py:207
  30.1 14.5 %copy-start.6 = (f32[48,64]{1,0:T(8,128)S(1)}, f32[48,64]{1,0:T(8,128)}, u32[]{:S(2)}) copy-start(f32[48,64]{1,0:T(8,128)} %get-tuple-element.60) | copy-start | bytes 36868
  30.1 14.5 %copy-start.7 = (f32[48,64]{1,0:T(8,128)S(1)}, f32[48,64]{1,0:T(8,128)}, u32[]{:S(2)}) copy-start(f32[48,64]{1,0:T(8,128)} %get-tuple-element.59) | copy-start | bytes 36868
  30.2 12.2 %collective-permute-start.8 = (bf16[80,256]{1,0:T(8,128)(2,1)S(1)}, bf16[80,256]{1,0:T(8,128)(2,1)S(1)}, u32[]{:S(2)}, u32[]{:S(2)}) collective-permute-start(bf16[80,256]{1,0:T(8,128)(2,1)S(1)} %pad_maximum_fusion.8), channel_id=1, source_target_pairs={{0,24},{2,26},{4,28},{6,30},{1,25},{3,27},{5,29},{7,31}} | collective-permute-start | bytes 122888 | tf_op jit(solution)/shard_map/ppermute | solution.py:327
  35.9 6.5 %collective-permute-start.7 = (bf16[80,256]{1,0:T(8,128)(2,1)S(1)}, bf16[80,256]{1,0:T(8,128)(2,1)S(1)}, u32[]{:S(2)}, u32[]{:S(2)}) collective-permute-start(bf16[80,256]{1,0:T(8,128)(2,1)S(1)} %pad_maximum_fusion.8), channel_id=1, source_target_pairs={{0,16},{2,18},{4,20},{6,22},{8,24},{10,26},{12,28},{14,30},{1,17},... | collective-permute-start | bytes 122888 | tf_op jit(solution)/shard_map/ppermute | solution.py:327
  37.2 5.2 %collective-permute-start.6 = (bf16[80,256]{1,0:T(8,128)(2,1)S(1)}, bf16[80,256]{1,0:T(8,128)(2,1)S(1)}, u32[]{:S(2)}, u32[]{:S(2)}) collective-permute-start(bf16[80,256]{1,0:T(8,128)(2,1)S(1)} %pad_maximum_fusion.8), channel_id=1, source_target_pairs={{0,8},{2,10},{4,12},{6,14},{8,16},{10,18},{12,20},{14,22},{16,24},... | collective-permute-start | bytes 122888 | tf_op jit(solution)/shard_map/ppermute | solution.py:327
  40.5 4.2 %collective-permute-start.5 = (f32[48,256]{1,0:T(8,128)S(1)}, f32[48,256]{1,0:T(8,128)S(1)}, u32[]{:S(2)}, u32[]{:S(2)}) collective-permute-start(f32[48,256]{1,0:T(8,128)S(1)} %pad_maximum_fusion.7), channel_id=1, source_target_pairs={{0,1},{1,0},{2,3},{3,2},{4,5},{5,4},{6,7},{7,6},{8,9},{9,8},{10,11... | collective-permute-start | bytes 147464 | tf_op jit(solution)/shard_map/ppermute | solution.py:305
  42.4 7.8 %collective-permute-start.12 = (bf16[320,256]{1,0:T(8,128)(2,1)S(1)}, bf16[320,256]{1,0:T(8,128)(2,1)S(1)}, u32[]{:S(2)}, u32[]{:S(2)}) collective-permute-start(bf16[320,256]{1,0:T(8,128)(2,1)S(1)} %pad_maximum_fusion.3), channel_id=1, source_target_pairs={{0,4},{2,6},{4,0},{6,2},{8,12},{10,14},{12,8},{14,10},{16,20},{18,... | collective-permute-start | bytes 491528 | tf_op jit(solution)/shard_map/ppermute | solution.py:341
  44.8 5.9 %collective-permute-start.11 = (bf16[48,256]{1,0:T(8,128)(2,1)S(1)}, bf16[48,256]{1,0:T(8,128)(2,1)S(1)}, u32[]{:S(2)}, u32[]{:S(2)}) collective-permute-start(bf16[48,256]{1,0:T(8,128)(2,1)S(1)} %pad_maximum_fusion.10), channel_id=1, source_target_pairs={{0,24},{2,26},{4,28},{6,30},{1,25},{3,27},{5,29},{7,31}} | collective-permute-start | bytes 73736 | tf_op jit(solution)/shard_map/ppermute | solution.py:327
  46.5 4.2 %collective-permute-start.10 = (bf16[48,256]{1,0:T(8,128)(2,1)S(1)}, bf16[48,256]{1,0:T(8,128)(2,1)S(1)}, u32[]{:S(2)}, u32[]{:S(2)}) collective-permute-start(bf16[48,256]{1,0:T(8,128)(2,1)S(1)} %pad_maximum_fusion.10), channel_id=1, source_target_pairs={{0,16},{2,18},{4,20},{6,22},{8,24},{10,26},{12,28},{14,30},{1,17},... | collective-permute-start | bytes 73736 | tf_op jit(solution)/shard_map/ppermute | solution.py:327
  47.8 4.0 %collective-permute-start.9 = (bf16[48,256]{1,0:T(8,128)(2,1)S(1)}, bf16[48,256]{1,0:T(8,128)(2,1)S(1)}, u32[]{:S(2)}, u32[]{:S(2)}) collective-permute-start(bf16[48,256]{1,0:T(8,128)(2,1)S(1)} %pad_maximum_fusion.10), channel_id=1, source_target_pairs={{0,8},{2,10},{4,12},{6,14},{8,16},{10,18},{12,20},{14,22},{16,24},... | collective-permute-start | bytes 73736 | tf_op jit(solution)/shard_map/ppermute | solution.py:327
  50.3 2.0 %collective-permute-start.14 = (bf16[640,256]{1,0:T(8,128)(2,1)S(1)}, bf16[640,256]{1,0:T(8,128)(2,1)S(1)}, u32[]{:S(2)}, u32[]{:S(2)}) collective-permute-start(bf16[640,256]{1,0:T(8,128)(2,1)S(1)} %pad_maximum_fusion.refs_0_), channel_id=1, source_target_pairs={{0,2},{2,0},{4,6},{6,4},{8,10},{10,8},{12,14},{14,12},{16,18},{18,... | collective-permute-start | bytes 983048 | tf_op jit(solution)/shard_map/ppermute | solution.py:341
  51.8 4.6 %collective-permute-start.13 = (bf16[192,256]{1,0:T(8,128)(2,1)S(1)}, bf16[192,256]{1,0:T(8,128)(2,1)S(1)}, u32[]{:S(2)}, u32[]{:S(2)}) collective-permute-start(bf16[192,256]{1,0:T(8,128)(2,1)S(1)} %pad_maximum_fusion.4), channel_id=1, source_target_pairs={{0,4},{2,6},{4,0},{6,2},{8,12},{10,14},{12,8},{14,10},{16,20},{18,... | collective-permute-start | bytes 294920 | tf_op jit(solution)/shard_map/ppermute | solution.py:341
  56.4 4.1 %collective-permute-start.15 = (bf16[384,256]{1,0:T(8,128)(2,1)S(1)}, bf16[384,256]{1,0:T(8,128)(2,1)S(1)}, u32[]{:S(2)}, u32[]{:S(2)}) collective-permute-start(bf16[384,256]{1,0:T(8,128)(2,1)S(1)} %pad_maximum_fusion.2.refs_0_), channel_id=1, source_target_pairs={{0,2},{2,0},{4,6},{6,4},{8,10},{10,8},{12,14},{14,12},{16,18},{18,... | collective-permute-start | bytes 589832 | tf_op jit(solution)/shard_map/ppermute | solution.py:341

commit v9 on v8

--- a/solution.py
+++ b/solution.py
@@ -30,9 +30,8 @@
 
 
 def attention_kernel(
-    span_ref, place_ref, query_ref, *refs, groups, carry, final, rows, own, head_size, stride
+    span_ref, place_ref, query_ref, *refs, count, order, carry, final, rows, own, head_size, stride
 ):
-    count = len(groups)
     pieces, refs = refs[:count], refs[count:]
     if carry:
         old_peak, old_total, old_sum = refs[:3]
@@ -41,12 +40,11 @@
     first = span_ref[1]
     factor = head_size ** (-0.5) * math.log2(math.e)
     flat = query_ref.shape[0]
-    ordered = []
-    for half in range(2):
-        for piece, group in zip(pieces, groups):
-            for top in range(0, piece.shape[0], group):
-                begin = top + half * (group // 2)
-                ordered.append(piece[begin : begin + group // 2, :])
+    blocks = []
+    size = sum(piece.shape[0] for piece in pieces) // len(order)
+    for piece in pieces:
+        blocks.extend(piece[top : top + size, :] for top in range(0, piece.shape[0], size))
+    ordered = [blocks[index] for index in order]
     everything = jnp.concatenate(ordered, axis=0)
 
     def run(width):
@@ -98,14 +96,9 @@
                 total_ref[place, :] = total
                 sum_ref[place, :] = numerator
 
-        if flat // stride <= 4:
-            for part in range(flat // stride):
-                one(part)
-        else:
-
-            @pl.loop(0, flat // stride)
-            def each(part):
-                one(part)
+        @pl.loop(0, flat // stride)
+        def each(part):
+            one(part)
 
     upper = span_ref[2]
 
@@ -125,10 +118,10 @@
             ]
 
 
-def attend(span, place, query_flat, pieces, groups, own, state, final, rows):
+def attend(span, place, query_flat, pieces, order, own, state, final, rows):
     flat, head_size = query_flat.shape
     width = sum(piece.shape[0] for piece in pieces)
-    stride = math.gcd(flat, 1024 if width <= 2048 else rows)
+    stride = math.gcd(flat, 256 if width <= 2048 else rows)
     whole = pl.BlockSpec(memory_space=pltpu.VMEM)
     if final:
         shapes = jax.ShapeDtypeStruct((rows, flat // rows * head_size), jnp.bfloat16)
@@ -143,7 +136,8 @@
     return pl.pallas_call(
         partial(
             attention_kernel,
-            groups=groups,
+            count=len(pieces),
+            order=order,
             carry=state is not None,
             final=final,
             rows=rows,
@@ -172,10 +166,7 @@
     while bit >= 1:
         bits.append(bit)
         bit //= 2
-    core = bits[-1:]
-    rest = bits[:-1]
-    stages = [rest[i : i + 2] for i in range(0, len(rest), 2)] + ([core] if core else [])
-    return stages
+    return bits
 
 
 def after(value, *earlier):
@@ -260,10 +251,8 @@
             .astype(jnp.bfloat16)
             .reshape(heads * rows, head_size)
         )
-        top_unit = min(stages[0])
-        top_count = contexts // top_unit
-        level = context // top_unit
-        upper = (2 * level >= top_count).astype(jnp.int32)
+        top_bit = stages[0]
+        upper = ((context & top_bit) != 0).astype(jnp.int32)
         span = jnp.stack([start, first, upper]).astype(jnp.int32)
         for part in parts:
             part.tables = tables(start + places_of(part.top, part.rows), head_size)
@@ -315,52 +304,27 @@
                 jnp.concatenate([keys_rot, sums[:, head_size:].astype(jnp.bfloat16)], axis=1)
             )
             part.cache = lax.dynamic_slice_in_dim(block, shard * part.rows, part.rows, 0)
-            part.known, part.fresh, part.masks = block, [], [(0, 0)]
+            part.known, part.fresh, part.masks = block, [], [0]
 
         def advance(part, *gate):
             fresh = lax.optimization_barrier((part.known, part.fresh, *gate))
             part.known = after(jnp.concatenate([fresh[0]] + list(fresh[1]), axis=0))
             part.fresh = []
-            if part.stage == 0:
-                climbs = range(1, top_count)
-                part.fresh = [
-                    lax.ppermute(
-                        part.known,
-                        "ctx",
-                        [(i, i + top_unit * up) for i in range(contexts - top_unit * up)],
-                    )
-                    for up in climbs
-                ]
-                part.masks = [(0, up) for up in range(top_count)]
-                part.group = top_count * part.known.shape[0]
-            elif part.stage < len(stages):
-                moves = [0]
-                for bit in stages[part.stage]:
-                    moves = moves + [move ^ bit for move in moves]
-                part.fresh = [
-                    lax.ppermute(part.known, "ctx", [(i, i ^ move) for i in range(contexts)])
-                    for move in moves[1:]
-                ]
-                part.known_masks = part.masks
-                part.masks = [(mask ^ move, up) for move in moves for mask, up in part.masks]
+            if part.stage < len(stages):
+                bit = stages[part.stage]
+                pairs = [(i, i ^ bit) for i in range(contexts)]
+                part.fresh = [lax.ppermute(part.known, "ctx", pairs)]
+                part.masks = part.masks + [mask ^ bit for mask in part.masks]
             part.stage += 1
 
         def absorb(part, pieces, masks, own, state, last, *gate):
             local_pos = places_of(part.top, part.rows)
-            turns, climbs = [], []
-            for half in range(2):
-                for index, (mask, up) in enumerate(masks):
-                    if (2 * up >= top_count) == (half == 1):
-                        turns.append(mask)
-                        climbs.append(up)
-            climbs = jnp.array(climbs, jnp.int32)
-            sources = (context ^ jnp.array(turns, jnp.int32)) - climbs * top_unit
-            place = sources[:, None] * group_rows + local_pos[None, :]
-            place = jnp.where((climbs <= level)[:, None], place, contexts * group_rows)
+            order = sorted(range(len(masks)), key=lambda index: masks[index] & top_bit)
+            turns = jnp.array([masks[index] for index in order], jnp.int32)
+            place = (context ^ turns)[:, None] * group_rows + local_pos[None, :]
             query = after(query_flat, *gate)
-            groups = tuple(min(part.group, piece.shape[0]) for piece in pieces)
             return attend(
-                span, place.reshape(1, -1), query, pieces, groups, own, state, last, rows
+                span, place.reshape(1, -1), query, pieces, tuple(order), own, state, last, rows
             )
 
         exchange(early, own_product)
@@ -369,17 +333,15 @@
         combine(early, *flying[early.end])
         advance(early)
         exchange(late, early.known)
-        for stage in range(len(stages)):
-            if early.stage < len(stages):
-                advance(early, late.sums if stage == 0 else late.known)
-            if stage == 0:
-                combine(late, early.known)
-                advance(late)
-            elif stage < len(stages) - 1:
-                advance(late, early.known)
+        advance(early, late.sums)
+        combine(late, early.known)
+        advance(late)
+        for stage in range(2, len(stages)):
+            advance(early, late.known)
+            advance(late, early.known)
         state = absorb(
             early,
-            [early.known] + list(early.fresh),
+            [early.known] + early.fresh,
             early.masks,
             shards * early.rows,
             None,
@@ -387,11 +349,9 @@
             late.known,
         )
         advance(late, *state)
-        state = absorb(
-            late, [late.known], late.known_masks, shards * late.rows, state, False
+        attended = absorb(
+            late, [late.known] + late.fresh, late.masks, shards * late.rows, state, True
         )
-        fresh_masks = late.masks[len(late.known_masks) :]
-        attended = absorb(late, list(late.fresh), fresh_masks, 0, state, True)
         kv_cache = jnp.concatenate([part.cache for part in parts], axis=0)
         return (kv_cache, attended)
 

time: 65.3 us -> 57.3 us (0.88)
  starting transfers between devices: 26.2 us -> 20.2 us
  other arithmetic: 5.02 us -> 8.34 us
  Pallas kernels: 9.83 us -> 6.56 us
  waiting for transfers between devices: 11.3 us -> 9.35 us
  matrix products: 5.95 us -> 7.15 us
  local copies, waits for them, and re-layouts: 5.34 us -> 4.19 us
    ppermute x10 -> x8, starting transfers between devices: 17.1 us -> 11.1 us  [advance(): part.fresh = [lax.ppermute(part.known, 'ctx', pairs)]]
    pallas_call x3 -> x2, Pallas kernels: 9.83 us -> 6.56 us  [attend(): pl.pallas_call(partial(attention_kernel, count=len(pieces), order=order,...]
    ppermute x4, waiting for transfers between devices: 5.95 us -> 2.73 us  [send_rows(): lax.ppermute(columns, 'fsdp', [(i, (i + step) % shards) for i in range(sh...]
    unnamed x34 -> x12, local copies, waits for them, and re-layouts: 3.38 us -> 1.6 us
    ppermute x10 -> x8, waiting for transfers between devices: 2.96 us -> 4.31 us  [advance(): part.fresh = [lax.ppermute(part.known, 'ctx', pairs)]]
    le x2 -> x0, other arithmetic: 1.25 us -> none  [absorb(): place = jnp.where((climbs <= level)[:, None], place, contexts * group_rows)]
    dot_general x10, matrix products: 5.95 us -> 7.15 us  [project(): jnp.dot(columns, weight, preferred_element_type=jnp.float32)]
    transpose x1, other arithmetic: 0.04 us -> 0.99 us  [local(): queries.astype(jnp.float32).reshape(rows, heads, head_size)]
  transfers between devices with their start and end apart: 16 -> 14, of which waited for: 6 -> 10; matrix products, arithmetic and copies ran while one was open for 19% -> 31% of each run, Pallas kernels for 9% -> 5%
where the time goes in v9:
time: 57.3 us; the launch traced here: 56.7 us
  starting transfers between devices  20.2 us (35%)
  waiting for transfers between devices  9.35 us (16%)
  other arithmetic  8.34 us (15%)
  matrix products  7.15 us (12%)
  Pallas kernels  6.56 us (11%)
  local copies, waits for them, and re-layouts  4.19 us (7%)
  between operations  0.9 us (2%)
    ppermute x8, starting transfers between devices, advance(): part.fresh = [lax.ppermute(part.known, 'ctx', pairs)]  11.1 us
    dot_general x10, matrix products, project(): jnp.dot(columns, weight, preferred_element_type=jnp.float32)  7.15 us
    pallas_call x2, Pallas kernels, attend(): pl.pallas_call(partial(attention_kernel, count=len(pieces), order=order,...  6.56 us
    ppermute x4, starting transfers between devices, send_rows(): lax.ppermute(columns, 'fsdp', [(i, (i + step) % shards) for i in range(sh...  5.13 us
    ppermute x8, waiting for transfers between devices, advance(): part.fresh = [lax.ppermute(part.known, 'ctx', pairs)]  4.31 us
    ppermute x2, starting transfers between devices, exchange(): lax.ppermute(part.sums, 'fsdp', [(i, i ^ reach) for i in range(shards)])  3.93 us
    ppermute x4, waiting for transfers between devices, send_rows(): lax.ppermute(columns, 'fsdp', [(i, (i + step) % shards) for i in range(sh...  2.73 us
    ppermute x2, waiting for transfers between devices, exchange(): lax.ppermute(part.sums, 'fsdp', [(i, i ^ reach) for i in range(shards)])  2.31 us
  transfers between devices with their start and end apart: 14, of which 10 were waited for; matrix products, arithmetic and copies ran while one was open for 31% of the time, Pallas kernels for 5%

profile of v9, /device:TPU:0, one launch (start us, length us, event | category | flops | bytes accessed | tf_op | source)
XLA Modules:
  0.0 56.7 jit_solution(45528141745419400)
XLA Ops:
  0.7 1.6 %copy-done = bf16[64,16384]{1,0:T(8,128)(2,1)S(1)} copy-done((bf16[64,16384]{1,0:T(8,128)(2,1)S(1)}, bf16[64,16384]{1,0:T(8,128)(2,1)}, u32[]{:S(2)}) %copy-start) | copy-done | bytes 2097176
  2.2 0.7 %constant_dynamic-slice_fusion.2 = bf16[8,8192]{1,0:T(8,128)(2,1)} fusion(bf16[64,16384]{1,0:T(8,128)(2,1)S(1)} %copy-done, s32[]{:T(128)S(6)} %select_n.40), kind=kLoop, calls=%fused_computation.47 | loop fusion | bytes 262148 | tf_op jit(solution)/shard_map/dynamic_slice | solution.py:193
  2.9 2.9 %collective-permute-start = (bf16[8,8192]{1,0:T(8,128)(2,1)}, bf16[8,8192]{1,0:T(8,128)(2,1)S(1)}, u32[]{:S(2)}, u32[]{:S(2)}) collective-permute-start(bf16[8,8192]{1,0:T(8,128)(2,1)} %constant_dynamic-slice_fusion.2), channel_id=1, source_target_pairs={{0,1},{1,0},{2,3},{3,2},{4,5},{5,4},{6,7},{7,6},{8,9},{9,8},{10,11... | collective-permute-start | bytes 393224 | tf_op jit(solution)/shard_map/ppermute | solution.py:198
  5.8 0.8 %constant_dynamic-slice_fusion.5 = bf16[32,8192]{1,0:T(8,128)(2,1)} fusion(bf16[64,16384]{1,0:T(8,128)(2,1)S(1)} %copy-done, s32[]{:T(128)S(6)} %select_n.40), kind=kLoop, calls=%fused_computation.58 | loop fusion | bytes 1048580 | tf_op jit(solution)/shard_map/dynamic_slice | solution.py:193
  6.7 0.7 %constant_dynamic-slice_fusion.4 = bf16[16,8192]{1,0:T(8,128)(2,1)} fusion(bf16[64,16384]{1,0:T(8,128)(2,1)S(1)} %copy-done, s32[]{:T(128)S(6)} %select_n.40), kind=kLoop, calls=%fused_computation.57 | loop fusion | bytes 524292 | tf_op jit(solution)/shard_map/dynamic_slice | solution.py:193
  7.4 2.0 %collective-permute-start.3 = (bf16[16,8192]{1,0:T(8,128)(2,1)}, bf16[16,8192]{1,0:T(8,128)(2,1)S(1)}, u32[]{:S(2)}, u32[]{:S(2)}) collective-permute-start(bf16[16,8192]{1,0:T(8,128)(2,1)} %constant_dynamic-slice_fusion.4), channel_id=1, source_target_pairs={{0,1},{1,0},{2,3},{3,2},{4,5},{5,4},{6,7},{7,6},{8,9},{9,8},{10,11... | collective-permute-start | bytes 786440 | tf_op jit(solution)/shard_map/ppermute | solution.py:198
  9.4 0.5 broadcast_add_fusion.2
  10.0 2.9 %fusion.2 = f32[64,128]{1,0:T(8,128)} fusion(bf16[8192,128]{1,0:T(8,128)(2,1)} %param.8, bf16[64,16384]{1,0:T(8,128)(2,1)S(1)} %copy-done, s32[]{:T(128)S(6)} %select_n.41), kind=kOutput, calls=%fused_computation.2 | convolution fusion | flops 134217728 | bytes 3178500 | tf_op jit(solution)/shard_map/dot_general | solution.py:236
  12.8 1.1 %fusion = f32[64,128]{1,0:T(8,128)} fusion(bf16[8192,128]{1,0:T(8,128)(2,1)S(1)} %copy-done.2, bf16[64,16384]{1,0:T(8,128)(2,1)S(1)} %copy-done, s32[]{:T(128)S(6)} %select_n.41), kind=kOutput, calls=%fused_computation | convolution fusion | flops 134217728 | bytes 3178500 | tf_op jit(solution)/shard_map/dot_general | solution.py:236
  14.0 1.0 %bitcast_bitcast_fusion = f32[16,64,128]{2,1,0:T(8,128)S(1)} fusion(bf16[64,2048]{1,0:T(8,128)(2,1)} %param.7), kind=kLoop, calls=%fused_computation.4 | loop fusion | flops 131072 | bytes 786432 | tf_op jit(solution)/shard_map/transpose | solution.py:248
  15.1 0.8 %multiply_cosine_fusion.1 = (f32[64,64]{1,0:T(8,128)}, f32[64,64]{1,0:T(8,128)}) fusion(f32[64]{0:T(128)S(1)} %multiply_power_fusion, f32[64]{0:T(128)S(1)} %add_convert_fusion.3), kind=kLoop, calls=%fused_computation.21 | loop fusion | flops 4096 | bytes 33280 | tf_op jit(solution)/shard_map/cos | solution.py:29
  16.0 0.9 %multiply_sine_fusion = (f32[80,64]{1,0:T(8,128)}, f32[80,64]{1,0:T(8,128)}) fusion(f32[64]{0:T(128)S(1)} %multiply_power_fusion, f32[80]{0:T(128)S(1)} %add_convert_fusion.5), kind=kLoop, calls=%fused_computation.16 | loop fusion | flops 5120 | bytes 41536 | tf_op jit(solution)/shard_map/sin | solution.py:29
  16.8 0.7 %iota_add_fusion = s32[2,24]{1,0:T(2,128)S(1)} fusion(s32[2]{0:T(128)} %broadcast_add_fusion.2), kind=kLoop, calls=%fused_computation.41 | loop fusion | flops 48 | bytes 200 | tf_op jit(solution)/shard_map/add | solution.py:206
  17.6 0.2 multiply_sine_fusion.2
  17.8 0.9 %pad_maximum_fusion.7 = f32[64,256]{1,0:T(8,128)S(1)} fusion(f32[64,128]{1,0:T(8,128)} %fusion, f32[64,128]{1,0:T(8,128)} %fusion.2), kind=kLoop, calls=%fused_computation.15 | loop fusion | flops 16384 | bytes 131072 | tf_op jit(solution)/shard_map/concatenate | solution.py:234
  18.7 1.2 %subtract_convert_fusion = (bf16[16,64,64]{2,1,0:T(8,128)(2,1)S(1)}, bf16[16,64,64]{2,1,0:T(8,128)(2,1)S(1)}) fusion(f32[16,64,128]{2,1,0:T(8,128)S(1)} %bitcast_bitcast_fusion, f32[64,64]{1,0:T(8,128)} %get-tuple-element.83, f32[64,64]{1,0:T(8,128)} %get-tuple-element.82), kind=kLoop, calls=%fused_computation.7 | loop fusion | flops 524288 | bytes 819200 | tf_op jit(solution)/shard_map/convert.12
  19.8 0.1 pad_maximum_fusion.1.query_ref
  20.1 0.7 %xor_multiply_fusion = s32[16]{0:T(128)S(1)} fusion(s32[16]{0:T(128)} %constant.47.clone, s32[]{:T(128)S(6)} %axis_index.25), kind=kLoop, calls=%fused_computation.49 | loop fusion | flops 32 | bytes 132 | tf_op jit(solution)/shard_map/mul | solution.py:324
  20.7 0.4 fusion.6
  21.1 0.4 fusion.7
  21.5 0.2 collective-permute-done.1
  21.7 0.4 fusion.8
  22.2 0.4 fusion.9
  22.7 2.0 %collective-permute-start.2 = (f32[80,256]{1,0:T(8,128)S(1)}, f32[80,256]{1,0:T(8,128)S(1)}, u32[]{:S(2)}, u32[]{:S(2)}) collective-permute-start(f32[80,256]{1,0:T(8,128)S(1)} %pad_maximum_fusion.5), channel_id=1, source_target_pairs={{0,1},{1,0},{2,3},{3,2},{4,5},{5,4},{6,7},{7,6},{8,9},{9,8},{10,11... | collective-permute-start | bytes 245768 | tf_op jit(solution)/shard_map/ppermute | solution.py:294
  24.7 0.2 collective-permute-start.4
  24.9 2.5 %collective-permute-done.3 = bf16[16,8192]{1,0:T(8,128)(2,1)S(1)} collective-permute-done((bf16[16,8192]{1,0:T(8,128)(2,1)}, bf16[16,8192]{1,0:T(8,128)(2,1)S(1)}, u32[]{:S(2)}, u32[]{:S(2)}) %collective-permute-start.3) | collective-permute-done | bytes 262176 | tf_op jit(solution)/shard_map/ppermute | solution.py:198
  27.4 1.8 %collective-permute-done.2 = f32[80,256]{1,0:T(8,128)S(1)} collective-permute-done((f32[80,256]{1,0:T(8,128)S(1)}, f32[80,256]{1,0:T(8,128)S(1)}, u32[]{:S(2)}, u32[]{:S(2)}) %collective-permute-start.2) | collective-permute-done | bytes 81952 | tf_op jit(solution)/shard_map/ppermute | solution.py:294
  29.3 0.4 fusion.10
  29.7 0.4 fusion.11
  30.1 2.7 %collective-permute-start.6 = (bf16[80,256]{1,0:T(8,128)(2,1)S(1)}, bf16[80,256]{1,0:T(8,128)(2,1)S(1)}, u32[]{:S(2)}, u32[]{:S(2)}) collective-permute-start(bf16[80,256]{1,0:T(8,128)(2,1)S(1)} %pad_maximum_fusion.10), channel_id=1, source_target_pairs={{0,16},{2,18},{4,20},{6,22},{8,24},{10,26},{12,28},{14,30},{16,0},... | collective-permute-start | bytes 122888 | tf_op jit(solution)/shard_map/ppermute | solution.py:316
  32.8 0.4 fusion.12
  33.2 0.4 fusion.13
  33.6 1.9 %collective-permute-start.5 = (f32[48,256]{1,0:T(8,128)S(1)}, f32[48,256]{1,0:T(8,128)S(1)}, u32[]{:S(2)}, u32[]{:S(2)}) collective-permute-start(f32[48,256]{1,0:T(8,128)S(1)} %pad_maximum_fusion.8), channel_id=1, source_target_pairs={{0,1},{1,0},{2,3},{3,2},{4,5},{5,4},{6,7},{7,6},{8,9},{9,8},{10,11... | collective-permute-start | bytes 147464 | tf_op jit(solution)/shard_map/ppermute | solution.py:294
  35.6 1.6 %collective-permute-start.8 = (bf16[160,256]{1,0:T(8,128)(2,1)S(1)}, bf16[160,256]{1,0:T(8,128)(2,1)S(1)}, u32[]{:S(2)}, u32[]{:S(2)}) collective-permute-start(bf16[160,256]{1,0:T(8,128)(2,1)S(1)} %pad_maximum_fusion.6), channel_id=1, source_target_pairs={{0,8},{2,10},{4,12},{6,14},{8,0},{10,2},{12,4},{14,6},{16,24},{18,... | collective-permute-start | bytes 245768 | tf_op jit(solution)/shard_map/ppermute | solution.py:316
  37.2 0.6 collective-permute-done.5
  38.0 1.9 %collective-permute-start.7 = (bf16[48,256]{1,0:T(8,128)(2,1)S(1)}, bf16[48,256]{1,0:T(8,128)(2,1)S(1)}, u32[]{:S(2)}, u32[]{:S(2)}) collective-permute-start(bf16[48,256]{1,0:T(8,128)(2,1)S(1)} %pad_maximum_fusion.12), channel_id=1, source_target_pairs={{0,16},{2,18},{4,20},{6,22},{8,24},{10,26},{12,28},{14,30},{16,0},... | collective-permute-start | bytes 73736 | tf_op jit(solution)/shard_map/ppermute | solution.py:316
  39.9 0.2 collective-permute-done.8
  40.1 1.6 %collective-permute-start.10 = (bf16[320,256]{1,0:T(8,128)(2,1)S(1)}, bf16[320,256]{1,0:T(8,128)(2,1)S(1)}, u32[]{:S(2)}, u32[]{:S(2)}) collective-permute-start(bf16[320,256]{1,0:T(8,128)(2,1)S(1)} %pad_maximum_fusion.3), channel_id=1, source_target_pairs={{0,4},{2,6},{4,0},{6,2},{8,12},{10,14},{12,8},{14,10},{16,20},{18,... | collective-permute-start | bytes 491528 | tf_op jit(solution)/shard_map/ppermute | solution.py:316
  41.8 1.0 %collective-permute-done.7 = bf16[48,256]{1,0:T(8,128)(2,1)S(1)} collective-permute-done((bf16[48,256]{1,0:T(8,128)(2,1)S(1)}, bf16[48,256]{1,0:T(8,128)(2,1)S(1)}, u32[]{:S(2)}, u32[]{:S(2)}) %collective-permute-start.7) | collective-permute-done | bytes 24608 | tf_op jit(solution)/shard_map/ppermute | solution.py:316
  42.7 1.6 %collective-permute-start.9 = (bf16[96,256]{1,0:T(8,128)(2,1)S(1)}, bf16[96,256]{1,0:T(8,128)(2,1)S(1)}, u32[]{:S(2)}, u32[]{:S(2)}) collective-permute-start(bf16[96,256]{1,0:T(8,128)(2,1)S(1)} %pad_maximum_fusion.9), channel_id=1, source_target_pairs={{0,8},{2,10},{4,12},{6,14},{8,0},{10,2},{12,4},{14,6},{16,24},{18,... | collective-permute-start | bytes 147464 | tf_op jit(solution)/shard_map/ppermute | solution.py:316
  44.3 1.2 %collective-permute-done.10 = bf16[320,256]{1,0:T(8,128)(2,1)S(1)} collective-permute-done((bf16[320,256]{1,0:T(8,128)(2,1)S(1)}, bf16[320,256]{1,0:T(8,128)(2,1)S(1)}, u32[]{:S(2)}, u32[]{:S(2)}) %collective-permute-start.10) | collective-permute-done | bytes 163872 | tf_op jit(solution)/shard_map/ppermute | solution.py:316
  45.9 1.0 %collective-permute-done.9 = bf16[96,256]{1,0:T(8,128)(2,1)S(1)} collective-permute-done((bf16[96,256]{1,0:T(8,128)(2,1)S(1)}, bf16[96,256]{1,0:T(8,128)(2,1)S(1)}, u32[]{:S(2)}, u32[]{:S(2)}) %collective-permute-start.9) | collective-permute-done | bytes 49184 | tf_op jit(solution)/shard_map/ppermute | solution.py:316
  46.8 1.6 %collective-permute-start.11 = (bf16[192,256]{1,0:T(8,128)(2,1)S(1)}, bf16[192,256]{1,0:T(8,128)(2,1)S(1)}, u32[]{:S(2)}, u32[]{:S(2)}) collective-permute-start(bf16[192,256]{1,0:T(8,128)(2,1)S(1)} %pad_maximum_fusion.4), channel_id=1, source_target_pairs={{0,4},{2,6},{4,0},{6,2},{8,12},{10,14},{12,8},{14,10},{16,20},{18,... | collective-permute-start | bytes 294920 | tf_op jit(solution)/shard_map/ppermute | solution.py:316
  48.4 2.9 %attend_part.1 = (f32[1024,1]{1,0:T(8,128)S(1)}, f32[1024,1]{1,0:T(8,128)S(1)}, f32[1024,128]{1,0:T(8,128)S(1)}) custom-call(s32[3]{0:T(128)S(1)} %pad_add_fusion.span_ref, s32[1,1280]{1,0:T(1,128)S(1)} %add.238.place_ref, bf16[1024,128]{1,0:T(8,128)(2,1)S(1)} %pad_maximum_fusion.1.query_ref, bf16[640,256]{1,0:T(8,128)(2,1)S(1)} %pad_maximum_fusion.refs_0_, ...), custom_call_target="tpu_custom_call" | custom-call | flops 671088640 | bytes 1179648 | tf_op jit(solution)/shard_map/attend_part/pallas_call | solution.py:136
  51.4 0.1 collective-permute-done.11
  51.6 0.6 %pad_maximum_fusion.11 = bf16[64,256]{1,0:T(8,128)(2,1)} fusion(bf16[24,256]{1,0:T(8,128)(2,1)S(1)} %constant_dynamic-slice_fusion, bf16[40,256]{1,0:T(8,128)(2,1)S(1)} %constant_dynamic-slice_fusion.1), kind=kLoop, calls=%fused_computation.31 | loop fusion | flops 65536 | bytes 65536 | tf_op jit(solution)/shard_map/concatenate | solution.py:355
  52.3 0.8 %collective-permute-done.13.refs_1_ = bf16[384,256]{1,0:T(8,128)(2,1)S(1)} collective-permute-done((bf16[384,256]{1,0:T(8,128)(2,1)S(1)}, bf16[384,256]{1,0:T(8,128)(2,1)S(1)}, u32[]{:S(2)}, u32[]{:S(2)}) %collective-permute-start.13) | collective-permute-done | bytes 196640 | tf_op jit(solution)/shard_map/ppermute | solution.py:316
  53.0 3.6 %attend_last.1 = bf16[64,2048]{1,0:T(8,128)(2,1)} custom-call(s32[3]{0:T(128)S(1)} %pad_add_fusion.span_ref, s32[1,768]{1,0:T(1,128)S(1)} %add.234.place_ref, bf16[1024,128]{1,0:T(8,128)(2,1)S(1)} %pad_maximum_fusion.1.query_ref, bf16[384,256]{1,0:T(8,128)(2,1)S(1)} %pad_maximum_fusion.2.refs_0_, bf16[384,256]{1,0:T(8,128)(2,1)S(1)} %collective-permute-done.13.refs_1_, ...), custom_call_target="tpu_custom_call" | custom-call | flops 402653184 | bytes 917504 | tf_op jit(solution)/shard_map/attend_last/pallas_call | solution.py:136
  (52 shorter events, 1.3 us)
Async XLA Ops:
  0.6 1.6 %copy-start = (bf16[64,16384]{1,0:T(8,128)(2,1)S(1)}, bf16[64,16384]{1,0:T(8,128)(2,1)}, u32[]{:S(2)}) copy-start(bf16[64,16384]{1,0:T(8,128)(2,1)} %param.6) | copy-start | bytes 6291460
  2.9 17.8 %collective-permute-start = (bf16[8,8192]{1,0:T(8,128)(2,1)}, bf16[8,8192]{1,0:T(8,128)(2,1)S(1)}, u32[]{:S(2)}, u32[]{:S(2)}) collective-permute-start(bf16[8,8192]{1,0:T(8,128)(2,1)} %constant_dynamic-slice_fusion.2), channel_id=1, source_target_pairs={{0,1},{1,0},{2,3},{3,2},{4,5},{5,4},{6,7},{7,6},{8,9},{9,8},{10,11... | collective-permute-start | bytes 393224 | tf_op jit(solution)/shard_map/ppermute | solution.py:198
  6.7 15.1 %collective-permute-start.1 = (bf16[32,8192]{1,0:T(8,128)(2,1)}, bf16[32,8192]{1,0:T(8,128)(2,1)S(1)}, u32[]{:S(2)}, u32[]{:S(2)}) collective-permute-start(bf16[32,8192]{1,0:T(8,128)(2,1)} %constant_dynamic-slice_fusion.5), channel_id=1, source_target_pairs={{0,1},{1,0},{2,3},{3,2},{4,5},{5,4},{6,7},{7,6},{8,9},{9,8},{10,11... | collective-permute-start | bytes 1572872 | tf_op jit(solution)/shard_map/ppermute | solution.py:198
  7.4 20.0 %collective-permute-start.3 = (bf16[16,8192]{1,0:T(8,128)(2,1)}, bf16[16,8192]{1,0:T(8,128)(2,1)S(1)}, u32[]{:S(2)}, u32[]{:S(2)}) collective-permute-start(bf16[16,8192]{1,0:T(8,128)(2,1)} %constant_dynamic-slice_fusion.4), channel_id=1, source_target_pairs={{0,1},{1,0},{2,3},{3,2},{4,5},{5,4},{6,7},{7,6},{8,9},{9,8},{10,11... | collective-permute-start | bytes 786440 | tf_op jit(solution)/shard_map/ppermute | solution.py:198
  10.0 2.9 %copy-start.2 = (bf16[8192,128]{1,0:T(8,128)(2,1)S(1)}, bf16[8192,128]{1,0:T(8,128)(2,1)}, u32[]{:S(2)}) copy-start(bf16[8192,128]{1,0:T(8,128)(2,1)} %param.9) | copy-start | bytes 6291460
  17.6 3.1 %copy-start.1 = (bf16[8192,128]{1,0:T(8,128)(2,1)S(1)}, bf16[8192,128]{1,0:T(8,128)(2,1)}, u32[]{:S(2)}) copy-start(bf16[8192,128]{1,0:T(8,128)(2,1)} %param.8) | copy-start | bytes 6291460
  18.7 2.4 %copy-start.3 = (bf16[8192,128]{1,0:T(8,128)(2,1)S(1)}, bf16[8192,128]{1,0:T(8,128)(2,1)}, u32[]{:S(2)}) copy-start(bf16[8192,128]{1,0:T(8,128)(2,1)} %param.9) | copy-start | bytes 6291460
  22.2 7.0 %copy-start.4 = (f32[80,64]{1,0:T(8,128)S(1)}, f32[80,64]{1,0:T(8,128)}, u32[]{:S(2)}) copy-start(f32[80,64]{1,0:T(8,128)} %get-tuple-element.46) | copy-start | bytes 61444
  22.2 7.0 %copy-start.5 = (f32[80,64]{1,0:T(8,128)S(1)}, f32[80,64]{1,0:T(8,128)}, u32[]{:S(2)}) copy-start(f32[80,64]{1,0:T(8,128)} %get-tuple-element.45) | copy-start | bytes 61444
  22.7 6.4 %collective-permute-start.2 = (f32[80,256]{1,0:T(8,128)S(1)}, f32[80,256]{1,0:T(8,128)S(1)}, u32[]{:S(2)}, u32[]{:S(2)}) collective-permute-start(f32[80,256]{1,0:T(8,128)S(1)} %pad_maximum_fusion.5), channel_id=1, source_target_pairs={{0,1},{1,0},{2,3},{3,2},{4,5},{5,4},{6,7},{7,6},{8,9},{9,8},{10,11... | collective-permute-start | bytes 245768 | tf_op jit(solution)/shard_map/ppermute | solution.py:294
  24.7 8.1 %collective-permute-start.4 = (bf16[8,8192]{1,0:T(8,128)(2,1)S(1)}, bf16[8,8192]{1,0:T(8,128)(2,1)S(1)}, u32[]{:S(2)}, u32[]{:S(2)}) collective-permute-start(bf16[8,8192]{1,0:T(8,128)(2,1)S(1)} %constant_dynamic-slice_fusion.3), channel_id=1, source_target_pairs={{0,1},{1,0},{2,3},{3,2},{4,5},{5,4},{6,7},{7,6},{8,9},{9,8},{10,11... | collective-permute-start | bytes 393224 | tf_op jit(solution)/shard_map/ppermute | solution.py:198
  30.1 5.5 %collective-permute-start.6 = (bf16[80,256]{1,0:T(8,128)(2,1)S(1)}, bf16[80,256]{1,0:T(8,128)(2,1)S(1)}, u32[]{:S(2)}, u32[]{:S(2)}) collective-permute-start(bf16[80,256]{1,0:T(8,128)(2,1)S(1)} %pad_maximum_fusion.10), channel_id=1, source_target_pairs={{0,16},{2,18},{4,20},{6,22},{8,24},{10,26},{12,28},{14,30},{16,0},... | collective-permute-start | bytes 122888 | tf_op jit(solution)/shard_map/ppermute | solution.py:316
  33.6 4.2 %collective-permute-start.5 = (f32[48,256]{1,0:T(8,128)S(1)}, f32[48,256]{1,0:T(8,128)S(1)}, u32[]{:S(2)}, u32[]{:S(2)}) collective-permute-start(f32[48,256]{1,0:T(8,128)S(1)} %pad_maximum_fusion.8), channel_id=1, source_target_pairs={{0,1},{1,0},{2,3},{3,2},{4,5},{5,4},{6,7},{7,6},{8,9},{9,8},{10,11... | collective-permute-start | bytes 147464 | tf_op jit(solution)/shard_map/ppermute | solution.py:294
  35.6 4.5 %collective-permute-start.8 = (bf16[160,256]{1,0:T(8,128)(2,1)S(1)}, bf16[160,256]{1,0:T(8,128)(2,1)S(1)}, u32[]{:S(2)}, u32[]{:S(2)}) collective-permute-start(bf16[160,256]{1,0:T(8,128)(2,1)S(1)} %pad_maximum_fusion.6), channel_id=1, source_target_pairs={{0,8},{2,10},{4,12},{6,14},{8,0},{10,2},{12,4},{14,6},{16,24},{18,... | collective-permute-start | bytes 245768 | tf_op jit(solution)/shard_map/ppermute | solution.py:316
  38.0 4.7 %collective-permute-start.7 = (bf16[48,256]{1,0:T(8,128)(2,1)S(1)}, bf16[48,256]{1,0:T(8,128)(2,1)S(1)}, u32[]{:S(2)}, u32[]{:S(2)}) collective-permute-start(bf16[48,256]{1,0:T(8,128)(2,1)S(1)} %pad_maximum_fusion.12), channel_id=1, source_target_pairs={{0,16},{2,18},{4,20},{6,22},{8,24},{10,26},{12,28},{14,30},{16,0},... | collective-permute-start | bytes 73736 | tf_op jit(solution)/shard_map/ppermute | solution.py:316
  40.1 5.4 %collective-permute-start.10 = (bf16[320,256]{1,0:T(8,128)(2,1)S(1)}, bf16[320,256]{1,0:T(8,128)(2,1)S(1)}, u32[]{:S(2)}, u32[]{:S(2)}) collective-permute-start(bf16[320,256]{1,0:T(8,128)(2,1)S(1)} %pad_maximum_fusion.3), channel_id=1, source_target_pairs={{0,4},{2,6},{4,0},{6,2},{8,12},{10,14},{12,8},{14,10},{16,20},{18,... | collective-permute-start | bytes 491528 | tf_op jit(solution)/shard_map/ppermute | solution.py:316
  42.7 4.1 %collective-permute-start.9 = (bf16[96,256]{1,0:T(8,128)(2,1)S(1)}, bf16[96,256]{1,0:T(8,128)(2,1)S(1)}, u32[]{:S(2)}, u32[]{:S(2)}) collective-permute-start(bf16[96,256]{1,0:T(8,128)(2,1)S(1)} %pad_maximum_fusion.9), channel_id=1, source_target_pairs={{0,8},{2,10},{4,12},{6,14},{8,0},{10,2},{12,4},{14,6},{16,24},{18,... | collective-permute-start | bytes 147464 | tf_op jit(solution)/shard_map/ppermute | solution.py:316
  45.5 2.9 %collective-permute-start.12 = (bf16[640,256]{1,0:T(8,128)(2,1)S(1)}, bf16[640,256]{1,0:T(8,128)(2,1)S(1)}, u32[]{:S(2)}, u32[]{:S(2)}) collective-permute-start(bf16[640,256]{1,0:T(8,128)(2,1)S(1)} %pad_maximum_fusion.refs_0_), channel_id=1, source_target_pairs={{0,2},{2,0},{4,6},{6,4},{8,10},{10,8},{12,14},{14,12},{16,18},{18,... | collective-permute-start | bytes 983048 | tf_op jit(solution)/shard_map/ppermute | solution.py:316
  46.8 4.7 %collective-permute-start.11 = (bf16[192,256]{1,0:T(8,128)(2,1)S(1)}, bf16[192,256]{1,0:T(8,128)(2,1)S(1)}, u32[]{:S(2)}, u32[]{:S(2)}) collective-permute-start(bf16[192,256]{1,0:T(8,128)(2,1)S(1)} %pad_maximum_fusion.4), channel_id=1, source_target_pairs={{0,4},{2,6},{4,0},{6,2},{8,12},{10,14},{12,8},{14,10},{16,20},{18,... | collective-permute-start | bytes 294920 | tf_op jit(solution)/shard_map/ppermute | solution.py:316
  51.5 1.5 %collective-permute-start.13 = (bf16[384,256]{1,0:T(8,128)(2,1)S(1)}, bf16[384,256]{1,0:T(8,128)(2,1)S(1)}, u32[]{:S(2)}, u32[]{:S(2)}) collective-permute-start(bf16[384,256]{1,0:T(8,128)(2,1)S(1)} %pad_maximum_fusion.2.refs_0_), channel_id=1, source_target_pairs={{0,2},{2,0},{4,6},{6,4},{8,10},{10,8},{12,14},{14,12},{16,18},{18,... | collective-permute-start | bytes 589832 | tf_op jit(solution)/shard_map/ppermute | solution.py:316

commit v10 on v9

--- a/solution.py
+++ b/solution.py
@@ -30,7 +30,7 @@
 
 
 def attention_kernel(
-    span_ref, place_ref, query_ref, *refs, count, order, carry, final, rows, own, head_size, stride
+    span_ref, place_ref, query_ref, *refs, count, slots, carry, final, rows, own, head_size, stride
 ):
     pieces, refs = refs[:count], refs[count:]
     if carry:
@@ -40,11 +40,13 @@
     first = span_ref[1]
     factor = head_size ** (-0.5) * math.log2(math.e)
     flat = query_ref.shape[0]
-    blocks = []
-    size = sum(piece.shape[0] for piece in pieces) // len(order)
-    for piece in pieces:
-        blocks.extend(piece[top : top + size, :] for top in range(0, piece.shape[0], size))
-    ordered = [blocks[index] for index in order]
+    size = sum(piece.shape[0] for piece in pieces) // (2 * slots * count)
+    ordered = []
+    for half in range(2):
+        for index, piece in enumerate(pieces):
+            for slot in range(slots):
+                number = span_ref[3 + (index * 2 + half) * slots + slot]
+                ordered.append(piece[pl.ds(pl.multiple_of(number * size, size), size), :])
     everything = jnp.concatenate(ordered, axis=0)
 
     def run(width):
@@ -96,9 +98,14 @@
                 total_ref[place, :] = total
                 sum_ref[place, :] = numerator
 
-        @pl.loop(0, flat // stride)
-        def each(part):
-            one(part)
+        if flat // stride <= 8:
+            for part in range(flat // stride):
+                one(part)
+        else:
+
+            @pl.loop(0, flat // stride)
+            def each(part):
+                one(part)
 
     upper = span_ref[2]
 
@@ -118,7 +125,7 @@
             ]
 
 
-def attend(span, place, query_flat, pieces, order, own, state, final, rows):
+def attend(span, place, query_flat, pieces, slots, own, state, final, rows):
     flat, head_size = query_flat.shape
     width = sum(piece.shape[0] for piece in pieces)
     stride = math.gcd(flat, 256 if width <= 2048 else rows)
@@ -137,7 +144,7 @@
         partial(
             attention_kernel,
             count=len(pieces),
-            order=order,
+            slots=slots,
             carry=state is not None,
             final=final,
             rows=rows,
@@ -166,7 +173,16 @@
     while bit >= 1:
         bits.append(bit)
         bit //= 2
-    return bits
+    inner = bits[:-1]
+    turn = len(inner) // 2 if len(inner) > 3 else len(inner) - 1
+    paths = (inner + bits[-1:], inner[turn:] + inner[:turn] + bits[-1:])
+    masks = ([0], [0])
+    for first, second in zip(*paths):
+        masks = (
+            masks[0] + [mask ^ first for mask in masks[0 if first > 1 else 1]],
+            masks[1] + [mask ^ second for mask in masks[1 if second > 1 else 0]],
+        )
+    return paths, masks
 
 
 def after(value, *earlier):
@@ -182,7 +198,9 @@
         context = lax.axis_index("ctx")
         shard = lax.axis_index("fsdp")
         unit = rows // sum(sum(part) for part in plan)
-        stages = stages_of(contexts)
+        paths, all_masks = stages_of(contexts)
+        stages = paths[0]
+        core = context & 1
 
         def send_rows(chunk, *earlier):
             top, count = chunk
@@ -304,28 +322,41 @@
                 jnp.concatenate([keys_rot, sums[:, head_size:].astype(jnp.bfloat16)], axis=1)
             )
             part.cache = lax.dynamic_slice_in_dim(block, shard * part.rows, part.rows, 0)
-            part.known, part.fresh, part.masks = block, [], [0]
+            part.known, part.fresh = block, []
 
         def advance(part, *gate):
             fresh = lax.optimization_barrier((part.known, part.fresh, *gate))
             part.known = after(jnp.concatenate([fresh[0]] + list(fresh[1]), axis=0))
             part.fresh = []
             if part.stage < len(stages):
-                bit = stages[part.stage]
-                pairs = [(i, i ^ bit) for i in range(contexts)]
+                pairs = [(i, i ^ paths[i & 1][part.stage]) for i in range(contexts)]
                 part.fresh = [lax.ppermute(part.known, "ctx", pairs)]
-                part.masks = part.masks + [mask ^ bit for mask in part.masks]
             part.stage += 1
 
-        def absorb(part, pieces, masks, own, state, last, *gate):
+        slots = contexts // 4
+        choices = []
+        for masks in all_masks:
+            order = []
+            for index in range(2):
+                held = range(index * 2 * slots, (index + 1) * 2 * slots)
+                order.append(sorted(held, key=lambda slot: masks[slot] & top_bit))
+            numbers = [slot - index * 2 * slots for index in range(2) for slot in order[index]]
+            turns = [
+                masks[slot]
+                for half in range(2)
+                for index in range(2)
+                for slot in order[index][half * slots : (half + 1) * slots]
+            ]
+            choices.append((jnp.array(numbers, jnp.int32), jnp.array(turns, jnp.int32)))
+        numbers = jnp.where(core == 0, choices[0][0], choices[1][0])
+        sources = context ^ jnp.where(core == 0, choices[0][1], choices[1][1])
+        span = jnp.concatenate([span, numbers])
+
+        def absorb(part, pieces, own, state, last, *gate):
             local_pos = places_of(part.top, part.rows)
-            order = sorted(range(len(masks)), key=lambda index: masks[index] & top_bit)
-            turns = jnp.array([masks[index] for index in order], jnp.int32)
-            place = (context ^ turns)[:, None] * group_rows + local_pos[None, :]
+            place = sources[:, None] * group_rows + local_pos[None, :]
             query = after(query_flat, *gate)
-            return attend(
-                span, place.reshape(1, -1), query, pieces, tuple(order), own, state, last, rows
-            )
+            return attend(span, place.reshape(1, -1), query, pieces, slots, own, state, last, rows)
 
         exchange(early, own_product)
         for chunk in chunks[early.end + 1 :]:
@@ -342,7 +373,6 @@
         state = absorb(
             early,
             [early.known] + early.fresh,
-            early.masks,
             shards * early.rows,
             None,
             False,
@@ -350,7 +380,7 @@
         )
         advance(late, *state)
         attended = absorb(
-            late, [late.known] + late.fresh, late.masks, shards * late.rows, state, True
+            late, [late.known] + late.fresh, shards * late.rows, state, True
         )
         kv_cache = jnp.concatenate([part.cache for part in parts], axis=0)
         return (kv_cache, attended)

time: 57.3 us -> 65.9 us (1.15)
  other arithmetic: 8.34 us -> 13.9 us
  waiting for transfers between devices: 9.35 us -> 12.8 us
  starting transfers between devices: 20.2 us -> 17.3 us
  local copies, waits for them, and re-layouts: 4.19 us -> 6.14 us
  matrix products: 7.15 us -> 8.86 us
  Pallas kernels: 6.56 us -> 5.47 us
    ppermute x8, waiting for transfers between devices: 4.31 us -> 9.52 us  [advance(): part.fresh = [lax.ppermute(part.known, 'ctx', pairs)]]
    ppermute x2, starting transfers between devices: 3.93 us -> 1.08 us  [exchange(): lax.ppermute(part.sums, 'fsdp', [(i, i ^ reach) for i in range(shards)])]
    ppermute x4, waiting for transfers between devices: 2.73 us -> 0.01 us  [send_rows(): lax.ppermute(columns, 'fsdp', [(i, (i + step) % shards) for i in range(sh...]
    add x2, local copies, waits for them, and re-layouts: 0.17 us -> 2.1 us  [places_of(): turns[:, None] + jnp.arange(count, dtype=jnp.int32)[None, :]]
    ppermute x8, starting transfers between devices: 11.1 us -> 9.19 us  [advance(): part.fresh = [lax.ppermute(part.known, 'ctx', pairs)]]
    ppermute x4, starting transfers between devices: 5.13 us -> 7.03 us  [send_rows(): lax.ppermute(columns, 'fsdp', [(i, (i + step) % shards) for i in range(sh...]
    add x2, other arithmetic: 0.77 us -> 2.64 us  [places_of(): turns[:, None] + jnp.arange(count, dtype=jnp.int32)[None, :]]
    dot_general x10, matrix products: 7.15 us -> 8.86 us  [project(): jnp.dot(columns, weight, preferred_element_type=jnp.float32)]
  transfers between devices with their start and end apart: 14 -> 14, of which waited for: 10 -> 7; matrix products, arithmetic and copies ran while one was open for 31% -> 41% of each run, Pallas kernels for 5% -> 4%
where the time goes in v10:
time: 65.9 us; the launch traced here: 65.5 us
  starting transfers between devices  17.3 us (26%)
  other arithmetic  13.9 us (21%)
  waiting for transfers between devices  12.8 us (19%)
  matrix products  8.86 us (13%)
  local copies, waits for them, and re-layouts  6.14 us (9%)
  Pallas kernels  5.47 us (8%)
  between operations  1.01 us (2%)
    ppermute x8, waiting for transfers between devices, advance(): part.fresh = [lax.ppermute(part.known, 'ctx', pairs)]  9.52 us
    ppermute x8, starting transfers between devices, advance(): part.fresh = [lax.ppermute(part.known, 'ctx', pairs)]  9.19 us
    dot_general x10, matrix products, project(): jnp.dot(columns, weight, preferred_element_type=jnp.float32)  8.86 us
    ppermute x4, starting transfers between devices, send_rows(): lax.ppermute(columns, 'fsdp', [(i, (i + step) % shards) for i in range(sh...  7.03 us
    pallas_call x2, Pallas kernels, attend(): pl.pallas_call(partial(attention_kernel, count=len(pieces), slots=slots,...  5.47 us
    ppermute x2, waiting for transfers between devices, exchange(): lax.ppermute(part.sums, 'fsdp', [(i, i ^ reach) for i in range(shards)])  3.27 us
    add x2, other arithmetic, places_of(): turns[:, None] + jnp.arange(count, dtype=jnp.int32)[None, :]  2.64 us
    dynamic_slice x4, local copies, waits for them, and re-layouts, send_rows(): lax.dynamic_slice(source, (jnp.int32(top), target * depth), (count, depth))  2.21 us
  transfers between devices with their start and end apart: 14, of which 7 were waited for; matrix products, arithmetic and copies ran while one was open for 41% of the time, Pallas kernels for 4%

profile of v10, /device:TPU:0, one launch (start us, length us, event | category | flops | bytes accessed | tf_op | source)
XLA Modules:
  0.0 65.5 jit_solution(5358585006892747516)
XLA Ops:
  0.7 1.6 %copy-done = bf16[64,16384]{1,0:T(8,128)(2,1)S(1)} copy-done((bf16[64,16384]{1,0:T(8,128)(2,1)S(1)}, bf16[64,16384]{1,0:T(8,128)(2,1)}, u32[]{:S(2)}) %copy-start) | copy-done | bytes 2097176
  2.2 0.7 constant_dynamic-slice_fusion.2
  2.9 2.9 %collective-permute-start = (bf16[8,8192]{1,0:T(8,128)(2,1)}, bf16[8,8192]{1,0:T(8,128)(2,1)S(1)}, u32[]{:S(2)}, u32[]{:S(2)}) collective-permute-start(bf16[8,8192]{1,0:T(8,128)(2,1)} %constant_dynamic-slice_fusion.2), channel_id=1, source_target_pairs={{0,1},{1,0},{2,3},{3,2},{4,5},{5,4},{6,7},{7,6},{8,9},{9,8},{10,11... | collective-permute-start | bytes 393224 | tf_op jit(solution)/shard_map/ppermute | solution.py:216
  5.8 0.8 %constant_dynamic-slice_fusion.5 = bf16[32,8192]{1,0:T(8,128)(2,1)} fusion(bf16[64,16384]{1,0:T(8,128)(2,1)S(1)} %copy-done, s32[]{:T(128)S(6)} %select_n.52), kind=kLoop, calls=%fused_computation.62 | loop fusion | bytes 1048580 | tf_op jit(solution)/shard_map/dynamic_slice | solution.py:211
  6.6 0.7 %constant_dynamic-slice_fusion.4 = bf16[16,8192]{1,0:T(8,128)(2,1)} fusion(bf16[64,16384]{1,0:T(8,128)(2,1)S(1)} %copy-done, s32[]{:T(128)S(6)} %select_n.52), kind=kLoop, calls=%fused_computation.61 | loop fusion | bytes 524292 | tf_op jit(solution)/shard_map/dynamic_slice | solution.py:211
  7.4 2.0 %collective-permute-start.3 = (bf16[16,8192]{1,0:T(8,128)(2,1)}, bf16[16,8192]{1,0:T(8,128)(2,1)S(1)}, u32[]{:S(2)}, u32[]{:S(2)}) collective-permute-start(bf16[16,8192]{1,0:T(8,128)(2,1)} %constant_dynamic-slice_fusion.4), channel_id=1, source_target_pairs={{0,1},{1,0},{2,3},{3,2},{4,5},{5,4},{6,7},{7,6},{8,9},{9,8},{10,11... | collective-permute-start | bytes 786440 | tf_op jit(solution)/shard_map/ppermute | solution.py:216
  9.4 0.6 iota_multiply_fusion
  10.0 0.6 broadcast_add_fusion.2
  10.5 2.8 %fusion.2 = f32[64,128]{1,0:T(8,128)} fusion(bf16[8192,128]{1,0:T(8,128)(2,1)} %param.10, bf16[64,16384]{1,0:T(8,128)(2,1)S(1)} %copy-done, s32[]{:T(128)S(6)} %select_n.53), kind=kOutput, calls=%fused_computation.2 | convolution fusion | flops 134217728 | bytes 3178500 | tf_op jit(solution)/shard_map/dot_general | solution.py:254
  13.4 1.1 %fusion = f32[64,128]{1,0:T(8,128)} fusion(bf16[8192,128]{1,0:T(8,128)(2,1)S(1)} %copy-done.2, bf16[64,16384]{1,0:T(8,128)(2,1)S(1)} %copy-done, s32[]{:T(128)S(6)} %select_n.53), kind=kOutput, calls=%fused_computation | convolution fusion | flops 134217728 | bytes 3178500 | tf_op jit(solution)/shard_map/dot_general | solution.py:254
  14.5 1.0 %bitcast_bitcast_fusion = f32[16,64,128]{2,1,0:T(8,128)S(1)} fusion(bf16[64,2048]{1,0:T(8,128)(2,1)} %param.9), kind=kLoop, calls=%fused_computation.4 | loop fusion | flops 131072 | bytes 786432 | tf_op jit(solution)/shard_map/transpose | solution.py:266
  15.5 1.3 %iota_add_fusion.1 = s32[2,40]{1,0:T(2,128)} fusion(s32[2]{0:T(128)} %iota_multiply_fusion), kind=kLoop, calls=%fused_computation.42 | loop fusion | flops 80 | bytes 328 | tf_op jit(solution)/shard_map/add | solution.py:224
  16.8 1.3 %add.212 = s32[80]{0:T(128)} reshape(s32[2,40]{1,0:T(2,128)} %iota_add_fusion.1) | data formatting | bytes 640 | tf_op jit(solution)/shard_map/add | solution.py:224
  18.2 0.7 %add_convert_fusion.5 = f32[80]{0:T(128)S(1)} fusion(s32[80]{0:T(128)} %add.212, s32[]{:T(128)} %mul.149), kind=kLoop, calls=%fused_computation.58 | loop fusion | flops 160 | bytes 644 | tf_op jit(solution)/shard_map/convert_element_type | solution.py:28
  18.9 0.8 %multiply_cosine_fusion.1 = (f32[64,64]{1,0:T(8,128)}, f32[64,64]{1,0:T(8,128)}) fusion(f32[64]{0:T(128)S(1)} %multiply_power_fusion, f32[64]{0:T(128)S(1)} %add_convert_fusion.3), kind=kLoop, calls=%fused_computation.21 | loop fusion | flops 4096 | bytes 33280 | tf_op jit(solution)/shard_map/cos | solution.py:29
  19.7 0.9 %multiply_sine_fusion = (f32[80,64]{1,0:T(8,128)}, f32[80,64]{1,0:T(8,128)}) fusion(f32[64]{0:T(128)S(1)} %multiply_power_fusion, f32[80]{0:T(128)S(1)} %add_convert_fusion.5), kind=kLoop, calls=%fused_computation.16 | loop fusion | flops 5120 | bytes 41536 | tf_op jit(solution)/shard_map/sin | solution.py:29
  20.5 1.3 %iota_add_fusion = s32[2,24]{1,0:T(2,128)} fusion(s32[2]{0:T(128)} %broadcast_add_fusion.2), kind=kLoop, calls=%fused_computation.41 | loop fusion | flops 48 | bytes 200 | tf_op jit(solution)/shard_map/add | solution.py:224
  21.9 0.8 %add.219 = s32[48]{0:T(128)S(1)} reshape(s32[2,24]{1,0:T(2,128)} %iota_add_fusion) | data formatting | bytes 384 | tf_op jit(solution)/shard_map/add | solution.py:224
  22.6 0.8 %multiply_sine_fusion.2 = (f32[48,64]{1,0:T(8,128)}, f32[48,64]{1,0:T(8,128)}) fusion(f32[64]{0:T(128)S(1)} %multiply_power_fusion, f32[48]{0:T(128)S(1)} %add_convert_fusion.4), kind=kLoop, calls=%fused_computation.29 | loop fusion | flops 3072 | bytes 25024 | tf_op jit(solution)/shard_map/sin | solution.py:29
  23.4 1.4 %pad_maximum_fusion.7 = f32[64,256]{1,0:T(8,128)} fusion(f32[64,128]{1,0:T(8,128)} %fusion, f32[64,128]{1,0:T(8,128)} %fusion.2), kind=kLoop, calls=%fused_computation.15 | loop fusion | flops 16384 | bytes 131072 | tf_op jit(solution)/shard_map/concatenate | solution.py:252
  24.8 1.0 %subtract_convert_fusion = (bf16[16,64,64]{2,1,0:T(8,128)(2,1)S(1)}, bf16[16,64,64]{2,1,0:T(8,128)(2,1)S(1)}) fusion(f32[16,64,128]{2,1,0:T(8,128)S(1)} %bitcast_bitcast_fusion, f32[64,64]{1,0:T(8,128)} %get-tuple-element.83, f32[64,64]{1,0:T(8,128)} %get-tuple-element.82), kind=kLoop, calls=%fused_computation.7 | loop fusion | flops 524288 | bytes 819200 | tf_op jit(solution)/shard_map/convert.12
  26.0 0.6 pad_add_fusion
  26.6 0.9 %broadcast_add_fusion = s32[16,80]{1,0:T(8,128)S(1)} fusion(s32[80]{0:T(128)} %add.212, s32[16]{0:T(128)S(1)} %fusion.7), kind=kLoop, calls=%fused_computation.39 | loop fusion | flops 1280 | bytes 5504 | tf_op jit(solution)/shard_map/add | solution.py:357
  27.5 0.7 %broadcast_add_fusion.1 = s32[16,48]{1,0:T(8,128)S(1)} fusion(s32[48]{0:T(128)} %copy-done.11, s32[16]{0:T(128)S(1)} %fusion.7), kind=kLoop, calls=%fused_computation.40 | loop fusion | flops 768 | bytes 3328 | tf_op jit(solution)/shard_map/add | solution.py:357
  28.2 2.1 %fusion.8 = f32[8,128]{1,0:T(8,128)S(1)} fusion(bf16[8,8192]{1,0:T(8,128)(2,1)S(1)} %collective-permute-done, bf16[8192,128]{1,0:T(8,128)(2,1)} %param.10), kind=kOutput, calls=%fused_computation.63 | convolution fusion | flops 16777216 | bytes 2232320 | tf_op jit(solution)/shard_map/dot_general | solution.py:254
  30.3 0.4 fusion.9
  30.8 0.4 fusion.10
  31.2 0.4 fusion.11
  31.8 2.1 %collective-permute-start.4 = (bf16[8,8192]{1,0:T(8,128)(2,1)S(1)}, bf16[8,8192]{1,0:T(8,128)(2,1)S(1)}, u32[]{:S(2)}, u32[]{:S(2)}) collective-permute-start(bf16[8,8192]{1,0:T(8,128)(2,1)S(1)} %constant_dynamic-slice_fusion.3), channel_id=1, source_target_pairs={{0,1},{1,0},{2,3},{3,2},{4,5},{5,4},{6,7},{7,6},{8,9},{9,8},{10,11... | collective-permute-start | bytes 393224 | tf_op jit(solution)/shard_map/ppermute | solution.py:216
  33.9 2.6 %collective-permute-done.2 = f32[80,256]{1,0:T(8,128)S(1)} collective-permute-done((f32[80,256]{1,0:T(8,128)S(1)}, f32[80,256]{1,0:T(8,128)S(1)}, u32[]{:S(2)}, u32[]{:S(2)}) %collective-permute-start.2) | collective-permute-done | bytes 81952 | tf_op jit(solution)/shard_map/ppermute | solution.py:312
  36.8 0.4 fusion.12
  37.2 0.4 fusion.13
  37.6 2.7 %collective-permute-start.6 = (bf16[80,256]{1,0:T(8,128)(2,1)S(1)}, bf16[80,256]{1,0:T(8,128)(2,1)S(1)}, u32[]{:S(2)}, u32[]{:S(2)}) collective-permute-start(bf16[80,256]{1,0:T(8,128)(2,1)S(1)} %pad_maximum_fusion.10), channel_id=1, source_target_pairs={{0,16},{2,6},{4,20},{6,2},{8,24},{10,14},{12,28},{14,10},{16,0},{1... | collective-permute-start | bytes 122888 | tf_op jit(solution)/shard_map/ppermute | solution.py:333
  40.2 0.4 fusion.14
  40.6 0.4 fusion.15
  41.0 1.0 %collective-permute-start.5 = (f32[48,256]{1,0:T(8,128)S(1)}, f32[48,256]{1,0:T(8,128)S(1)}, u32[]{:S(2)}, u32[]{:S(2)}) collective-permute-start(f32[48,256]{1,0:T(8,128)S(1)} %pad_maximum_fusion.8), channel_id=1, source_target_pairs={{0,1},{1,0},{2,3},{3,2},{4,5},{5,4},{6,7},{7,6},{8,9},{9,8},{10,11... | collective-permute-start | bytes 147464 | tf_op jit(solution)/shard_map/ppermute | solution.py:312
  42.1 2.2 %collective-permute-done.6 = bf16[80,256]{1,0:T(8,128)(2,1)S(1)} collective-permute-done((bf16[80,256]{1,0:T(8,128)(2,1)S(1)}, bf16[80,256]{1,0:T(8,128)(2,1)S(1)}, u32[]{:S(2)}, u32[]{:S(2)}) %collective-permute-start.6) | collective-permute-done | bytes 40992 | tf_op jit(solution)/shard_map/ppermute | solution.py:333
  44.6 0.6 collective-permute-done.5
  45.4 2.8 %collective-permute-start.7 = (bf16[48,256]{1,0:T(8,128)(2,1)S(1)}, bf16[48,256]{1,0:T(8,128)(2,1)S(1)}, u32[]{:S(2)}, u32[]{:S(2)}) collective-permute-start(bf16[48,256]{1,0:T(8,128)(2,1)S(1)} %pad_maximum_fusion.12), channel_id=1, source_target_pairs={{0,16},{2,6},{4,20},{6,2},{8,24},{10,14},{12,28},{14,10},{16,0},{1... | collective-permute-start | bytes 73736 | tf_op jit(solution)/shard_map/ppermute | solution.py:333
  48.2 2.1 %collective-permute-done.8 = bf16[160,256]{1,0:T(8,128)(2,1)S(1)} collective-permute-done((bf16[160,256]{1,0:T(8,128)(2,1)S(1)}, bf16[160,256]{1,0:T(8,128)(2,1)S(1)}, u32[]{:S(2)}, u32[]{:S(2)}) %collective-permute-start.8) | collective-permute-done | bytes 81952 | tf_op jit(solution)/shard_map/ppermute | solution.py:333
  50.3 1.6 %collective-permute-start.10 = (bf16[320,256]{1,0:T(8,128)(2,1)S(1)}, bf16[320,256]{1,0:T(8,128)(2,1)S(1)}, u32[]{:S(2)}, u32[]{:S(2)}) collective-permute-start(bf16[320,256]{1,0:T(8,128)(2,1)S(1)} %pad_maximum_fusion.3), channel_id=1, source_target_pairs={{0,4},{2,10},{4,0},{6,14},{8,12},{10,2},{12,8},{14,6},{16,20},{18,... | collective-permute-start | bytes 491528 | tf_op jit(solution)/shard_map/ppermute | solution.py:333
  52.1 3.6 %collective-permute-done.10 = bf16[320,256]{1,0:T(8,128)(2,1)S(1)} collective-permute-done((bf16[320,256]{1,0:T(8,128)(2,1)S(1)}, bf16[320,256]{1,0:T(8,128)(2,1)S(1)}, u32[]{:S(2)}, u32[]{:S(2)}) %collective-permute-start.10) | collective-permute-done | bytes 163872 | tf_op jit(solution)/shard_map/ppermute | solution.py:333
  56.1 1.6 %collective-permute-start.11 = (bf16[192,256]{1,0:T(8,128)(2,1)S(1)}, bf16[192,256]{1,0:T(8,128)(2,1)S(1)}, u32[]{:S(2)}, u32[]{:S(2)}) collective-permute-start(bf16[192,256]{1,0:T(8,128)(2,1)S(1)} %pad_maximum_fusion.4), channel_id=1, source_target_pairs={{0,4},{2,10},{4,0},{6,14},{8,12},{10,2},{12,8},{14,6},{16,20},{18,... | collective-permute-start | bytes 294920 | tf_op jit(solution)/shard_map/ppermute | solution.py:333
  57.7 2.3 %attend_part.1 = (f32[1024,1]{1,0:T(8,128)S(1)}, f32[1024,1]{1,0:T(8,128)S(1)}, f32[1024,128]{1,0:T(8,128)S(1)}) custom-call(s32[19]{0:T(128)S(1)} %pad_add_fusion.1.span_ref, s32[1,1280]{1,0:T(1,128)S(1)} %add.238.place_ref, bf16[1024,128]{1,0:T(8,128)(2,1)S(1)} %pad_maximum_fusion.1.query_ref, bf16[640,256]{1,0:T(8,128)(2,1)S(1)} %pad_maximum_fusion.refs_0_, ...), custom_call_target="tpu_custom_call" | custom-call | flops 671088640 | bytes 1179648 | tf_op jit(solution)/shard_map/attend_part/pallas_call | solution.py:143
  60.0 0.8 %collective-permute-done.11 = bf16[192,256]{1,0:T(8,128)(2,1)S(1)} collective-permute-done((bf16[192,256]{1,0:T(8,128)(2,1)S(1)}, bf16[192,256]{1,0:T(8,128)(2,1)S(1)}, u32[]{:S(2)}, u32[]{:S(2)}) %collective-permute-start.11) | collective-permute-done | bytes 98336 | tf_op jit(solution)/shard_map/ppermute | solution.py:333
  60.9 0.6 pad_maximum_fusion.11
  61.5 0.8 %collective-permute-done.13.refs_1_ = bf16[384,256]{1,0:T(8,128)(2,1)S(1)} collective-permute-done((bf16[384,256]{1,0:T(8,128)(2,1)S(1)}, bf16[384,256]{1,0:T(8,128)(2,1)S(1)}, u32[]{:S(2)}, u32[]{:S(2)}) %collective-permute-start.13) | collective-permute-done | bytes 196640 | tf_op jit(solution)/shard_map/ppermute | solution.py:333
  62.3 3.2 %attend_last.1 = bf16[64,2048]{1,0:T(8,128)(2,1)} custom-call(s32[19]{0:T(128)S(1)} %pad_add_fusion.1.span_ref, s32[1,768]{1,0:T(1,128)S(1)} %add.234.place_ref, bf16[1024,128]{1,0:T(8,128)(2,1)S(1)} %pad_maximum_fusion.1.query_ref, bf16[384,256]{1,0:T(8,128)(2,1)S(1)} %pad_maximum_fusion.2.refs_0_, bf16[384,256]{1,0:T(8,128)(2,1)S(1)} %collective-permute-done.13.refs_1_, ...), custom_call_target="tpu_custom_call" | custom-call | flops 402653184 | bytes 917504 | tf_op jit(solution)/shard_map/attend_last/pallas_call | solution.py:143
  (72 shorter events, 1.7 us)
Async XLA Ops:
  0.6 1.6 %copy-start = (bf16[64,16384]{1,0:T(8,128)(2,1)S(1)}, bf16[64,16384]{1,0:T(8,128)(2,1)}, u32[]{:S(2)}) copy-start(bf16[64,16384]{1,0:T(8,128)(2,1)} %param.8) | copy-start | bytes 6291460
  2.9 25.3 %collective-permute-start = (bf16[8,8192]{1,0:T(8,128)(2,1)}, bf16[8,8192]{1,0:T(8,128)(2,1)S(1)}, u32[]{:S(2)}, u32[]{:S(2)}) collective-permute-start(bf16[8,8192]{1,0:T(8,128)(2,1)} %constant_dynamic-slice_fusion.2), channel_id=1, source_target_pairs={{0,1},{1,0},{2,3},{3,2},{4,5},{5,4},{6,7},{7,6},{8,9},{9,8},{10,11... | collective-permute-start | bytes 393224 | tf_op jit(solution)/shard_map/ppermute | solution.py:216
  6.6 24.1 %collective-permute-start.1 = (bf16[32,8192]{1,0:T(8,128)(2,1)}, bf16[32,8192]{1,0:T(8,128)(2,1)S(1)}, u32[]{:S(2)}, u32[]{:S(2)}) collective-permute-start(bf16[32,8192]{1,0:T(8,128)(2,1)} %constant_dynamic-slice_fusion.5), channel_id=1, source_target_pairs={{0,1},{1,0},{2,3},{3,2},{4,5},{5,4},{6,7},{7,6},{8,9},{9,8},{10,11... | collective-permute-start | bytes 1572872 | tf_op jit(solution)/shard_map/ppermute | solution.py:216
  7.4 26.5 %collective-permute-start.3 = (bf16[16,8192]{1,0:T(8,128)(2,1)}, bf16[16,8192]{1,0:T(8,128)(2,1)S(1)}, u32[]{:S(2)}, u32[]{:S(2)}) collective-permute-start(bf16[16,8192]{1,0:T(8,128)(2,1)} %constant_dynamic-slice_fusion.4), channel_id=1, source_target_pairs={{0,1},{1,0},{2,3},{3,2},{4,5},{5,4},{6,7},{7,6},{8,9},{9,8},{10,11... | collective-permute-start | bytes 786440 | tf_op jit(solution)/shard_map/ppermute | solution.py:216
  10.5 2.8 %copy-start.2 = (bf16[8192,128]{1,0:T(8,128)(2,1)S(1)}, bf16[8192,128]{1,0:T(8,128)(2,1)}, u32[]{:S(2)}) copy-start(bf16[8192,128]{1,0:T(8,128)(2,1)} %param.11) | copy-start | bytes 6291460
  14.5 12.1 %copy-start.9 = (s32[16]{0:T(128)S(1)}, s32[16]{0:T(128)}, u32[]{:S(2)}) copy-start(s32[16]{0:T(128)} %constant.54.clone) | copy-start | bytes 196
  14.5 12.1 %copy-start.10 = (s32[16]{0:T(128)S(1)}, s32[16]{0:T(128)}, u32[]{:S(2)}) copy-start(s32[16]{0:T(128)} %constant.56.clone) | copy-start | bytes 196
  22.6 4.0 %copy-start.11 = (s32[48]{0:T(128)}, s32[48]{0:T(128)S(1)}, u32[]{:S(2)}) copy-start(s32[48]{0:T(128)S(1)} %add.219) | copy-start | bytes 580
  26.6 3.7 %copy-start.3 = (bf16[8192,128]{1,0:T(8,128)(2,1)S(1)}, bf16[8192,128]{1,0:T(8,128)(2,1)}, u32[]{:S(2)}) copy-start(bf16[8192,128]{1,0:T(8,128)(2,1)} %param.11) | copy-start | bytes 6291460
  28.2 2.5 %copy-start.1 = (bf16[8192,128]{1,0:T(8,128)(2,1)S(1)}, bf16[8192,128]{1,0:T(8,128)(2,1)}, u32[]{:S(2)}) copy-start(bf16[8192,128]{1,0:T(8,128)(2,1)} %param.10) | copy-start | bytes 6291460
  30.7 0.9 %copy-start.4 = (f32[64,256]{1,0:T(8,128)S(1)}, f32[64,256]{1,0:T(8,128)}, u32[]{:S(2)}) copy-start(f32[64,256]{1,0:T(8,128)} %pad_maximum_fusion.7) | copy-start | bytes 196612
  31.2 5.4 %copy-start.5 = (f32[80,64]{1,0:T(8,128)S(1)}, f32[80,64]{1,0:T(8,128)}, u32[]{:S(2)}) copy-start(f32[80,64]{1,0:T(8,128)} %get-tuple-element.46) | copy-start | bytes 61444
  31.2 5.4 %copy-start.6 = (f32[80,64]{1,0:T(8,128)S(1)}, f32[80,64]{1,0:T(8,128)}, u32[]{:S(2)}) copy-start(f32[80,64]{1,0:T(8,128)} %get-tuple-element.45) | copy-start | bytes 61444
  31.7 4.8 %collective-permute-start.2 = (f32[80,256]{1,0:T(8,128)S(1)}, f32[80,256]{1,0:T(8,128)S(1)}, u32[]{:S(2)}, u32[]{:S(2)}) collective-permute-start(f32[80,256]{1,0:T(8,128)S(1)} %pad_maximum_fusion.5), channel_id=1, source_target_pairs={{0,1},{1,0},{2,3},{3,2},{4,5},{5,4},{6,7},{7,6},{8,9},{9,8},{10,11... | collective-permute-start | bytes 245768 | tf_op jit(solution)/shard_map/ppermute | solution.py:312
  31.8 8.4 %collective-permute-start.4 = (bf16[8,8192]{1,0:T(8,128)(2,1)S(1)}, bf16[8,8192]{1,0:T(8,128)(2,1)S(1)}, u32[]{:S(2)}, u32[]{:S(2)}) collective-permute-start(bf16[8,8192]{1,0:T(8,128)(2,1)S(1)} %constant_dynamic-slice_fusion.3), channel_id=1, source_target_pairs={{0,1},{1,0},{2,3},{3,2},{4,5},{5,4},{6,7},{7,6},{8,9},{9,8},{10,11... | collective-permute-start | bytes 393224 | tf_op jit(solution)/shard_map/ppermute | solution.py:216
  37.6 7.7 %copy-start.7 = (f32[48,64]{1,0:T(8,128)S(1)}, f32[48,64]{1,0:T(8,128)}, u32[]{:S(2)}) copy-start(f32[48,64]{1,0:T(8,128)} %get-tuple-element.55) | copy-start | bytes 36868
  37.6 7.7 %copy-start.8 = (f32[48,64]{1,0:T(8,128)S(1)}, f32[48,64]{1,0:T(8,128)}, u32[]{:S(2)}) copy-start(f32[48,64]{1,0:T(8,128)} %get-tuple-element.54) | copy-start | bytes 36868
  37.6 6.6 %collective-permute-start.6 = (bf16[80,256]{1,0:T(8,128)(2,1)S(1)}, bf16[80,256]{1,0:T(8,128)(2,1)S(1)}, u32[]{:S(2)}, u32[]{:S(2)}) collective-permute-start(bf16[80,256]{1,0:T(8,128)(2,1)S(1)} %pad_maximum_fusion.10), channel_id=1, source_target_pairs={{0,16},{2,6},{4,20},{6,2},{8,24},{10,14},{12,28},{14,10},{16,0},{1... | collective-permute-start | bytes 122888 | tf_op jit(solution)/shard_map/ppermute | solution.py:333
  40.6 11.3 %copy-start.12 = (s32[16]{0:T(128)S(1)}, s32[16]{0:T(128)}, u32[]{:S(2)}) copy-start(s32[16]{0:T(128)} %constant.53.clone) | copy-start | bytes 196
  40.6 11.3 %copy-start.13 = (s32[16]{0:T(128)S(1)}, s32[16]{0:T(128)}, u32[]{:S(2)}) copy-start(s32[16]{0:T(128)} %constant.55.clone) | copy-start | bytes 196
  40.6 15.2 %copy-start.14 = (s32[3]{0:T(128)S(1)}, s32[3]{0:T(128)}, u32[]{:S(2)}) copy-start(s32[3]{0:T(128)} %pad_add_fusion) | copy-start | bytes 40
  41.0 4.2 %collective-permute-start.5 = (f32[48,256]{1,0:T(8,128)S(1)}, f32[48,256]{1,0:T(8,128)S(1)}, u32[]{:S(2)}, u32[]{:S(2)}) collective-permute-start(f32[48,256]{1,0:T(8,128)S(1)} %pad_maximum_fusion.8), channel_id=1, source_target_pairs={{0,1},{1,0},{2,3},{3,2},{4,5},{5,4},{6,7},{7,6},{8,9},{9,8},{10,11... | collective-permute-start | bytes 147464 | tf_op jit(solution)/shard_map/ppermute | solution.py:312
  44.2 6.1 %collective-permute-start.8 = (bf16[160,256]{1,0:T(8,128)(2,1)S(1)}, bf16[160,256]{1,0:T(8,128)(2,1)S(1)}, u32[]{:S(2)}, u32[]{:S(2)}) collective-permute-start(bf16[160,256]{1,0:T(8,128)(2,1)S(1)} %pad_maximum_fusion.6), channel_id=1, source_target_pairs={{0,8},{2,18},{4,12},{6,22},{8,0},{10,26},{12,4},{14,30},{16,24},{1... | collective-permute-start | bytes 245768 | tf_op jit(solution)/shard_map/ppermute | solution.py:333
  45.4 6.5 %collective-permute-start.7 = (bf16[48,256]{1,0:T(8,128)(2,1)S(1)}, bf16[48,256]{1,0:T(8,128)(2,1)S(1)}, u32[]{:S(2)}, u32[]{:S(2)}) collective-permute-start(bf16[48,256]{1,0:T(8,128)(2,1)S(1)} %pad_maximum_fusion.12), channel_id=1, source_target_pairs={{0,16},{2,6},{4,20},{6,2},{8,24},{10,14},{12,28},{14,10},{16,0},{1... | collective-permute-start | bytes 73736 | tf_op jit(solution)/shard_map/ppermute | solution.py:333
  50.3 5.4 %collective-permute-start.10 = (bf16[320,256]{1,0:T(8,128)(2,1)S(1)}, bf16[320,256]{1,0:T(8,128)(2,1)S(1)}, u32[]{:S(2)}, u32[]{:S(2)}) collective-permute-start(bf16[320,256]{1,0:T(8,128)(2,1)S(1)} %pad_maximum_fusion.3), channel_id=1, source_target_pairs={{0,4},{2,10},{4,0},{6,14},{8,12},{10,2},{12,8},{14,6},{16,20},{18,... | collective-permute-start | bytes 491528 | tf_op jit(solution)/shard_map/ppermute | solution.py:333
  51.9 4.2 %collective-permute-start.9 = (bf16[96,256]{1,0:T(8,128)(2,1)S(1)}, bf16[96,256]{1,0:T(8,128)(2,1)S(1)}, u32[]{:S(2)}, u32[]{:S(2)}) collective-permute-start(bf16[96,256]{1,0:T(8,128)(2,1)S(1)} %pad_maximum_fusion.9), channel_id=1, source_target_pairs={{0,8},{2,18},{4,12},{6,22},{8,0},{10,26},{12,4},{14,30},{16,24},{1... | collective-permute-start | bytes 147464 | tf_op jit(solution)/shard_map/ppermute | solution.py:333
  55.7 1.9 %collective-permute-start.12 = (bf16[640,256]{1,0:T(8,128)(2,1)S(1)}, bf16[640,256]{1,0:T(8,128)(2,1)S(1)}, u32[]{:S(2)}, u32[]{:S(2)}) collective-permute-start(bf16[640,256]{1,0:T(8,128)(2,1)S(1)} %pad_maximum_fusion.refs_0_), channel_id=1, source_target_pairs={{0,2},{2,0},{4,6},{6,4},{8,10},{10,8},{12,14},{14,12},{16,18},{18,... | collective-permute-start | bytes 983048 | tf_op jit(solution)/shard_map/ppermute | solution.py:333
  56.1 4.7 %collective-permute-start.11 = (bf16[192,256]{1,0:T(8,128)(2,1)S(1)}, bf16[192,256]{1,0:T(8,128)(2,1)S(1)}, u32[]{:S(2)}, u32[]{:S(2)}) collective-permute-start(bf16[192,256]{1,0:T(8,128)(2,1)S(1)} %pad_maximum_fusion.4), channel_id=1, source_target_pairs={{0,4},{2,10},{4,0},{6,14},{8,12},{10,2},{12,8},{14,6},{16,20},{18,... | collective-permute-start | bytes 294920 | tf_op jit(solution)/shard_map/ppermute | solution.py:333
  60.8 1.5 %collective-permute-start.13 = (bf16[384,256]{1,0:T(8,128)(2,1)S(1)}, bf16[384,256]{1,0:T(8,128)(2,1)S(1)}, u32[]{:S(2)}, u32[]{:S(2)}) collective-permute-start(bf16[384,256]{1,0:T(8,128)(2,1)S(1)} %pad_maximum_fusion.2.refs_0_), channel_id=1, source_target_pairs={{0,2},{2,0},{4,6},{6,4},{8,10},{10,8},{12,14},{14,12},{16,18},{18,... | collective-permute-start | bytes 589832 | tf_op jit(solution)/shard_map/ppermute | solution.py:333

commit v11 on v9

--- a/solution.py
+++ b/solution.py
@@ -96,9 +96,14 @@
                 total_ref[place, :] = total
                 sum_ref[place, :] = numerator
 
-        @pl.loop(0, flat // stride)
-        def each(part):
-            one(part)
+        if flat // stride <= 8:
+            for part in range(flat // stride):
+                one(part)
+        else:
+
+            @pl.loop(0, flat // stride)
+            def each(part):
+                one(part)
 
     upper = span_ref[2]
 
@@ -184,22 +189,27 @@
         unit = rows // sum(sum(part) for part in plan)
         stages = stages_of(contexts)
 
-        def send_rows(chunk, *earlier):
+        def cut(chunk, *earlier):
             top, count = chunk
             source = after(tokens, *earlier) if earlier else tokens
-            arrived, sent = [], []
-            for step in range(1, shards):
-                target = lax.rem(shard + step, shards)
-                columns = lax.dynamic_slice(
-                    source, (jnp.int32(top), target * depth), (count, depth)
-                )
-                sent.append(columns)
-                arrived.append(
-                    lax.ppermute(
-                        columns, "fsdp", [(i, (i + step) % shards) for i in range(shards)]
-                    )
-                )
-            return arrived, sent
+            return [
+                lax.dynamic_slice(
+                    source,
+                    (jnp.int32(top), lax.rem(shard + step, shards) * depth),
+                    (count, depth),
+                )
+                for step in range(1, shards)
+            ]
+
+        def send(columns, *earlier):
+            return [
+                lax.ppermute(
+                    after(columns[step - 1], *earlier) if earlier else columns[step - 1],
+                    "fsdp",
+                    [(i, (i + step) % shards) for i in range(shards)],
+                )
+                for step in range(1, shards)
+            ]
 
         def places_of(top, count):
             turns = jnp.arange(shards, dtype=jnp.int32) * rows + top
@@ -227,8 +237,12 @@
         flying = []
         sent = ()
         for chunk in chunks[: early.end + 1]:
-            arrived, sent = send_rows(chunk, *sent)
-            flying.append(arrived)
+            sent = cut(chunk, *sent)
+            flying.append(send(sent))
+        kept = []
+        for chunk in chunks[early.end + 1 :]:
+            sent = cut(chunk, *sent)
+            kept.append(sent)
 
         def project(columns):
             return jnp.concatenate(
@@ -244,20 +258,9 @@
 
         start = context * group_rows
         first = start + shard * rows
-        own_cosine, own_sine = tables(first + jnp.arange(rows, dtype=jnp.int32), head_size)
-        by_head = queries.astype(jnp.float32).reshape(rows, heads, head_size).transpose(1, 0, 2)
-        query_flat = (
-            rotate(by_head, own_cosine[None], own_sine[None])
-            .astype(jnp.bfloat16)
-            .reshape(heads * rows, head_size)
-        )
-        top_bit = stages[0]
-        upper = ((context & top_bit) != 0).astype(jnp.int32)
-        span = jnp.stack([start, first, upper]).astype(jnp.int32)
-        for part in parts:
-            part.tables = tables(start + places_of(part.top, part.rows), head_size)
-        own_product, early.tables, late.tables, query_flat, span = lax.optimization_barrier(
-            (own_product, early.tables, late.tables, query_flat, span)
+        early.tables = tables(start + places_of(early.top, early.rows), head_size)
+        own_product, early.tables, kept = lax.optimization_barrier(
+            (own_product, early.tables, kept)
         )
 
         def exchange(part, gate):
@@ -328,9 +331,23 @@
             )
 
         exchange(early, own_product)
-        for chunk in chunks[early.end + 1 :]:
-            flying.append(send_rows(chunk, early.sums)[0])
-        combine(early, *flying[early.end])
+        for columns in kept:
+            flying.append(send(columns, early.sums))
+        raw_queries, first = lax.optimization_barrier((queries, first, early.sums))[:2]
+        own_cosine, own_sine = tables(first + jnp.arange(rows, dtype=jnp.int32), head_size)
+        by_head = raw_queries.astype(jnp.float32).reshape(rows, heads, head_size)
+        query_flat = (
+            rotate(by_head.transpose(1, 0, 2), own_cosine[None], own_sine[None])
+            .astype(jnp.bfloat16)
+            .reshape(heads * rows, head_size)
+        )
+        base = first - shard * rows
+        late.tables = tables(base + places_of(late.top, late.rows), head_size)
+        top_bit = stages[0]
+        upper = ((context & top_bit) != 0).astype(jnp.int32)
+        span = jnp.stack([base, first, upper]).astype(jnp.int32)
+        query_flat, late.tables, span = lax.optimization_barrier((query_flat, late.tables, span))
+        combine(early, query_flat, *late.tables, *flying[early.end])
         advance(early)
         exchange(late, early.known)
         advance(early, late.sums)

time: 57.3 us -> 57.6 us (level)
  waiting for transfers between devices: 9.35 us -> 11.9 us
  other arithmetic: 8.34 us -> 6.08 us
  matrix products: 7.15 us -> 8.87 us
  Pallas kernels: 6.56 us -> 5.45 us
    dot_general x10, matrix products: 7.15 us -> 8.87 us  [project(): jnp.dot(columns, weight, preferred_element_type=jnp.float32)]
    ppermute x8, waiting for transfers between devices: 4.31 us -> 5.65 us  [advance(): part.fresh = [lax.ppermute(part.known, 'ctx', pairs)]]
    pallas_call x2, Pallas kernels: 6.56 us -> 5.45 us  [attend(): pl.pallas_call(partial(attention_kernel, count=len(pieces), order=order,...]
    transpose x1, other arithmetic: 0.99 us -> 0.04 us  [local(): by_head.transpose(1, 0, 2)]
    another operation x4, other arithmetic: 1.39 us -> 0.5 us
    ppermute x4, waiting for transfers between devices: 2.73 us -> 3.57 us  [send(): lax.ppermute(after(columns[step - 1], *earlier) if earlier else columns[s...]
    select_n x2, other arithmetic: 0.03 us -> 0.77 us  [exchange(): jnp.where(shard == 0, products[0], products[1])]
    cos x1, other arithmetic: 0.83 us -> 0.19 us  [tables(): return (jnp.cos(angles), jnp.sin(angles))]
  transfers between devices with their start and end apart: 14 -> 14, of which waited for: 10 -> 10; matrix products, arithmetic and copies ran while one was open for 31% -> 29% of each run, Pallas kernels for 5% -> 4%
where the time goes in v11:
time: 57.6 us; the launch traced here: 57.3 us
  starting transfers between devices  19.9 us (35%)
  waiting for transfers between devices  11.9 us (21%)
  matrix products  8.87 us (15%)
  other arithmetic  6.08 us (11%)
  Pallas kernels  5.45 us (9%)
  local copies, waits for them, and re-layouts  4.06 us (7%)
  between operations  0.98 us (2%)
    ppermute x8, starting transfers between devices, advance(): part.fresh = [lax.ppermute(part.known, 'ctx', pairs)]  10.9 us
    dot_general x10, matrix products, project(): jnp.dot(columns, weight, preferred_element_type=jnp.float32)  8.87 us
    ppermute x8, waiting for transfers between devices, advance(): part.fresh = [lax.ppermute(part.known, 'ctx', pairs)]  5.65 us
    pallas_call x2, Pallas kernels, attend(): pl.pallas_call(partial(attention_kernel, count=len(pieces), order=order,...  5.45 us
    ppermute x4, starting transfers between devices, send(): lax.ppermute(after(columns[step - 1], *earlier) if earlier else columns[s...  5.35 us
    ppermute x2, starting transfers between devices, exchange(): lax.ppermute(part.sums, 'fsdp', [(i, i ^ reach) for i in range(shards)])  3.68 us
    ppermute x4, waiting for transfers between devices, send(): lax.ppermute(after(columns[step - 1], *earlier) if earlier else columns[s...  3.57 us
    ppermute x2, waiting for transfers between devices, exchange(): lax.ppermute(part.sums, 'fsdp', [(i, i ^ reach) for i in range(shards)])  2.7 us
  transfers between devices with their start and end apart: 14, of which 10 were waited for; matrix products, arithmetic and copies ran while one was open for 29% of the time, Pallas kernels for 4%

profile of v11, /device:TPU:0, one launch (start us, length us, event | category | flops | bytes accessed | tf_op | source)
XLA Modules:
  0.0 57.3 jit_solution(7879286115335728932)
XLA Ops:
  0.7 1.6 %copy-done = bf16[64,16384]{1,0:T(8,128)(2,1)S(1)} copy-done((bf16[64,16384]{1,0:T(8,128)(2,1)S(1)}, bf16[64,16384]{1,0:T(8,128)(2,1)}, u32[]{:S(2)}) %copy-start) | copy-done | bytes 2097176
  2.2 0.7 %constant_dynamic-slice_fusion.2 = bf16[8,8192]{1,0:T(8,128)(2,1)} fusion(bf16[64,16384]{1,0:T(8,128)(2,1)S(1)} %copy-done, s32[]{:T(128)S(6)} %select_n.40), kind=kLoop, calls=%fused_computation.47 | loop fusion | bytes 262148 | tf_op jit(solution)/shard_map/dynamic_slice | solution.py:196
  2.9 2.9 %collective-permute-start = (bf16[8,8192]{1,0:T(8,128)(2,1)}, bf16[8,8192]{1,0:T(8,128)(2,1)S(1)}, u32[]{:S(2)}, u32[]{:S(2)}) collective-permute-start(bf16[8,8192]{1,0:T(8,128)(2,1)} %constant_dynamic-slice_fusion.2), channel_id=1, source_target_pairs={{0,1},{1,0},{2,3},{3,2},{4,5},{5,4},{6,7},{7,6},{8,9},{9,8},{10,11... | collective-permute-start | bytes 393224 | tf_op jit(solution)/shard_map/ppermute | solution.py:206
  5.9 0.7 %constant_dynamic-slice_fusion.4 = bf16[16,8192]{1,0:T(8,128)(2,1)} fusion(bf16[64,16384]{1,0:T(8,128)(2,1)S(1)} %copy-done, s32[]{:T(128)S(6)} %select_n.40), kind=kLoop, calls=%fused_computation.57 | loop fusion | bytes 524292 | tf_op jit(solution)/shard_map/dynamic_slice | solution.py:196
  6.7 2.0 %collective-permute-start.3 = (bf16[16,8192]{1,0:T(8,128)(2,1)}, bf16[16,8192]{1,0:T(8,128)(2,1)S(1)}, u32[]{:S(2)}, u32[]{:S(2)}) collective-permute-start(bf16[16,8192]{1,0:T(8,128)(2,1)} %constant_dynamic-slice_fusion.4), channel_id=1, source_target_pairs={{0,1},{1,0},{2,3},{3,2},{4,5},{5,4},{6,7},{7,6},{8,9},{9,8},{10,11... | collective-permute-start | bytes 786440 | tf_op jit(solution)/shard_map/ppermute | solution.py:206
  8.7 0.7 %constant_dynamic-slice_fusion.3 = bf16[8,8192]{1,0:T(8,128)(2,1)} fusion(bf16[64,16384]{1,0:T(8,128)(2,1)S(1)} %copy-done, s32[]{:T(128)S(6)} %select_n.40), kind=kLoop, calls=%fused_computation.55 | loop fusion | bytes 262148 | tf_op jit(solution)/shard_map/dynamic_slice | solution.py:196
  9.4 2.8 %fusion.2 = f32[64,128]{1,0:T(8,128)} fusion(bf16[8192,128]{1,0:T(8,128)(2,1)} %param.8, bf16[64,16384]{1,0:T(8,128)(2,1)S(1)} %copy-done, s32[]{:T(128)S(6)} %select_n.41), kind=kOutput, calls=%fused_computation.2 | convolution fusion | flops 134217728 | bytes 3178500 | tf_op jit(solution)/shard_map/dot_general | solution.py:250
  12.2 1.1 %fusion = f32[64,128]{1,0:T(8,128)} fusion(bf16[8192,128]{1,0:T(8,128)(2,1)S(1)} %copy-done.3, bf16[64,16384]{1,0:T(8,128)(2,1)S(1)} %copy-done, s32[]{:T(128)S(6)} %select_n.41), kind=kOutput, calls=%fused_computation | convolution fusion | flops 134217728 | bytes 3178500 | tf_op jit(solution)/shard_map/dot_general | solution.py:250
  13.4 0.1 add.212
  13.5 1.4 %pad_maximum_fusion.7 = f32[64,256]{1,0:T(8,128)} fusion(f32[64,128]{1,0:T(8,128)} %fusion, f32[64,128]{1,0:T(8,128)} %fusion.2), kind=kLoop, calls=%fused_computation.15 | loop fusion | flops 16384 | bytes 131072 | tf_op jit(solution)/shard_map/concatenate | solution.py:248
  14.9 0.9 %multiply_sine_fusion = (f32[80,64]{1,0:T(8,128)}, f32[80,64]{1,0:T(8,128)}) fusion(f32[64]{0:T(128)S(1)} %multiply_power_fusion, f32[80]{0:T(128)S(1)} %add_convert_fusion.5), kind=kLoop, calls=%fused_computation.16 | loop fusion | flops 5120 | bytes 41536 | tf_op jit(solution)/shard_map/sin | solution.py:29
  15.9 0.8 %xor_multiply_fusion = s32[16]{0:T(128)S(1)} fusion(s32[16]{0:T(128)} %constant.47.clone, s32[]{:T(128)S(6)} %axis_index.25), kind=kLoop, calls=%fused_computation.49 | loop fusion | flops 32 | bytes 132 | tf_op jit(solution)/shard_map/mul | solution.py:327
  16.7 2.1 %fusion.6 = f32[8,128]{1,0:T(8,128)S(1)} fusion(bf16[8,8192]{1,0:T(8,128)(2,1)S(1)} %collective-permute-done, bf16[8192,128]{1,0:T(8,128)(2,1)} %param.8), kind=kOutput, calls=%fused_computation.59 | convolution fusion | flops 16777216 | bytes 2232320 | tf_op jit(solution)/shard_map/dot_general | solution.py:250
  18.8 0.4 fusion.7
  19.2 2.4 %collective-permute-done.1 = bf16[32,8192]{1,0:T(8,128)(2,1)S(1)} collective-permute-done((bf16[32,8192]{1,0:T(8,128)(2,1)S(1)}, bf16[32,8192]{1,0:T(8,128)(2,1)S(1)}, u32[]{:S(2)}, u32[]{:S(2)}) %collective-permute-start.1) | collective-permute-done | bytes 524320 | tf_op jit(solution)/shard_map/ppermute | solution.py:206
  21.6 0.4 fusion.8
  22.0 0.4 fusion.9
  22.6 2.1 %collective-permute-start.2 = (f32[80,256]{1,0:T(8,128)S(1)}, f32[80,256]{1,0:T(8,128)S(1)}, u32[]{:S(2)}, u32[]{:S(2)}) collective-permute-start(f32[80,256]{1,0:T(8,128)S(1)} %pad_maximum_fusion.5), channel_id=1, source_target_pairs={{0,1},{1,0},{2,3},{3,2},{4,5},{5,4},{6,7},{7,6},{8,9},{9,8},{10,11... | collective-permute-start | bytes 245768 | tf_op jit(solution)/shard_map/ppermute | solution.py:297
  24.8 0.2 multiply_cosine_fusion.1
  25.0 0.3 subtract_convert_fusion
  25.3 0.2 multiply_sine_fusion.2
  25.4 0.1 pad_maximum_fusion.1.query_ref
  25.7 0.3 collective-permute-start.4
  26.0 1.2 %collective-permute-done.3 = bf16[16,8192]{1,0:T(8,128)(2,1)S(1)} collective-permute-done((bf16[16,8192]{1,0:T(8,128)(2,1)}, bf16[16,8192]{1,0:T(8,128)(2,1)S(1)}, u32[]{:S(2)}, u32[]{:S(2)}) %collective-permute-start.3) | collective-permute-done | bytes 262176 | tf_op jit(solution)/shard_map/ppermute | solution.py:206
  27.2 1.8 %collective-permute-done.2 = f32[80,256]{1,0:T(8,128)S(1)} collective-permute-done((f32[80,256]{1,0:T(8,128)S(1)}, f32[80,256]{1,0:T(8,128)S(1)}, u32[]{:S(2)}, u32[]{:S(2)}) %collective-permute-start.2) | collective-permute-done | bytes 81952 | tf_op jit(solution)/shard_map/ppermute | solution.py:297
  29.1 0.1 pad_maximum_fusion.10
  29.2 0.4 fusion.10
  29.6 0.4 fusion.11
  30.0 3.2 %collective-permute-start.6 = (bf16[80,256]{1,0:T(8,128)(2,1)S(1)}, bf16[80,256]{1,0:T(8,128)(2,1)S(1)}, u32[]{:S(2)}, u32[]{:S(2)}) collective-permute-start(bf16[80,256]{1,0:T(8,128)(2,1)S(1)} %pad_maximum_fusion.10), channel_id=1, source_target_pairs={{0,16},{2,18},{4,20},{6,22},{8,24},{10,26},{12,28},{14,30},{16,0},... | collective-permute-start | bytes 122888 | tf_op jit(solution)/shard_map/ppermute | solution.py:319
  33.2 0.4 fusion.12
  33.6 0.4 fusion.13
  34.0 0.8 %slice_select_fusion.3 = (f32[24,256]{1,0:T(8,128)S(1)}, f32[24,256]{1,0:T(8,128)S(1)}) fusion(f32[64,256]{1,0:T(8,128)} %pad_maximum_fusion.7, f32[8,128]{1,0:T(8,128)S(1)} %fusion.13, f32[8,128]{1,0:T(8,128)S(1)} %fusion.12, f32[16,128]{1,0:T(8,128)S(1)} %fusion.11, f32[16,128]{1,0:T(8,128)S(1)} %fusion.10, pred[]{:T(512)S(6)} %eq.2), kind=kLoop, calls=%fused_computation.38 | loop fusion | flops 30720 | bytes 98305 | tf_op jit(solution)/shard_map/jit(_where)/select_n | solution.py:279
  34.8 1.6 %collective-permute-start.5 = (f32[48,256]{1,0:T(8,128)S(1)}, f32[48,256]{1,0:T(8,128)S(1)}, u32[]{:S(2)}, u32[]{:S(2)}) collective-permute-start(f32[48,256]{1,0:T(8,128)S(1)} %pad_maximum_fusion.8), channel_id=1, source_target_pairs={{0,1},{1,0},{2,3},{3,2},{4,5},{5,4},{6,7},{7,6},{8,9},{9,8},{10,11... | collective-permute-start | bytes 147464 | tf_op jit(solution)/shard_map/ppermute | solution.py:297
  36.3 1.6 %collective-permute-start.8 = (bf16[160,256]{1,0:T(8,128)(2,1)S(1)}, bf16[160,256]{1,0:T(8,128)(2,1)S(1)}, u32[]{:S(2)}, u32[]{:S(2)}) collective-permute-start(bf16[160,256]{1,0:T(8,128)(2,1)S(1)} %pad_maximum_fusion.6), channel_id=1, source_target_pairs={{0,8},{2,10},{4,12},{6,14},{8,0},{10,2},{12,4},{14,6},{16,24},{18,... | collective-permute-start | bytes 245768 | tf_op jit(solution)/shard_map/ppermute | solution.py:319
  38.0 0.9 %collective-permute-done.5 = f32[48,256]{1,0:T(8,128)S(1)} collective-permute-done((f32[48,256]{1,0:T(8,128)S(1)}, f32[48,256]{1,0:T(8,128)S(1)}, u32[]{:S(2)}, u32[]{:S(2)}) %collective-permute-start.5) | collective-permute-done | bytes 49184 | tf_op jit(solution)/shard_map/ppermute | solution.py:297
  39.1 1.2 %collective-permute-start.7 = (bf16[48,256]{1,0:T(8,128)(2,1)S(1)}, bf16[48,256]{1,0:T(8,128)(2,1)S(1)}, u32[]{:S(2)}, u32[]{:S(2)}) collective-permute-start(bf16[48,256]{1,0:T(8,128)(2,1)S(1)} %pad_maximum_fusion.12), channel_id=1, source_target_pairs={{0,16},{2,18},{4,20},{6,22},{8,24},{10,26},{12,28},{14,30},{16,0},... | collective-permute-start | bytes 73736 | tf_op jit(solution)/shard_map/ppermute | solution.py:319
  40.3 0.6 %collective-permute-done.8 = bf16[160,256]{1,0:T(8,128)(2,1)S(1)} collective-permute-done((bf16[160,256]{1,0:T(8,128)(2,1)S(1)}, bf16[160,256]{1,0:T(8,128)(2,1)S(1)}, u32[]{:S(2)}, u32[]{:S(2)}) %collective-permute-start.8) | collective-permute-done | bytes 81952 | tf_op jit(solution)/shard_map/ppermute | solution.py:319
  40.8 1.6 %collective-permute-start.10 = (bf16[320,256]{1,0:T(8,128)(2,1)S(1)}, bf16[320,256]{1,0:T(8,128)(2,1)S(1)}, u32[]{:S(2)}, u32[]{:S(2)}) collective-permute-start(bf16[320,256]{1,0:T(8,128)(2,1)S(1)} %pad_maximum_fusion.3), channel_id=1, source_target_pairs={{0,4},{2,6},{4,0},{6,2},{8,12},{10,14},{12,8},{14,10},{16,20},{18,... | collective-permute-start | bytes 491528 | tf_op jit(solution)/shard_map/ppermute | solution.py:319
  42.5 1.3 %collective-permute-done.7 = bf16[48,256]{1,0:T(8,128)(2,1)S(1)} collective-permute-done((bf16[48,256]{1,0:T(8,128)(2,1)S(1)}, bf16[48,256]{1,0:T(8,128)(2,1)S(1)}, u32[]{:S(2)}, u32[]{:S(2)}) %collective-permute-start.7) | collective-permute-done | bytes 24608 | tf_op jit(solution)/shard_map/ppermute | solution.py:319
  43.8 1.6 %collective-permute-start.9 = (bf16[96,256]{1,0:T(8,128)(2,1)S(1)}, bf16[96,256]{1,0:T(8,128)(2,1)S(1)}, u32[]{:S(2)}, u32[]{:S(2)}) collective-permute-start(bf16[96,256]{1,0:T(8,128)(2,1)S(1)} %pad_maximum_fusion.9), channel_id=1, source_target_pairs={{0,8},{2,10},{4,12},{6,14},{8,0},{10,2},{12,4},{14,6},{16,24},{18,... | collective-permute-start | bytes 147464 | tf_op jit(solution)/shard_map/ppermute | solution.py:319
  45.4 0.8 %collective-permute-done.10 = bf16[320,256]{1,0:T(8,128)(2,1)S(1)} collective-permute-done((bf16[320,256]{1,0:T(8,128)(2,1)S(1)}, bf16[320,256]{1,0:T(8,128)(2,1)S(1)}, u32[]{:S(2)}, u32[]{:S(2)}) %collective-permute-start.10) | collective-permute-done | bytes 163872 | tf_op jit(solution)/shard_map/ppermute | solution.py:319
  46.6 1.4 %collective-permute-done.9 = bf16[96,256]{1,0:T(8,128)(2,1)S(1)} collective-permute-done((bf16[96,256]{1,0:T(8,128)(2,1)S(1)}, bf16[96,256]{1,0:T(8,128)(2,1)S(1)}, u32[]{:S(2)}, u32[]{:S(2)}) %collective-permute-start.9) | collective-permute-done | bytes 49184 | tf_op jit(solution)/shard_map/ppermute | solution.py:319
  47.9 1.6 %collective-permute-start.11 = (bf16[192,256]{1,0:T(8,128)(2,1)S(1)}, bf16[192,256]{1,0:T(8,128)(2,1)S(1)}, u32[]{:S(2)}, u32[]{:S(2)}) collective-permute-start(bf16[192,256]{1,0:T(8,128)(2,1)S(1)} %pad_maximum_fusion.4), channel_id=1, source_target_pairs={{0,4},{2,6},{4,0},{6,2},{8,12},{10,14},{12,8},{14,10},{16,20},{18,... | collective-permute-start | bytes 294920 | tf_op jit(solution)/shard_map/ppermute | solution.py:319
  49.5 2.3 %attend_part.1 = (f32[1024,1]{1,0:T(8,128)S(1)}, f32[1024,1]{1,0:T(8,128)S(1)}, f32[1024,128]{1,0:T(8,128)S(1)}) custom-call(s32[3]{0:T(128)S(1)} %pad_add_fusion.span_ref, s32[1,1280]{1,0:T(1,128)S(1)} %add.238.place_ref, bf16[1024,128]{1,0:T(8,128)(2,1)S(1)} %pad_maximum_fusion.1.query_ref, bf16[640,256]{1,0:T(8,128)(2,1)S(1)} %pad_maximum_fusion.refs_0_, ...), custom_call_target="tpu_custom_call" | custom-call | flops 671088640 | bytes 1179648 | tf_op jit(solution)/shard_map/attend_part/pallas_call | solution.py:141
  51.9 0.8 %collective-permute-done.11 = bf16[192,256]{1,0:T(8,128)(2,1)S(1)} collective-permute-done((bf16[192,256]{1,0:T(8,128)(2,1)S(1)}, bf16[192,256]{1,0:T(8,128)(2,1)S(1)}, u32[]{:S(2)}, u32[]{:S(2)}) %collective-permute-start.11) | collective-permute-done | bytes 98336 | tf_op jit(solution)/shard_map/ppermute | solution.py:319
  52.7 0.6 %pad_maximum_fusion.11 = bf16[64,256]{1,0:T(8,128)(2,1)} fusion(bf16[24,256]{1,0:T(8,128)(2,1)S(1)} %constant_dynamic-slice_fusion, bf16[40,256]{1,0:T(8,128)(2,1)S(1)} %constant_dynamic-slice_fusion.1), kind=kLoop, calls=%fused_computation.31 | loop fusion | flops 65536 | bytes 65536 | tf_op jit(solution)/shard_map/concatenate | solution.py:372
  53.4 0.8 %collective-permute-done.13.refs_1_ = bf16[384,256]{1,0:T(8,128)(2,1)S(1)} collective-permute-done((bf16[384,256]{1,0:T(8,128)(2,1)S(1)}, bf16[384,256]{1,0:T(8,128)(2,1)S(1)}, u32[]{:S(2)}, u32[]{:S(2)}) %collective-permute-start.13) | collective-permute-done | bytes 196640 | tf_op jit(solution)/shard_map/ppermute | solution.py:319
  54.2 3.1 %attend_last.1 = bf16[64,2048]{1,0:T(8,128)(2,1)} custom-call(s32[3]{0:T(128)S(1)} %pad_add_fusion.span_ref, s32[1,768]{1,0:T(1,128)S(1)} %add.234.place_ref, bf16[1024,128]{1,0:T(8,128)(2,1)S(1)} %pad_maximum_fusion.1.query_ref, bf16[384,256]{1,0:T(8,128)(2,1)S(1)} %pad_maximum_fusion.2.refs_0_, bf16[384,256]{1,0:T(8,128)(2,1)S(1)} %collective-permute-done.13.refs_1_, ...), custom_call_target="tpu_custom_call" | custom-call | flops 402653184 | bytes 917504 | tf_op jit(solution)/shard_map/attend_last/pallas_call | solution.py:141
  (62 shorter events, 1.4 us)
Async XLA Ops:
  0.6 1.6 %copy-start = (bf16[64,16384]{1,0:T(8,128)(2,1)S(1)}, bf16[64,16384]{1,0:T(8,128)(2,1)}, u32[]{:S(2)}) copy-start(bf16[64,16384]{1,0:T(8,128)(2,1)} %param.6) | copy-start | bytes 6291460
  2.9 13.8 %collective-permute-start = (bf16[8,8192]{1,0:T(8,128)(2,1)}, bf16[8,8192]{1,0:T(8,128)(2,1)S(1)}, u32[]{:S(2)}, u32[]{:S(2)}) collective-permute-start(bf16[8,8192]{1,0:T(8,128)(2,1)} %constant_dynamic-slice_fusion.2), channel_id=1, source_target_pairs={{0,1},{1,0},{2,3},{3,2},{4,5},{5,4},{6,7},{7,6},{8,9},{9,8},{10,11... | collective-permute-start | bytes 393224 | tf_op jit(solution)/shard_map/ppermute | solution.py:206
  5.9 15.7 %collective-permute-start.1 = (bf16[32,8192]{1,0:T(8,128)(2,1)S(1)}, bf16[32,8192]{1,0:T(8,128)(2,1)S(1)}, u32[]{:S(2)}, u32[]{:S(2)}) collective-permute-start(bf16[32,8192]{1,0:T(8,128)(2,1)S(1)} %constant_dynamic-slice_fusion.5), channel_id=1, source_target_pairs={{0,1},{1,0},{2,3},{3,2},{4,5},{5,4},{6,7},{7,6},{8,9},{9,8},{10,11... | collective-permute-start | bytes 1572872 | tf_op jit(solution)/shard_map/ppermute | solution.py:206
  6.7 20.5 %collective-permute-start.3 = (bf16[16,8192]{1,0:T(8,128)(2,1)}, bf16[16,8192]{1,0:T(8,128)(2,1)S(1)}, u32[]{:S(2)}, u32[]{:S(2)}) collective-permute-start(bf16[16,8192]{1,0:T(8,128)(2,1)} %constant_dynamic-slice_fusion.4), channel_id=1, source_target_pairs={{0,1},{1,0},{2,3},{3,2},{4,5},{5,4},{6,7},{7,6},{8,9},{9,8},{10,11... | collective-permute-start | bytes 786440 | tf_op jit(solution)/shard_map/ppermute | solution.py:206
  9.4 2.8 %copy-start.3 = (bf16[8192,128]{1,0:T(8,128)(2,1)S(1)}, bf16[8192,128]{1,0:T(8,128)(2,1)}, u32[]{:S(2)}) copy-start(bf16[8192,128]{1,0:T(8,128)(2,1)} %param.9) | copy-start | bytes 6291460
  15.9 2.9 %copy-start.4 = (bf16[8192,128]{1,0:T(8,128)(2,1)S(1)}, bf16[8192,128]{1,0:T(8,128)(2,1)}, u32[]{:S(2)}) copy-start(bf16[8192,128]{1,0:T(8,128)(2,1)} %param.9) | copy-start | bytes 6291460
  16.7 4.9 %copy-start.1 = (bf16[8192,128]{1,0:T(8,128)(2,1)S(1)}, bf16[8192,128]{1,0:T(8,128)(2,1)}, u32[]{:S(2)}) copy-start(bf16[8192,128]{1,0:T(8,128)(2,1)} %param.8) | copy-start | bytes 6291460
  19.2 3.3 %copy-start.7 = (f32[64,256]{1,0:T(8,128)S(1)}, f32[64,256]{1,0:T(8,128)}, u32[]{:S(2)}) copy-start(f32[64,256]{1,0:T(8,128)} %pad_maximum_fusion.7) | copy-start | bytes 196612
  22.0 2.7 %copy-start.6 = (bf16[64,2048]{1,0:T(8,128)(2,1)S(1)}, bf16[64,2048]{1,0:T(8,128)(2,1)}, u32[]{:S(2)}) copy-start(bf16[64,2048]{1,0:T(8,128)(2,1)} %param.7) | copy-start | bytes 786436
  22.5 3.2 %copy-start.10 = (bf16[8,8192]{1,0:T(8,128)(2,1)S(1)}, bf16[8,8192]{1,0:T(8,128)(2,1)}, u32[]{:S(2)}) copy-start(bf16[8,8192]{1,0:T(8,128)(2,1)} %constant_dynamic-slice_fusion.3) | copy-start | bytes 393220
  22.5 6.5 %copy-start.8 = (f32[80,64]{1,0:T(8,128)S(1)}, f32[80,64]{1,0:T(8,128)}, u32[]{:S(2)}) copy-start(f32[80,64]{1,0:T(8,128)} %get-tuple-element.56) | copy-start | bytes 61444
  22.5 6.5 %copy-start.9 = (f32[80,64]{1,0:T(8,128)S(1)}, f32[80,64]{1,0:T(8,128)}, u32[]{:S(2)}) copy-start(f32[80,64]{1,0:T(8,128)} %get-tuple-element.55) | copy-start | bytes 61444
  22.6 6.6 %copy-start.2 = (bf16[8192,128]{1,0:T(8,128)(2,1)S(1)}, bf16[8192,128]{1,0:T(8,128)(2,1)}, u32[]{:S(2)}) copy-start(bf16[8192,128]{1,0:T(8,128)(2,1)} %param.8) | copy-start | bytes 6291460
  22.6 6.4 %collective-permute-start.2 = (f32[80,256]{1,0:T(8,128)S(1)}, f32[80,256]{1,0:T(8,128)S(1)}, u32[]{:S(2)}, u32[]{:S(2)}) collective-permute-start(f32[80,256]{1,0:T(8,128)S(1)} %pad_maximum_fusion.5), channel_id=1, source_target_pairs={{0,1},{1,0},{2,3},{3,2},{4,5},{5,4},{6,7},{7,6},{8,9},{9,8},{10,11... | collective-permute-start | bytes 245768 | tf_op jit(solution)/shard_map/ppermute | solution.py:297
  25.3 4.3 %copy-start.5 = (bf16[8192,128]{1,0:T(8,128)(2,1)S(1)}, bf16[8192,128]{1,0:T(8,128)(2,1)}, u32[]{:S(2)}) copy-start(bf16[8192,128]{1,0:T(8,128)(2,1)} %param.9) | copy-start | bytes 6291460
  25.7 7.5 %collective-permute-start.4 = (bf16[8,8192]{1,0:T(8,128)(2,1)S(1)}, bf16[8,8192]{1,0:T(8,128)(2,1)S(1)}, u32[]{:S(2)}, u32[]{:S(2)}) collective-permute-start(bf16[8,8192]{1,0:T(8,128)(2,1)S(1)} %copy-done.10), channel_id=1, source_target_pairs={{0,1},{1,0},{2,3},{3,2},{4,5},{5,4},{6,7},{7,6},{8,9},{9,8},{10,11... | collective-permute-start | bytes 393224 | tf_op jit(solution)/shard_map/ppermute | solution.py:206
  30.0 6.3 %collective-permute-start.6 = (bf16[80,256]{1,0:T(8,128)(2,1)S(1)}, bf16[80,256]{1,0:T(8,128)(2,1)S(1)}, u32[]{:S(2)}, u32[]{:S(2)}) collective-permute-start(bf16[80,256]{1,0:T(8,128)(2,1)S(1)} %pad_maximum_fusion.10), channel_id=1, source_target_pairs={{0,16},{2,18},{4,20},{6,22},{8,24},{10,26},{12,28},{14,30},{16,0},... | collective-permute-start | bytes 122888 | tf_op jit(solution)/shard_map/ppermute | solution.py:319
  34.8 4.2 %collective-permute-start.5 = (f32[48,256]{1,0:T(8,128)S(1)}, f32[48,256]{1,0:T(8,128)S(1)}, u32[]{:S(2)}, u32[]{:S(2)}) collective-permute-start(f32[48,256]{1,0:T(8,128)S(1)} %pad_maximum_fusion.8), channel_id=1, source_target_pairs={{0,1},{1,0},{2,3},{3,2},{4,5},{5,4},{6,7},{7,6},{8,9},{9,8},{10,11... | collective-permute-start | bytes 147464 | tf_op jit(solution)/shard_map/ppermute | solution.py:297
  36.3 4.5 %collective-permute-start.8 = (bf16[160,256]{1,0:T(8,128)(2,1)S(1)}, bf16[160,256]{1,0:T(8,128)(2,1)S(1)}, u32[]{:S(2)}, u32[]{:S(2)}) collective-permute-start(bf16[160,256]{1,0:T(8,128)(2,1)S(1)} %pad_maximum_fusion.6), channel_id=1, source_target_pairs={{0,8},{2,10},{4,12},{6,14},{8,0},{10,2},{12,4},{14,6},{16,24},{18,... | collective-permute-start | bytes 245768 | tf_op jit(solution)/shard_map/ppermute | solution.py:319
  39.1 4.7 %collective-permute-start.7 = (bf16[48,256]{1,0:T(8,128)(2,1)S(1)}, bf16[48,256]{1,0:T(8,128)(2,1)S(1)}, u32[]{:S(2)}, u32[]{:S(2)}) collective-permute-start(bf16[48,256]{1,0:T(8,128)(2,1)S(1)} %pad_maximum_fusion.12), channel_id=1, source_target_pairs={{0,16},{2,18},{4,20},{6,22},{8,24},{10,26},{12,28},{14,30},{16,0},... | collective-permute-start | bytes 73736 | tf_op jit(solution)/shard_map/ppermute | solution.py:319
  40.8 5.4 %collective-permute-start.10 = (bf16[320,256]{1,0:T(8,128)(2,1)S(1)}, bf16[320,256]{1,0:T(8,128)(2,1)S(1)}, u32[]{:S(2)}, u32[]{:S(2)}) collective-permute-start(bf16[320,256]{1,0:T(8,128)(2,1)S(1)} %pad_maximum_fusion.3), channel_id=1, source_target_pairs={{0,4},{2,6},{4,0},{6,2},{8,12},{10,14},{12,8},{14,10},{16,20},{18,... | collective-permute-start | bytes 491528 | tf_op jit(solution)/shard_map/ppermute | solution.py:319
  43.8 4.1 %collective-permute-start.9 = (bf16[96,256]{1,0:T(8,128)(2,1)S(1)}, bf16[96,256]{1,0:T(8,128)(2,1)S(1)}, u32[]{:S(2)}, u32[]{:S(2)}) collective-permute-start(bf16[96,256]{1,0:T(8,128)(2,1)S(1)} %pad_maximum_fusion.9), channel_id=1, source_target_pairs={{0,8},{2,10},{4,12},{6,14},{8,0},{10,2},{12,4},{14,6},{16,24},{18,... | collective-permute-start | bytes 147464 | tf_op jit(solution)/shard_map/ppermute | solution.py:319
  46.3 3.3 %collective-permute-start.12 = (bf16[640,256]{1,0:T(8,128)(2,1)S(1)}, bf16[640,256]{1,0:T(8,128)(2,1)S(1)}, u32[]{:S(2)}, u32[]{:S(2)}) collective-permute-start(bf16[640,256]{1,0:T(8,128)(2,1)S(1)} %pad_maximum_fusion.refs_0_), channel_id=1, source_target_pairs={{0,2},{2,0},{4,6},{6,4},{8,10},{10,8},{12,14},{14,12},{16,18},{18,... | collective-permute-start | bytes 983048 | tf_op jit(solution)/shard_map/ppermute | solution.py:319
  47.9 4.7 %collective-permute-start.11 = (bf16[192,256]{1,0:T(8,128)(2,1)S(1)}, bf16[192,256]{1,0:T(8,128)(2,1)S(1)}, u32[]{:S(2)}, u32[]{:S(2)}) collective-permute-start(bf16[192,256]{1,0:T(8,128)(2,1)S(1)} %pad_maximum_fusion.4), channel_id=1, source_target_pairs={{0,4},{2,6},{4,0},{6,2},{8,12},{10,14},{12,8},{14,10},{16,20},{18,... | collective-permute-start | bytes 294920 | tf_op jit(solution)/shard_map/ppermute | solution.py:319
  52.6 1.5 %collective-permute-start.13 = (bf16[384,256]{1,0:T(8,128)(2,1)S(1)}, bf16[384,256]{1,0:T(8,128)(2,1)S(1)}, u32[]{:S(2)}, u32[]{:S(2)}) collective-permute-start(bf16[384,256]{1,0:T(8,128)(2,1)S(1)} %pad_maximum_fusion.2.refs_0_), channel_id=1, source_target_pairs={{0,2},{2,0},{4,6},{6,4},{8,10},{10,8},{12,14},{14,12},{16,18},{18,... | collective-permute-start | bytes 589832 | tf_op jit(solution)/shard_map/ppermute | solution.py:319

commit v12 on v11

--- a/solution.py
+++ b/solution.py
@@ -349,11 +349,12 @@
         query_flat, late.tables, span = lax.optimization_barrier((query_flat, late.tables, span))
         combine(early, query_flat, *late.tables, *flying[early.end])
         advance(early)
+        advance(early, *[piece for chunk in flying[early.end + 1 : -1] for piece in chunk])
         exchange(late, early.known)
         advance(early, late.sums)
         combine(late, early.known)
         advance(late)
-        for stage in range(2, len(stages)):
+        for stage in range(3, len(stages)):
             advance(early, late.known)
             advance(late, early.known)
         state = absorb(
@@ -366,6 +367,8 @@
             late.known,
         )
         advance(late, *state)
+        while late.stage < len(stages):
+            advance(late)
         attended = absorb(
             late, [late.known] + late.fresh, late.masks, shards * late.rows, state, True
         )
@@ -378,7 +381,7 @@
 def solution(mesh):
     placed = (P(("ctx", "fsdp"), None), P(("ctx", "fsdp"), None), P("fsdp", None), P("fsdp", None))
     return jax.shard_map(
-        make_local(mesh.shape["ctx"], mesh.shape["fsdp"], ((1, 4), (2, 1))),
+        make_local(mesh.shape["ctx"], mesh.shape["fsdp"], ((1, 2), (2, 1, 2))),
         mesh=mesh,
         in_specs=placed,
         out_specs=(P(("ctx", "fsdp"), None), P(("ctx", "fsdp"), None)),

time: 57.6 us -> 66.3 us (1.15)
  local copies, waits for them, and re-layouts: 4.06 us -> 10.6 us
  other arithmetic: 6.08 us -> 7.67 us
  starting transfers between devices: 19.9 us -> 21.3 us
  waiting for transfers between devices: 11.9 us -> 11.2 us
    unnamed x22 -> x34, local copies, waits for them, and re-layouts: 1.62 us -> 6.96 us
    concatenate x6, other arithmetic: 0.07 us -> 2.61 us  [advance(): part.known = after(jnp.concatenate([fresh[0]] + list(fresh[1]), axis=0))]
    ppermute x4 -> x5, starting transfers between devices: 5.35 us -> 7.43 us  [send(): lax.ppermute(after(columns[step - 1], *earlier) if earlier else columns[s...]
    ppermute x4 -> x5, waiting for transfers between devices: 3.57 us -> 1.76 us  [send(): lax.ppermute(after(columns[step - 1], *earlier) if earlier else columns[s...]
    ppermute x8, waiting for transfers between devices: 5.65 us -> 7.27 us  [advance(): part.fresh = [lax.ppermute(part.known, 'ctx', pairs)]]
    concatenate x1, other arithmetic: 1.4 us -> 0.01 us  [project(): jnp.concatenate([jnp.dot(columns, weight, preferred_element_type=jnp.floa...]
    select_n x2, other arithmetic: 0.77 us -> 0.02 us  [exchange(): jnp.where(shard == 0, products[0], products[1])]
    another operation x3, other arithmetic: 0.42 us -> 1.16 us
  transfers between devices with their start and end apart: 14 -> 15, of which waited for: 10 -> 8; matrix products, arithmetic and copies ran while one was open for 29% -> 25% of each run, Pallas kernels for 4% -> 3%
where the time goes in v12:
time: 66.3 us; the launch traced here: 65.9 us
  starting transfers between devices  21.3 us (32%)
  waiting for transfers between devices  11.2 us (17%)
  local copies, waits for them, and re-layouts  10.6 us (16%)
  matrix products  8.36 us (13%)
  other arithmetic  7.67 us (12%)
  Pallas kernels  5.66 us (9%)
  between operations  1.06 us (2%)
    ppermute x8, starting transfers between devices, advance(): part.fresh = [lax.ppermute(part.known, 'ctx', pairs)]  10.6 us
    dot_general x12, matrix products, project(): jnp.dot(columns, weight, preferred_element_type=jnp.float32)  8.36 us
    ppermute x5, starting transfers between devices, send(): lax.ppermute(after(columns[step - 1], *earlier) if earlier else columns[s...  7.43 us
    ppermute x8, waiting for transfers between devices, advance(): part.fresh = [lax.ppermute(part.known, 'ctx', pairs)]  7.27 us
    unnamed x34, local copies, waits for them, and re-layouts  6.96 us
    pallas_call x2, Pallas kernels, attend(): pl.pallas_call(partial(attention_kernel, count=len(pieces), order=order,...  5.66 us
    ppermute x2, starting transfers between devices, exchange(): lax.ppermute(part.sums, 'fsdp', [(i, i ^ reach) for i in range(shards)])  3.31 us
    concatenate x6, other arithmetic, advance(): part.known = after(jnp.concatenate([fresh[0]] + list(fresh[1]), axis=0))  2.61 us
  transfers between devices with their start and end apart: 15, of which 8 were waited for; matrix products, arithmetic and copies ran while one was open for 25% of the time, Pallas kernels for 3%

profile of v12, /device:TPU:0, one launch (start us, length us, event | category | flops | bytes accessed | tf_op | source)
XLA Modules:
  0.0 65.9 jit_solution(18348012368480796152)
XLA Ops:
  0.7 1.6 %copy-done = bf16[64,16384]{1,0:T(8,128)(2,1)S(1)} copy-done((bf16[64,16384]{1,0:T(8,128)(2,1)S(1)}, bf16[64,16384]{1,0:T(8,128)(2,1)}, u32[]{:S(2)}) %copy-start) | copy-done | bytes 2097176
  2.2 0.7 %constant_dynamic-slice_fusion.2 = bf16[8,8192]{1,0:T(8,128)(2,1)} fusion(bf16[64,16384]{1,0:T(8,128)(2,1)S(1)} %copy-done, s32[]{:T(128)S(6)} %select_n.41), kind=kLoop, calls=%fused_computation.47 | loop fusion | bytes 262148 | tf_op jit(solution)/shard_map/dynamic_slice | solution.py:196
  2.9 2.9 %collective-permute-start = (bf16[8,8192]{1,0:T(8,128)(2,1)}, bf16[8,8192]{1,0:T(8,128)(2,1)S(1)}, u32[]{:S(2)}, u32[]{:S(2)}) collective-permute-start(bf16[8,8192]{1,0:T(8,128)(2,1)} %constant_dynamic-slice_fusion.2), channel_id=1, source_target_pairs={{0,1},{1,0},{2,3},{3,2},{4,5},{5,4},{6,7},{7,6},{8,9},{9,8},{10,11... | collective-permute-start | bytes 393224 | tf_op jit(solution)/shard_map/ppermute | solution.py:206
  5.8 0.7 %constant_dynamic-slice_fusion.6 = bf16[16,8192]{1,0:T(8,128)(2,1)} fusion(bf16[64,16384]{1,0:T(8,128)(2,1)S(1)} %copy-done, s32[]{:T(128)S(6)} %select_n.41), kind=kLoop, calls=%fused_computation.59 | loop fusion | bytes 524292 | tf_op jit(solution)/shard_map/dynamic_slice | solution.py:196
  6.6 2.1 %collective-permute-start.3 = (bf16[16,8192]{1,0:T(8,128)(2,1)S(1)}, bf16[16,8192]{1,0:T(8,128)(2,1)S(1)}, u32[]{:S(2)}, u32[]{:S(2)}) collective-permute-start(bf16[16,8192]{1,0:T(8,128)(2,1)S(1)} %constant_dynamic-slice_fusion.5), channel_id=1, source_target_pairs={{0,1},{1,0},{2,3},{3,2},{4,5},{5,4},{6,7},{7,6},{8,9},{9,8},{10,11... | collective-permute-start | bytes 786440 | tf_op jit(solution)/shard_map/ppermute | solution.py:206
  8.9 0.7 %constant_dynamic-slice_fusion.4 = bf16[8,8192]{1,0:T(8,128)(2,1)} fusion(bf16[64,16384]{1,0:T(8,128)(2,1)S(1)} %copy-done, s32[]{:T(128)S(6)} %select_n.41), kind=kLoop, calls=%fused_computation.57 | loop fusion | bytes 262148 | tf_op jit(solution)/shard_map/dynamic_slice | solution.py:196
  9.6 2.2 %fusion = f32[64,128]{1,0:T(8,128)S(1)} fusion(bf16[8192,128]{1,0:T(8,128)(2,1)} %param.9, bf16[64,16384]{1,0:T(8,128)(2,1)S(1)} %copy-done, s32[]{:T(128)S(6)} %select_n.42), kind=kOutput, calls=%fused_computation | convolution fusion | flops 134217728 | bytes 3178500 | tf_op jit(solution)/shard_map/dot_general | solution.py:250
  11.8 0.5 fusion.2
  12.3 0.8 %multiply_sine_fusion.2 = (f32[48,64]{1,0:T(8,128)S(1)}, f32[48,64]{1,0:T(8,128)}) fusion(f32[64]{0:T(128)S(1)} %multiply_power_fusion, f32[48]{0:T(128)S(1)} %add_convert_fusion.5), kind=kLoop, calls=%fused_computation.29 | loop fusion | flops 3072 | bytes 25024 | tf_op jit(solution)/shard_map/sin | solution.py:29
  13.2 0.6 add.225
  13.8 2.1 %fusion.7 = f32[8,128]{1,0:T(8,128)S(1)} fusion(bf16[8,8192]{1,0:T(8,128)(2,1)S(1)} %collective-permute-done, bf16[8192,128]{1,0:T(8,128)(2,1)} %param.9), kind=kOutput, calls=%fused_computation.61 | convolution fusion | flops 16777216 | bytes 2232320 | tf_op jit(solution)/shard_map/dot_general | solution.py:250
  16.6 0.4 fusion.9
  17.0 0.4 fusion.8
  17.5 1.5 %collective-permute-start.2 = (f32[48,256]{1,0:T(8,128)S(1)}, f32[48,256]{1,0:T(8,128)S(1)}, u32[]{:S(2)}, u32[]{:S(2)}) collective-permute-start(f32[48,256]{1,0:T(8,128)S(1)} %pad_maximum_fusion.8), channel_id=1, source_target_pairs={{0,1},{1,0},{2,3},{3,2},{4,5},{5,4},{6,7},{7,6},{8,9},{9,8},{10,11... | collective-permute-start | bytes 147464 | tf_op jit(solution)/shard_map/ppermute | solution.py:297
  19.2 0.6 add_convert_fusion.3
  20.0 0.7 %collective-permute-start.5 = (bf16[8,8192]{1,0:T(8,128)(2,1)}, bf16[8,8192]{1,0:T(8,128)(2,1)S(1)}, u32[]{:S(2)}, u32[]{:S(2)}) collective-permute-start(bf16[8,8192]{1,0:T(8,128)(2,1)} %constant_dynamic-slice_fusion.4), channel_id=1, source_target_pairs={{0,1},{1,0},{2,3},{3,2},{4,5},{5,4},{6,7},{7,6},{8,9},{9,8},{10,11... | collective-permute-start | bytes 393224 | tf_op jit(solution)/shard_map/ppermute | solution.py:206
  21.6 1.1 %collective-permute-done.2 = f32[48,256]{1,0:T(8,128)S(1)} collective-permute-done((f32[48,256]{1,0:T(8,128)S(1)}, f32[48,256]{1,0:T(8,128)S(1)}, u32[]{:S(2)}, u32[]{:S(2)}) %collective-permute-start.2) | collective-permute-done | bytes 49184 | tf_op jit(solution)/shard_map/ppermute | solution.py:297
  22.7 0.8 %subtract_convert_fusion.2 = (bf16[48,64]{1,0:T(8,128)(2,1)S(1)}, bf16[48,64]{1,0:T(8,128)(2,1)S(1)}) fusion(f32[48,64]{1,0:T(8,128)S(1)} %get-tuple-element.61, f32[48,64]{1,0:T(8,128)} %get-tuple-element.60, f32[48,256]{1,0:T(8,128)S(1)} %add.227), kind=kLoop, calls=%fused_computation.36 | loop fusion | flops 24576 | bytes 61440 | tf_op jit(solution)/shard_map/convert.7
  23.6 3.0 %collective-permute-start.4 = (bf16[48,256]{1,0:T(8,128)(2,1)S(1)}, bf16[48,256]{1,0:T(8,128)(2,1)S(1)}, u32[]{:S(2)}, u32[]{:S(2)}) collective-permute-start(bf16[48,256]{1,0:T(8,128)(2,1)S(1)} %pad_maximum_fusion.12), channel_id=1, source_target_pairs={{0,16},{2,18},{4,20},{6,22},{8,24},{10,26},{12,28},{14,30},{16,0},... | collective-permute-start | bytes 73736 | tf_op jit(solution)/shard_map/ppermute | solution.py:319
  26.6 0.7 xor_multiply_fusion
  27.2 1.7 %collective-permute-start.6 = (bf16[16,8192]{1,0:T(8,128)(2,1)S(1)}, bf16[16,8192]{1,0:T(8,128)(2,1)S(1)}, u32[]{:S(2)}, u32[]{:S(2)}) collective-permute-start(bf16[16,8192]{1,0:T(8,128)(2,1)S(1)} %constant_dynamic-slice_fusion.3), channel_id=1, source_target_pairs={{0,1},{1,0},{2,3},{3,2},{4,5},{5,4},{6,7},{7,6},{8,9},{9,8},{10,11... | collective-permute-start | bytes 786440 | tf_op jit(solution)/shard_map/ppermute | solution.py:206
  29.0 0.4 fusion.11
  29.4 0.4 fusion.10
  29.8 1.6 %collective-permute-start.8 = (bf16[96,256]{1,0:T(8,128)(2,1)S(1)}, bf16[96,256]{1,0:T(8,128)(2,1)S(1)}, u32[]{:S(2)}, u32[]{:S(2)}) collective-permute-start(bf16[96,256]{1,0:T(8,128)(2,1)S(1)} %pad_maximum_fusion.9), channel_id=1, source_target_pairs={{0,8},{2,10},{4,12},{6,14},{8,0},{10,2},{12,4},{14,6},{16,24},{18,... | collective-permute-start | bytes 147464 | tf_op jit(solution)/shard_map/ppermute | solution.py:319
  32.2 1.4 %collective-permute-done.6 = bf16[16,8192]{1,0:T(8,128)(2,1)S(1)} collective-permute-done((bf16[16,8192]{1,0:T(8,128)(2,1)S(1)}, bf16[16,8192]{1,0:T(8,128)(2,1)S(1)}, u32[]{:S(2)}, u32[]{:S(2)}) %collective-permute-start.6) | collective-permute-done | bytes 262176 | tf_op jit(solution)/shard_map/ppermute | solution.py:206
  33.6 0.4 fusion.15
  34.0 0.4 fusion.14
  34.5 1.8 %collective-permute-start.7 = (f32[80,256]{1,0:T(8,128)S(1)}, f32[80,256]{1,0:T(8,128)S(1)}, u32[]{:S(2)}, u32[]{:S(2)}) collective-permute-start(f32[80,256]{1,0:T(8,128)S(1)} %pad_maximum_fusion.5), channel_id=1, source_target_pairs={{0,1},{1,0},{2,3},{3,2},{4,5},{5,4},{6,7},{7,6},{8,9},{9,8},{10,11... | collective-permute-start | bytes 245768 | tf_op jit(solution)/shard_map/ppermute | solution.py:297
  36.3 1.6 %collective-permute-start.10 = (bf16[192,256]{1,0:T(8,128)(2,1)S(1)}, bf16[192,256]{1,0:T(8,128)(2,1)S(1)}, u32[]{:S(2)}, u32[]{:S(2)}) collective-permute-start(bf16[192,256]{1,0:T(8,128)(2,1)S(1)} %pad_maximum_fusion.4), channel_id=1, source_target_pairs={{0,4},{2,6},{4,0},{6,2},{8,12},{10,14},{12,8},{14,10},{16,20},{18,... | collective-permute-start | bytes 294920 | tf_op jit(solution)/shard_map/ppermute | solution.py:319
  37.9 1.1 %collective-permute-done.7 = f32[80,256]{1,0:T(8,128)S(1)} collective-permute-done((f32[80,256]{1,0:T(8,128)S(1)}, f32[80,256]{1,0:T(8,128)S(1)}, u32[]{:S(2)}, u32[]{:S(2)}) %collective-permute-start.7) | collective-permute-done | bytes 81952 | tf_op jit(solution)/shard_map/ppermute | solution.py:297
  39.2 1.2 %collective-permute-start.9 = (bf16[80,256]{1,0:T(8,128)(2,1)S(1)}, bf16[80,256]{1,0:T(8,128)(2,1)S(1)}, u32[]{:S(2)}, u32[]{:S(2)}) collective-permute-start(bf16[80,256]{1,0:T(8,128)(2,1)S(1)} %pad_maximum_fusion.10), channel_id=1, source_target_pairs={{0,16},{2,18},{4,20},{6,22},{8,24},{10,26},{12,28},{14,30},{16,0},... | collective-permute-start | bytes 122888 | tf_op jit(solution)/shard_map/ppermute | solution.py:319
  40.4 0.6 collective-permute-done.10
  41.1 0.7 %copy-done.3 = bf16[384,256]{1,0:T(8,128)(2,1)} copy-done((bf16[384,256]{1,0:T(8,128)(2,1)}, bf16[384,256]{1,0:T(8,128)(2,1)S(1)}, u32[]{:S(2)}) %copy-start.3) | copy-done | bytes 196632
  41.8 2.4 %collective-permute-done.9 = bf16[80,256]{1,0:T(8,128)(2,1)S(1)} collective-permute-done((bf16[80,256]{1,0:T(8,128)(2,1)S(1)}, bf16[80,256]{1,0:T(8,128)(2,1)S(1)}, u32[]{:S(2)}, u32[]{:S(2)}) %collective-permute-start.9) | collective-permute-done | bytes 40992 | tf_op jit(solution)/shard_map/ppermute | solution.py:319
  44.2 1.6 %collective-permute-start.11 = (bf16[160,256]{1,0:T(8,128)(2,1)S(1)}, bf16[160,256]{1,0:T(8,128)(2,1)}, u32[]{:S(2)}, u32[]{:S(2)}) collective-permute-start(bf16[160,256]{1,0:T(8,128)(2,1)S(1)} %pad_maximum_fusion.6), channel_id=1, source_target_pairs={{0,8},{2,10},{4,12},{6,14},{8,0},{10,2},{12,4},{14,6},{16,24},{18,... | collective-permute-start | bytes 245768 | tf_op jit(solution)/shard_map/ppermute | solution.py:319
  45.9 0.7 %copy-done.5 = bf16[384,256]{1,0:T(8,128)(2,1)} copy-done((bf16[384,256]{1,0:T(8,128)(2,1)}, bf16[384,256]{1,0:T(8,128)(2,1)S(1)}, u32[]{:S(2)}) %copy-start.5) | copy-done | bytes 196632
  46.6 0.9 %copy-done.4 = bf16[384,256]{1,0:T(8,128)(2,1)S(1)} copy-done((bf16[384,256]{1,0:T(8,128)(2,1)S(1)}, bf16[384,256]{1,0:T(8,128)(2,1)}, u32[]{:S(2)}) %copy-start.4) | copy-done | bytes 196632
  47.5 0.9 %copy-done.6 = bf16[384,256]{1,0:T(8,128)(2,1)S(1)} copy-done((bf16[384,256]{1,0:T(8,128)(2,1)S(1)}, bf16[384,256]{1,0:T(8,128)(2,1)}, u32[]{:S(2)}) %copy-start.6) | copy-done | bytes 196632
  48.4 1.9 %attend_part.1 = (f32[1024,1]{1,0:T(8,128)S(1)}, f32[1024,1]{1,0:T(8,128)S(1)}, f32[1024,128]{1,0:T(8,128)S(1)}) custom-call(s32[3]{0:T(128)S(1)} %pad_add_fusion.span_ref, s32[1,768]{1,0:T(1,128)S(1)} %add.240.place_ref, bf16[1024,128]{1,0:T(8,128)(2,1)S(1)} %pad_maximum_fusion.1.query_ref, bf16[384,256]{1,0:T(8,128)(2,1)S(1)} %copy-done.4, ...), custom_call_target="tpu_custom_call" | custom-call | flops 402653184 | bytes 917504 | tf_op jit(solution)/shard_map/attend_part/pallas_call | solution.py:141
  50.3 0.8 %copy-done.1 = f32[1024,128]{1,0:T(8,128)} copy-done((f32[1024,128]{1,0:T(8,128)}, f32[1024,128]{1,0:T(8,128)S(1)}, u32[]{:S(2)}) %copy-start.1) | copy-done | bytes 524312
  51.1 1.6 %pad_maximum_fusion.3 = bf16[320,256]{1,0:T(8,128)(2,1)} fusion(bf16[160,256]{1,0:T(8,128)(2,1)} %collective-permute-done.11, bf16[160,256]{1,0:T(8,128)(2,1)S(1)} %pad_maximum_fusion.6), kind=kLoop, calls=%fused_computation.11 | loop fusion | flops 327680 | bytes 327680 | tf_op jit(solution)/shard_map/concatenate | solution.py:314
  52.7 1.5 %collective-permute-start.13 = (bf16[320,256]{1,0:T(8,128)(2,1)}, bf16[320,256]{1,0:T(8,128)(2,1)}, u32[]{:S(2)}, u32[]{:S(2)}) collective-permute-start(bf16[320,256]{1,0:T(8,128)(2,1)} %pad_maximum_fusion.3), channel_id=1, source_target_pairs={{0,4},{2,6},{4,0},{6,2},{8,12},{10,14},{12,8},{14,10},{16,20},{18,... | collective-permute-start | bytes 491528 | tf_op jit(solution)/shard_map/ppermute | solution.py:319
  54.4 4.0 %collective-permute-done.13 = bf16[320,256]{1,0:T(8,128)(2,1)} collective-permute-done((bf16[320,256]{1,0:T(8,128)(2,1)}, bf16[320,256]{1,0:T(8,128)(2,1)}, u32[]{:S(2)}, u32[]{:S(2)}) %collective-permute-start.13) | collective-permute-done | bytes 163872 | tf_op jit(solution)/shard_map/ppermute | solution.py:319
  58.3 1.0 %pad_maximum_fusion.refs_0_ = bf16[640,256]{1,0:T(8,128)(2,1)S(1)} fusion(bf16[320,256]{1,0:T(8,128)(2,1)} %collective-permute-done.13, bf16[320,256]{1,0:T(8,128)(2,1)} %pad_maximum_fusion.3), kind=kLoop, calls=%fused_computation.8 | loop fusion | flops 655360 | bytes 655360 | tf_op jit(solution)/shard_map/concatenate | solution.py:314
  59.4 0.7 %constant_dynamic-slice_fusion.1 = bf16[24,256]{1,0:T(8,128)(2,1)S(1)} fusion(bf16[48,256]{1,0:T(8,128)(2,1)} %copy-done.13, s32[]{:T(128)S(6)} %select_n.45), kind=kLoop, calls=%fused_computation.45 | loop fusion | bytes 24580 | tf_op jit(solution)/shard_map/dynamic_slice | solution.py:309
  60.2 0.6 pad_maximum_fusion.11
  61.1 1.0 %copy-done.2 = f32[1024,128]{1,0:T(8,128)S(1)} copy-done((f32[1024,128]{1,0:T(8,128)S(1)}, f32[1024,128]{1,0:T(8,128)}, u32[]{:S(2)}) %copy-start.2) | copy-done | bytes 524312
  62.1 3.8 %attend_last.1 = bf16[64,2048]{1,0:T(8,128)(2,1)} custom-call(s32[3]{0:T(128)S(1)} %pad_add_fusion.span_ref, s32[1,1280]{1,0:T(1,128)S(1)} %add.236.place_ref, bf16[1024,128]{1,0:T(8,128)(2,1)S(1)} %pad_maximum_fusion.1.query_ref, bf16[640,256]{1,0:T(8,128)(2,1)S(1)} %pad_maximum_fusion.refs_0_, bf16[640,256]{1,0:T(8,128)(2,1)S(1)} %collective-permute-done.14.refs_1_, ...), custom_call_target="tpu_custom_call" | custom-call | flops 671088640 | bytes 1179648 | tf_op jit(solution)/shard_map/attend_last/pallas_call | solution.py:141
  (79 shorter events, 4.2 us)
Async XLA Ops:
  0.6 1.6 %copy-start = (bf16[64,16384]{1,0:T(8,128)(2,1)S(1)}, bf16[64,16384]{1,0:T(8,128)(2,1)}, u32[]{:S(2)}) copy-start(bf16[64,16384]{1,0:T(8,128)(2,1)} %param.6) | copy-start | bytes 6291460
  2.9 10.9 %collective-permute-start = (bf16[8,8192]{1,0:T(8,128)(2,1)}, bf16[8,8192]{1,0:T(8,128)(2,1)S(1)}, u32[]{:S(2)}, u32[]{:S(2)}) collective-permute-start(bf16[8,8192]{1,0:T(8,128)(2,1)} %constant_dynamic-slice_fusion.2), channel_id=1, source_target_pairs={{0,1},{1,0},{2,3},{3,2},{4,5},{5,4},{6,7},{7,6},{8,9},{9,8},{10,11... | collective-permute-start | bytes 393224 | tf_op jit(solution)/shard_map/ppermute | solution.py:206
  6.6 9.8 %collective-permute-start.1 = (bf16[16,8192]{1,0:T(8,128)(2,1)}, bf16[16,8192]{1,0:T(8,128)(2,1)S(1)}, u32[]{:S(2)}, u32[]{:S(2)}) collective-permute-start(bf16[16,8192]{1,0:T(8,128)(2,1)} %constant_dynamic-slice_fusion.6), channel_id=1, source_target_pairs={{0,1},{1,0},{2,3},{3,2},{4,5},{5,4},{6,7},{7,6},{8,9},{9,8},{10,11... | collective-permute-start | bytes 786440 | tf_op jit(solution)/shard_map/ppermute | solution.py:206
  6.6 15.0 %collective-permute-start.3 = (bf16[16,8192]{1,0:T(8,128)(2,1)S(1)}, bf16[16,8192]{1,0:T(8,128)(2,1)S(1)}, u32[]{:S(2)}, u32[]{:S(2)}) collective-permute-start(bf16[16,8192]{1,0:T(8,128)(2,1)S(1)} %constant_dynamic-slice_fusion.5), channel_id=1, source_target_pairs={{0,1},{1,0},{2,3},{3,2},{4,5},{5,4},{6,7},{7,6},{8,9},{9,8},{10,11... | collective-permute-start | bytes 786440 | tf_op jit(solution)/shard_map/ppermute | solution.py:206
  8.9 3.4 %copy-start.15 = (s32[48]{0:T(128)}, s32[48]{0:T(128)S(1)}, u32[]{:S(2)}) copy-start(s32[48]{0:T(128)S(1)} %add.214) | copy-start | bytes 580
  9.5 2.3 %copy-start.9 = (bf16[8192,128]{1,0:T(8,128)(2,1)S(1)}, bf16[8192,128]{1,0:T(8,128)(2,1)}, u32[]{:S(2)}) copy-start(bf16[8192,128]{1,0:T(8,128)(2,1)} %param.8) | copy-start | bytes 6291460
  13.8 2.2 %copy-start.10 = (bf16[8192,128]{1,0:T(8,128)(2,1)S(1)}, bf16[8192,128]{1,0:T(8,128)(2,1)}, u32[]{:S(2)}) copy-start(bf16[8192,128]{1,0:T(8,128)(2,1)} %param.8) | copy-start | bytes 6291460
  13.8 2.8 %copy-start.7 = (bf16[8192,128]{1,0:T(8,128)(2,1)S(1)}, bf16[8192,128]{1,0:T(8,128)(2,1)}, u32[]{:S(2)}) copy-start(bf16[8192,128]{1,0:T(8,128)(2,1)} %param.9) | copy-start | bytes 6291460
  16.4 4.3 %copy-start.12 = (bf16[64,2048]{1,0:T(8,128)(2,1)S(1)}, bf16[64,2048]{1,0:T(8,128)(2,1)}, u32[]{:S(2)}) copy-start(bf16[64,2048]{1,0:T(8,128)(2,1)} %param.7) | copy-start | bytes 786436
  17.5 11.5 %copy-start.8 = (bf16[8192,128]{1,0:T(8,128)(2,1)S(1)}, bf16[8192,128]{1,0:T(8,128)(2,1)}, u32[]{:S(2)}) copy-start(bf16[8192,128]{1,0:T(8,128)(2,1)} %param.9) | copy-start | bytes 6291460
  17.5 5.2 %collective-permute-start.2 = (f32[48,256]{1,0:T(8,128)S(1)}, f32[48,256]{1,0:T(8,128)S(1)}, u32[]{:S(2)}, u32[]{:S(2)}) collective-permute-start(f32[48,256]{1,0:T(8,128)S(1)} %pad_maximum_fusion.8), channel_id=1, source_target_pairs={{0,1},{1,0},{2,3},{3,2},{4,5},{5,4},{6,7},{7,6},{8,9},{9,8},{10,11... | collective-permute-start | bytes 147464 | tf_op jit(solution)/shard_map/ppermute | solution.py:297
  20.0 8.9 %collective-permute-start.5 = (bf16[8,8192]{1,0:T(8,128)(2,1)}, bf16[8,8192]{1,0:T(8,128)(2,1)S(1)}, u32[]{:S(2)}, u32[]{:S(2)}) collective-permute-start(bf16[8,8192]{1,0:T(8,128)(2,1)} %constant_dynamic-slice_fusion.4), channel_id=1, source_target_pairs={{0,1},{1,0},{2,3},{3,2},{4,5},{5,4},{6,7},{7,6},{8,9},{9,8},{10,11... | collective-permute-start | bytes 393224 | tf_op jit(solution)/shard_map/ppermute | solution.py:206
  21.0 8.4 %copy-start.11 = (bf16[8192,128]{1,0:T(8,128)(2,1)S(1)}, bf16[8192,128]{1,0:T(8,128)(2,1)}, u32[]{:S(2)}) copy-start(bf16[8192,128]{1,0:T(8,128)(2,1)} %param.8) | copy-start | bytes 6291460
  23.6 10.8 %copy-start.13 = (bf16[48,256]{1,0:T(8,128)(2,1)}, bf16[48,256]{1,0:T(8,128)(2,1)S(1)}, u32[]{:S(2)}) copy-start(bf16[48,256]{1,0:T(8,128)(2,1)S(1)} %pad_maximum_fusion.12) | copy-start | bytes 73732
  23.6 5.4 %collective-permute-start.4 = (bf16[48,256]{1,0:T(8,128)(2,1)S(1)}, bf16[48,256]{1,0:T(8,128)(2,1)S(1)}, u32[]{:S(2)}, u32[]{:S(2)}) collective-permute-start(bf16[48,256]{1,0:T(8,128)(2,1)S(1)} %pad_maximum_fusion.12), channel_id=1, source_target_pairs={{0,16},{2,18},{4,20},{6,22},{8,24},{10,26},{12,28},{14,30},{16,0},... | collective-permute-start | bytes 73736 | tf_op jit(solution)/shard_map/ppermute | solution.py:319
  27.2 6.4 %collective-permute-start.6 = (bf16[16,8192]{1,0:T(8,128)(2,1)S(1)}, bf16[16,8192]{1,0:T(8,128)(2,1)S(1)}, u32[]{:S(2)}, u32[]{:S(2)}) collective-permute-start(bf16[16,8192]{1,0:T(8,128)(2,1)S(1)} %constant_dynamic-slice_fusion.3), channel_id=1, source_target_pairs={{0,1},{1,0},{2,3},{3,2},{4,5},{5,4},{6,7},{7,6},{8,9},{9,8},{10,11... | collective-permute-start | bytes 786440 | tf_op jit(solution)/shard_map/ppermute | solution.py:206
  29.8 6.5 %collective-permute-start.8 = (bf16[96,256]{1,0:T(8,128)(2,1)S(1)}, bf16[96,256]{1,0:T(8,128)(2,1)S(1)}, u32[]{:S(2)}, u32[]{:S(2)}) collective-permute-start(bf16[96,256]{1,0:T(8,128)(2,1)S(1)} %pad_maximum_fusion.9), channel_id=1, source_target_pairs={{0,8},{2,10},{4,12},{6,14},{8,0},{10,2},{12,4},{14,6},{16,24},{18,... | collective-permute-start | bytes 147464 | tf_op jit(solution)/shard_map/ppermute | solution.py:319
  34.0 11.7 %copy-start.16 = (s32[48]{0:T(128)S(1)}, s32[48]{0:T(128)}, u32[]{:S(2)}) copy-start(s32[48]{0:T(128)} %copy-done.15) | copy-start | bytes 580
  34.4 19.8 %copy-start.14 = (s32[80]{0:T(128)S(1)}, s32[80]{0:T(128)}, u32[]{:S(2)}) copy-start(s32[80]{0:T(128)} %add.225) | copy-start | bytes 964
  34.5 4.5 %collective-permute-start.7 = (f32[80,256]{1,0:T(8,128)S(1)}, f32[80,256]{1,0:T(8,128)S(1)}, u32[]{:S(2)}, u32[]{:S(2)}) collective-permute-start(f32[80,256]{1,0:T(8,128)S(1)} %pad_maximum_fusion.5), channel_id=1, source_target_pairs={{0,1},{1,0},{2,3},{3,2},{4,5},{5,4},{6,7},{7,6},{8,9},{9,8},{10,11... | collective-permute-start | bytes 245768 | tf_op jit(solution)/shard_map/ppermute | solution.py:297
  36.3 4.7 %collective-permute-start.10 = (bf16[192,256]{1,0:T(8,128)(2,1)S(1)}, bf16[192,256]{1,0:T(8,128)(2,1)S(1)}, u32[]{:S(2)}, u32[]{:S(2)}) collective-permute-start(bf16[192,256]{1,0:T(8,128)(2,1)S(1)} %pad_maximum_fusion.4), channel_id=1, source_target_pairs={{0,4},{2,6},{4,0},{6,2},{8,12},{10,14},{12,8},{14,10},{16,20},{18,... | collective-permute-start | bytes 294920 | tf_op jit(solution)/shard_map/ppermute | solution.py:319
  39.2 5.0 %collective-permute-start.9 = (bf16[80,256]{1,0:T(8,128)(2,1)S(1)}, bf16[80,256]{1,0:T(8,128)(2,1)S(1)}, u32[]{:S(2)}, u32[]{:S(2)}) collective-permute-start(bf16[80,256]{1,0:T(8,128)(2,1)S(1)} %pad_maximum_fusion.10), channel_id=1, source_target_pairs={{0,16},{2,18},{4,20},{6,22},{8,24},{10,26},{12,28},{14,30},{16,0},... | collective-permute-start | bytes 122888 | tf_op jit(solution)/shard_map/ppermute | solution.py:319
  41.0 4.9 %collective-permute-start.12 = (bf16[384,256]{1,0:T(8,128)(2,1)S(1)}, bf16[384,256]{1,0:T(8,128)(2,1)S(1)}, u32[]{:S(2)}, u32[]{:S(2)}) collective-permute-start(bf16[384,256]{1,0:T(8,128)(2,1)S(1)} %pad_maximum_fusion.2.refs_0_), channel_id=1, source_target_pairs={{0,2},{2,0},{4,6},{6,4},{8,10},{10,8},{12,14},{14,12},{16,18},{18,... | collective-permute-start | bytes 589832 | tf_op jit(solution)/shard_map/ppermute | solution.py:319
  41.1 0.7 %copy-start.3 = (bf16[384,256]{1,0:T(8,128)(2,1)}, bf16[384,256]{1,0:T(8,128)(2,1)S(1)}, u32[]{:S(2)}) copy-start(bf16[384,256]{1,0:T(8,128)(2,1)S(1)} %pad_maximum_fusion.2.refs_0_) | copy-start | bytes 589828
  44.2 7.0 %collective-permute-start.11 = (bf16[160,256]{1,0:T(8,128)(2,1)S(1)}, bf16[160,256]{1,0:T(8,128)(2,1)}, u32[]{:S(2)}, u32[]{:S(2)}) collective-permute-start(bf16[160,256]{1,0:T(8,128)(2,1)S(1)} %pad_maximum_fusion.6), channel_id=1, source_target_pairs={{0,8},{2,10},{4,12},{6,14},{8,0},{10,2},{12,4},{14,6},{16,24},{18,... | collective-permute-start | bytes 245768 | tf_op jit(solution)/shard_map/ppermute | solution.py:319
  45.9 0.7 %copy-start.5 = (bf16[384,256]{1,0:T(8,128)(2,1)}, bf16[384,256]{1,0:T(8,128)(2,1)S(1)}, u32[]{:S(2)}) copy-start(bf16[384,256]{1,0:T(8,128)(2,1)S(1)} %collective-permute-done.12.refs_1_) | copy-start | bytes 589828
  46.6 0.9 %copy-start.4 = (bf16[384,256]{1,0:T(8,128)(2,1)S(1)}, bf16[384,256]{1,0:T(8,128)(2,1)}, u32[]{:S(2)}) copy-start(bf16[384,256]{1,0:T(8,128)(2,1)} %copy-done.3) | copy-start | bytes 589828
  47.5 0.9 %copy-start.6 = (bf16[384,256]{1,0:T(8,128)(2,1)S(1)}, bf16[384,256]{1,0:T(8,128)(2,1)}, u32[]{:S(2)}) copy-start(bf16[384,256]{1,0:T(8,128)(2,1)} %copy-done.5) | copy-start | bytes 589828
  50.3 0.8 %copy-start.1 = (f32[1024,128]{1,0:T(8,128)}, f32[1024,128]{1,0:T(8,128)S(1)}, u32[]{:S(2)}) copy-start(f32[1024,128]{1,0:T(8,128)S(1)} %get-tuple-element.83.refs_4_) | copy-start | bytes 1572868
  52.7 5.6 %collective-permute-start.13 = (bf16[320,256]{1,0:T(8,128)(2,1)}, bf16[320,256]{1,0:T(8,128)(2,1)}, u32[]{:S(2)}, u32[]{:S(2)}) collective-permute-start(bf16[320,256]{1,0:T(8,128)(2,1)} %pad_maximum_fusion.3), channel_id=1, source_target_pairs={{0,4},{2,6},{4,0},{6,2},{8,12},{10,14},{12,8},{14,10},{16,20},{18,... | collective-permute-start | bytes 491528 | tf_op jit(solution)/shard_map/ppermute | solution.py:319
  59.4 1.7 %collective-permute-start.14 = (bf16[640,256]{1,0:T(8,128)(2,1)S(1)}, bf16[640,256]{1,0:T(8,128)(2,1)S(1)}, u32[]{:S(2)}, u32[]{:S(2)}) collective-permute-start(bf16[640,256]{1,0:T(8,128)(2,1)S(1)} %pad_maximum_fusion.refs_0_), channel_id=1, source_target_pairs={{0,2},{2,0},{4,6},{6,4},{8,10},{10,8},{12,14},{14,12},{16,18},{18,... | collective-permute-start | bytes 983048 | tf_op jit(solution)/shard_map/ppermute | solution.py:319
  61.1 1.0 %copy-start.2 = (f32[1024,128]{1,0:T(8,128)S(1)}, f32[1024,128]{1,0:T(8,128)}, u32[]{:S(2)}) copy-start(f32[1024,128]{1,0:T(8,128)} %copy-done.1) | copy-start | bytes 1572868

commit v13 on v11

--- a/solution.py
+++ b/solution.py
@@ -40,11 +40,10 @@
     first = span_ref[1]
     factor = head_size ** (-0.5) * math.log2(math.e)
     flat = query_ref.shape[0]
-    blocks = []
-    size = sum(piece.shape[0] for piece in pieces) // len(order)
-    for piece in pieces:
-        blocks.extend(piece[top : top + size, :] for top in range(0, piece.shape[0], size))
-    ordered = [blocks[index] for index in order]
+    ordered = []
+    for index, slot in order:
+        size = pieces[index].shape[0] * len(pieces) // len(order)
+        ordered.append(pieces[index][slot * size : (slot + 1) * size, :])
     everything = jnp.concatenate(ordered, axis=0)
 
     def run(width):
@@ -155,7 +154,7 @@
         + [whole] * (2 + len(pieces) + (0 if state is None else 3)),
         out_specs=out_specs,
         scratch_shapes=scratch,
-        compiler_params=pltpu.CompilerParams(vmem_limit_bytes=32 * 1024 * 1024),
+        compiler_params=pltpu.CompilerParams(vmem_limit_bytes=24 * 1024 * 1024),
         cost_estimate=pl.CostEstimate(
             flops=4 * flat * width * head_size,
             bytes_accessed=4 * flat * head_size + 4 * width * head_size,
@@ -320,16 +319,6 @@
                 part.masks = part.masks + [mask ^ bit for mask in part.masks]
             part.stage += 1
 
-        def absorb(part, pieces, masks, own, state, last, *gate):
-            local_pos = places_of(part.top, part.rows)
-            order = sorted(range(len(masks)), key=lambda index: masks[index] & top_bit)
-            turns = jnp.array([masks[index] for index in order], jnp.int32)
-            place = (context ^ turns)[:, None] * group_rows + local_pos[None, :]
-            query = after(query_flat, *gate)
-            return attend(
-                span, place.reshape(1, -1), query, pieces, tuple(order), own, state, last, rows
-            )
-
         exchange(early, own_product)
         for columns in kept:
             flying.append(send(columns, early.sums))
@@ -346,28 +335,47 @@
         top_bit = stages[0]
         upper = ((context & top_bit) != 0).astype(jnp.int32)
         span = jnp.stack([base, first, upper]).astype(jnp.int32)
-        query_flat, late.tables, span = lax.optimization_barrier((query_flat, late.tables, span))
-        combine(early, query_flat, *late.tables, *flying[early.end])
+        def halves(masks):
+            return sorted(range(len(masks)), key=lambda slot: masks[slot] & top_bit)
+
+        all_masks = [0]
+        for bit in stages:
+            all_masks = all_masks + [mask ^ bit for mask in all_masks]
+        sorted_slots = halves(all_masks)
+        middle = len(all_masks) // 2
+        turns = jnp.array([all_masks[slot] for slot in sorted_slots], jnp.int32)
+        sources = (context ^ turns)[:, None] * group_rows
+        spots = [
+            (sources + places_of(part.top, part.rows)[None, :]).reshape(-1) for part in parts
+        ]
+        cuts = [(0, 1), (1, middle), (middle, 2 * middle)]
+        place = jnp.concatenate(
+            [
+                spot[low * shards * part.rows : high * shards * part.rows]
+                for low, high in cuts
+                for spot, part in zip(spots, parts)
+            ]
+        ).reshape(1, -1)
+        order = tuple(
+            (2 * number + slot // middle, slot % middle)
+            for low, high in cuts
+            for number in range(len(parts))
+            for slot in sorted_slots[low:high]
+        )
+        query_flat, late.tables, span, place = lax.optimization_barrier(
+            (query_flat, late.tables, span, place)
+        )
+        exchange(late, query_flat)
+        combine(early, late.sums)
         advance(early)
-        exchange(late, early.known)
-        advance(early, late.sums)
         combine(late, early.known)
         advance(late)
-        for stage in range(2, len(stages)):
+        for stage in range(1, len(stages)):
             advance(early, late.known)
             advance(late, early.known)
-        state = absorb(
-            early,
-            [early.known] + early.fresh,
-            early.masks,
-            shards * early.rows,
-            None,
-            False,
-            late.known,
-        )
-        advance(late, *state)
-        attended = absorb(
-            late, [late.known] + late.fresh, late.masks, shards * late.rows, state, True
+        pieces = [early.known] + early.fresh + [late.known] + late.fresh
+        attended = attend(
+            span, place, query_flat, pieces, order, shards * rows, None, True, rows
         )
         kv_cache = jnp.concatenate([part.cache for part in parts], axis=0)
         return (kv_cache, attended)
@@ -378,7 +386,7 @@
 def solution(mesh):
     placed = (P(("ctx", "fsdp"), None), P(("ctx", "fsdp"), None), P("fsdp", None), P("fsdp", None))
     return jax.shard_map(
-        make_local(mesh.shape["ctx"], mesh.shape["fsdp"], ((1, 4), (2, 1))),
+        make_local(mesh.shape["ctx"], mesh.shape["fsdp"], ((1, 4), (3,))),
         mesh=mesh,
         in_specs=placed,
         out_specs=(P(("ctx", "fsdp"), None), P(("ctx", "fsdp"), None)),

time: 57.6 us -> 62.9 us (1.092)
  local copies, waits for them, and re-layouts: 4.06 us -> 11.4 us
  other arithmetic: 6.08 us -> 9.92 us
  starting transfers between devices: 19.9 us -> 16.8 us
  waiting for transfers between devices: 11.9 us -> 9.68 us
  Pallas kernels: 5.45 us -> 3.44 us
  matrix products: 8.87 us -> 10 us
    slice x0 -> x10, local copies, waits for them, and re-layouts: none -> 5.12 us  [local(): spot[low * shards * part.rows:high * shards * part.rows]]
    ppermute x4 -> x3, waiting for transfers between devices: 3.57 us -> 0.01 us  [send(): lax.ppermute(after(columns[step - 1], *earlier) if earlier else columns[s...]
    pallas_call x2 -> x1, Pallas kernels: 5.45 us -> 3.44 us  [attend(): pl.pallas_call(partial(attention_kernel, count=len(pieces), order=order,...]
    ppermute x8, waiting for transfers between devices: 5.65 us -> 7.33 us  [advance(): part.fresh = [lax.ppermute(part.known, 'ctx', pairs)]]
    ppermute x2, starting transfers between devices: 3.68 us -> 2.16 us  [exchange(): lax.ppermute(part.sums, 'fsdp', [(i, i ^ reach) for i in range(shards)])]
    ppermute x8, starting transfers between devices: 10.9 us -> 9.65 us  [advance(): part.fresh = [lax.ppermute(part.known, 'ctx', pairs)]]
    add x2, local copies, waits for them, and re-layouts: 0.17 us -> 1.39 us  [places_of(): turns[:, None] + jnp.arange(count, dtype=jnp.int32)[None, :]]
    add x2, other arithmetic: 0.14 us -> 1.34 us  [places_of(): turns[:, None] + jnp.arange(count, dtype=jnp.int32)[None, :]]
  transfers between devices with their start and end apart: 14 -> 13, of which waited for: 10 -> 8; matrix products, arithmetic and copies ran while one was open for 29% -> 44% of each run, Pallas kernels for 4% -> 0%
where the time goes in v13:
time: 62.9 us; the launch traced here: 62.3 us
  starting transfers between devices  16.8 us (27%)
  local copies, waits for them, and re-layouts  11.4 us (18%)
  matrix products  10 us (16%)
  other arithmetic  9.92 us (16%)
  waiting for transfers between devices  9.68 us (15%)
  Pallas kernels  3.44 us (5%)
  between operations  0.97 us (2%)
    dot_general x8, matrix products, project(): jnp.dot(columns, weight, preferred_element_type=jnp.float32)  10 us
    ppermute x8, starting transfers between devices, advance(): part.fresh = [lax.ppermute(part.known, 'ctx', pairs)]  9.65 us
    ppermute x8, waiting for transfers between devices, advance(): part.fresh = [lax.ppermute(part.known, 'ctx', pairs)]  7.33 us
    slice x10, local copies, waits for them, and re-layouts, local(): spot[low * shards * part.rows:high * shards * part.rows]  5.12 us
    ppermute x3, starting transfers between devices, send(): lax.ppermute(after(columns[step - 1], *earlier) if earlier else columns[s...  5.03 us
    pallas_call x1, Pallas kernels, attend(): pl.pallas_call(partial(attention_kernel, count=len(pieces), order=order,...  3.44 us
    unnamed x28, local copies, waits for them, and re-layouts  2.62 us
    ppermute x2, waiting for transfers between devices, exchange(): lax.ppermute(part.sums, 'fsdp', [(i, i ^ reach) for i in range(shards)])  2.34 us
  transfers between devices with their start and end apart: 13, of which 8 were waited for; matrix products, arithmetic and copies ran while one was open for 44% of the time, Pallas kernels for 0%

profile of v13, /device:TPU:0, one launch (start us, length us, event | category | flops | bytes accessed | tf_op | source)
XLA Modules:
  0.0 62.3 jit_solution(13807351180165667969)
XLA Ops:
  0.7 1.6 %copy-done = bf16[64,16384]{1,0:T(8,128)(2,1)S(1)} copy-done((bf16[64,16384]{1,0:T(8,128)(2,1)S(1)}, bf16[64,16384]{1,0:T(8,128)(2,1)}, u32[]{:S(2)}) %copy-start) | copy-done | bytes 2097176
  2.2 0.7 %constant_dynamic-slice_fusion.2 = bf16[8,8192]{1,0:T(8,128)(2,1)} fusion(bf16[64,16384]{1,0:T(8,128)(2,1)S(1)} %copy-done, s32[]{:T(128)S(6)} %select_n.39), kind=kLoop, calls=%fused_computation.47 | loop fusion | bytes 262148 | tf_op jit(solution)/shard_map/dynamic_slice | solution.py:195
  2.9 2.9 %collective-permute-start = (bf16[8,8192]{1,0:T(8,128)(2,1)}, bf16[8,8192]{1,0:T(8,128)(2,1)S(1)}, u32[]{:S(2)}, u32[]{:S(2)}) collective-permute-start(bf16[8,8192]{1,0:T(8,128)(2,1)} %constant_dynamic-slice_fusion.2), channel_id=1, source_target_pairs={{0,1},{1,0},{2,3},{3,2},{4,5},{5,4},{6,7},{7,6},{8,9},{9,8},{10,11... | collective-permute-start | bytes 393224 | tf_op jit(solution)/shard_map/ppermute | solution.py:205
  5.8 0.8 %constant_dynamic-slice_fusion.4 = bf16[32,8192]{1,0:T(8,128)(2,1)} fusion(bf16[64,16384]{1,0:T(8,128)(2,1)S(1)} %copy-done, s32[]{:T(128)S(6)} %select_n.39), kind=kLoop, calls=%fused_computation.59 | loop fusion | bytes 1048580 | tf_op jit(solution)/shard_map/dynamic_slice | solution.py:195
  6.7 2.1 %collective-permute-start.3 = (bf16[24,8192]{1,0:T(8,128)(2,1)S(1)}, bf16[24,8192]{1,0:T(8,128)(2,1)S(1)}, u32[]{:S(2)}, u32[]{:S(2)}) collective-permute-start(bf16[24,8192]{1,0:T(8,128)(2,1)S(1)} %constant_dynamic-slice_fusion.3), channel_id=1, source_target_pairs={{0,1},{1,0},{2,3},{3,2},{4,5},{5,4},{6,7},{7,6},{8,9},{9,8},{10,11... | collective-permute-start | bytes 1179656 | tf_op jit(solution)/shard_map/ppermute | solution.py:205
  8.8 0.6 multiply_power_fusion
  9.4 0.5 broadcast_add_fusion.2
  10.2 0.4 copy-done.12
  10.7 1.3 %iota_add_fusion = s32[2,24]{1,0:T(2,128)} fusion(s32[2]{0:T(128)} %broadcast_add_fusion.2), kind=kLoop, calls=%fused_computation.41 | loop fusion | flops 48 | bytes 200 | tf_op jit(solution)/shard_map/add | solution.py:215
  11.9 1.3 %add.201 = s32[48]{0:T(128)} reshape(s32[2,24]{1,0:T(2,128)} %iota_add_fusion) | data formatting | bytes 384 | tf_op jit(solution)/shard_map/add | solution.py:215
  13.3 0.7 %broadcast_add_fusion = s32[16,48]{1,0:T(8,128)S(1)} fusion(s32[48]{0:T(128)} %add.201, s32[16]{0:T(128)} %copy-done.10), kind=kLoop, calls=%fused_computation.39 | loop fusion | flops 768 | bytes 3328 | tf_op jit(solution)/shard_map/add | solution.py:349
  14.0 0.6 slice.101
  14.6 0.6 slice.103
  15.2 0.5 slice_bitcast_fusion
  15.7 2.9 %fusion.2 = f32[64,128]{1,0:T(8,128)} fusion(bf16[8192,128]{1,0:T(8,128)(2,1)} %param.7, bf16[64,16384]{1,0:T(8,128)(2,1)S(1)} %copy-done, s32[]{:T(128)S(6)} %select_n.40), kind=kOutput, calls=%fused_computation.2 | convolution fusion | flops 134217728 | bytes 3178500 | tf_op jit(solution)/shard_map/dot_general | solution.py:249
  18.5 1.1 %fusion = f32[64,128]{1,0:T(8,128)} fusion(bf16[8192,128]{1,0:T(8,128)(2,1)S(1)} %copy-done.3, bf16[64,16384]{1,0:T(8,128)(2,1)S(1)} %copy-done, s32[]{:T(128)S(6)} %select_n.40), kind=kOutput, calls=%fused_computation | convolution fusion | flops 134217728 | bytes 3178500 | tf_op jit(solution)/shard_map/dot_general | solution.py:249
  19.7 0.6 add_convert_fusion.5
  20.3 1.4 %pad_maximum_fusion.7 = f32[64,256]{1,0:T(8,128)} fusion(f32[64,128]{1,0:T(8,128)} %fusion, f32[64,128]{1,0:T(8,128)} %fusion.2), kind=kLoop, calls=%fused_computation.15 | loop fusion | flops 16384 | bytes 131072 | tf_op jit(solution)/shard_map/concatenate | solution.py:247
  21.7 1.5 %multiply_sine_fusion = (f32[80,64]{1,0:T(8,128)}, f32[80,64]{1,0:T(8,128)}) fusion(f32[64]{0:T(128)} %multiply_power_fusion, f32[80]{0:T(128)S(1)} %add_convert_fusion.5), kind=kLoop, calls=%fused_computation.16 | loop fusion | flops 5120 | bytes 41536 | tf_op jit(solution)/shard_map/sin | solution.py:29
  23.2 0.7 %slice.83 = s32[560]{0:T(1024)} reshape(s32[7,80]{1,0:T(8,128)S(1)} %slice.100) | data formatting | bytes 4480 | tf_op jit(solution)/shard_map/slice | solution.py:354
  23.9 0.8 %slice.85 = s32[336]{0:T(512)S(1)} reshape(s32[7,48]{1,0:T(8,128)} %slice.101) | data formatting | bytes 2688 | tf_op jit(solution)/shard_map/slice | solution.py:354
  24.7 1.3 %slice.89 = s32[384]{0:T(512)} reshape(s32[8,48]{1,0:T(8,128)} %slice.103) | data formatting | bytes 3072 | tf_op jit(solution)/shard_map/slice | solution.py:354
  26.0 0.6 slice_bitcast_fusion.1
  26.6 0.8 %concatenate.74 = s32[2048]{0:T(1024)S(1)} concatenate(s32[80]{0:T(128)} %slice_bitcast_fusion.1, s32[48]{0:T(128)} %slice_bitcast_fusion, s32[560]{0:T(1024)} %slice.83, s32[336]{0:T(512)S(1)} %slice.85, s32[640]{0:T(1024)S(1)} %slice.87, s32[384]{0:T(512)} %slice.89), dimensions={0} | concatenate | bytes 16384 | tf_op jit(solution)/shard_map/concatenate | solution.py:352
  27.4 2.1 %fusion.6 = f32[8,128]{1,0:T(8,128)S(1)} fusion(bf16[8,8192]{1,0:T(8,128)(2,1)S(1)} %collective-permute-done, bf16[8192,128]{1,0:T(8,128)(2,1)} %param.7), kind=kOutput, calls=%fused_computation.60 | convolution fusion | flops 16777216 | bytes 2232320 | tf_op jit(solution)/shard_map/dot_general | solution.py:249
  29.5 2.1 %fusion.7 = f32[8,128]{1,0:T(8,128)S(1)} fusion(bf16[8,8192]{1,0:T(8,128)(2,1)S(1)} %collective-permute-done, bf16[8192,128]{1,0:T(8,128)(2,1)} %param.8), kind=kOutput, calls=%fused_computation.61 | convolution fusion | flops 16777216 | bytes 2232320 | tf_op jit(solution)/shard_map/dot_general | solution.py:249
  31.7 0.5 fusion.8
  32.2 0.5 fusion.9
  32.7 1.1 %bitcast_bitcast_fusion = f32[16,64,128]{2,1,0:T(8,128)S(1)} fusion(bf16[64,2048]{1,0:T(8,128)(2,1)} %param.6), kind=kLoop, calls=%fused_computation.4 | loop fusion | flops 131072 | bytes 786432 | tf_op jit(solution)/shard_map/transpose | solution.py:329
  34.8 0.5 fusion.10
  35.2 0.5 copy-done.5
  35.8 0.4 fusion.11
  36.3 2.1 %collective-permute-start.4 = (f32[48,256]{1,0:T(8,128)S(1)}, f32[48,256]{1,0:T(8,128)S(1)}, u32[]{:S(2)}, u32[]{:S(2)}) collective-permute-start(f32[48,256]{1,0:T(8,128)S(1)} %pad_maximum_fusion.8), channel_id=1, source_target_pairs={{0,1},{1,0},{2,3},{3,2},{4,5},{5,4},{6,7},{7,6},{8,9},{9,8},{10,11... | collective-permute-start | bytes 147464 | tf_op jit(solution)/shard_map/ppermute | solution.py:296
  38.4 2.3 %collective-permute-done.2 = f32[80,256]{1,0:T(8,128)S(1)} collective-permute-done((f32[80,256]{1,0:T(8,128)S(1)}, f32[80,256]{1,0:T(8,128)S(1)}, u32[]{:S(2)}, u32[]{:S(2)}) %collective-permute-start.2) | collective-permute-done | bytes 81952 | tf_op jit(solution)/shard_map/ppermute | solution.py:296
  40.9 2.7 %collective-permute-start.5 = (bf16[80,256]{1,0:T(8,128)(2,1)S(1)}, bf16[80,256]{1,0:T(8,128)(2,1)S(1)}, u32[]{:S(2)}, u32[]{:S(2)}) collective-permute-start(bf16[80,256]{1,0:T(8,128)(2,1)S(1)} %pad_maximum_fusion.10), channel_id=1, source_target_pairs={{0,16},{2,18},{4,20},{6,22},{8,24},{10,26},{12,28},{14,30},{16,0},... | collective-permute-start | bytes 122888 | tf_op jit(solution)/shard_map/ppermute | solution.py:318
  43.8 0.4 collective-permute-start.7
  44.2 1.9 %collective-permute-done.5 = bf16[80,256]{1,0:T(8,128)(2,1)S(1)} collective-permute-done((bf16[80,256]{1,0:T(8,128)(2,1)S(1)}, bf16[80,256]{1,0:T(8,128)(2,1)S(1)}, u32[]{:S(2)}, u32[]{:S(2)}) %collective-permute-start.5) | collective-permute-done | bytes 40992 | tf_op jit(solution)/shard_map/ppermute | solution.py:318
  46.0 1.5 %collective-permute-start.6 = (bf16[160,256]{1,0:T(8,128)(2,1)S(1)}, bf16[160,256]{1,0:T(8,128)(2,1)S(1)}, u32[]{:S(2)}, u32[]{:S(2)}) collective-permute-start(bf16[160,256]{1,0:T(8,128)(2,1)S(1)} %pad_maximum_fusion.6), channel_id=1, source_target_pairs={{0,8},{2,10},{4,12},{6,14},{8,0},{10,2},{12,4},{14,6},{16,24},{18,... | collective-permute-start | bytes 245768 | tf_op jit(solution)/shard_map/ppermute | solution.py:318
  47.5 1.0 %collective-permute-done.7 = bf16[48,256]{1,0:T(8,128)(2,1)S(1)} collective-permute-done((bf16[48,256]{1,0:T(8,128)(2,1)S(1)}, bf16[48,256]{1,0:T(8,128)(2,1)S(1)}, u32[]{:S(2)}, u32[]{:S(2)}) %collective-permute-start.7) | collective-permute-done | bytes 24608 | tf_op jit(solution)/shard_map/ppermute | solution.py:318
  48.5 1.8 %collective-permute-start.9 = (bf16[96,256]{1,0:T(8,128)(2,1)S(1)}, bf16[96,256]{1,0:T(8,128)(2,1)S(1)}, u32[]{:S(2)}, u32[]{:S(2)}) collective-permute-start(bf16[96,256]{1,0:T(8,128)(2,1)S(1)} %pad_maximum_fusion.9), channel_id=1, source_target_pairs={{0,8},{2,10},{4,12},{6,14},{8,0},{10,2},{12,4},{14,6},{16,24},{18,... | collective-permute-start | bytes 147464 | tf_op jit(solution)/shard_map/ppermute | solution.py:318
  50.5 1.6 %collective-permute-start.8 = (bf16[320,256]{1,0:T(8,128)(2,1)S(1)}, bf16[320,256]{1,0:T(8,128)(2,1)S(1)}, u32[]{:S(2)}, u32[]{:S(2)}) collective-permute-start(bf16[320,256]{1,0:T(8,128)(2,1)S(1)} %pad_maximum_fusion.3), channel_id=1, source_target_pairs={{0,4},{2,6},{4,0},{6,2},{8,12},{10,14},{12,8},{14,10},{16,20},{18,... | collective-permute-start | bytes 491528 | tf_op jit(solution)/shard_map/ppermute | solution.py:318
  52.1 0.6 collective-permute-done.9
  52.6 1.6 %collective-permute-start.11 = (bf16[192,256]{1,0:T(8,128)(2,1)S(1)}, bf16[192,256]{1,0:T(8,128)(2,1)S(1)}, u32[]{:S(2)}, u32[]{:S(2)}) collective-permute-start(bf16[192,256]{1,0:T(8,128)(2,1)S(1)} %pad_maximum_fusion.4), channel_id=1, source_target_pairs={{0,4},{2,6},{4,0},{6,2},{8,12},{10,14},{12,8},{14,10},{16,20},{18,... | collective-permute-start | bytes 294920 | tf_op jit(solution)/shard_map/ppermute | solution.py:318
  54.2 1.7 %collective-permute-done.8 = bf16[320,256]{1,0:T(8,128)(2,1)S(1)} collective-permute-done((bf16[320,256]{1,0:T(8,128)(2,1)S(1)}, bf16[320,256]{1,0:T(8,128)(2,1)S(1)}, u32[]{:S(2)}, u32[]{:S(2)}) %collective-permute-start.8) | collective-permute-done | bytes 163872 | tf_op jit(solution)/shard_map/ppermute | solution.py:318
  56.0 1.3 %collective-permute-done.11 = bf16[192,256]{1,0:T(8,128)(2,1)S(1)} collective-permute-done((bf16[192,256]{1,0:T(8,128)(2,1)S(1)}, bf16[192,256]{1,0:T(8,128)(2,1)S(1)}, u32[]{:S(2)}, u32[]{:S(2)}) %collective-permute-start.11) | collective-permute-done | bytes 98336 | tf_op jit(solution)/shard_map/ppermute | solution.py:318
  57.4 0.6 pad_maximum_fusion.11
  58.1 0.8 %collective-permute-done.12.refs_3_ = bf16[384,256]{1,0:T(8,128)(2,1)S(1)} collective-permute-done((bf16[384,256]{1,0:T(8,128)(2,1)S(1)}, bf16[384,256]{1,0:T(8,128)(2,1)S(1)}, u32[]{:S(2)}, u32[]{:S(2)}) %collective-permute-start.12) | collective-permute-done | bytes 196640 | tf_op jit(solution)/shard_map/ppermute | solution.py:318
  58.9 3.4 %attend_last.1 = bf16[64,2048]{1,0:T(8,128)(2,1)} custom-call(s32[3]{0:T(128)S(1)} %pad_add_fusion.span_ref, s32[1,2048]{1,0:T(1,128)S(1)} %bitcast.31, bf16[1024,128]{1,0:T(8,128)(2,1)S(1)} %pad_maximum_fusion.1.query_ref, bf16[640,256]{1,0:T(8,128)(2,1)S(1)} %pad_maximum_fusion.refs_0_, bf16[640,256]{1,0:T(8,128)(2,1)S(1)} %collective-permute-done.10.refs_1_, ...), custom_call_target="tpu_custom_call" | custom-call | flops 1073741824 | bytes 1572864 | tf_op jit(solution)/shard_map/attend_last/pallas_call | solution.py:140
  (71 shorter events, 2.1 us)
Async XLA Ops:
  0.6 1.6 %copy-start = (bf16[64,16384]{1,0:T(8,128)(2,1)S(1)}, bf16[64,16384]{1,0:T(8,128)(2,1)}, u32[]{:S(2)}) copy-start(bf16[64,16384]{1,0:T(8,128)(2,1)} %param.5) | copy-start | bytes 6291460
  0.6 9.5 %copy-start.13 = (s32[16]{0:T(128)S(1)}, s32[16]{0:T(128)}, u32[]{:S(2)}) copy-start(s32[16]{0:T(128)} %constant.45.clone) | copy-start | bytes 196
  2.9 24.5 %collective-permute-start = (bf16[8,8192]{1,0:T(8,128)(2,1)}, bf16[8,8192]{1,0:T(8,128)(2,1)S(1)}, u32[]{:S(2)}, u32[]{:S(2)}) collective-permute-start(bf16[8,8192]{1,0:T(8,128)(2,1)} %constant_dynamic-slice_fusion.2), channel_id=1, source_target_pairs={{0,1},{1,0},{2,3},{3,2},{4,5},{5,4},{6,7},{7,6},{8,9},{9,8},{10,11... | collective-permute-start | bytes 393224 | tf_op jit(solution)/shard_map/ppermute | solution.py:205
  6.7 25.0 %collective-permute-start.1 = (bf16[32,8192]{1,0:T(8,128)(2,1)}, bf16[32,8192]{1,0:T(8,128)(2,1)S(1)}, u32[]{:S(2)}, u32[]{:S(2)}) collective-permute-start(bf16[32,8192]{1,0:T(8,128)(2,1)} %constant_dynamic-slice_fusion.4), channel_id=1, source_target_pairs={{0,1},{1,0},{2,3},{3,2},{4,5},{5,4},{6,7},{7,6},{8,9},{9,8},{10,11... | collective-permute-start | bytes 1572872 | tf_op jit(solution)/shard_map/ppermute | solution.py:205
  6.7 28.1 %collective-permute-start.3 = (bf16[24,8192]{1,0:T(8,128)(2,1)S(1)}, bf16[24,8192]{1,0:T(8,128)(2,1)S(1)}, u32[]{:S(2)}, u32[]{:S(2)}) collective-permute-start(bf16[24,8192]{1,0:T(8,128)(2,1)S(1)} %constant_dynamic-slice_fusion.3), channel_id=1, source_target_pairs={{0,1},{1,0},{2,3},{3,2},{4,5},{5,4},{6,7},{7,6},{8,9},{9,8},{10,11... | collective-permute-start | bytes 1179656 | tf_op jit(solution)/shard_map/ppermute | solution.py:205
  10.1 0.5 copy-start.12
  10.1 0.6 copy-start.10
  15.7 2.9 %copy-start.3 = (bf16[8192,128]{1,0:T(8,128)(2,1)S(1)}, bf16[8192,128]{1,0:T(8,128)(2,1)}, u32[]{:S(2)}) copy-start(bf16[8192,128]{1,0:T(8,128)(2,1)} %param.8) | copy-start | bytes 6291460
  27.4 4.3 %copy-start.1 = (bf16[8192,128]{1,0:T(8,128)(2,1)S(1)}, bf16[8192,128]{1,0:T(8,128)(2,1)}, u32[]{:S(2)}) copy-start(bf16[8192,128]{1,0:T(8,128)(2,1)} %param.7) | copy-start | bytes 6291460
  29.5 2.6 %copy-start.4 = (bf16[8192,128]{1,0:T(8,128)(2,1)S(1)}, bf16[8192,128]{1,0:T(8,128)(2,1)}, u32[]{:S(2)}) copy-start(bf16[8192,128]{1,0:T(8,128)(2,1)} %param.8) | copy-start | bytes 6291460
  31.7 1.0 %copy-start.6 = (f32[64,256]{1,0:T(8,128)S(1)}, f32[64,256]{1,0:T(8,128)}, u32[]{:S(2)}) copy-start(f32[64,256]{1,0:T(8,128)} %pad_maximum_fusion.7) | copy-start | bytes 196612
  32.2 1.7 %copy-start.9 = (f32[64]{0:T(128)S(1)}, f32[64]{0:T(128)}, u32[]{:S(2)}) copy-start(f32[64]{0:T(128)} %multiply_power_fusion) | copy-start | bytes 772
  32.2 1.9 %copy-start.11 = (s32[48]{0:T(128)S(1)}, s32[48]{0:T(128)}, u32[]{:S(2)}) copy-start(s32[48]{0:T(128)} %add.201) | copy-start | bytes 580
  32.7 2.1 %copy-start.2 = (bf16[8192,128]{1,0:T(8,128)(2,1)S(1)}, bf16[8192,128]{1,0:T(8,128)(2,1)}, u32[]{:S(2)}) copy-start(bf16[8192,128]{1,0:T(8,128)(2,1)} %param.7) | copy-start | bytes 6291460
  34.1 1.7 %copy-start.5 = (bf16[8192,128]{1,0:T(8,128)(2,1)S(1)}, bf16[8192,128]{1,0:T(8,128)(2,1)}, u32[]{:S(2)}) copy-start(bf16[8192,128]{1,0:T(8,128)(2,1)} %param.8) | copy-start | bytes 6291460
  35.7 5.0 %copy-start.7 = (f32[80,64]{1,0:T(8,128)S(1)}, f32[80,64]{1,0:T(8,128)}, u32[]{:S(2)}) copy-start(f32[80,64]{1,0:T(8,128)} %get-tuple-element.47) | copy-start | bytes 61444
  35.8 5.0 %copy-start.8 = (f32[80,64]{1,0:T(8,128)S(1)}, f32[80,64]{1,0:T(8,128)}, u32[]{:S(2)}) copy-start(f32[80,64]{1,0:T(8,128)} %get-tuple-element.46) | copy-start | bytes 61444
  36.2 4.5 %collective-permute-start.2 = (f32[80,256]{1,0:T(8,128)S(1)}, f32[80,256]{1,0:T(8,128)S(1)}, u32[]{:S(2)}, u32[]{:S(2)}) collective-permute-start(f32[80,256]{1,0:T(8,128)S(1)} %pad_maximum_fusion.5), channel_id=1, source_target_pairs={{0,1},{1,0},{2,3},{3,2},{4,5},{5,4},{6,7},{7,6},{8,9},{9,8},{10,11... | collective-permute-start | bytes 245768 | tf_op jit(solution)/shard_map/ppermute | solution.py:296
  36.3 7.3 %collective-permute-start.4 = (f32[48,256]{1,0:T(8,128)S(1)}, f32[48,256]{1,0:T(8,128)S(1)}, u32[]{:S(2)}, u32[]{:S(2)}) collective-permute-start(f32[48,256]{1,0:T(8,128)S(1)} %pad_maximum_fusion.8), channel_id=1, source_target_pairs={{0,1},{1,0},{2,3},{3,2},{4,5},{5,4},{6,7},{7,6},{8,9},{9,8},{10,11... | collective-permute-start | bytes 147464 | tf_op jit(solution)/shard_map/ppermute | solution.py:296
  40.9 5.1 %collective-permute-start.5 = (bf16[80,256]{1,0:T(8,128)(2,1)S(1)}, bf16[80,256]{1,0:T(8,128)(2,1)S(1)}, u32[]{:S(2)}, u32[]{:S(2)}) collective-permute-start(bf16[80,256]{1,0:T(8,128)(2,1)S(1)} %pad_maximum_fusion.10), channel_id=1, source_target_pairs={{0,16},{2,18},{4,20},{6,22},{8,24},{10,26},{12,28},{14,30},{16,0},... | collective-permute-start | bytes 122888 | tf_op jit(solution)/shard_map/ppermute | solution.py:318
  43.8 4.7 %collective-permute-start.7 = (bf16[48,256]{1,0:T(8,128)(2,1)S(1)}, bf16[48,256]{1,0:T(8,128)(2,1)S(1)}, u32[]{:S(2)}, u32[]{:S(2)}) collective-permute-start(bf16[48,256]{1,0:T(8,128)(2,1)S(1)} %pad_maximum_fusion.13), channel_id=1, source_target_pairs={{0,16},{2,18},{4,20},{6,22},{8,24},{10,26},{12,28},{14,30},{16,0},... | collective-permute-start | bytes 73736 | tf_op jit(solution)/shard_map/ppermute | solution.py:318
  46.0 4.4 %collective-permute-start.6 = (bf16[160,256]{1,0:T(8,128)(2,1)S(1)}, bf16[160,256]{1,0:T(8,128)(2,1)S(1)}, u32[]{:S(2)}, u32[]{:S(2)}) collective-permute-start(bf16[160,256]{1,0:T(8,128)(2,1)S(1)} %pad_maximum_fusion.6), channel_id=1, source_target_pairs={{0,8},{2,10},{4,12},{6,14},{8,0},{10,2},{12,4},{14,6},{16,24},{18,... | collective-permute-start | bytes 245768 | tf_op jit(solution)/shard_map/ppermute | solution.py:318
  48.5 4.1 %collective-permute-start.9 = (bf16[96,256]{1,0:T(8,128)(2,1)S(1)}, bf16[96,256]{1,0:T(8,128)(2,1)S(1)}, u32[]{:S(2)}, u32[]{:S(2)}) collective-permute-start(bf16[96,256]{1,0:T(8,128)(2,1)S(1)} %pad_maximum_fusion.9), channel_id=1, source_target_pairs={{0,8},{2,10},{4,12},{6,14},{8,0},{10,2},{12,4},{14,6},{16,24},{18,... | collective-permute-start | bytes 147464 | tf_op jit(solution)/shard_map/ppermute | solution.py:318
  50.5 5.4 %collective-permute-start.8 = (bf16[320,256]{1,0:T(8,128)(2,1)S(1)}, bf16[320,256]{1,0:T(8,128)(2,1)S(1)}, u32[]{:S(2)}, u32[]{:S(2)}) collective-permute-start(bf16[320,256]{1,0:T(8,128)(2,1)S(1)} %pad_maximum_fusion.3), channel_id=1, source_target_pairs={{0,4},{2,6},{4,0},{6,2},{8,12},{10,14},{12,8},{14,10},{16,20},{18,... | collective-permute-start | bytes 491528 | tf_op jit(solution)/shard_map/ppermute | solution.py:318
  52.6 4.7 %collective-permute-start.11 = (bf16[192,256]{1,0:T(8,128)(2,1)S(1)}, bf16[192,256]{1,0:T(8,128)(2,1)S(1)}, u32[]{:S(2)}, u32[]{:S(2)}) collective-permute-start(bf16[192,256]{1,0:T(8,128)(2,1)S(1)} %pad_maximum_fusion.4), channel_id=1, source_target_pairs={{0,4},{2,6},{4,0},{6,2},{8,12},{10,14},{12,8},{14,10},{16,20},{18,... | collective-permute-start | bytes 294920 | tf_op jit(solution)/shard_map/ppermute | solution.py:318
  55.9 2.9 %collective-permute-start.10 = (bf16[640,256]{1,0:T(8,128)(2,1)S(1)}, bf16[640,256]{1,0:T(8,128)(2,1)S(1)}, u32[]{:S(2)}, u32[]{:S(2)}) collective-permute-start(bf16[640,256]{1,0:T(8,128)(2,1)S(1)} %pad_maximum_fusion.refs_0_), channel_id=1, source_target_pairs={{0,2},{2,0},{4,6},{6,4},{8,10},{10,8},{12,14},{14,12},{16,18},{18,... | collective-permute-start | bytes 983048 | tf_op jit(solution)/shard_map/ppermute | solution.py:318
  57.3 1.5 %collective-permute-start.12 = (bf16[384,256]{1,0:T(8,128)(2,1)S(1)}, bf16[384,256]{1,0:T(8,128)(2,1)S(1)}, u32[]{:S(2)}, u32[]{:S(2)}) collective-permute-start(bf16[384,256]{1,0:T(8,128)(2,1)S(1)} %pad_maximum_fusion.2.refs_2_), channel_id=1, source_target_pairs={{0,2},{2,0},{4,6},{6,4},{8,10},{10,8},{12,14},{14,12},{16,18},{18,... | collective-permute-start | bytes 589832 | tf_op jit(solution)/shard_map/ppermute | solution.py:318

commit v14 on v13

--- a/solution.py
+++ b/solution.py
@@ -30,35 +30,44 @@
 
 
 def attention_kernel(
-    span_ref, place_ref, query_ref, *refs, count, order, carry, final, rows, own, head_size, stride
+    span_ref, query_ref, *refs, count, slots, owns, rows, head_size, stride
 ):
-    pieces, refs = refs[:count], refs[count:]
-    if carry:
-        old_peak, old_total, old_sum = refs[:3]
-        refs = refs[3:]
+    places, refs = refs[:count], refs[count:]
+    pieces, (out_ref, scratch) = refs[: 2 * count], refs[2 * count :]
     start = span_ref[0]
     first = span_ref[1]
     factor = head_size ** (-0.5) * math.log2(math.e)
     flat = query_ref.shape[0]
-    ordered = []
-    for index, slot in order:
-        size = pieces[index].shape[0] * len(pieces) // len(order)
-        ordered.append(pieces[index][slot * size : (slot + 1) * size, :])
-    everything = jnp.concatenate(ordered, axis=0)
-
-    def run(width):
-        keys = everything[:width, :head_size]
-        values = everything[:width, head_size:]
-        edge = min(width, -(-own // 128) * 128)
-        if edge:
+    middle = len(slots) // 2
+    sorted_parts = []
+    for number in range(count):
+        size = pieces[2 * number].shape[0] // middle
+        blocks = []
+        for slot in slots:
+            top = (slot % middle) * size
+            blocks.append(pieces[2 * number + slot // middle][top : top + size, :])
+        sorted_parts.append(jnp.concatenate(blocks, axis=0))
+
+    def run(share):
+        chosen = [part[: part.shape[0] // share, :] for part in sorted_parts]
+        everything = jnp.concatenate(chosen, axis=0)
+        keys = everything[:, :head_size]
+        values = everything[:, head_size:]
+        segments = []
+        top = 0
+        for part, place_ref, own in zip(chosen, places, owns):
+            width = part.shape[0]
+            edge = min(width, -(-own // 128) * 128)
             query_pos = first + lax.rem(
                 lax.broadcasted_iota(jnp.int32, (stride, edge), 0), jnp.int32(rows)
             )
             diagonal = place_ref[:, :edge] <= query_pos
-        bias = jnp.where(place_ref[:, :width] < start, 0.0, floor_value).astype(jnp.float32)
-
-        def one(part):
-            place = pl.ds(pl.multiple_of(part * stride, stride), stride)
+            bias = jnp.where(place_ref[:, edge:width] < start, 0.0, floor_value)
+            segments.append((top, edge, width, diagonal, bias.astype(jnp.float32)))
+            top += width
+
+        def one(turn):
+            place = pl.ds(pl.multiple_of(turn * stride, stride), stride)
             scores = (
                 lax.dot_general(
                     query_ref[place, :],
@@ -69,99 +78,72 @@
                 * factor
             )
             masked = []
-            if edge:
-                masked.append(jnp.where(diagonal, scores[:, :edge], floor_value))
-            if edge < width:
-                masked.append(scores[:, edge:] + bias[:, edge:])
-            masked = jnp.concatenate(masked, axis=1) if len(masked) > 1 else masked[0]
+            for top, edge, width, diagonal, bias in segments:
+                masked.append(jnp.where(diagonal, scores[:, top : top + edge], floor_value))
+                if edge < width:
+                    masked.append(scores[:, top + edge : top + width] + bias)
+            masked = jnp.concatenate(masked, axis=1)
             peak = jnp.max(masked, axis=1, keepdims=True)
-            if carry:
-                peak = jnp.maximum(peak, old_peak[place, :])
             weights = jnp.exp2(masked - peak)
             total = jnp.sum(weights, axis=1, keepdims=True)
             numerator = jnp.dot(
                 weights.astype(jnp.bfloat16), values, preferred_element_type=jnp.float32
             )
-            if carry:
-                shrink = jnp.exp2(old_peak[place, :] - peak)
-                total = total + shrink * old_total[place, :]
-                numerator = numerator + shrink * old_sum[place, :]
-            if final:
-                out_ref, scratch = refs
-                scratch[place, :] = (numerator / total).astype(jnp.bfloat16)
-            else:
-                peak_ref, total_ref, sum_ref = refs
-                peak_ref[place, :] = peak
-                total_ref[place, :] = total
-                sum_ref[place, :] = numerator
+            scratch[place, :] = (numerator / total).astype(jnp.bfloat16)
 
         if flat // stride <= 8:
-            for part in range(flat // stride):
-                one(part)
+            for turn in range(flat // stride):
+                one(turn)
         else:
 
             @pl.loop(0, flat // stride)
-            def each(part):
-                one(part)
+            def each(turn):
+                one(turn)
 
     upper = span_ref[2]
 
     @pl.when(upper == 1)
     def all_keys():
-        run(everything.shape[0])
+        run(1)
 
     @pl.when(upper == 0)
     def lower_keys():
-        run(everything.shape[0] // 2)
-
-    if final:
-        out_ref, scratch = refs
-        for head in range(flat // rows):
-            out_ref[:, head * head_size : (head + 1) * head_size] = scratch[
-                head * rows : (head + 1) * rows, :
-            ]
-
-
-def attend(span, place, query_flat, pieces, order, own, state, final, rows):
+        run(2)
+
+    for head in range(flat // rows):
+        out_ref[:, head * head_size : (head + 1) * head_size] = scratch[
+            head * rows : (head + 1) * rows, :
+        ]
+
+
+def attend(span, places, query_flat, pieces, slots, owns, rows):
     flat, head_size = query_flat.shape
     width = sum(piece.shape[0] for piece in pieces)
     stride = math.gcd(flat, 256 if width <= 2048 else rows)
     whole = pl.BlockSpec(memory_space=pltpu.VMEM)
-    if final:
-        shapes = jax.ShapeDtypeStruct((rows, flat // rows * head_size), jnp.bfloat16)
-        out_specs, scratch = whole, [pltpu.VMEM((flat, head_size), jnp.bfloat16)]
-    else:
-        shapes = [
-            jax.ShapeDtypeStruct((flat, 1), jnp.float32),
-            jax.ShapeDtypeStruct((flat, 1), jnp.float32),
-            jax.ShapeDtypeStruct((flat, head_size), jnp.float32),
-        ]
-        out_specs, scratch = [whole] * 3, []
     return pl.pallas_call(
         partial(
             attention_kernel,
-            count=len(pieces),
-            order=order,
-            carry=state is not None,
-            final=final,
+            count=len(places),
+            slots=slots,
+            owns=owns,
             rows=rows,
-            own=own,
             head_size=head_size,
             stride=stride,
         ),
-        out_shape=shapes,
+        out_shape=jax.ShapeDtypeStruct((rows, flat // rows * head_size), jnp.bfloat16),
         in_specs=[pl.BlockSpec(memory_space=pltpu.SMEM)]
-        + [whole] * (2 + len(pieces) + (0 if state is None else 3)),
-        out_specs=out_specs,
-        scratch_shapes=scratch,
+        + [whole] * (1 + len(places) + len(pieces)),
+        out_specs=whole,
+        scratch_shapes=[pltpu.VMEM((flat, head_size), jnp.bfloat16)],
         compiler_params=pltpu.CompilerParams(vmem_limit_bytes=24 * 1024 * 1024),
         cost_estimate=pl.CostEstimate(
             flops=4 * flat * width * head_size,
             bytes_accessed=4 * flat * head_size + 4 * width * head_size,
             transcendentals=flat * width,
         ),
-        name="attend_last" if final else "attend_part",
-    )(span, place, query_flat, *pieces, *(() if state is None else state))
+        name="attend",
+    )(span, query_flat, *places, *pieces)
 
 
 def stages_of(contexts):
@@ -335,36 +317,13 @@
         top_bit = stages[0]
         upper = ((context & top_bit) != 0).astype(jnp.int32)
         span = jnp.stack([base, first, upper]).astype(jnp.int32)
-        def halves(masks):
-            return sorted(range(len(masks)), key=lambda slot: masks[slot] & top_bit)
-
         all_masks = [0]
         for bit in stages:
             all_masks = all_masks + [mask ^ bit for mask in all_masks]
-        sorted_slots = halves(all_masks)
-        middle = len(all_masks) // 2
-        turns = jnp.array([all_masks[slot] for slot in sorted_slots], jnp.int32)
+        slots = tuple(sorted(range(contexts), key=lambda slot: all_masks[slot] & top_bit))
+        turns = jnp.array([all_masks[slot] for slot in slots], jnp.int32)
         sources = (context ^ turns)[:, None] * group_rows
-        spots = [
-            (sources + places_of(part.top, part.rows)[None, :]).reshape(-1) for part in parts
-        ]
-        cuts = [(0, 1), (1, middle), (middle, 2 * middle)]
-        place = jnp.concatenate(
-            [
-                spot[low * shards * part.rows : high * shards * part.rows]
-                for low, high in cuts
-                for spot, part in zip(spots, parts)
-            ]
-        ).reshape(1, -1)
-        order = tuple(
-            (2 * number + slot // middle, slot % middle)
-            for low, high in cuts
-            for number in range(len(parts))
-            for slot in sorted_slots[low:high]
-        )
-        query_flat, late.tables, span, place = lax.optimization_barrier(
-            (query_flat, late.tables, span, place)
-        )
+        query_flat, late.tables, span = lax.optimization_barrier((query_flat, late.tables, span))
         exchange(late, query_flat)
         combine(early, late.sums)
         advance(early)
@@ -373,10 +332,12 @@
         for stage in range(1, len(stages)):
             advance(early, late.known)
             advance(late, early.known)
+        places = [
+            (sources + places_of(part.top, part.rows)[None, :]).reshape(1, -1) for part in parts
+        ]
         pieces = [early.known] + early.fresh + [late.known] + late.fresh
-        attended = attend(
-            span, place, query_flat, pieces, order, shards * rows, None, True, rows
-        )
+        owns = tuple(shards * part.rows for part in parts)
+        attended = attend(span, places, query_flat, pieces, slots, owns, rows)
         kv_cache = jnp.concatenate([part.cache for part in parts], axis=0)
         return (kv_cache, attended)
 
@@ -386,7 +347,7 @@
 def solution(mesh):
     placed = (P(("ctx", "fsdp"), None), P(("ctx", "fsdp"), None), P("fsdp", None), P("fsdp", None))
     return jax.shard_map(
-        make_local(mesh.shape["ctx"], mesh.shape["fsdp"], ((1, 4), (3,))),
+        make_local(mesh.shape["ctx"], mesh.shape["fsdp"], ((1, 4), (2, 1))),
         mesh=mesh,
         in_specs=placed,
         out_specs=(P(("ctx", "fsdp"), None), P(("ctx", "fsdp"), None)),

time: 62.9 us -> 57.1 us (0.908)
  local copies, waits for them, and re-layouts: 11.4 us -> 7.25 us
  waiting for transfers between devices: 9.68 us -> 7.09 us
  starting transfers between devices: 16.8 us -> 19.1 us
  other arithmetic: 9.92 us -> 7.73 us
    slice x10 -> x0, local copies, waits for them, and re-layouts: 5.12 us -> none  [local(): spot[low * shards * part.rows:high * shards * part.rows]]
    ppermute x8, starting transfers between devices: 9.65 us -> 12.3 us  [advance(): part.fresh = [lax.ppermute(part.known, 'ctx', pairs)]]
    ppermute x8, waiting for transfers between devices: 7.33 us -> 5.19 us  [advance(): part.fresh = [lax.ppermute(part.known, 'ctx', pairs)]]
    ppermute x2, waiting for transfers between devices: 2.34 us -> 0.68 us  [exchange(): lax.ppermute(part.sums, 'fsdp', [(i, i ^ reach) for i in range(shards)])]
    add x0 -> x2, local copies, waits for them, and re-layouts: none -> 1.54 us  [local(): sources + places_of(part.top, part.rows)[None, :]]
    ppermute x3 -> x4, waiting for transfers between devices: 0.01 us -> 1.23 us  [send(): lax.ppermute(after(columns[step - 1], *earlier) if earlier else columns[s...]
    add x2, other arithmetic: 1.34 us -> 0.14 us  [places_of(): turns[:, None] + jnp.arange(count, dtype=jnp.int32)[None, :]]
    add x2, other arithmetic: 0.81 us -> 1.94 us  [local(): sources + places_of(part.top, part.rows)[None, :]]
  transfers between devices with their start and end apart: 13 -> 14, of which waited for: 8 -> 9; matrix products, arithmetic and copies ran while one was open for 44% -> 39% of each run, Pallas kernels for 0% -> 0%
where the time goes in v14:
time: 57.1 us; the launch traced here: 56.2 us
  starting transfers between devices  19.1 us (33%)
  matrix products  10.6 us (19%)
  other arithmetic  7.73 us (14%)
  local copies, waits for them, and re-layouts  7.25 us (13%)
  waiting for transfers between devices  7.09 us (12%)
  Pallas kernels  3.44 us (6%)
  between operations  1.02 us (2%)
    ppermute x8, starting transfers between devices, advance(): part.fresh = [lax.ppermute(part.known, 'ctx', pairs)]  12.3 us
    dot_general x10, matrix products, project(): jnp.dot(columns, weight, preferred_element_type=jnp.float32)  10.6 us
    ppermute x8, waiting for transfers between devices, advance(): part.fresh = [lax.ppermute(part.known, 'ctx', pairs)]  5.19 us
    ppermute x4, starting transfers between devices, send(): lax.ppermute(after(columns[step - 1], *earlier) if earlier else columns[s...  5.03 us
    pallas_call x1, Pallas kernels, attend(): pl.pallas_call(partial(attention_kernel, count=len(places), slots=slots,...  3.44 us
    unnamed x24, local copies, waits for them, and re-layouts  2.92 us
    dynamic_slice x4, local copies, waits for them, and re-layouts, cut(): lax.dynamic_slice(source, (jnp.int32(top), lax.rem(shard + step, shards)...  2.08 us
    add x2, other arithmetic, local(): sources + places_of(part.top, part.rows)[None, :]  1.94 us
  transfers between devices with their start and end apart: 14, of which 9 were waited for; matrix products, arithmetic and copies ran while one was open for 39% of the time, Pallas kernels for 0%

profile of v14, /device:TPU:0, one launch (start us, length us, event | category | flops | bytes accessed | tf_op | source)
XLA Modules:
  0.0 56.2 jit_solution(5278232014786524317)
XLA Ops:
  0.7 1.6 %copy-done = bf16[64,16384]{1,0:T(8,128)(2,1)S(1)} copy-done((bf16[64,16384]{1,0:T(8,128)(2,1)S(1)}, bf16[64,16384]{1,0:T(8,128)(2,1)}, u32[]{:S(2)}) %copy-start) | copy-done | bytes 2097176
  2.2 0.7 %constant_dynamic-slice_fusion.2 = bf16[8,8192]{1,0:T(8,128)(2,1)} fusion(bf16[64,16384]{1,0:T(8,128)(2,1)S(1)} %copy-done, s32[]{:T(128)S(6)} %select_n.40), kind=kLoop, calls=%fused_computation.47 | loop fusion | bytes 262148 | tf_op jit(solution)/shard_map/dynamic_slice | solution.py:177
  2.9 2.9 %collective-permute-start = (bf16[8,8192]{1,0:T(8,128)(2,1)}, bf16[8,8192]{1,0:T(8,128)(2,1)S(1)}, u32[]{:S(2)}, u32[]{:S(2)}) collective-permute-start(bf16[8,8192]{1,0:T(8,128)(2,1)} %constant_dynamic-slice_fusion.2), channel_id=1, source_target_pairs={{0,1},{1,0},{2,3},{3,2},{4,5},{5,4},{6,7},{7,6},{8,9},{9,8},{10,11... | collective-permute-start | bytes 393224 | tf_op jit(solution)/shard_map/ppermute | solution.py:187
  5.9 0.7 %constant_dynamic-slice_fusion.4 = bf16[16,8192]{1,0:T(8,128)(2,1)} fusion(bf16[64,16384]{1,0:T(8,128)(2,1)S(1)} %copy-done, s32[]{:T(128)S(6)} %select_n.40), kind=kLoop, calls=%fused_computation.57 | loop fusion | bytes 524292 | tf_op jit(solution)/shard_map/dynamic_slice | solution.py:177
  6.7 2.0 %collective-permute-start.3 = (bf16[16,8192]{1,0:T(8,128)(2,1)}, bf16[16,8192]{1,0:T(8,128)(2,1)S(1)}, u32[]{:S(2)}, u32[]{:S(2)}) collective-permute-start(bf16[16,8192]{1,0:T(8,128)(2,1)} %constant_dynamic-slice_fusion.4), channel_id=1, source_target_pairs={{0,1},{1,0},{2,3},{3,2},{4,5},{5,4},{6,7},{7,6},{8,9},{9,8},{10,11... | collective-permute-start | bytes 786440 | tf_op jit(solution)/shard_map/ppermute | solution.py:187
  8.7 0.7 %constant_dynamic-slice_fusion.3 = bf16[8,8192]{1,0:T(8,128)(2,1)} fusion(bf16[64,16384]{1,0:T(8,128)(2,1)S(1)} %copy-done, s32[]{:T(128)S(6)} %select_n.40), kind=kLoop, calls=%fused_computation.55 | loop fusion | bytes 262148 | tf_op jit(solution)/shard_map/dynamic_slice | solution.py:177
  9.4 2.8 %fusion = f32[64,128]{1,0:T(8,128)} fusion(bf16[8192,128]{1,0:T(8,128)(2,1)} %param.8, bf16[64,16384]{1,0:T(8,128)(2,1)S(1)} %copy-done, s32[]{:T(128)S(6)} %select_n.41), kind=kOutput, calls=%fused_computation | convolution fusion | flops 134217728 | bytes 3178500 | tf_op jit(solution)/shard_map/dot_general | solution.py:231
  12.2 1.1 %fusion.2 = f32[64,128]{1,0:T(8,128)} fusion(bf16[8192,128]{1,0:T(8,128)(2,1)S(1)} %copy-done.3, bf16[64,16384]{1,0:T(8,128)(2,1)S(1)} %copy-done, s32[]{:T(128)S(6)} %select_n.41), kind=kOutput, calls=%fused_computation.2 | convolution fusion | flops 134217728 | bytes 3178500 | tf_op jit(solution)/shard_map/dot_general | solution.py:231
  13.5 1.4 %pad_maximum_fusion.7 = f32[64,256]{1,0:T(8,128)} fusion(f32[64,128]{1,0:T(8,128)} %fusion, f32[64,128]{1,0:T(8,128)} %fusion.2), kind=kLoop, calls=%fused_computation.15 | loop fusion | flops 16384 | bytes 131072 | tf_op jit(solution)/shard_map/concatenate | solution.py:229
  14.9 0.9 %multiply_sine_fusion = (f32[80,64]{1,0:T(8,128)}, f32[80,64]{1,0:T(8,128)}) fusion(f32[64]{0:T(128)S(1)} %multiply_power_fusion, f32[80]{0:T(128)S(1)} %add_convert_fusion.5), kind=kLoop, calls=%fused_computation.16 | loop fusion | flops 5120 | bytes 41536 | tf_op jit(solution)/shard_map/sin | solution.py:29
  15.8 0.6 %add.223 = s32[48]{0:T(128)} reshape(s32[2,24]{1,0:T(2,128)S(1)} %iota_add_fusion) | data formatting | bytes 384 | tf_op jit(solution)/shard_map/add | solution.py:197
  16.4 0.7 %xor_multiply_fusion = s32[16]{0:T(128)S(1)} fusion(s32[16]{0:T(128)} %constant.47.clone, s32[]{:T(128)S(6)} %axis_index.25), kind=kLoop, calls=%fused_computation.49 | loop fusion | flops 32 | bytes 132 | tf_op jit(solution)/shard_map/mul | solution.py:325
  17.1 0.7 %broadcast_add_fusion.1 = s32[16,80]{1,0:T(8,128)} fusion(s32[80]{0:T(128)S(1)} %add.212, s32[16]{0:T(128)S(1)} %xor_multiply_fusion), kind=kLoop, calls=%fused_computation.40 | loop fusion | flops 1280 | bytes 5504 | tf_op jit(solution)/shard_map/add | solution.py:336
  17.7 0.8 %add.234.refs_0_ = s32[1,1280]{1,0:T(1,128)S(1)} reshape(s32[16,80]{1,0:T(8,128)} %broadcast_add_fusion.1) | data formatting | bytes 10240 | tf_op jit(solution)/shard_map/add | solution.py:336
  18.5 1.3 %broadcast_add_fusion = s32[16,48]{1,0:T(8,128)} fusion(s32[48]{0:T(128)} %add.223, s32[16]{0:T(128)S(1)} %xor_multiply_fusion), kind=kLoop, calls=%fused_computation.39 | loop fusion | flops 768 | bytes 3328 | tf_op jit(solution)/shard_map/add | solution.py:336
  19.8 0.8 %add.238.refs_1_ = s32[1,768]{1,0:T(1,128)S(1)} reshape(s32[16,48]{1,0:T(8,128)} %broadcast_add_fusion) | data formatting | bytes 6144 | tf_op jit(solution)/shard_map/add | solution.py:336
  20.6 2.1 %fusion.7 = f32[8,128]{1,0:T(8,128)S(1)} fusion(bf16[8,8192]{1,0:T(8,128)(2,1)S(1)} %collective-permute-done, bf16[8192,128]{1,0:T(8,128)(2,1)} %param.8), kind=kOutput, calls=%fused_computation.60 | convolution fusion | flops 16777216 | bytes 2232320 | tf_op jit(solution)/shard_map/dot_general | solution.py:231
  22.7 2.1 %fusion.6 = f32[8,128]{1,0:T(8,128)S(1)} fusion(bf16[8,8192]{1,0:T(8,128)(2,1)S(1)} %collective-permute-done, bf16[8192,128]{1,0:T(8,128)(2,1)} %param.7), kind=kOutput, calls=%fused_computation.59 | convolution fusion | flops 16777216 | bytes 2232320 | tf_op jit(solution)/shard_map/dot_general | solution.py:231
  24.9 0.4 fusion.9
  25.4 0.4 fusion.8
  25.9 0.4 copy-done.10
  26.4 0.2 multiply_cosine_fusion.1
  26.6 0.3 subtract_convert_fusion
  27.1 0.2 multiply_sine_fusion.2
  27.3 0.5 copy-done.2
  27.9 0.4 fusion.11
  28.2 0.3 copy-done.5
  28.6 0.4 fusion.10
  29.0 1.6 %collective-permute-start.2 = (f32[80,256]{1,0:T(8,128)S(1)}, f32[80,256]{1,0:T(8,128)S(1)}, u32[]{:S(2)}, u32[]{:S(2)}) collective-permute-start(f32[80,256]{1,0:T(8,128)S(1)} %pad_maximum_fusion.5), channel_id=1, source_target_pairs={{0,1},{1,0},{2,3},{3,2},{4,5},{5,4},{6,7},{7,6},{8,9},{9,8},{10,11... | collective-permute-start | bytes 245768 | tf_op jit(solution)/shard_map/ppermute | solution.py:278
  30.6 1.2 %collective-permute-done.4 = bf16[8,8192]{1,0:T(8,128)(2,1)S(1)} collective-permute-done((bf16[8,8192]{1,0:T(8,128)(2,1)S(1)}, bf16[8,8192]{1,0:T(8,128)(2,1)S(1)}, u32[]{:S(2)}, u32[]{:S(2)}) %collective-permute-start.4) | collective-permute-done | bytes 131104 | tf_op jit(solution)/shard_map/ppermute | solution.py:187
  31.8 0.4 fusion.13
  32.2 0.4 fusion.12
  32.6 0.8 %slice_select_fusion.3 = (f32[24,256]{1,0:T(8,128)S(1)}, f32[24,256]{1,0:T(8,128)S(1)}) fusion(f32[64,256]{1,0:T(8,128)} %pad_maximum_fusion.7, f32[8,128]{1,0:T(8,128)S(1)} %fusion.13, f32[8,128]{1,0:T(8,128)S(1)} %fusion.12, f32[16,128]{1,0:T(8,128)S(1)} %fusion.11, f32[16,128]{1,0:T(8,128)S(1)} %fusion.10, pred[]{:T(512)S(6)} %eq.2), kind=kLoop, calls=%fused_computation.38 | loop fusion | flops 30720 | bytes 98305 | tf_op jit(solution)/shard_map/jit(_where)/select_n | solution.py:260
  33.4 0.3 collective-permute-done.2
  34.0 3.2 %collective-permute-start.6 = (bf16[80,256]{1,0:T(8,128)(2,1)S(1)}, bf16[80,256]{1,0:T(8,128)(2,1)S(1)}, u32[]{:S(2)}, u32[]{:S(2)}) collective-permute-start(bf16[80,256]{1,0:T(8,128)(2,1)S(1)} %pad_maximum_fusion.10), channel_id=1, source_target_pairs={{0,16},{2,18},{4,20},{6,22},{8,24},{10,26},{12,28},{14,30},{16,0},... | collective-permute-start | bytes 122888 | tf_op jit(solution)/shard_map/ppermute | solution.py:300
  37.1 0.4 collective-permute-done.5
  37.7 2.6 %collective-permute-start.8 = (bf16[48,256]{1,0:T(8,128)(2,1)S(1)}, bf16[48,256]{1,0:T(8,128)(2,1)S(1)}, u32[]{:S(2)}, u32[]{:S(2)}) collective-permute-start(bf16[48,256]{1,0:T(8,128)(2,1)S(1)} %pad_maximum_fusion.12), channel_id=1, source_target_pairs={{0,16},{2,18},{4,20},{6,22},{8,24},{10,26},{12,28},{14,30},{16,0},... | collective-permute-start | bytes 73736 | tf_op jit(solution)/shard_map/ppermute | solution.py:300
  40.3 1.6 %collective-permute-start.7 = (bf16[160,256]{1,0:T(8,128)(2,1)S(1)}, bf16[160,256]{1,0:T(8,128)(2,1)S(1)}, u32[]{:S(2)}, u32[]{:S(2)}) collective-permute-start(bf16[160,256]{1,0:T(8,128)(2,1)S(1)} %pad_maximum_fusion.6), channel_id=1, source_target_pairs={{0,8},{2,10},{4,12},{6,14},{8,0},{10,2},{12,4},{14,6},{16,24},{18,... | collective-permute-start | bytes 245768 | tf_op jit(solution)/shard_map/ppermute | solution.py:300
  41.9 0.5 collective-permute-done.8
  42.5 1.7 %collective-permute-start.10 = (bf16[96,256]{1,0:T(8,128)(2,1)S(1)}, bf16[96,256]{1,0:T(8,128)(2,1)S(1)}, u32[]{:S(2)}, u32[]{:S(2)}) collective-permute-start(bf16[96,256]{1,0:T(8,128)(2,1)S(1)} %pad_maximum_fusion.9), channel_id=1, source_target_pairs={{0,8},{2,10},{4,12},{6,14},{8,0},{10,2},{12,4},{14,6},{16,24},{18,... | collective-permute-start | bytes 147464 | tf_op jit(solution)/shard_map/ppermute | solution.py:300
  44.1 0.7 %collective-permute-done.7 = bf16[160,256]{1,0:T(8,128)(2,1)S(1)} collective-permute-done((bf16[160,256]{1,0:T(8,128)(2,1)S(1)}, bf16[160,256]{1,0:T(8,128)(2,1)S(1)}, u32[]{:S(2)}, u32[]{:S(2)}) %collective-permute-start.7) | collective-permute-done | bytes 81952 | tf_op jit(solution)/shard_map/ppermute | solution.py:300
  44.8 1.6 %collective-permute-start.9 = (bf16[320,256]{1,0:T(8,128)(2,1)S(1)}, bf16[320,256]{1,0:T(8,128)(2,1)S(1)}, u32[]{:S(2)}, u32[]{:S(2)}) collective-permute-start(bf16[320,256]{1,0:T(8,128)(2,1)S(1)} %pad_maximum_fusion.3), channel_id=1, source_target_pairs={{0,4},{2,6},{4,0},{6,2},{8,12},{10,14},{12,8},{14,10},{16,20},{18,... | collective-permute-start | bytes 491528 | tf_op jit(solution)/shard_map/ppermute | solution.py:300
  46.6 1.5 %collective-permute-start.12 = (bf16[192,256]{1,0:T(8,128)(2,1)S(1)}, bf16[192,256]{1,0:T(8,128)(2,1)S(1)}, u32[]{:S(2)}, u32[]{:S(2)}) collective-permute-start(bf16[192,256]{1,0:T(8,128)(2,1)S(1)} %pad_maximum_fusion.4), channel_id=1, source_target_pairs={{0,4},{2,6},{4,0},{6,2},{8,12},{10,14},{12,8},{14,10},{16,20},{18,... | collective-permute-start | bytes 294920 | tf_op jit(solution)/shard_map/ppermute | solution.py:300
  48.1 2.1 %collective-permute-done.9 = bf16[320,256]{1,0:T(8,128)(2,1)S(1)} collective-permute-done((bf16[320,256]{1,0:T(8,128)(2,1)S(1)}, bf16[320,256]{1,0:T(8,128)(2,1)S(1)}, u32[]{:S(2)}, u32[]{:S(2)}) %collective-permute-start.9) | collective-permute-done | bytes 163872 | tf_op jit(solution)/shard_map/ppermute | solution.py:300
  50.3 0.9 %collective-permute-done.12 = bf16[192,256]{1,0:T(8,128)(2,1)S(1)} collective-permute-done((bf16[192,256]{1,0:T(8,128)(2,1)S(1)}, bf16[192,256]{1,0:T(8,128)(2,1)S(1)}, u32[]{:S(2)}, u32[]{:S(2)}) %collective-permute-start.12) | collective-permute-done | bytes 98336 | tf_op jit(solution)/shard_map/ppermute | solution.py:300
  51.4 0.6 %pad_maximum_fusion.11 = bf16[64,256]{1,0:T(8,128)(2,1)} fusion(bf16[24,256]{1,0:T(8,128)(2,1)S(1)} %constant_dynamic-slice_fusion, bf16[40,256]{1,0:T(8,128)(2,1)S(1)} %constant_dynamic-slice_fusion.1), kind=kLoop, calls=%fused_computation.31 | loop fusion | flops 65536 | bytes 65536 | tf_op jit(solution)/shard_map/concatenate | solution.py:341
  52.0 0.8 %collective-permute-done.13.refs_5_ = bf16[384,256]{1,0:T(8,128)(2,1)S(1)} collective-permute-done((bf16[384,256]{1,0:T(8,128)(2,1)S(1)}, bf16[384,256]{1,0:T(8,128)(2,1)S(1)}, u32[]{:S(2)}, u32[]{:S(2)}) %collective-permute-start.13) | collective-permute-done | bytes 196640 | tf_op jit(solution)/shard_map/ppermute | solution.py:300
  52.8 3.4 %attend.1 = bf16[64,2048]{1,0:T(8,128)(2,1)} custom-call(s32[3]{0:T(128)S(1)} %pad_add_fusion.span_ref, bf16[1024,128]{1,0:T(8,128)(2,1)S(1)} %pad_maximum_fusion.1.query_ref, s32[1,1280]{1,0:T(1,128)S(1)} %add.234.refs_0_, s32[1,768]{1,0:T(1,128)S(1)} %add.238.refs_1_, bf16[640,256]{1,0:T(8,128)(2,1)S(1)} %pad_maximum_fusion.refs_2_, ...), custom_call_target="tpu_custom_call" | custom-call | flops 1073741824 | bytes 1572864 | tf_op jit(solution)/shard_map/attend/pallas_call | solution.py:124
  (63 shorter events, 1.6 us)
Async XLA Ops:
  0.6 1.6 %copy-start = (bf16[64,16384]{1,0:T(8,128)(2,1)S(1)}, bf16[64,16384]{1,0:T(8,128)(2,1)}, u32[]{:S(2)}) copy-start(bf16[64,16384]{1,0:T(8,128)(2,1)} %param.5) | copy-start | bytes 6291460
  2.9 17.7 %collective-permute-start = (bf16[8,8192]{1,0:T(8,128)(2,1)}, bf16[8,8192]{1,0:T(8,128)(2,1)S(1)}, u32[]{:S(2)}, u32[]{:S(2)}) collective-permute-start(bf16[8,8192]{1,0:T(8,128)(2,1)} %constant_dynamic-slice_fusion.2), channel_id=1, source_target_pairs={{0,1},{1,0},{2,3},{3,2},{4,5},{5,4},{6,7},{7,6},{8,9},{9,8},{10,11... | collective-permute-start | bytes 393224 | tf_op jit(solution)/shard_map/ppermute | solution.py:187
  5.9 19.0 %collective-permute-start.1 = (bf16[32,8192]{1,0:T(8,128)(2,1)S(1)}, bf16[32,8192]{1,0:T(8,128)(2,1)S(1)}, u32[]{:S(2)}, u32[]{:S(2)}) collective-permute-start(bf16[32,8192]{1,0:T(8,128)(2,1)S(1)} %constant_dynamic-slice_fusion.5), channel_id=1, source_target_pairs={{0,1},{1,0},{2,3},{3,2},{4,5},{5,4},{6,7},{7,6},{8,9},{9,8},{10,11... | collective-permute-start | bytes 1572872 | tf_op jit(solution)/shard_map/ppermute | solution.py:187
  6.7 20.7 %collective-permute-start.3 = (bf16[16,8192]{1,0:T(8,128)(2,1)}, bf16[16,8192]{1,0:T(8,128)(2,1)S(1)}, u32[]{:S(2)}, u32[]{:S(2)}) collective-permute-start(bf16[16,8192]{1,0:T(8,128)(2,1)} %constant_dynamic-slice_fusion.4), channel_id=1, source_target_pairs={{0,1},{1,0},{2,3},{3,2},{4,5},{5,4},{6,7},{7,6},{8,9},{9,8},{10,11... | collective-permute-start | bytes 786440 | tf_op jit(solution)/shard_map/ppermute | solution.py:187
  9.4 2.9 %copy-start.3 = (bf16[8192,128]{1,0:T(8,128)(2,1)S(1)}, bf16[8192,128]{1,0:T(8,128)(2,1)}, u32[]{:S(2)}) copy-start(bf16[8192,128]{1,0:T(8,128)(2,1)} %param.7) | copy-start | bytes 6291460
  20.6 4.3 %copy-start.1 = (bf16[8192,128]{1,0:T(8,128)(2,1)S(1)}, bf16[8192,128]{1,0:T(8,128)(2,1)}, u32[]{:S(2)}) copy-start(bf16[8192,128]{1,0:T(8,128)(2,1)} %param.8) | copy-start | bytes 6291460
  22.7 2.6 %copy-start.4 = (bf16[8192,128]{1,0:T(8,128)(2,1)S(1)}, bf16[8192,128]{1,0:T(8,128)(2,1)}, u32[]{:S(2)}) copy-start(bf16[8192,128]{1,0:T(8,128)(2,1)} %param.7) | copy-start | bytes 6291460
  24.9 1.0 %copy-start.7 = (f32[64,256]{1,0:T(8,128)S(1)}, f32[64,256]{1,0:T(8,128)}, u32[]{:S(2)}) copy-start(f32[64,256]{1,0:T(8,128)} %pad_maximum_fusion.7) | copy-start | bytes 196612
  25.3 0.9 %copy-start.10 = (bf16[8,8192]{1,0:T(8,128)(2,1)S(1)}, bf16[8,8192]{1,0:T(8,128)(2,1)}, u32[]{:S(2)}) copy-start(bf16[8,8192]{1,0:T(8,128)(2,1)} %constant_dynamic-slice_fusion.3) | copy-start | bytes 393220
  25.3 1.0 %copy-start.6 = (bf16[64,2048]{1,0:T(8,128)(2,1)S(1)}, bf16[64,2048]{1,0:T(8,128)(2,1)}, u32[]{:S(2)}) copy-start(bf16[64,2048]{1,0:T(8,128)(2,1)} %param.6) | copy-start | bytes 786436
  25.4 1.3 %copy-start.11 = (s32[48]{0:T(128)S(1)}, s32[48]{0:T(128)}, u32[]{:S(2)}) copy-start(s32[48]{0:T(128)} %add.223) | copy-start | bytes 580
  26.2 1.6 %copy-start.2 = (bf16[8192,128]{1,0:T(8,128)(2,1)S(1)}, bf16[8192,128]{1,0:T(8,128)(2,1)}, u32[]{:S(2)}) copy-start(bf16[8192,128]{1,0:T(8,128)(2,1)} %param.8) | copy-start | bytes 6291460
  26.2 5.6 %collective-permute-start.4 = (bf16[8,8192]{1,0:T(8,128)(2,1)S(1)}, bf16[8,8192]{1,0:T(8,128)(2,1)S(1)}, u32[]{:S(2)}, u32[]{:S(2)}) collective-permute-start(bf16[8,8192]{1,0:T(8,128)(2,1)S(1)} %copy-done.10), channel_id=1, source_target_pairs={{0,1},{1,0},{2,3},{3,2},{4,5},{5,4},{6,7},{7,6},{8,9},{9,8},{10,11... | collective-permute-start | bytes 393224 | tf_op jit(solution)/shard_map/ppermute | solution.py:187
  26.6 1.9 %copy-start.5 = (bf16[8192,128]{1,0:T(8,128)(2,1)S(1)}, bf16[8192,128]{1,0:T(8,128)(2,1)}, u32[]{:S(2)}) copy-start(bf16[8192,128]{1,0:T(8,128)(2,1)} %param.7) | copy-start | bytes 6291460
  28.9 4.8 %copy-start.8 = (f32[80,64]{1,0:T(8,128)S(1)}, f32[80,64]{1,0:T(8,128)}, u32[]{:S(2)}) copy-start(f32[80,64]{1,0:T(8,128)} %get-tuple-element.54) | copy-start | bytes 61444
  29.0 4.8 %copy-start.9 = (f32[80,64]{1,0:T(8,128)S(1)}, f32[80,64]{1,0:T(8,128)}, u32[]{:S(2)}) copy-start(f32[80,64]{1,0:T(8,128)} %get-tuple-element.53) | copy-start | bytes 61444
  29.0 4.8 %collective-permute-start.2 = (f32[80,256]{1,0:T(8,128)S(1)}, f32[80,256]{1,0:T(8,128)S(1)}, u32[]{:S(2)}, u32[]{:S(2)}) collective-permute-start(f32[80,256]{1,0:T(8,128)S(1)} %pad_maximum_fusion.5), channel_id=1, source_target_pairs={{0,1},{1,0},{2,3},{3,2},{4,5},{5,4},{6,7},{7,6},{8,9},{9,8},{10,11... | collective-permute-start | bytes 245768 | tf_op jit(solution)/shard_map/ppermute | solution.py:278
  33.4 4.2 %collective-permute-start.5 = (f32[48,256]{1,0:T(8,128)S(1)}, f32[48,256]{1,0:T(8,128)S(1)}, u32[]{:S(2)}, u32[]{:S(2)}) collective-permute-start(f32[48,256]{1,0:T(8,128)S(1)} %pad_maximum_fusion.8), channel_id=1, source_target_pairs={{0,1},{1,0},{2,3},{3,2},{4,5},{5,4},{6,7},{7,6},{8,9},{9,8},{10,11... | collective-permute-start | bytes 147464 | tf_op jit(solution)/shard_map/ppermute | solution.py:278
  34.0 6.3 %collective-permute-start.6 = (bf16[80,256]{1,0:T(8,128)(2,1)S(1)}, bf16[80,256]{1,0:T(8,128)(2,1)S(1)}, u32[]{:S(2)}, u32[]{:S(2)}) collective-permute-start(bf16[80,256]{1,0:T(8,128)(2,1)S(1)} %pad_maximum_fusion.10), channel_id=1, source_target_pairs={{0,16},{2,18},{4,20},{6,22},{8,24},{10,26},{12,28},{14,30},{16,0},... | collective-permute-start | bytes 122888 | tf_op jit(solution)/shard_map/ppermute | solution.py:300
  37.7 4.7 %collective-permute-start.8 = (bf16[48,256]{1,0:T(8,128)(2,1)S(1)}, bf16[48,256]{1,0:T(8,128)(2,1)S(1)}, u32[]{:S(2)}, u32[]{:S(2)}) collective-permute-start(bf16[48,256]{1,0:T(8,128)(2,1)S(1)} %pad_maximum_fusion.12), channel_id=1, source_target_pairs={{0,16},{2,18},{4,20},{6,22},{8,24},{10,26},{12,28},{14,30},{16,0},... | collective-permute-start | bytes 73736 | tf_op jit(solution)/shard_map/ppermute | solution.py:300
  40.3 4.5 %collective-permute-start.7 = (bf16[160,256]{1,0:T(8,128)(2,1)S(1)}, bf16[160,256]{1,0:T(8,128)(2,1)S(1)}, u32[]{:S(2)}, u32[]{:S(2)}) collective-permute-start(bf16[160,256]{1,0:T(8,128)(2,1)S(1)} %pad_maximum_fusion.6), channel_id=1, source_target_pairs={{0,8},{2,10},{4,12},{6,14},{8,0},{10,2},{12,4},{14,6},{16,24},{18,... | collective-permute-start | bytes 245768 | tf_op jit(solution)/shard_map/ppermute | solution.py:300
  42.5 4.1 %collective-permute-start.10 = (bf16[96,256]{1,0:T(8,128)(2,1)S(1)}, bf16[96,256]{1,0:T(8,128)(2,1)S(1)}, u32[]{:S(2)}, u32[]{:S(2)}) collective-permute-start(bf16[96,256]{1,0:T(8,128)(2,1)S(1)} %pad_maximum_fusion.9), channel_id=1, source_target_pairs={{0,8},{2,10},{4,12},{6,14},{8,0},{10,2},{12,4},{14,6},{16,24},{18,... | collective-permute-start | bytes 147464 | tf_op jit(solution)/shard_map/ppermute | solution.py:300
  44.8 5.4 %collective-permute-start.9 = (bf16[320,256]{1,0:T(8,128)(2,1)S(1)}, bf16[320,256]{1,0:T(8,128)(2,1)S(1)}, u32[]{:S(2)}, u32[]{:S(2)}) collective-permute-start(bf16[320,256]{1,0:T(8,128)(2,1)S(1)} %pad_maximum_fusion.3), channel_id=1, source_target_pairs={{0,4},{2,6},{4,0},{6,2},{8,12},{10,14},{12,8},{14,10},{16,20},{18,... | collective-permute-start | bytes 491528 | tf_op jit(solution)/shard_map/ppermute | solution.py:300
  46.6 4.7 %collective-permute-start.12 = (bf16[192,256]{1,0:T(8,128)(2,1)S(1)}, bf16[192,256]{1,0:T(8,128)(2,1)S(1)}, u32[]{:S(2)}, u32[]{:S(2)}) collective-permute-start(bf16[192,256]{1,0:T(8,128)(2,1)S(1)} %pad_maximum_fusion.4), channel_id=1, source_target_pairs={{0,4},{2,6},{4,0},{6,2},{8,12},{10,14},{12,8},{14,10},{16,20},{18,... | collective-permute-start | bytes 294920 | tf_op jit(solution)/shard_map/ppermute | solution.py:300
  50.2 2.6 %collective-permute-start.11 = (bf16[640,256]{1,0:T(8,128)(2,1)S(1)}, bf16[640,256]{1,0:T(8,128)(2,1)S(1)}, u32[]{:S(2)}, u32[]{:S(2)}) collective-permute-start(bf16[640,256]{1,0:T(8,128)(2,1)S(1)} %pad_maximum_fusion.refs_2_), channel_id=1, source_target_pairs={{0,2},{2,0},{4,6},{6,4},{8,10},{10,8},{12,14},{14,12},{16,18},{18,... | collective-permute-start | bytes 983048 | tf_op jit(solution)/shard_map/ppermute | solution.py:300
  51.3 1.5 %collective-permute-start.13 = (bf16[384,256]{1,0:T(8,128)(2,1)S(1)}, bf16[384,256]{1,0:T(8,128)(2,1)S(1)}, u32[]{:S(2)}, u32[]{:S(2)}) collective-permute-start(bf16[384,256]{1,0:T(8,128)(2,1)S(1)} %pad_maximum_fusion.2.refs_4_), channel_id=1, source_target_pairs={{0,2},{2,0},{4,6},{6,4},{8,10},{10,8},{12,14},{14,12},{16,18},{18,... | collective-permute-start | bytes 589832 | tf_op jit(solution)/shard_map/ppermute | solution.py:300

commit v15 on v14

--- a/solution.py
+++ b/solution.py
@@ -239,10 +239,7 @@
 
         start = context * group_rows
         first = start + shard * rows
-        early.tables = tables(start + places_of(early.top, early.rows), head_size)
-        own_product, early.tables, kept = lax.optimization_barrier(
-            (own_product, early.tables, kept)
-        )
+        own_product, kept = lax.optimization_barrier((own_product, kept))
 
         def exchange(part, gate):
             arrived = []
@@ -313,6 +310,7 @@
             .reshape(heads * rows, head_size)
         )
         base = first - shard * rows
+        early.tables = tables(base + places_of(early.top, early.rows), head_size)
         late.tables = tables(base + places_of(late.top, late.rows), head_size)
         top_bit = stages[0]
         upper = ((context & top_bit) != 0).astype(jnp.int32)
@@ -322,16 +320,18 @@
             all_masks = all_masks + [mask ^ bit for mask in all_masks]
         slots = tuple(sorted(range(contexts), key=lambda slot: all_masks[slot] & top_bit))
         turns = jnp.array([all_masks[slot] for slot in slots], jnp.int32)
-        sources = (context ^ turns)[:, None] * group_rows
-        query_flat, late.tables, span = lax.optimization_barrier((query_flat, late.tables, span))
-        exchange(late, query_flat)
-        combine(early, late.sums)
-        advance(early)
+        query_flat, early.tables, late.tables, span = lax.optimization_barrier(
+            (query_flat, early.tables, late.tables, span)
+        )
+        combine(early, query_flat, *flying[early.end])
+        exchange(late, early.known)
+        advance(early, late.sums)
         combine(late, early.known)
         advance(late)
         for stage in range(1, len(stages)):
             advance(early, late.known)
             advance(late, early.known)
+        sources = (after(context, late.known) ^ turns)[:, None] * group_rows
         places = [
             (sources + places_of(part.top, part.rows)[None, :]).reshape(1, -1) for part in parts
         ]

time: 57.1 us -> 56.6 us (level)
  waiting for transfers between devices: 7.09 us -> 15.6 us
  other arithmetic: 7.73 us -> 3.87 us
  local copies, waits for them, and re-layouts: 7.25 us -> 4.1 us
  matrix products: 10.6 us -> 7.63 us
  starting transfers between devices: 19.1 us -> 20.5 us
    ppermute x4, waiting for transfers between devices: 1.23 us -> 7.95 us  [send(): lax.ppermute(after(columns[step - 1], *earlier) if earlier else columns[s...]
    dot_general x10, matrix products: 10.6 us -> 7.63 us  [project(): jnp.dot(columns, weight, preferred_element_type=jnp.float32)]
    ppermute x2, starting transfers between devices: 1.72 us -> 3.93 us  [exchange(): lax.ppermute(part.sums, 'fsdp', [(i, i ^ reach) for i in range(shards)])]
    add x2, other arithmetic: 1.94 us -> 0.14 us  [local(): sources + places_of(part.top, part.rows)[None, :]]
    add x2, local copies, waits for them, and re-layouts: 1.54 us -> 0.17 us  [local(): sources + places_of(part.top, part.rows)[None, :]]
    unnamed x24 -> x20, local copies, waits for them, and re-layouts: 2.92 us -> 1.68 us
    ppermute x8, starting transfers between devices: 12.3 us -> 11.2 us  [advance(): part.fresh = [lax.ppermute(part.known, 'ctx', pairs)]]
    ppermute x2, waiting for transfers between devices: 0.68 us -> 1.76 us  [exchange(): lax.ppermute(part.sums, 'fsdp', [(i, i ^ reach) for i in range(shards)])]
  transfers between devices with their start and end apart: 14 -> 14, of which waited for: 9 -> 9; matrix products, arithmetic and copies ran while one was open for 39% -> 21% of each run, Pallas kernels for 0% -> 0%
where the time goes in v15:
time: 56.6 us; the launch traced here: 56.1 us
  starting transfers between devices  20.5 us (36%)
  waiting for transfers between devices  15.6 us (28%)
  matrix products  7.63 us (13%)
  local copies, waits for them, and re-layouts  4.1 us (7%)
  other arithmetic  3.87 us (7%)
  Pallas kernels  3.43 us (6%)
  between operations  0.98 us (2%)
    ppermute x8, starting transfers between devices, advance(): part.fresh = [lax.ppermute(part.known, 'ctx', pairs)]  11.2 us
    ppermute x4, waiting for transfers between devices, send(): lax.ppermute(after(columns[step - 1], *earlier) if earlier else columns[s...  7.95 us
    dot_general x10, matrix products, project(): jnp.dot(columns, weight, preferred_element_type=jnp.float32)  7.63 us
    ppermute x8, waiting for transfers between devices, advance(): part.fresh = [lax.ppermute(part.known, 'ctx', pairs)]  5.89 us
    ppermute x4, starting transfers between devices, send(): lax.ppermute(after(columns[step - 1], *earlier) if earlier else columns[s...  5.33 us
    ppermute x2, starting transfers between devices, exchange(): lax.ppermute(part.sums, 'fsdp', [(i, i ^ reach) for i in range(shards)])  3.93 us
    pallas_call x1, Pallas kernels, attend(): pl.pallas_call(partial(attention_kernel, count=len(places), slots=slots,...  3.43 us
    dynamic_slice x4, local copies, waits for them, and re-layouts, cut(): lax.dynamic_slice(source, (jnp.int32(top), lax.rem(shard + step, shards)...  2.07 us
  transfers between devices with their start and end apart: 14, of which 9 were waited for; matrix products, arithmetic and copies ran while one was open for 21% of the time, Pallas kernels for 0%

profile of v15, /device:TPU:0, one launch (start us, length us, event | category | flops | bytes accessed | tf_op | source)
XLA Modules:
  0.0 56.1 jit_solution(12037272358475467980)
XLA Ops:
  0.7 1.6 %copy-done = bf16[64,16384]{1,0:T(8,128)(2,1)S(1)} copy-done((bf16[64,16384]{1,0:T(8,128)(2,1)S(1)}, bf16[64,16384]{1,0:T(8,128)(2,1)}, u32[]{:S(2)}) %copy-start) | copy-done | bytes 2097176
  2.2 0.6 %constant_dynamic-slice_fusion.2 = bf16[8,8192]{1,0:T(8,128)(2,1)} fusion(bf16[64,16384]{1,0:T(8,128)(2,1)S(1)} %copy-done, s32[]{:T(128)S(6)} %select_n.40), kind=kLoop, calls=%fused_computation.47 | loop fusion | bytes 262148 | tf_op jit(solution)/shard_map/dynamic_slice | solution.py:177
  2.9 2.9 %collective-permute-start = (bf16[8,8192]{1,0:T(8,128)(2,1)}, bf16[8,8192]{1,0:T(8,128)(2,1)S(1)}, u32[]{:S(2)}, u32[]{:S(2)}) collective-permute-start(bf16[8,8192]{1,0:T(8,128)(2,1)} %constant_dynamic-slice_fusion.2), channel_id=1, source_target_pairs={{0,1},{1,0},{2,3},{3,2},{4,5},{5,4},{6,7},{7,6},{8,9},{9,8},{10,11... | collective-permute-start | bytes 393224 | tf_op jit(solution)/shard_map/ppermute | solution.py:187
  5.9 0.7 %constant_dynamic-slice_fusion.4 = bf16[16,8192]{1,0:T(8,128)(2,1)} fusion(bf16[64,16384]{1,0:T(8,128)(2,1)S(1)} %copy-done, s32[]{:T(128)S(6)} %select_n.40), kind=kLoop, calls=%fused_computation.57 | loop fusion | bytes 524292 | tf_op jit(solution)/shard_map/dynamic_slice | solution.py:177
  6.7 2.0 %collective-permute-start.3 = (bf16[16,8192]{1,0:T(8,128)(2,1)}, bf16[16,8192]{1,0:T(8,128)(2,1)S(1)}, u32[]{:S(2)}, u32[]{:S(2)}) collective-permute-start(bf16[16,8192]{1,0:T(8,128)(2,1)} %constant_dynamic-slice_fusion.4), channel_id=1, source_target_pairs={{0,1},{1,0},{2,3},{3,2},{4,5},{5,4},{6,7},{7,6},{8,9},{9,8},{10,11... | collective-permute-start | bytes 786440 | tf_op jit(solution)/shard_map/ppermute | solution.py:187
  8.7 0.7 %constant_dynamic-slice_fusion.3 = bf16[8,8192]{1,0:T(8,128)(2,1)} fusion(bf16[64,16384]{1,0:T(8,128)(2,1)S(1)} %copy-done, s32[]{:T(128)S(6)} %select_n.40), kind=kLoop, calls=%fused_computation.55 | loop fusion | bytes 262148 | tf_op jit(solution)/shard_map/dynamic_slice | solution.py:177
  9.3 2.2 %fusion = f32[64,128]{1,0:T(8,128)S(1)} fusion(bf16[8192,128]{1,0:T(8,128)(2,1)} %param.8, bf16[64,16384]{1,0:T(8,128)(2,1)S(1)} %copy-done, s32[]{:T(128)S(6)} %select_n.41), kind=kOutput, calls=%fused_computation | convolution fusion | flops 134217728 | bytes 3178500 | tf_op jit(solution)/shard_map/dot_general | solution.py:231
  11.6 0.5 fusion.2
  12.2 0.6 %pad_maximum_fusion.7 = f32[64,256]{1,0:T(8,128)} fusion(f32[64,128]{1,0:T(8,128)S(1)} %fusion, f32[64,128]{1,0:T(8,128)S(1)} %fusion.2), kind=kLoop, calls=%fused_computation.15 | loop fusion | flops 16384 | bytes 131072 | tf_op jit(solution)/shard_map/concatenate | solution.py:229
  13.0 2.1 %fusion.7 = f32[8,128]{1,0:T(8,128)S(1)} fusion(bf16[8,8192]{1,0:T(8,128)(2,1)S(1)} %collective-permute-done, bf16[8192,128]{1,0:T(8,128)(2,1)} %param.8), kind=kOutput, calls=%fused_computation.60 | convolution fusion | flops 16777216 | bytes 2232320 | tf_op jit(solution)/shard_map/dot_general | solution.py:231
  15.2 0.4 fusion.6
  15.6 6.0 %collective-permute-done.1 = bf16[32,8192]{1,0:T(8,128)(2,1)S(1)} collective-permute-done((bf16[32,8192]{1,0:T(8,128)(2,1)S(1)}, bf16[32,8192]{1,0:T(8,128)(2,1)S(1)}, u32[]{:S(2)}, u32[]{:S(2)}) %collective-permute-start.1) | collective-permute-done | bytes 524320 | tf_op jit(solution)/shard_map/ppermute | solution.py:187
  21.6 0.4 fusion.9
  22.1 0.4 fusion.8
  22.5 2.1 %collective-permute-start.2 = (f32[80,256]{1,0:T(8,128)S(1)}, f32[80,256]{1,0:T(8,128)S(1)}, u32[]{:S(2)}, u32[]{:S(2)}) collective-permute-start(f32[80,256]{1,0:T(8,128)S(1)} %pad_maximum_fusion.5), channel_id=1, source_target_pairs={{0,1},{1,0},{2,3},{3,2},{4,5},{5,4},{6,7},{7,6},{8,9},{9,8},{10,11... | collective-permute-start | bytes 245768 | tf_op jit(solution)/shard_map/ppermute | solution.py:275
  24.7 0.3 collective-permute-start.4
  25.1 0.2 multiply_cosine_fusion.1
  25.3 0.2 multiply_sine_fusion
  25.5 0.3 subtract_convert_fusion
  25.8 0.2 multiply_sine_fusion.2
  26.0 0.1 pad_maximum_fusion.1.query_ref
  26.2 1.0 %collective-permute-done.3 = bf16[16,8192]{1,0:T(8,128)(2,1)S(1)} collective-permute-done((bf16[16,8192]{1,0:T(8,128)(2,1)}, bf16[16,8192]{1,0:T(8,128)(2,1)S(1)}, u32[]{:S(2)}, u32[]{:S(2)}) %collective-permute-start.3) | collective-permute-done | bytes 262176 | tf_op jit(solution)/shard_map/ppermute | solution.py:187
  27.2 1.8 %collective-permute-done.2 = f32[80,256]{1,0:T(8,128)S(1)} collective-permute-done((f32[80,256]{1,0:T(8,128)S(1)}, f32[80,256]{1,0:T(8,128)S(1)}, u32[]{:S(2)}, u32[]{:S(2)}) %collective-permute-start.2) | collective-permute-done | bytes 81952 | tf_op jit(solution)/shard_map/ppermute | solution.py:275
  29.0 0.1 subtract_convert_fusion.1
  29.1 0.1 pad_maximum_fusion.10
  29.2 0.4 fusion.11
  29.6 0.4 fusion.10
  30.0 1.0 %collective-permute-done.4 = bf16[8,8192]{1,0:T(8,128)(2,1)S(1)} collective-permute-done((bf16[8,8192]{1,0:T(8,128)(2,1)S(1)}, bf16[8,8192]{1,0:T(8,128)(2,1)S(1)}, u32[]{:S(2)}, u32[]{:S(2)}) %collective-permute-start.4) | collective-permute-done | bytes 131104 | tf_op jit(solution)/shard_map/ppermute | solution.py:187
  30.9 0.4 fusion.13
  31.3 0.4 fusion.12
  31.7 0.8 %slice_select_fusion.3 = (f32[24,256]{1,0:T(8,128)S(1)}, f32[24,256]{1,0:T(8,128)S(1)}) fusion(f32[64,256]{1,0:T(8,128)} %pad_maximum_fusion.7, f32[8,128]{1,0:T(8,128)S(1)} %fusion.13, f32[8,128]{1,0:T(8,128)S(1)} %fusion.12, f32[16,128]{1,0:T(8,128)S(1)} %fusion.11, f32[16,128]{1,0:T(8,128)S(1)} %fusion.10, pred[]{:T(512)S(6)} %eq.2), kind=kLoop, calls=%fused_computation.38 | loop fusion | flops 30720 | bytes 98305 | tf_op jit(solution)/shard_map/jit(_where)/select_n | solution.py:257
  32.5 1.8 %collective-permute-start.5 = (f32[48,256]{1,0:T(8,128)S(1)}, f32[48,256]{1,0:T(8,128)S(1)}, u32[]{:S(2)}, u32[]{:S(2)}) collective-permute-start(f32[48,256]{1,0:T(8,128)S(1)} %pad_maximum_fusion.8), channel_id=1, source_target_pairs={{0,1},{1,0},{2,3},{3,2},{4,5},{5,4},{6,7},{7,6},{8,9},{9,8},{10,11... | collective-permute-start | bytes 147464 | tf_op jit(solution)/shard_map/ppermute | solution.py:275
  34.3 2.6 %collective-permute-start.7 = (bf16[80,256]{1,0:T(8,128)(2,1)S(1)}, bf16[80,256]{1,0:T(8,128)(2,1)S(1)}, u32[]{:S(2)}, u32[]{:S(2)}) collective-permute-start(bf16[80,256]{1,0:T(8,128)(2,1)S(1)} %pad_maximum_fusion.10), channel_id=1, source_target_pairs={{0,16},{2,18},{4,20},{6,22},{8,24},{10,26},{12,28},{14,30},{16,0},... | collective-permute-start | bytes 122888 | tf_op jit(solution)/shard_map/ppermute | solution.py:297
  37.0 0.1 pad_maximum_fusion.12
  37.1 2.6 %collective-permute-start.6 = (bf16[48,256]{1,0:T(8,128)(2,1)S(1)}, bf16[48,256]{1,0:T(8,128)(2,1)S(1)}, u32[]{:S(2)}, u32[]{:S(2)}) collective-permute-start(bf16[48,256]{1,0:T(8,128)(2,1)S(1)} %pad_maximum_fusion.12), channel_id=1, source_target_pairs={{0,16},{2,18},{4,20},{6,22},{8,24},{10,26},{12,28},{14,30},{16,0},... | collective-permute-start | bytes 73736 | tf_op jit(solution)/shard_map/ppermute | solution.py:297
  39.7 1.6 %collective-permute-start.9 = (bf16[160,256]{1,0:T(8,128)(2,1)S(1)}, bf16[160,256]{1,0:T(8,128)(2,1)S(1)}, u32[]{:S(2)}, u32[]{:S(2)}) collective-permute-start(bf16[160,256]{1,0:T(8,128)(2,1)S(1)} %pad_maximum_fusion.6), channel_id=1, source_target_pairs={{0,8},{2,10},{4,12},{6,14},{8,0},{10,2},{12,4},{14,6},{16,24},{18,... | collective-permute-start | bytes 245768 | tf_op jit(solution)/shard_map/ppermute | solution.py:297
  41.3 0.5 collective-permute-done.6
  41.8 1.6 %collective-permute-start.8 = (bf16[96,256]{1,0:T(8,128)(2,1)S(1)}, bf16[96,256]{1,0:T(8,128)(2,1)S(1)}, u32[]{:S(2)}, u32[]{:S(2)}) collective-permute-start(bf16[96,256]{1,0:T(8,128)(2,1)S(1)} %pad_maximum_fusion.9), channel_id=1, source_target_pairs={{0,8},{2,10},{4,12},{6,14},{8,0},{10,2},{12,4},{14,6},{16,24},{18,... | collective-permute-start | bytes 147464 | tf_op jit(solution)/shard_map/ppermute | solution.py:297
  43.4 0.8 %collective-permute-done.9 = bf16[160,256]{1,0:T(8,128)(2,1)S(1)} collective-permute-done((bf16[160,256]{1,0:T(8,128)(2,1)S(1)}, bf16[160,256]{1,0:T(8,128)(2,1)S(1)}, u32[]{:S(2)}, u32[]{:S(2)}) %collective-permute-start.9) | collective-permute-done | bytes 81952 | tf_op jit(solution)/shard_map/ppermute | solution.py:297
  44.2 1.6 %collective-permute-start.11 = (bf16[320,256]{1,0:T(8,128)(2,1)S(1)}, bf16[320,256]{1,0:T(8,128)(2,1)S(1)}, u32[]{:S(2)}, u32[]{:S(2)}) collective-permute-start(bf16[320,256]{1,0:T(8,128)(2,1)S(1)} %pad_maximum_fusion.3), channel_id=1, source_target_pairs={{0,4},{2,6},{4,0},{6,2},{8,12},{10,14},{12,8},{14,10},{16,20},{18,... | collective-permute-start | bytes 491528 | tf_op jit(solution)/shard_map/ppermute | solution.py:297
  45.8 0.6 %pad_maximum_fusion.11 = bf16[64,256]{1,0:T(8,128)(2,1)} fusion(bf16[24,256]{1,0:T(8,128)(2,1)S(1)} %constant_dynamic-slice_fusion, bf16[40,256]{1,0:T(8,128)(2,1)S(1)} %constant_dynamic-slice_fusion.1), kind=kLoop, calls=%fused_computation.31 | loop fusion | flops 65536 | bytes 65536 | tf_op jit(solution)/shard_map/concatenate | solution.py:341
  46.4 1.1 %collective-permute-start.10 = (bf16[192,256]{1,0:T(8,128)(2,1)S(1)}, bf16[192,256]{1,0:T(8,128)(2,1)S(1)}, u32[]{:S(2)}, u32[]{:S(2)}) collective-permute-start(bf16[192,256]{1,0:T(8,128)(2,1)S(1)} %pad_maximum_fusion.4), channel_id=1, source_target_pairs={{0,4},{2,6},{4,0},{6,2},{8,12},{10,14},{12,8},{14,10},{16,20},{18,... | collective-permute-start | bytes 294920 | tf_op jit(solution)/shard_map/ppermute | solution.py:297
  47.5 2.1 %collective-permute-done.11 = bf16[320,256]{1,0:T(8,128)(2,1)S(1)} collective-permute-done((bf16[320,256]{1,0:T(8,128)(2,1)S(1)}, bf16[320,256]{1,0:T(8,128)(2,1)S(1)}, u32[]{:S(2)}, u32[]{:S(2)}) %collective-permute-start.11) | collective-permute-done | bytes 163872 | tf_op jit(solution)/shard_map/ppermute | solution.py:297
  49.7 1.4 %collective-permute-done.10 = bf16[192,256]{1,0:T(8,128)(2,1)S(1)} collective-permute-done((bf16[192,256]{1,0:T(8,128)(2,1)S(1)}, bf16[192,256]{1,0:T(8,128)(2,1)S(1)}, u32[]{:S(2)}, u32[]{:S(2)}) %collective-permute-start.10) | collective-permute-done | bytes 98336 | tf_op jit(solution)/shard_map/ppermute | solution.py:297
  51.3 0.1 add.234.refs_0_
  51.5 0.1 add.238.refs_1_
  51.6 1.1 %collective-permute-done.13.refs_5_ = bf16[384,256]{1,0:T(8,128)(2,1)S(1)} collective-permute-done((bf16[384,256]{1,0:T(8,128)(2,1)S(1)}, bf16[384,256]{1,0:T(8,128)(2,1)S(1)}, u32[]{:S(2)}, u32[]{:S(2)}) %collective-permute-start.13) | collective-permute-done | bytes 196640 | tf_op jit(solution)/shard_map/ppermute | solution.py:297
  52.7 3.4 %attend.1 = bf16[64,2048]{1,0:T(8,128)(2,1)} custom-call(s32[3]{0:T(128)S(1)} %pad_add_fusion.span_ref, bf16[1024,128]{1,0:T(8,128)(2,1)S(1)} %pad_maximum_fusion.1.query_ref, s32[1,1280]{1,0:T(1,128)S(1)} %add.234.refs_0_, s32[1,768]{1,0:T(1,128)S(1)} %add.238.refs_1_, bf16[640,256]{1,0:T(8,128)(2,1)S(1)} %pad_maximum_fusion.refs_2_, ...), custom_call_target="tpu_custom_call" | custom-call | flops 1073741824 | bytes 1572864 | tf_op jit(solution)/shard_map/attend/pallas_call | solution.py:124
  (59 shorter events, 1.2 us)
Async XLA Ops:
  0.6 1.6 %copy-start = (bf16[64,16384]{1,0:T(8,128)(2,1)S(1)}, bf16[64,16384]{1,0:T(8,128)(2,1)}, u32[]{:S(2)}) copy-start(bf16[64,16384]{1,0:T(8,128)(2,1)} %param.5) | copy-start | bytes 6291460
  2.9 10.2 %collective-permute-start = (bf16[8,8192]{1,0:T(8,128)(2,1)}, bf16[8,8192]{1,0:T(8,128)(2,1)S(1)}, u32[]{:S(2)}, u32[]{:S(2)}) collective-permute-start(bf16[8,8192]{1,0:T(8,128)(2,1)} %constant_dynamic-slice_fusion.2), channel_id=1, source_target_pairs={{0,1},{1,0},{2,3},{3,2},{4,5},{5,4},{6,7},{7,6},{8,9},{9,8},{10,11... | collective-permute-start | bytes 393224 | tf_op jit(solution)/shard_map/ppermute | solution.py:187
  5.8 15.7 %collective-permute-start.1 = (bf16[32,8192]{1,0:T(8,128)(2,1)S(1)}, bf16[32,8192]{1,0:T(8,128)(2,1)S(1)}, u32[]{:S(2)}, u32[]{:S(2)}) collective-permute-start(bf16[32,8192]{1,0:T(8,128)(2,1)S(1)} %constant_dynamic-slice_fusion.5), channel_id=1, source_target_pairs={{0,1},{1,0},{2,3},{3,2},{4,5},{5,4},{6,7},{7,6},{8,9},{9,8},{10,11... | collective-permute-start | bytes 1572872 | tf_op jit(solution)/shard_map/ppermute | solution.py:187
  6.7 20.5 %collective-permute-start.3 = (bf16[16,8192]{1,0:T(8,128)(2,1)}, bf16[16,8192]{1,0:T(8,128)(2,1)S(1)}, u32[]{:S(2)}, u32[]{:S(2)}) collective-permute-start(bf16[16,8192]{1,0:T(8,128)(2,1)} %constant_dynamic-slice_fusion.4), channel_id=1, source_target_pairs={{0,1},{1,0},{2,3},{3,2},{4,5},{5,4},{6,7},{7,6},{8,9},{9,8},{10,11... | collective-permute-start | bytes 786440 | tf_op jit(solution)/shard_map/ppermute | solution.py:187
  9.3 2.2 %copy-start.3 = (bf16[8192,128]{1,0:T(8,128)(2,1)S(1)}, bf16[8192,128]{1,0:T(8,128)(2,1)}, u32[]{:S(2)}) copy-start(bf16[8192,128]{1,0:T(8,128)(2,1)} %param.7) | copy-start | bytes 6291460
  13.0 2.2 %copy-start.4 = (bf16[8192,128]{1,0:T(8,128)(2,1)S(1)}, bf16[8192,128]{1,0:T(8,128)(2,1)}, u32[]{:S(2)}) copy-start(bf16[8192,128]{1,0:T(8,128)(2,1)} %param.7) | copy-start | bytes 6291460
  13.0 8.6 %copy-start.1 = (bf16[8192,128]{1,0:T(8,128)(2,1)S(1)}, bf16[8192,128]{1,0:T(8,128)(2,1)}, u32[]{:S(2)}) copy-start(bf16[8192,128]{1,0:T(8,128)(2,1)} %param.8) | copy-start | bytes 6291460
  15.6 6.9 %copy-start.7 = (f32[64,256]{1,0:T(8,128)S(1)}, f32[64,256]{1,0:T(8,128)}, u32[]{:S(2)}) copy-start(f32[64,256]{1,0:T(8,128)} %pad_maximum_fusion.7) | copy-start | bytes 196612
  22.0 2.7 %copy-start.8 = (bf16[8,8192]{1,0:T(8,128)(2,1)S(1)}, bf16[8,8192]{1,0:T(8,128)(2,1)}, u32[]{:S(2)}) copy-start(bf16[8,8192]{1,0:T(8,128)(2,1)} %constant_dynamic-slice_fusion.3) | copy-start | bytes 393220
  22.0 3.0 %copy-start.6 = (bf16[64,2048]{1,0:T(8,128)(2,1)S(1)}, bf16[64,2048]{1,0:T(8,128)(2,1)}, u32[]{:S(2)}) copy-start(bf16[64,2048]{1,0:T(8,128)(2,1)} %param.6) | copy-start | bytes 786436
  22.5 6.4 %collective-permute-start.2 = (f32[80,256]{1,0:T(8,128)S(1)}, f32[80,256]{1,0:T(8,128)S(1)}, u32[]{:S(2)}, u32[]{:S(2)}) collective-permute-start(f32[80,256]{1,0:T(8,128)S(1)} %pad_maximum_fusion.5), channel_id=1, source_target_pairs={{0,1},{1,0},{2,3},{3,2},{4,5},{5,4},{6,7},{7,6},{8,9},{9,8},{10,11... | collective-permute-start | bytes 245768 | tf_op jit(solution)/shard_map/ppermute | solution.py:275
  24.7 4.5 %copy-start.2 = (bf16[8192,128]{1,0:T(8,128)(2,1)S(1)}, bf16[8192,128]{1,0:T(8,128)(2,1)}, u32[]{:S(2)}) copy-start(bf16[8192,128]{1,0:T(8,128)(2,1)} %param.8) | copy-start | bytes 6291460
  24.7 6.2 %collective-permute-start.4 = (bf16[8,8192]{1,0:T(8,128)(2,1)S(1)}, bf16[8,8192]{1,0:T(8,128)(2,1)S(1)}, u32[]{:S(2)}, u32[]{:S(2)}) collective-permute-start(bf16[8,8192]{1,0:T(8,128)(2,1)S(1)} %copy-done.8), channel_id=1, source_target_pairs={{0,1},{1,0},{2,3},{3,2},{4,5},{5,4},{6,7},{7,6},{8,9},{9,8},{10,11... | collective-permute-start | bytes 393224 | tf_op jit(solution)/shard_map/ppermute | solution.py:187
  25.8 3.8 %copy-start.5 = (bf16[8192,128]{1,0:T(8,128)(2,1)S(1)}, bf16[8192,128]{1,0:T(8,128)(2,1)}, u32[]{:S(2)}) copy-start(bf16[8192,128]{1,0:T(8,128)(2,1)} %param.7) | copy-start | bytes 6291460
  31.3 19.9 %copy-start.9 = (s32[16]{0:T(128)S(1)}, s32[16]{0:T(128)}, u32[]{:S(2)}) copy-start(s32[16]{0:T(128)} %constant.47.clone) | copy-start | bytes 196
  32.5 4.4 %collective-permute-start.5 = (f32[48,256]{1,0:T(8,128)S(1)}, f32[48,256]{1,0:T(8,128)S(1)}, u32[]{:S(2)}, u32[]{:S(2)}) collective-permute-start(f32[48,256]{1,0:T(8,128)S(1)} %pad_maximum_fusion.8), channel_id=1, source_target_pairs={{0,1},{1,0},{2,3},{3,2},{4,5},{5,4},{6,7},{7,6},{8,9},{9,8},{10,11... | collective-permute-start | bytes 147464 | tf_op jit(solution)/shard_map/ppermute | solution.py:275
  34.3 5.4 %collective-permute-start.7 = (bf16[80,256]{1,0:T(8,128)(2,1)S(1)}, bf16[80,256]{1,0:T(8,128)(2,1)S(1)}, u32[]{:S(2)}, u32[]{:S(2)}) collective-permute-start(bf16[80,256]{1,0:T(8,128)(2,1)S(1)} %pad_maximum_fusion.10), channel_id=1, source_target_pairs={{0,16},{2,18},{4,20},{6,22},{8,24},{10,26},{12,28},{14,30},{16,0},... | collective-permute-start | bytes 122888 | tf_op jit(solution)/shard_map/ppermute | solution.py:297
  37.1 4.7 %collective-permute-start.6 = (bf16[48,256]{1,0:T(8,128)(2,1)S(1)}, bf16[48,256]{1,0:T(8,128)(2,1)S(1)}, u32[]{:S(2)}, u32[]{:S(2)}) collective-permute-start(bf16[48,256]{1,0:T(8,128)(2,1)S(1)} %pad_maximum_fusion.12), channel_id=1, source_target_pairs={{0,16},{2,18},{4,20},{6,22},{8,24},{10,26},{12,28},{14,30},{16,0},... | collective-permute-start | bytes 73736 | tf_op jit(solution)/shard_map/ppermute | solution.py:297
  39.7 4.5 %collective-permute-start.9 = (bf16[160,256]{1,0:T(8,128)(2,1)S(1)}, bf16[160,256]{1,0:T(8,128)(2,1)S(1)}, u32[]{:S(2)}, u32[]{:S(2)}) collective-permute-start(bf16[160,256]{1,0:T(8,128)(2,1)S(1)} %pad_maximum_fusion.6), channel_id=1, source_target_pairs={{0,8},{2,10},{4,12},{6,14},{8,0},{10,2},{12,4},{14,6},{16,24},{18,... | collective-permute-start | bytes 245768 | tf_op jit(solution)/shard_map/ppermute | solution.py:297
  41.8 4.6 %collective-permute-start.8 = (bf16[96,256]{1,0:T(8,128)(2,1)S(1)}, bf16[96,256]{1,0:T(8,128)(2,1)S(1)}, u32[]{:S(2)}, u32[]{:S(2)}) collective-permute-start(bf16[96,256]{1,0:T(8,128)(2,1)S(1)} %pad_maximum_fusion.9), channel_id=1, source_target_pairs={{0,8},{2,10},{4,12},{6,14},{8,0},{10,2},{12,4},{14,6},{16,24},{18,... | collective-permute-start | bytes 147464 | tf_op jit(solution)/shard_map/ppermute | solution.py:297
  44.2 5.4 %collective-permute-start.11 = (bf16[320,256]{1,0:T(8,128)(2,1)S(1)}, bf16[320,256]{1,0:T(8,128)(2,1)S(1)}, u32[]{:S(2)}, u32[]{:S(2)}) collective-permute-start(bf16[320,256]{1,0:T(8,128)(2,1)S(1)} %pad_maximum_fusion.3), channel_id=1, source_target_pairs={{0,4},{2,6},{4,0},{6,2},{8,12},{10,14},{12,8},{14,10},{16,20},{18,... | collective-permute-start | bytes 491528 | tf_op jit(solution)/shard_map/ppermute | solution.py:297
  46.4 4.7 %collective-permute-start.10 = (bf16[192,256]{1,0:T(8,128)(2,1)S(1)}, bf16[192,256]{1,0:T(8,128)(2,1)S(1)}, u32[]{:S(2)}, u32[]{:S(2)}) collective-permute-start(bf16[192,256]{1,0:T(8,128)(2,1)S(1)} %pad_maximum_fusion.4), channel_id=1, source_target_pairs={{0,4},{2,6},{4,0},{6,2},{8,12},{10,14},{12,8},{14,10},{16,20},{18,... | collective-permute-start | bytes 294920 | tf_op jit(solution)/shard_map/ppermute | solution.py:297
  49.6 3.0 %collective-permute-start.12 = (bf16[640,256]{1,0:T(8,128)(2,1)S(1)}, bf16[640,256]{1,0:T(8,128)(2,1)S(1)}, u32[]{:S(2)}, u32[]{:S(2)}) collective-permute-start(bf16[640,256]{1,0:T(8,128)(2,1)S(1)} %pad_maximum_fusion.refs_2_), channel_id=1, source_target_pairs={{0,2},{2,0},{4,6},{6,4},{8,10},{10,8},{12,14},{14,12},{16,18},{18,... | collective-permute-start | bytes 983048 | tf_op jit(solution)/shard_map/ppermute | solution.py:297
  51.1 1.5 %collective-permute-start.13 = (bf16[384,256]{1,0:T(8,128)(2,1)S(1)}, bf16[384,256]{1,0:T(8,128)(2,1)S(1)}, u32[]{:S(2)}, u32[]{:S(2)}) collective-permute-start(bf16[384,256]{1,0:T(8,128)(2,1)S(1)} %pad_maximum_fusion.2.refs_4_), channel_id=1, source_target_pairs={{0,2},{2,0},{4,6},{6,4},{8,10},{10,8},{12,14},{14,12},{16,18},{18,... | collective-permute-start | bytes 589832 | tf_op jit(solution)/shard_map/ppermute | solution.py:297

commit v16 on v15

--- a/solution.py
+++ b/solution.py
@@ -241,13 +241,12 @@
         first = start + shard * rows
         own_product, kept = lax.optimization_barrier((own_product, kept))
 
-        def exchange(part, gate):
-            arrived = []
-            for number in range(part.first, part.end):
+        def exchange(part, own, arrived, gate):
+            for number in range(part.first + len(arrived), part.end):
                 chunk, gate = lax.optimization_barrier((flying[number], gate))
                 gate = [project(columns) for columns in chunk]
                 arrived.append(gate)
-            products = [own_product[part.top : part.top + part.rows]] + [
+            products = [own] + [
                 jnp.concatenate([chunk[step] for chunk in arrived], axis=0)
                 for step in range(shards - 1)
             ]
@@ -298,7 +297,8 @@
                 part.masks = part.masks + [mask ^ bit for mask in part.masks]
             part.stage += 1
 
-        exchange(early, own_product)
+        early_own, late_own = own_product[: late.top], own_product[late.top :]
+        exchange(early, early_own, [], own_product)
         for columns in kept:
             flying.append(send(columns, early.sums))
         raw_queries, first = lax.optimization_barrier((queries, first, early.sums))[:2]
@@ -320,11 +320,12 @@
             all_masks = all_masks + [mask ^ bit for mask in all_masks]
         slots = tuple(sorted(range(contexts), key=lambda slot: all_masks[slot] & top_bit))
         turns = jnp.array([all_masks[slot] for slot in slots], jnp.int32)
-        query_flat, early.tables, late.tables, span = lax.optimization_barrier(
-            (query_flat, early.tables, late.tables, span)
+        late_own = after(late_own, early.sums)
+        query_flat, early.tables, late.tables, span, late_own = lax.optimization_barrier(
+            (query_flat, early.tables, late.tables, span, late_own)
         )
         combine(early, query_flat, *flying[early.end])
-        exchange(late, early.known)
+        exchange(late, late_own, [], early.known)
         advance(early, late.sums)
         combine(late, early.known)
         advance(late)

time: 56.6 us -> 55.8 us (0.986)
  other arithmetic: 3.87 us -> 3.13 us
    select_n x2, other arithmetic: 0.77 us -> 0.03 us  [exchange(): jnp.where(shard == 0, products[0], products[1])]
where the time goes in v16:
time: 55.8 us; the launch traced here: 55.4 us
  starting transfers between devices  20.5 us (37%)
  waiting for transfers between devices  15.5 us (28%)
  matrix products  7.64 us (14%)
  local copies, waits for them, and re-layouts  4.11 us (7%)
  Pallas kernels  3.44 us (6%)
  other arithmetic  3.13 us (6%)
  between operations  1.01 us (2%)
    ppermute x8, starting transfers between devices, advance(): part.fresh = [lax.ppermute(part.known, 'ctx', pairs)]  11.2 us
    ppermute x4, waiting for transfers between devices, send(): lax.ppermute(after(columns[step - 1], *earlier) if earlier else columns[s...  7.88 us
    dot_general x10, matrix products, project(): jnp.dot(columns, weight, preferred_element_type=jnp.float32)  7.64 us
    ppermute x8, waiting for transfers between devices, advance(): part.fresh = [lax.ppermute(part.known, 'ctx', pairs)]  5.87 us
    ppermute x4, starting transfers between devices, send(): lax.ppermute(after(columns[step - 1], *earlier) if earlier else columns[s...  5.37 us
    ppermute x2, starting transfers between devices, exchange(): lax.ppermute(part.sums, 'fsdp', [(i, i ^ reach) for i in range(shards)])  3.94 us
    pallas_call x1, Pallas kernels, attend(): pl.pallas_call(partial(attention_kernel, count=len(places), slots=slots,...  3.44 us
    dynamic_slice x4, local copies, waits for them, and re-layouts, cut(): lax.dynamic_slice(source, (jnp.int32(top), lax.rem(shard + step, shards)...  2.08 us
  transfers between devices with their start and end apart: 14, of which 9 were waited for; matrix products, arithmetic and copies ran while one was open for 21% of the time, Pallas kernels for 0%

profile of v16, /device:TPU:0, one launch (start us, length us, event | category | flops | bytes accessed | tf_op | source)
XLA Modules:
  0.0 55.4 jit_solution(6002229265234304823)
XLA Ops:
  0.7 1.6 %copy-done = bf16[64,16384]{1,0:T(8,128)(2,1)S(1)} copy-done((bf16[64,16384]{1,0:T(8,128)(2,1)S(1)}, bf16[64,16384]{1,0:T(8,128)(2,1)}, u32[]{:S(2)}) %copy-start) | copy-done | bytes 2097176
  2.2 0.7 %constant_dynamic-slice_fusion.2 = bf16[8,8192]{1,0:T(8,128)(2,1)} fusion(bf16[64,16384]{1,0:T(8,128)(2,1)S(1)} %copy-done, s32[]{:T(128)S(6)} %select_n.40), kind=kLoop, calls=%fused_computation.47 | loop fusion | bytes 262148 | tf_op jit(solution)/shard_map/dynamic_slice | solution.py:177
  2.9 2.9 %collective-permute-start = (bf16[8,8192]{1,0:T(8,128)(2,1)}, bf16[8,8192]{1,0:T(8,128)(2,1)S(1)}, u32[]{:S(2)}, u32[]{:S(2)}) collective-permute-start(bf16[8,8192]{1,0:T(8,128)(2,1)} %constant_dynamic-slice_fusion.2), channel_id=1, source_target_pairs={{0,1},{1,0},{2,3},{3,2},{4,5},{5,4},{6,7},{7,6},{8,9},{9,8},{10,11... | collective-permute-start | bytes 393224 | tf_op jit(solution)/shard_map/ppermute | solution.py:187
  5.9 0.7 %constant_dynamic-slice_fusion.4 = bf16[16,8192]{1,0:T(8,128)(2,1)} fusion(bf16[64,16384]{1,0:T(8,128)(2,1)S(1)} %copy-done, s32[]{:T(128)S(6)} %select_n.40), kind=kLoop, calls=%fused_computation.57 | loop fusion | bytes 524292 | tf_op jit(solution)/shard_map/dynamic_slice | solution.py:177
  6.7 2.0 %collective-permute-start.3 = (bf16[16,8192]{1,0:T(8,128)(2,1)}, bf16[16,8192]{1,0:T(8,128)(2,1)S(1)}, u32[]{:S(2)}, u32[]{:S(2)}) collective-permute-start(bf16[16,8192]{1,0:T(8,128)(2,1)} %constant_dynamic-slice_fusion.4), channel_id=1, source_target_pairs={{0,1},{1,0},{2,3},{3,2},{4,5},{5,4},{6,7},{7,6},{8,9},{9,8},{10,11... | collective-permute-start | bytes 786440 | tf_op jit(solution)/shard_map/ppermute | solution.py:187
  8.7 0.7 %constant_dynamic-slice_fusion.3 = bf16[8,8192]{1,0:T(8,128)(2,1)} fusion(bf16[64,16384]{1,0:T(8,128)(2,1)S(1)} %copy-done, s32[]{:T(128)S(6)} %select_n.40), kind=kLoop, calls=%fused_computation.55 | loop fusion | bytes 262148 | tf_op jit(solution)/shard_map/dynamic_slice | solution.py:177
  9.3 2.2 %fusion.2 = f32[64,128]{1,0:T(8,128)S(1)} fusion(bf16[8192,128]{1,0:T(8,128)(2,1)} %param.7, bf16[64,16384]{1,0:T(8,128)(2,1)S(1)} %copy-done, s32[]{:T(128)S(6)} %select_n.41), kind=kOutput, calls=%fused_computation.2 | convolution fusion | flops 134217728 | bytes 3178500 | tf_op jit(solution)/shard_map/dot_general | solution.py:231
  11.6 0.5 fusion
  12.2 0.6 %pad_maximum_fusion.7 = f32[64,256]{1,0:T(8,128)} fusion(f32[64,128]{1,0:T(8,128)S(1)} %fusion, f32[64,128]{1,0:T(8,128)S(1)} %fusion.2), kind=kLoop, calls=%fused_computation.15 | loop fusion | flops 16384 | bytes 131072 | tf_op jit(solution)/shard_map/concatenate | solution.py:229
  12.9 0.1 add.216
  13.0 2.1 %fusion.8 = f32[8,128]{1,0:T(8,128)S(1)} fusion(bf16[8,8192]{1,0:T(8,128)(2,1)S(1)} %collective-permute-done, bf16[8192,128]{1,0:T(8,128)(2,1)} %param.7), kind=kOutput, calls=%fused_computation.59 | convolution fusion | flops 16777216 | bytes 2232320 | tf_op jit(solution)/shard_map/dot_general | solution.py:231
  15.2 0.4 fusion.9
  15.6 6.0 %collective-permute-done.1 = bf16[32,8192]{1,0:T(8,128)(2,1)S(1)} collective-permute-done((bf16[32,8192]{1,0:T(8,128)(2,1)S(1)}, bf16[32,8192]{1,0:T(8,128)(2,1)S(1)}, u32[]{:S(2)}, u32[]{:S(2)}) %collective-permute-start.1) | collective-permute-done | bytes 524320 | tf_op jit(solution)/shard_map/ppermute | solution.py:187
  21.6 0.4 fusion.10
  22.0 0.4 fusion.11
  22.6 2.1 %collective-permute-start.2 = (f32[80,256]{1,0:T(8,128)S(1)}, f32[80,256]{1,0:T(8,128)S(1)}, u32[]{:S(2)}, u32[]{:S(2)}) collective-permute-start(f32[80,256]{1,0:T(8,128)S(1)} %pad_maximum_fusion.5), channel_id=1, source_target_pairs={{0,1},{1,0},{2,3},{3,2},{4,5},{5,4},{6,7},{7,6},{8,9},{9,8},{10,11... | collective-permute-start | bytes 245768 | tf_op jit(solution)/shard_map/ppermute | solution.py:274
  24.8 0.2 multiply_cosine_fusion.1
  25.0 0.2 multiply_sine_fusion
  25.2 0.3 subtract_convert_fusion
  25.5 0.2 multiply_sine_fusion.2
  25.7 0.1 pad_maximum_fusion.1.query_ref
  25.9 0.4 collective-permute-start.4
  26.3 0.9 %collective-permute-done.3 = bf16[16,8192]{1,0:T(8,128)(2,1)S(1)} collective-permute-done((bf16[16,8192]{1,0:T(8,128)(2,1)}, bf16[16,8192]{1,0:T(8,128)(2,1)S(1)}, u32[]{:S(2)}, u32[]{:S(2)}) %collective-permute-start.3) | collective-permute-done | bytes 262176 | tf_op jit(solution)/shard_map/ppermute | solution.py:187
  27.2 1.8 %collective-permute-done.2 = f32[80,256]{1,0:T(8,128)S(1)} collective-permute-done((f32[80,256]{1,0:T(8,128)S(1)}, f32[80,256]{1,0:T(8,128)S(1)}, u32[]{:S(2)}, u32[]{:S(2)}) %collective-permute-start.2) | collective-permute-done | bytes 81952 | tf_op jit(solution)/shard_map/ppermute | solution.py:274
  29.0 0.1 subtract_convert_fusion.1
  29.1 0.1 pad_maximum_fusion.10
  29.2 0.4 fusion.12
  29.6 0.4 fusion.13
  30.0 1.0 %collective-permute-done.4 = bf16[8,8192]{1,0:T(8,128)(2,1)S(1)} collective-permute-done((bf16[8,8192]{1,0:T(8,128)(2,1)S(1)}, bf16[8,8192]{1,0:T(8,128)(2,1)S(1)}, u32[]{:S(2)}, u32[]{:S(2)}) %collective-permute-start.4) | collective-permute-done | bytes 131104 | tf_op jit(solution)/shard_map/ppermute | solution.py:187
  30.9 0.4 fusion.14
  31.3 0.4 fusion.15
  31.8 1.8 %collective-permute-start.5 = (f32[48,256]{1,0:T(8,128)S(1)}, f32[48,256]{1,0:T(8,128)S(1)}, u32[]{:S(2)}, u32[]{:S(2)}) collective-permute-start(f32[48,256]{1,0:T(8,128)S(1)} %pad_maximum_fusion.8), channel_id=1, source_target_pairs={{0,1},{1,0},{2,3},{3,2},{4,5},{5,4},{6,7},{7,6},{8,9},{9,8},{10,11... | collective-permute-start | bytes 147464 | tf_op jit(solution)/shard_map/ppermute | solution.py:274
  33.6 2.6 %collective-permute-start.7 = (bf16[80,256]{1,0:T(8,128)(2,1)S(1)}, bf16[80,256]{1,0:T(8,128)(2,1)S(1)}, u32[]{:S(2)}, u32[]{:S(2)}) collective-permute-start(bf16[80,256]{1,0:T(8,128)(2,1)S(1)} %pad_maximum_fusion.10), channel_id=1, source_target_pairs={{0,16},{2,18},{4,20},{6,22},{8,24},{10,26},{12,28},{14,30},{16,0},... | collective-permute-start | bytes 122888 | tf_op jit(solution)/shard_map/ppermute | solution.py:296
  36.3 0.1 pad_maximum_fusion.12
  36.3 2.6 %collective-permute-start.6 = (bf16[48,256]{1,0:T(8,128)(2,1)S(1)}, bf16[48,256]{1,0:T(8,128)(2,1)S(1)}, u32[]{:S(2)}, u32[]{:S(2)}) collective-permute-start(bf16[48,256]{1,0:T(8,128)(2,1)S(1)} %pad_maximum_fusion.12), channel_id=1, source_target_pairs={{0,16},{2,18},{4,20},{6,22},{8,24},{10,26},{12,28},{14,30},{16,0},... | collective-permute-start | bytes 73736 | tf_op jit(solution)/shard_map/ppermute | solution.py:296
  39.0 1.6 %collective-permute-start.9 = (bf16[160,256]{1,0:T(8,128)(2,1)S(1)}, bf16[160,256]{1,0:T(8,128)(2,1)S(1)}, u32[]{:S(2)}, u32[]{:S(2)}) collective-permute-start(bf16[160,256]{1,0:T(8,128)(2,1)S(1)} %pad_maximum_fusion.6), channel_id=1, source_target_pairs={{0,8},{2,10},{4,12},{6,14},{8,0},{10,2},{12,4},{14,6},{16,24},{18,... | collective-permute-start | bytes 245768 | tf_op jit(solution)/shard_map/ppermute | solution.py:296
  40.6 0.5 collective-permute-done.6
  41.1 1.6 %collective-permute-start.8 = (bf16[96,256]{1,0:T(8,128)(2,1)S(1)}, bf16[96,256]{1,0:T(8,128)(2,1)S(1)}, u32[]{:S(2)}, u32[]{:S(2)}) collective-permute-start(bf16[96,256]{1,0:T(8,128)(2,1)S(1)} %pad_maximum_fusion.9), channel_id=1, source_target_pairs={{0,8},{2,10},{4,12},{6,14},{8,0},{10,2},{12,4},{14,6},{16,24},{18,... | collective-permute-start | bytes 147464 | tf_op jit(solution)/shard_map/ppermute | solution.py:296
  42.7 0.8 %collective-permute-done.9 = bf16[160,256]{1,0:T(8,128)(2,1)S(1)} collective-permute-done((bf16[160,256]{1,0:T(8,128)(2,1)S(1)}, bf16[160,256]{1,0:T(8,128)(2,1)S(1)}, u32[]{:S(2)}, u32[]{:S(2)}) %collective-permute-start.9) | collective-permute-done | bytes 81952 | tf_op jit(solution)/shard_map/ppermute | solution.py:296
  43.5 1.6 %collective-permute-start.11 = (bf16[320,256]{1,0:T(8,128)(2,1)S(1)}, bf16[320,256]{1,0:T(8,128)(2,1)S(1)}, u32[]{:S(2)}, u32[]{:S(2)}) collective-permute-start(bf16[320,256]{1,0:T(8,128)(2,1)S(1)} %pad_maximum_fusion.3), channel_id=1, source_target_pairs={{0,4},{2,6},{4,0},{6,2},{8,12},{10,14},{12,8},{14,10},{16,20},{18,... | collective-permute-start | bytes 491528 | tf_op jit(solution)/shard_map/ppermute | solution.py:296
  45.1 0.6 %pad_maximum_fusion.11 = bf16[64,256]{1,0:T(8,128)(2,1)} fusion(bf16[24,256]{1,0:T(8,128)(2,1)S(1)} %constant_dynamic-slice_fusion, bf16[40,256]{1,0:T(8,128)(2,1)S(1)} %constant_dynamic-slice_fusion.1), kind=kLoop, calls=%fused_computation.31 | loop fusion | flops 65536 | bytes 65536 | tf_op jit(solution)/shard_map/concatenate | solution.py:342
  45.7 1.1 %collective-permute-start.10 = (bf16[192,256]{1,0:T(8,128)(2,1)S(1)}, bf16[192,256]{1,0:T(8,128)(2,1)S(1)}, u32[]{:S(2)}, u32[]{:S(2)}) collective-permute-start(bf16[192,256]{1,0:T(8,128)(2,1)S(1)} %pad_maximum_fusion.4), channel_id=1, source_target_pairs={{0,4},{2,6},{4,0},{6,2},{8,12},{10,14},{12,8},{14,10},{16,20},{18,... | collective-permute-start | bytes 294920 | tf_op jit(solution)/shard_map/ppermute | solution.py:296
  46.8 2.1 %collective-permute-done.11 = bf16[320,256]{1,0:T(8,128)(2,1)S(1)} collective-permute-done((bf16[320,256]{1,0:T(8,128)(2,1)S(1)}, bf16[320,256]{1,0:T(8,128)(2,1)S(1)}, u32[]{:S(2)}, u32[]{:S(2)}) %collective-permute-start.11) | collective-permute-done | bytes 163872 | tf_op jit(solution)/shard_map/ppermute | solution.py:296
  49.0 1.4 %collective-permute-done.10 = bf16[192,256]{1,0:T(8,128)(2,1)S(1)} collective-permute-done((bf16[192,256]{1,0:T(8,128)(2,1)S(1)}, bf16[192,256]{1,0:T(8,128)(2,1)S(1)}, u32[]{:S(2)}, u32[]{:S(2)}) %collective-permute-start.10) | collective-permute-done | bytes 98336 | tf_op jit(solution)/shard_map/ppermute | solution.py:296
  50.6 0.1 add.234.refs_0_
  50.7 0.1 add.238.refs_1_
  50.8 1.1 %collective-permute-done.13.refs_5_ = bf16[384,256]{1,0:T(8,128)(2,1)S(1)} collective-permute-done((bf16[384,256]{1,0:T(8,128)(2,1)S(1)}, bf16[384,256]{1,0:T(8,128)(2,1)S(1)}, u32[]{:S(2)}, u32[]{:S(2)}) %collective-permute-start.13) | collective-permute-done | bytes 196640 | tf_op jit(solution)/shard_map/ppermute | solution.py:296
  51.9 3.4 %attend.1 = bf16[64,2048]{1,0:T(8,128)(2,1)} custom-call(s32[3]{0:T(128)S(1)} %pad_add_fusion.span_ref, bf16[1024,128]{1,0:T(8,128)(2,1)S(1)} %pad_maximum_fusion.1.query_ref, s32[1,1280]{1,0:T(1,128)S(1)} %add.234.refs_0_, s32[1,768]{1,0:T(1,128)S(1)} %add.238.refs_1_, bf16[640,256]{1,0:T(8,128)(2,1)S(1)} %pad_maximum_fusion.refs_2_, ...), custom_call_target="tpu_custom_call" | custom-call | flops 1073741824 | bytes 1572864 | tf_op jit(solution)/shard_map/attend/pallas_call | solution.py:124
  (61 shorter events, 1.1 us)
Async XLA Ops:
  0.6 1.6 %copy-start = (bf16[64,16384]{1,0:T(8,128)(2,1)S(1)}, bf16[64,16384]{1,0:T(8,128)(2,1)}, u32[]{:S(2)}) copy-start(bf16[64,16384]{1,0:T(8,128)(2,1)} %param.5) | copy-start | bytes 6291460
  2.9 10.2 %collective-permute-start = (bf16[8,8192]{1,0:T(8,128)(2,1)}, bf16[8,8192]{1,0:T(8,128)(2,1)S(1)}, u32[]{:S(2)}, u32[]{:S(2)}) collective-permute-start(bf16[8,8192]{1,0:T(8,128)(2,1)} %constant_dynamic-slice_fusion.2), channel_id=1, source_target_pairs={{0,1},{1,0},{2,3},{3,2},{4,5},{5,4},{6,7},{7,6},{8,9},{9,8},{10,11... | collective-permute-start | bytes 393224 | tf_op jit(solution)/shard_map/ppermute | solution.py:187
  5.9 15.7 %collective-permute-start.1 = (bf16[32,8192]{1,0:T(8,128)(2,1)S(1)}, bf16[32,8192]{1,0:T(8,128)(2,1)S(1)}, u32[]{:S(2)}, u32[]{:S(2)}) collective-permute-start(bf16[32,8192]{1,0:T(8,128)(2,1)S(1)} %constant_dynamic-slice_fusion.5), channel_id=1, source_target_pairs={{0,1},{1,0},{2,3},{3,2},{4,5},{5,4},{6,7},{7,6},{8,9},{9,8},{10,11... | collective-permute-start | bytes 1572872 | tf_op jit(solution)/shard_map/ppermute | solution.py:187
  6.7 20.5 %collective-permute-start.3 = (bf16[16,8192]{1,0:T(8,128)(2,1)}, bf16[16,8192]{1,0:T(8,128)(2,1)S(1)}, u32[]{:S(2)}, u32[]{:S(2)}) collective-permute-start(bf16[16,8192]{1,0:T(8,128)(2,1)} %constant_dynamic-slice_fusion.4), channel_id=1, source_target_pairs={{0,1},{1,0},{2,3},{3,2},{4,5},{5,4},{6,7},{7,6},{8,9},{9,8},{10,11... | collective-permute-start | bytes 786440 | tf_op jit(solution)/shard_map/ppermute | solution.py:187
  9.3 2.2 %copy-start.3 = (bf16[8192,128]{1,0:T(8,128)(2,1)S(1)}, bf16[8192,128]{1,0:T(8,128)(2,1)}, u32[]{:S(2)}) copy-start(bf16[8192,128]{1,0:T(8,128)(2,1)} %param.8) | copy-start | bytes 6291460
  13.0 2.2 %copy-start.4 = (bf16[8192,128]{1,0:T(8,128)(2,1)S(1)}, bf16[8192,128]{1,0:T(8,128)(2,1)}, u32[]{:S(2)}) copy-start(bf16[8192,128]{1,0:T(8,128)(2,1)} %param.8) | copy-start | bytes 6291460
  13.0 8.6 %copy-start.1 = (bf16[8192,128]{1,0:T(8,128)(2,1)S(1)}, bf16[8192,128]{1,0:T(8,128)(2,1)}, u32[]{:S(2)}) copy-start(bf16[8192,128]{1,0:T(8,128)(2,1)} %param.7) | copy-start | bytes 6291460
  15.6 6.9 %copy-start.7 = (f32[64,256]{1,0:T(8,128)S(1)}, f32[64,256]{1,0:T(8,128)}, u32[]{:S(2)}) copy-start(f32[64,256]{1,0:T(8,128)} %pad_maximum_fusion.7) | copy-start | bytes 196612
  22.0 2.7 %copy-start.6 = (bf16[64,2048]{1,0:T(8,128)(2,1)S(1)}, bf16[64,2048]{1,0:T(8,128)(2,1)}, u32[]{:S(2)}) copy-start(bf16[64,2048]{1,0:T(8,128)(2,1)} %param.6) | copy-start | bytes 786436
  22.5 3.4 %copy-start.8 = (bf16[8,8192]{1,0:T(8,128)(2,1)S(1)}, bf16[8,8192]{1,0:T(8,128)(2,1)}, u32[]{:S(2)}) copy-start(bf16[8,8192]{1,0:T(8,128)(2,1)} %constant_dynamic-slice_fusion.3) | copy-start | bytes 393220
  22.6 6.6 %copy-start.2 = (bf16[8192,128]{1,0:T(8,128)(2,1)S(1)}, bf16[8192,128]{1,0:T(8,128)(2,1)}, u32[]{:S(2)}) copy-start(bf16[8192,128]{1,0:T(8,128)(2,1)} %param.7) | copy-start | bytes 6291460
  22.6 6.4 %collective-permute-start.2 = (f32[80,256]{1,0:T(8,128)S(1)}, f32[80,256]{1,0:T(8,128)S(1)}, u32[]{:S(2)}, u32[]{:S(2)}) collective-permute-start(f32[80,256]{1,0:T(8,128)S(1)} %pad_maximum_fusion.5), channel_id=1, source_target_pairs={{0,1},{1,0},{2,3},{3,2},{4,5},{5,4},{6,7},{7,6},{8,9},{9,8},{10,11... | collective-permute-start | bytes 245768 | tf_op jit(solution)/shard_map/ppermute | solution.py:274
  25.5 4.1 %copy-start.5 = (bf16[8192,128]{1,0:T(8,128)(2,1)S(1)}, bf16[8192,128]{1,0:T(8,128)(2,1)}, u32[]{:S(2)}) copy-start(bf16[8192,128]{1,0:T(8,128)(2,1)} %param.8) | copy-start | bytes 6291460
  25.9 5.0 %collective-permute-start.4 = (bf16[8,8192]{1,0:T(8,128)(2,1)S(1)}, bf16[8,8192]{1,0:T(8,128)(2,1)S(1)}, u32[]{:S(2)}, u32[]{:S(2)}) collective-permute-start(bf16[8,8192]{1,0:T(8,128)(2,1)S(1)} %copy-done.8), channel_id=1, source_target_pairs={{0,1},{1,0},{2,3},{3,2},{4,5},{5,4},{6,7},{7,6},{8,9},{9,8},{10,11... | collective-permute-start | bytes 393224 | tf_op jit(solution)/shard_map/ppermute | solution.py:187
  30.0 1.7 %slice-start = ((f32[64,256]{1,0:T(8,128)}), f32[24,256]{1,0:T(8,128)S(1)}, s32[]{:S(2)}) async-start(f32[64,256]{1,0:T(8,128)} %pad_maximum_fusion.7), calls=%async_computation | async-start | bytes 49152 | tf_op jit(solution)/shard_map/slice | solution.py:300
  31.3 19.2 %copy-start.9 = (s32[16]{0:T(128)S(1)}, s32[16]{0:T(128)}, u32[]{:S(2)}) copy-start(s32[16]{0:T(128)} %constant.47.clone) | copy-start | bytes 196
  31.8 4.4 %collective-permute-start.5 = (f32[48,256]{1,0:T(8,128)S(1)}, f32[48,256]{1,0:T(8,128)S(1)}, u32[]{:S(2)}, u32[]{:S(2)}) collective-permute-start(f32[48,256]{1,0:T(8,128)S(1)} %pad_maximum_fusion.8), channel_id=1, source_target_pairs={{0,1},{1,0},{2,3},{3,2},{4,5},{5,4},{6,7},{7,6},{8,9},{9,8},{10,11... | collective-permute-start | bytes 147464 | tf_op jit(solution)/shard_map/ppermute | solution.py:274
  33.6 5.4 %collective-permute-start.7 = (bf16[80,256]{1,0:T(8,128)(2,1)S(1)}, bf16[80,256]{1,0:T(8,128)(2,1)S(1)}, u32[]{:S(2)}, u32[]{:S(2)}) collective-permute-start(bf16[80,256]{1,0:T(8,128)(2,1)S(1)} %pad_maximum_fusion.10), channel_id=1, source_target_pairs={{0,16},{2,18},{4,20},{6,22},{8,24},{10,26},{12,28},{14,30},{16,0},... | collective-permute-start | bytes 122888 | tf_op jit(solution)/shard_map/ppermute | solution.py:296
  36.3 4.7 %collective-permute-start.6 = (bf16[48,256]{1,0:T(8,128)(2,1)S(1)}, bf16[48,256]{1,0:T(8,128)(2,1)S(1)}, u32[]{:S(2)}, u32[]{:S(2)}) collective-permute-start(bf16[48,256]{1,0:T(8,128)(2,1)S(1)} %pad_maximum_fusion.12), channel_id=1, source_target_pairs={{0,16},{2,18},{4,20},{6,22},{8,24},{10,26},{12,28},{14,30},{16,0},... | collective-permute-start | bytes 73736 | tf_op jit(solution)/shard_map/ppermute | solution.py:296
  39.0 4.5 %collective-permute-start.9 = (bf16[160,256]{1,0:T(8,128)(2,1)S(1)}, bf16[160,256]{1,0:T(8,128)(2,1)S(1)}, u32[]{:S(2)}, u32[]{:S(2)}) collective-permute-start(bf16[160,256]{1,0:T(8,128)(2,1)S(1)} %pad_maximum_fusion.6), channel_id=1, source_target_pairs={{0,8},{2,10},{4,12},{6,14},{8,0},{10,2},{12,4},{14,6},{16,24},{18,... | collective-permute-start | bytes 245768 | tf_op jit(solution)/shard_map/ppermute | solution.py:296
  41.1 4.6 %collective-permute-start.8 = (bf16[96,256]{1,0:T(8,128)(2,1)S(1)}, bf16[96,256]{1,0:T(8,128)(2,1)S(1)}, u32[]{:S(2)}, u32[]{:S(2)}) collective-permute-start(bf16[96,256]{1,0:T(8,128)(2,1)S(1)} %pad_maximum_fusion.9), channel_id=1, source_target_pairs={{0,8},{2,10},{4,12},{6,14},{8,0},{10,2},{12,4},{14,6},{16,24},{18,... | collective-permute-start | bytes 147464 | tf_op jit(solution)/shard_map/ppermute | solution.py:296
  43.5 5.4 %collective-permute-start.11 = (bf16[320,256]{1,0:T(8,128)(2,1)S(1)}, bf16[320,256]{1,0:T(8,128)(2,1)S(1)}, u32[]{:S(2)}, u32[]{:S(2)}) collective-permute-start(bf16[320,256]{1,0:T(8,128)(2,1)S(1)} %pad_maximum_fusion.3), channel_id=1, source_target_pairs={{0,4},{2,6},{4,0},{6,2},{8,12},{10,14},{12,8},{14,10},{16,20},{18,... | collective-permute-start | bytes 491528 | tf_op jit(solution)/shard_map/ppermute | solution.py:296
  45.7 4.7 %collective-permute-start.10 = (bf16[192,256]{1,0:T(8,128)(2,1)S(1)}, bf16[192,256]{1,0:T(8,128)(2,1)S(1)}, u32[]{:S(2)}, u32[]{:S(2)}) collective-permute-start(bf16[192,256]{1,0:T(8,128)(2,1)S(1)} %pad_maximum_fusion.4), channel_id=1, source_target_pairs={{0,4},{2,6},{4,0},{6,2},{8,12},{10,14},{12,8},{14,10},{16,20},{18,... | collective-permute-start | bytes 294920 | tf_op jit(solution)/shard_map/ppermute | solution.py:296
  48.9 3.0 %collective-permute-start.12 = (bf16[640,256]{1,0:T(8,128)(2,1)S(1)}, bf16[640,256]{1,0:T(8,128)(2,1)S(1)}, u32[]{:S(2)}, u32[]{:S(2)}) collective-permute-start(bf16[640,256]{1,0:T(8,128)(2,1)S(1)} %pad_maximum_fusion.refs_2_), channel_id=1, source_target_pairs={{0,2},{2,0},{4,6},{6,4},{8,10},{10,8},{12,14},{14,12},{16,18},{18,... | collective-permute-start | bytes 983048 | tf_op jit(solution)/shard_map/ppermute | solution.py:296
  50.4 1.5 %collective-permute-start.13 = (bf16[384,256]{1,0:T(8,128)(2,1)S(1)}, bf16[384,256]{1,0:T(8,128)(2,1)S(1)}, u32[]{:S(2)}, u32[]{:S(2)}) collective-permute-start(bf16[384,256]{1,0:T(8,128)(2,1)S(1)} %pad_maximum_fusion.2.refs_4_), channel_id=1, source_target_pairs={{0,2},{2,0},{4,6},{6,4},{8,10},{10,8},{12,14},{14,12},{16,18},{18,... | collective-permute-start | bytes 589832 | tf_op jit(solution)/shard_map/ppermute | solution.py:296

commit v17 on v16

--- a/solution.py
+++ b/solution.py
@@ -33,7 +33,7 @@
     span_ref, query_ref, *refs, count, slots, owns, rows, head_size, stride
 ):
     places, refs = refs[:count], refs[count:]
-    pieces, (out_ref, scratch) = refs[: 2 * count], refs[2 * count :]
+    pieces, out_ref = refs[: 2 * count], refs[2 * count]
     start = span_ref[0]
     first = span_ref[1]
     factor = head_size ** (-0.5) * math.log2(math.e)
@@ -89,7 +89,12 @@
             numerator = jnp.dot(
                 weights.astype(jnp.bfloat16), values, preferred_element_type=jnp.float32
             )
-            scratch[place, :] = (numerator / total).astype(jnp.bfloat16)
+            result = (numerator * (1.0 / total)).astype(out_ref.dtype)
+            for head in range(stride // rows):
+                column = (turn * (stride // rows) + head) * head_size
+                out_ref[:, pl.ds(pl.multiple_of(column, head_size), head_size)] = result[
+                    head * rows : (head + 1) * rows, :
+                ]
 
         if flat // stride <= 8:
             for turn in range(flat // stride):
@@ -109,11 +114,6 @@
     @pl.when(upper == 0)
     def lower_keys():
         run(2)
-
-    for head in range(flat // rows):
-        out_ref[:, head * head_size : (head + 1) * head_size] = scratch[
-            head * rows : (head + 1) * rows, :
-        ]
 
 
 def attend(span, places, query_flat, pieces, slots, owns, rows):
@@ -135,7 +135,6 @@
         in_specs=[pl.BlockSpec(memory_space=pltpu.SMEM)]
         + [whole] * (1 + len(places) + len(pieces)),
         out_specs=whole,
-        scratch_shapes=[pltpu.VMEM((flat, head_size), jnp.bfloat16)],
         compiler_params=pltpu.CompilerParams(vmem_limit_bytes=24 * 1024 * 1024),
         cost_estimate=pl.CostEstimate(
             flops=4 * flat * width * head_size,

time: 55.8 us -> 55.7 us (level)
  no operation moved by 1% of the time
where the time goes in v17:
time: 55.7 us; the launch traced here: 55.3 us
  starting transfers between devices  20.5 us (37%)
  waiting for transfers between devices  15.5 us (28%)
  matrix products  7.64 us (14%)
  local copies, waits for them, and re-layouts  4.11 us (7%)
  Pallas kernels  3.39 us (6%)
  other arithmetic  3.13 us (6%)
  between operations  1.01 us (2%)
    ppermute x8, starting transfers between devices, advance(): part.fresh = [lax.ppermute(part.known, 'ctx', pairs)]  11.2 us
    ppermute x4, waiting for transfers between devices, send(): lax.ppermute(after(columns[step - 1], *earlier) if earlier else columns[s...  7.88 us
    dot_general x10, matrix products, project(): jnp.dot(columns, weight, preferred_element_type=jnp.float32)  7.64 us
    ppermute x8, waiting for transfers between devices, advance(): part.fresh = [lax.ppermute(part.known, 'ctx', pairs)]  5.87 us
    ppermute x4, starting transfers between devices, send(): lax.ppermute(after(columns[step - 1], *earlier) if earlier else columns[s...  5.37 us
    ppermute x2, starting transfers between devices, exchange(): lax.ppermute(part.sums, 'fsdp', [(i, i ^ reach) for i in range(shards)])  3.94 us
    pallas_call x1, Pallas kernels, attend(): pl.pallas_call(partial(attention_kernel, count=len(places), slots=slots,...  3.39 us
    dynamic_slice x4, local copies, waits for them, and re-layouts, cut(): lax.dynamic_slice(source, (jnp.int32(top), lax.rem(shard + step, shards)...  2.08 us
  transfers between devices with their start and end apart: 14, of which 9 were waited for; matrix products, arithmetic and copies ran while one was open for 21% of the time, Pallas kernels for 0%

profile of v17, /device:TPU:0, one launch (start us, length us, event | category | flops | bytes accessed | tf_op | source)
XLA Modules:
  0.0 55.3 jit_solution(826789154957796243)
XLA Ops:
  0.7 1.6 %copy-done = bf16[64,16384]{1,0:T(8,128)(2,1)S(1)} copy-done((bf16[64,16384]{1,0:T(8,128)(2,1)S(1)}, bf16[64,16384]{1,0:T(8,128)(2,1)}, u32[]{:S(2)}) %copy-start) | copy-done | bytes 2097176
  2.2 0.7 %constant_dynamic-slice_fusion.2 = bf16[8,8192]{1,0:T(8,128)(2,1)} fusion(bf16[64,16384]{1,0:T(8,128)(2,1)S(1)} %copy-done, s32[]{:T(128)S(6)} %select_n.40), kind=kLoop, calls=%fused_computation.47 | loop fusion | bytes 262148 | tf_op jit(solution)/shard_map/dynamic_slice | solution.py:176
  2.9 2.9 %collective-permute-start = (bf16[8,8192]{1,0:T(8,128)(2,1)}, bf16[8,8192]{1,0:T(8,128)(2,1)S(1)}, u32[]{:S(2)}, u32[]{:S(2)}) collective-permute-start(bf16[8,8192]{1,0:T(8,128)(2,1)} %constant_dynamic-slice_fusion.2), channel_id=1, source_target_pairs={{0,1},{1,0},{2,3},{3,2},{4,5},{5,4},{6,7},{7,6},{8,9},{9,8},{10,11... | collective-permute-start | bytes 393224 | tf_op jit(solution)/shard_map/ppermute | solution.py:186
  5.9 0.7 %constant_dynamic-slice_fusion.4 = bf16[16,8192]{1,0:T(8,128)(2,1)} fusion(bf16[64,16384]{1,0:T(8,128)(2,1)S(1)} %copy-done, s32[]{:T(128)S(6)} %select_n.40), kind=kLoop, calls=%fused_computation.57 | loop fusion | bytes 524292 | tf_op jit(solution)/shard_map/dynamic_slice | solution.py:176
  6.7 2.0 %collective-permute-start.3 = (bf16[16,8192]{1,0:T(8,128)(2,1)}, bf16[16,8192]{1,0:T(8,128)(2,1)S(1)}, u32[]{:S(2)}, u32[]{:S(2)}) collective-permute-start(bf16[16,8192]{1,0:T(8,128)(2,1)} %constant_dynamic-slice_fusion.4), channel_id=1, source_target_pairs={{0,1},{1,0},{2,3},{3,2},{4,5},{5,4},{6,7},{7,6},{8,9},{9,8},{10,11... | collective-permute-start | bytes 786440 | tf_op jit(solution)/shard_map/ppermute | solution.py:186
  8.7 0.7 %constant_dynamic-slice_fusion.3 = bf16[8,8192]{1,0:T(8,128)(2,1)} fusion(bf16[64,16384]{1,0:T(8,128)(2,1)S(1)} %copy-done, s32[]{:T(128)S(6)} %select_n.40), kind=kLoop, calls=%fused_computation.55 | loop fusion | bytes 262148 | tf_op jit(solution)/shard_map/dynamic_slice | solution.py:176
  9.3 2.2 %fusion.2 = f32[64,128]{1,0:T(8,128)S(1)} fusion(bf16[8192,128]{1,0:T(8,128)(2,1)} %param.7, bf16[64,16384]{1,0:T(8,128)(2,1)S(1)} %copy-done, s32[]{:T(128)S(6)} %select_n.41), kind=kOutput, calls=%fused_computation.2 | convolution fusion | flops 134217728 | bytes 3178500 | tf_op jit(solution)/shard_map/dot_general | solution.py:230
  11.6 0.5 fusion
  12.2 0.6 %pad_maximum_fusion.7 = f32[64,256]{1,0:T(8,128)} fusion(f32[64,128]{1,0:T(8,128)S(1)} %fusion, f32[64,128]{1,0:T(8,128)S(1)} %fusion.2), kind=kLoop, calls=%fused_computation.15 | loop fusion | flops 16384 | bytes 131072 | tf_op jit(solution)/shard_map/concatenate | solution.py:228
  12.9 0.1 add.216
  13.0 2.1 %fusion.8 = f32[8,128]{1,0:T(8,128)S(1)} fusion(bf16[8,8192]{1,0:T(8,128)(2,1)S(1)} %collective-permute-done, bf16[8192,128]{1,0:T(8,128)(2,1)} %param.7), kind=kOutput, calls=%fused_computation.59 | convolution fusion | flops 16777216 | bytes 2232320 | tf_op jit(solution)/shard_map/dot_general | solution.py:230
  15.2 0.4 fusion.9
  15.6 6.0 %collective-permute-done.1 = bf16[32,8192]{1,0:T(8,128)(2,1)S(1)} collective-permute-done((bf16[32,8192]{1,0:T(8,128)(2,1)S(1)}, bf16[32,8192]{1,0:T(8,128)(2,1)S(1)}, u32[]{:S(2)}, u32[]{:S(2)}) %collective-permute-start.1) | collective-permute-done | bytes 524320 | tf_op jit(solution)/shard_map/ppermute | solution.py:186
  21.6 0.4 fusion.10
  22.0 0.4 fusion.11
  22.6 2.1 %collective-permute-start.2 = (f32[80,256]{1,0:T(8,128)S(1)}, f32[80,256]{1,0:T(8,128)S(1)}, u32[]{:S(2)}, u32[]{:S(2)}) collective-permute-start(f32[80,256]{1,0:T(8,128)S(1)} %pad_maximum_fusion.5), channel_id=1, source_target_pairs={{0,1},{1,0},{2,3},{3,2},{4,5},{5,4},{6,7},{7,6},{8,9},{9,8},{10,11... | collective-permute-start | bytes 245768 | tf_op jit(solution)/shard_map/ppermute | solution.py:273
  24.8 0.2 multiply_cosine_fusion.1
  25.0 0.2 multiply_sine_fusion
  25.2 0.3 subtract_convert_fusion
  25.5 0.2 multiply_sine_fusion.2
  25.7 0.1 pad_maximum_fusion.1.query_ref
  25.9 0.4 collective-permute-start.4
  26.3 0.9 %collective-permute-done.3 = bf16[16,8192]{1,0:T(8,128)(2,1)S(1)} collective-permute-done((bf16[16,8192]{1,0:T(8,128)(2,1)}, bf16[16,8192]{1,0:T(8,128)(2,1)S(1)}, u32[]{:S(2)}, u32[]{:S(2)}) %collective-permute-start.3) | collective-permute-done | bytes 262176 | tf_op jit(solution)/shard_map/ppermute | solution.py:186
  27.2 1.8 %collective-permute-done.2 = f32[80,256]{1,0:T(8,128)S(1)} collective-permute-done((f32[80,256]{1,0:T(8,128)S(1)}, f32[80,256]{1,0:T(8,128)S(1)}, u32[]{:S(2)}, u32[]{:S(2)}) %collective-permute-start.2) | collective-permute-done | bytes 81952 | tf_op jit(solution)/shard_map/ppermute | solution.py:273
  29.0 0.1 subtract_convert_fusion.1
  29.1 0.1 pad_maximum_fusion.10
  29.2 0.4 fusion.12
  29.6 0.4 fusion.13
  30.0 1.0 %collective-permute-done.4 = bf16[8,8192]{1,0:T(8,128)(2,1)S(1)} collective-permute-done((bf16[8,8192]{1,0:T(8,128)(2,1)S(1)}, bf16[8,8192]{1,0:T(8,128)(2,1)S(1)}, u32[]{:S(2)}, u32[]{:S(2)}) %collective-permute-start.4) | collective-permute-done | bytes 131104 | tf_op jit(solution)/shard_map/ppermute | solution.py:186
  30.9 0.4 fusion.14
  31.3 0.4 fusion.15
  31.8 1.8 %collective-permute-start.5 = (f32[48,256]{1,0:T(8,128)S(1)}, f32[48,256]{1,0:T(8,128)S(1)}, u32[]{:S(2)}, u32[]{:S(2)}) collective-permute-start(f32[48,256]{1,0:T(8,128)S(1)} %pad_maximum_fusion.8), channel_id=1, source_target_pairs={{0,1},{1,0},{2,3},{3,2},{4,5},{5,4},{6,7},{7,6},{8,9},{9,8},{10,11... | collective-permute-start | bytes 147464 | tf_op jit(solution)/shard_map/ppermute | solution.py:273
  33.6 2.6 %collective-permute-start.7 = (bf16[80,256]{1,0:T(8,128)(2,1)S(1)}, bf16[80,256]{1,0:T(8,128)(2,1)S(1)}, u32[]{:S(2)}, u32[]{:S(2)}) collective-permute-start(bf16[80,256]{1,0:T(8,128)(2,1)S(1)} %pad_maximum_fusion.10), channel_id=1, source_target_pairs={{0,16},{2,18},{4,20},{6,22},{8,24},{10,26},{12,28},{14,30},{16,0},... | collective-permute-start | bytes 122888 | tf_op jit(solution)/shard_map/ppermute | solution.py:295
  36.3 0.1 pad_maximum_fusion.12
  36.3 2.6 %collective-permute-start.6 = (bf16[48,256]{1,0:T(8,128)(2,1)S(1)}, bf16[48,256]{1,0:T(8,128)(2,1)S(1)}, u32[]{:S(2)}, u32[]{:S(2)}) collective-permute-start(bf16[48,256]{1,0:T(8,128)(2,1)S(1)} %pad_maximum_fusion.12), channel_id=1, source_target_pairs={{0,16},{2,18},{4,20},{6,22},{8,24},{10,26},{12,28},{14,30},{16,0},... | collective-permute-start | bytes 73736 | tf_op jit(solution)/shard_map/ppermute | solution.py:295
  39.0 1.6 %collective-permute-start.9 = (bf16[160,256]{1,0:T(8,128)(2,1)S(1)}, bf16[160,256]{1,0:T(8,128)(2,1)S(1)}, u32[]{:S(2)}, u32[]{:S(2)}) collective-permute-start(bf16[160,256]{1,0:T(8,128)(2,1)S(1)} %pad_maximum_fusion.6), channel_id=1, source_target_pairs={{0,8},{2,10},{4,12},{6,14},{8,0},{10,2},{12,4},{14,6},{16,24},{18,... | collective-permute-start | bytes 245768 | tf_op jit(solution)/shard_map/ppermute | solution.py:295
  40.6 0.5 collective-permute-done.6
  41.1 1.6 %collective-permute-start.8 = (bf16[96,256]{1,0:T(8,128)(2,1)S(1)}, bf16[96,256]{1,0:T(8,128)(2,1)S(1)}, u32[]{:S(2)}, u32[]{:S(2)}) collective-permute-start(bf16[96,256]{1,0:T(8,128)(2,1)S(1)} %pad_maximum_fusion.9), channel_id=1, source_target_pairs={{0,8},{2,10},{4,12},{6,14},{8,0},{10,2},{12,4},{14,6},{16,24},{18,... | collective-permute-start | bytes 147464 | tf_op jit(solution)/shard_map/ppermute | solution.py:295
  42.7 0.8 %collective-permute-done.9 = bf16[160,256]{1,0:T(8,128)(2,1)S(1)} collective-permute-done((bf16[160,256]{1,0:T(8,128)(2,1)S(1)}, bf16[160,256]{1,0:T(8,128)(2,1)S(1)}, u32[]{:S(2)}, u32[]{:S(2)}) %collective-permute-start.9) | collective-permute-done | bytes 81952 | tf_op jit(solution)/shard_map/ppermute | solution.py:295
  43.5 1.6 %collective-permute-start.11 = (bf16[320,256]{1,0:T(8,128)(2,1)S(1)}, bf16[320,256]{1,0:T(8,128)(2,1)S(1)}, u32[]{:S(2)}, u32[]{:S(2)}) collective-permute-start(bf16[320,256]{1,0:T(8,128)(2,1)S(1)} %pad_maximum_fusion.3), channel_id=1, source_target_pairs={{0,4},{2,6},{4,0},{6,2},{8,12},{10,14},{12,8},{14,10},{16,20},{18,... | collective-permute-start | bytes 491528 | tf_op jit(solution)/shard_map/ppermute | solution.py:295
  45.1 0.6 %pad_maximum_fusion.11 = bf16[64,256]{1,0:T(8,128)(2,1)} fusion(bf16[24,256]{1,0:T(8,128)(2,1)S(1)} %constant_dynamic-slice_fusion, bf16[40,256]{1,0:T(8,128)(2,1)S(1)} %constant_dynamic-slice_fusion.1), kind=kLoop, calls=%fused_computation.31 | loop fusion | flops 65536 | bytes 65536 | tf_op jit(solution)/shard_map/concatenate | solution.py:341
  45.7 1.1 %collective-permute-start.10 = (bf16[192,256]{1,0:T(8,128)(2,1)S(1)}, bf16[192,256]{1,0:T(8,128)(2,1)S(1)}, u32[]{:S(2)}, u32[]{:S(2)}) collective-permute-start(bf16[192,256]{1,0:T(8,128)(2,1)S(1)} %pad_maximum_fusion.4), channel_id=1, source_target_pairs={{0,4},{2,6},{4,0},{6,2},{8,12},{10,14},{12,8},{14,10},{16,20},{18,... | collective-permute-start | bytes 294920 | tf_op jit(solution)/shard_map/ppermute | solution.py:295
  46.8 2.1 %collective-permute-done.11 = bf16[320,256]{1,0:T(8,128)(2,1)S(1)} collective-permute-done((bf16[320,256]{1,0:T(8,128)(2,1)S(1)}, bf16[320,256]{1,0:T(8,128)(2,1)S(1)}, u32[]{:S(2)}, u32[]{:S(2)}) %collective-permute-start.11) | collective-permute-done | bytes 163872 | tf_op jit(solution)/shard_map/ppermute | solution.py:295
  49.0 1.4 %collective-permute-done.10 = bf16[192,256]{1,0:T(8,128)(2,1)S(1)} collective-permute-done((bf16[192,256]{1,0:T(8,128)(2,1)S(1)}, bf16[192,256]{1,0:T(8,128)(2,1)S(1)}, u32[]{:S(2)}, u32[]{:S(2)}) %collective-permute-start.10) | collective-permute-done | bytes 98336 | tf_op jit(solution)/shard_map/ppermute | solution.py:295
  50.6 0.1 add.234.refs_0_
  50.7 0.1 add.238.refs_1_
  50.8 1.1 %collective-permute-done.13.refs_5_ = bf16[384,256]{1,0:T(8,128)(2,1)S(1)} collective-permute-done((bf16[384,256]{1,0:T(8,128)(2,1)S(1)}, bf16[384,256]{1,0:T(8,128)(2,1)S(1)}, u32[]{:S(2)}, u32[]{:S(2)}) %collective-permute-start.13) | collective-permute-done | bytes 196640 | tf_op jit(solution)/shard_map/ppermute | solution.py:295
  51.9 3.4 %attend.1 = bf16[64,2048]{1,0:T(8,128)(2,1)} custom-call(s32[3]{0:T(128)S(1)} %pad_add_fusion.span_ref, bf16[1024,128]{1,0:T(8,128)(2,1)S(1)} %pad_maximum_fusion.1.query_ref, s32[1,1280]{1,0:T(1,128)S(1)} %add.234.refs_0_, s32[1,768]{1,0:T(1,128)S(1)} %add.238.refs_1_, bf16[640,256]{1,0:T(8,128)(2,1)S(1)} %pad_maximum_fusion.refs_2_, ...), custom_call_target="tpu_custom_call" | custom-call | flops 1073741824 | bytes 1572864 | tf_op jit(solution)/shard_map/attend/pallas_call | solution.py:124
  (61 shorter events, 1.1 us)
Async XLA Ops:
  0.6 1.6 %copy-start = (bf16[64,16384]{1,0:T(8,128)(2,1)S(1)}, bf16[64,16384]{1,0:T(8,128)(2,1)}, u32[]{:S(2)}) copy-start(bf16[64,16384]{1,0:T(8,128)(2,1)} %param.5) | copy-start | bytes 6291460
  2.9 10.2 %collective-permute-start = (bf16[8,8192]{1,0:T(8,128)(2,1)}, bf16[8,8192]{1,0:T(8,128)(2,1)S(1)}, u32[]{:S(2)}, u32[]{:S(2)}) collective-permute-start(bf16[8,8192]{1,0:T(8,128)(2,1)} %constant_dynamic-slice_fusion.2), channel_id=1, source_target_pairs={{0,1},{1,0},{2,3},{3,2},{4,5},{5,4},{6,7},{7,6},{8,9},{9,8},{10,11... | collective-permute-start | bytes 393224 | tf_op jit(solution)/shard_map/ppermute | solution.py:186
  5.9 15.7 %collective-permute-start.1 = (bf16[32,8192]{1,0:T(8,128)(2,1)S(1)}, bf16[32,8192]{1,0:T(8,128)(2,1)S(1)}, u32[]{:S(2)}, u32[]{:S(2)}) collective-permute-start(bf16[32,8192]{1,0:T(8,128)(2,1)S(1)} %constant_dynamic-slice_fusion.5), channel_id=1, source_target_pairs={{0,1},{1,0},{2,3},{3,2},{4,5},{5,4},{6,7},{7,6},{8,9},{9,8},{10,11... | collective-permute-start | bytes 1572872 | tf_op jit(solution)/shard_map/ppermute | solution.py:186
  6.7 20.5 %collective-permute-start.3 = (bf16[16,8192]{1,0:T(8,128)(2,1)}, bf16[16,8192]{1,0:T(8,128)(2,1)S(1)}, u32[]{:S(2)}, u32[]{:S(2)}) collective-permute-start(bf16[16,8192]{1,0:T(8,128)(2,1)} %constant_dynamic-slice_fusion.4), channel_id=1, source_target_pairs={{0,1},{1,0},{2,3},{3,2},{4,5},{5,4},{6,7},{7,6},{8,9},{9,8},{10,11... | collective-permute-start | bytes 786440 | tf_op jit(solution)/shard_map/ppermute | solution.py:186
  9.3 2.2 %copy-start.3 = (bf16[8192,128]{1,0:T(8,128)(2,1)S(1)}, bf16[8192,128]{1,0:T(8,128)(2,1)}, u32[]{:S(2)}) copy-start(bf16[8192,128]{1,0:T(8,128)(2,1)} %param.8) | copy-start | bytes 6291460
  13.0 2.2 %copy-start.4 = (bf16[8192,128]{1,0:T(8,128)(2,1)S(1)}, bf16[8192,128]{1,0:T(8,128)(2,1)}, u32[]{:S(2)}) copy-start(bf16[8192,128]{1,0:T(8,128)(2,1)} %param.8) | copy-start | bytes 6291460
  13.0 8.6 %copy-start.1 = (bf16[8192,128]{1,0:T(8,128)(2,1)S(1)}, bf16[8192,128]{1,0:T(8,128)(2,1)}, u32[]{:S(2)}) copy-start(bf16[8192,128]{1,0:T(8,128)(2,1)} %param.7) | copy-start | bytes 6291460
  15.6 6.9 %copy-start.7 = (f32[64,256]{1,0:T(8,128)S(1)}, f32[64,256]{1,0:T(8,128)}, u32[]{:S(2)}) copy-start(f32[64,256]{1,0:T(8,128)} %pad_maximum_fusion.7) | copy-start | bytes 196612
  22.0 2.7 %copy-start.6 = (bf16[64,2048]{1,0:T(8,128)(2,1)S(1)}, bf16[64,2048]{1,0:T(8,128)(2,1)}, u32[]{:S(2)}) copy-start(bf16[64,2048]{1,0:T(8,128)(2,1)} %param.6) | copy-start | bytes 786436
  22.5 3.4 %copy-start.8 = (bf16[8,8192]{1,0:T(8,128)(2,1)S(1)}, bf16[8,8192]{1,0:T(8,128)(2,1)}, u32[]{:S(2)}) copy-start(bf16[8,8192]{1,0:T(8,128)(2,1)} %constant_dynamic-slice_fusion.3) | copy-start | bytes 393220
  22.6 6.6 %copy-start.2 = (bf16[8192,128]{1,0:T(8,128)(2,1)S(1)}, bf16[8192,128]{1,0:T(8,128)(2,1)}, u32[]{:S(2)}) copy-start(bf16[8192,128]{1,0:T(8,128)(2,1)} %param.7) | copy-start | bytes 6291460
  22.6 6.4 %collective-permute-start.2 = (f32[80,256]{1,0:T(8,128)S(1)}, f32[80,256]{1,0:T(8,128)S(1)}, u32[]{:S(2)}, u32[]{:S(2)}) collective-permute-start(f32[80,256]{1,0:T(8,128)S(1)} %pad_maximum_fusion.5), channel_id=1, source_target_pairs={{0,1},{1,0},{2,3},{3,2},{4,5},{5,4},{6,7},{7,6},{8,9},{9,8},{10,11... | collective-permute-start | bytes 245768 | tf_op jit(solution)/shard_map/ppermute | solution.py:273
  25.5 4.1 %copy-start.5 = (bf16[8192,128]{1,0:T(8,128)(2,1)S(1)}, bf16[8192,128]{1,0:T(8,128)(2,1)}, u32[]{:S(2)}) copy-start(bf16[8192,128]{1,0:T(8,128)(2,1)} %param.8) | copy-start | bytes 6291460
  25.9 5.0 %collective-permute-start.4 = (bf16[8,8192]{1,0:T(8,128)(2,1)S(1)}, bf16[8,8192]{1,0:T(8,128)(2,1)S(1)}, u32[]{:S(2)}, u32[]{:S(2)}) collective-permute-start(bf16[8,8192]{1,0:T(8,128)(2,1)S(1)} %copy-done.8), channel_id=1, source_target_pairs={{0,1},{1,0},{2,3},{3,2},{4,5},{5,4},{6,7},{7,6},{8,9},{9,8},{10,11... | collective-permute-start | bytes 393224 | tf_op jit(solution)/shard_map/ppermute | solution.py:186
  30.0 1.7 %slice-start = ((f32[64,256]{1,0:T(8,128)}), f32[24,256]{1,0:T(8,128)S(1)}, s32[]{:S(2)}) async-start(f32[64,256]{1,0:T(8,128)} %pad_maximum_fusion.7), calls=%async_computation | async-start | bytes 49152 | tf_op jit(solution)/shard_map/slice | solution.py:299
  31.3 19.2 %copy-start.9 = (s32[16]{0:T(128)S(1)}, s32[16]{0:T(128)}, u32[]{:S(2)}) copy-start(s32[16]{0:T(128)} %constant.47.clone) | copy-start | bytes 196
  31.8 4.4 %collective-permute-start.5 = (f32[48,256]{1,0:T(8,128)S(1)}, f32[48,256]{1,0:T(8,128)S(1)}, u32[]{:S(2)}, u32[]{:S(2)}) collective-permute-start(f32[48,256]{1,0:T(8,128)S(1)} %pad_maximum_fusion.8), channel_id=1, source_target_pairs={{0,1},{1,0},{2,3},{3,2},{4,5},{5,4},{6,7},{7,6},{8,9},{9,8},{10,11... | collective-permute-start | bytes 147464 | tf_op jit(solution)/shard_map/ppermute | solution.py:273
  33.6 5.4 %collective-permute-start.7 = (bf16[80,256]{1,0:T(8,128)(2,1)S(1)}, bf16[80,256]{1,0:T(8,128)(2,1)S(1)}, u32[]{:S(2)}, u32[]{:S(2)}) collective-permute-start(bf16[80,256]{1,0:T(8,128)(2,1)S(1)} %pad_maximum_fusion.10), channel_id=1, source_target_pairs={{0,16},{2,18},{4,20},{6,22},{8,24},{10,26},{12,28},{14,30},{16,0},... | collective-permute-start | bytes 122888 | tf_op jit(solution)/shard_map/ppermute | solution.py:295
  36.3 4.7 %collective-permute-start.6 = (bf16[48,256]{1,0:T(8,128)(2,1)S(1)}, bf16[48,256]{1,0:T(8,128)(2,1)S(1)}, u32[]{:S(2)}, u32[]{:S(2)}) collective-permute-start(bf16[48,256]{1,0:T(8,128)(2,1)S(1)} %pad_maximum_fusion.12), channel_id=1, source_target_pairs={{0,16},{2,18},{4,20},{6,22},{8,24},{10,26},{12,28},{14,30},{16,0},... | collective-permute-start | bytes 73736 | tf_op jit(solution)/shard_map/ppermute | solution.py:295
  39.0 4.5 %collective-permute-start.9 = (bf16[160,256]{1,0:T(8,128)(2,1)S(1)}, bf16[160,256]{1,0:T(8,128)(2,1)S(1)}, u32[]{:S(2)}, u32[]{:S(2)}) collective-permute-start(bf16[160,256]{1,0:T(8,128)(2,1)S(1)} %pad_maximum_fusion.6), channel_id=1, source_target_pairs={{0,8},{2,10},{4,12},{6,14},{8,0},{10,2},{12,4},{14,6},{16,24},{18,... | collective-permute-start | bytes 245768 | tf_op jit(solution)/shard_map/ppermute | solution.py:295
  41.1 4.6 %collective-permute-start.8 = (bf16[96,256]{1,0:T(8,128)(2,1)S(1)}, bf16[96,256]{1,0:T(8,128)(2,1)S(1)}, u32[]{:S(2)}, u32[]{:S(2)}) collective-permute-start(bf16[96,256]{1,0:T(8,128)(2,1)S(1)} %pad_maximum_fusion.9), channel_id=1, source_target_pairs={{0,8},{2,10},{4,12},{6,14},{8,0},{10,2},{12,4},{14,6},{16,24},{18,... | collective-permute-start | bytes 147464 | tf_op jit(solution)/shard_map/ppermute | solution.py:295
  43.5 5.4 %collective-permute-start.11 = (bf16[320,256]{1,0:T(8,128)(2,1)S(1)}, bf16[320,256]{1,0:T(8,128)(2,1)S(1)}, u32[]{:S(2)}, u32[]{:S(2)}) collective-permute-start(bf16[320,256]{1,0:T(8,128)(2,1)S(1)} %pad_maximum_fusion.3), channel_id=1, source_target_pairs={{0,4},{2,6},{4,0},{6,2},{8,12},{10,14},{12,8},{14,10},{16,20},{18,... | collective-permute-start | bytes 491528 | tf_op jit(solution)/shard_map/ppermute | solution.py:295
  45.7 4.7 %collective-permute-start.10 = (bf16[192,256]{1,0:T(8,128)(2,1)S(1)}, bf16[192,256]{1,0:T(8,128)(2,1)S(1)}, u32[]{:S(2)}, u32[]{:S(2)}) collective-permute-start(bf16[192,256]{1,0:T(8,128)(2,1)S(1)} %pad_maximum_fusion.4), channel_id=1, source_target_pairs={{0,4},{2,6},{4,0},{6,2},{8,12},{10,14},{12,8},{14,10},{16,20},{18,... | collective-permute-start | bytes 294920 | tf_op jit(solution)/shard_map/ppermute | solution.py:295
  48.9 3.0 %collective-permute-start.12 = (bf16[640,256]{1,0:T(8,128)(2,1)S(1)}, bf16[640,256]{1,0:T(8,128)(2,1)S(1)}, u32[]{:S(2)}, u32[]{:S(2)}) collective-permute-start(bf16[640,256]{1,0:T(8,128)(2,1)S(1)} %pad_maximum_fusion.refs_2_), channel_id=1, source_target_pairs={{0,2},{2,0},{4,6},{6,4},{8,10},{10,8},{12,14},{14,12},{16,18},{18,... | collective-permute-start | bytes 983048 | tf_op jit(solution)/shard_map/ppermute | solution.py:295
  50.4 1.5 %collective-permute-start.13 = (bf16[384,256]{1,0:T(8,128)(2,1)S(1)}, bf16[384,256]{1,0:T(8,128)(2,1)S(1)}, u32[]{:S(2)}, u32[]{:S(2)}) collective-permute-start(bf16[384,256]{1,0:T(8,128)(2,1)S(1)} %pad_maximum_fusion.2.refs_4_), channel_id=1, source_target_pairs={{0,2},{2,0},{4,6},{6,4},{8,10},{10,8},{12,14},{14,12},{16,18},{18,... | collective-permute-start | bytes 589832 | tf_op jit(solution)/shard_map/ppermute | solution.py:295
